TPU v7x, 32 devices: a whole 2x2x4 slice. The times are simulated.
32 devices in a mesh: orb: 4 (over x, core), sx: 2 (over y), sy: 4 (over z).
Axes of the slice: x: 2, y: 2, z: 4, core: 2. Of those that a mesh axis runs over, the one named last changes fastest.
Arguments:
- orbitals: bfloat16 [16, 32, 8192], P('sx', 'sy', 'orb'), may hold values from -6 to 6
- src_owner: int32 [2, 2], replicated, may hold values from 0 to 3
- src_slot: int32 [2, 2], replicated, may hold values from 0 to 63
Outputs:
- exchange_field: float32 [16, 32, 8192], P('sx', 'sy', 'orb')
All inputs are finite; a program needn't handle non-finite values.
Results may differ from a plain program's by a relative error of at most 0.0003.
Values may be sent and summed in bfloat16 or wider, within the bound.
No kernel may reach another device: no remote copies, remote signals or barrier semaphores. Data moves between devices by JAX's collectives and lax.ppermute only.
A program may use at most 128 MiB of HBM per device.

v0:
```python
import jax
import jax.numpy as jnp
from jax import lax
from jax.sharding import PartitionSpec as P

NZ = 32
SRC = 2
ROUNDS = 2
DEGREE = 4


cheb_coeffs = (
    1.021021021021021,
    -1.7357357357357357,
    1.4753753753753753,
    -1.254069069069069,
    1.0659587087087088,
)


def extended(block, sides, width):
    for axis, dim in sides:
        count = lax.axis_size(axis)
        forward = [(i, i + 1) for i in range(count - 1)]
        forward.append((count - 1, 0))
        backward = [(target, source) for source, target in forward]
        low = lax.ppermute(
            lax.slice_in_dim(block, block.shape[dim] - width, None, axis=dim), axis, forward
        )
        high = lax.ppermute(lax.slice_in_dim(block, 0, width, axis=dim), axis, backward)
        block = jnp.concatenate([low, block, high], axis=dim)
    return block


def spread_2(block, axis, owner):
    block = jnp.where(lax.axis_index(axis) == owner, block, jnp.zeros_like(block))
    return lax.psum(block, axis)


def crop(field, margin):
    return field[margin : field.shape[0] - margin, margin : field.shape[1] - margin]


def screened(padded):
    core = crop(padded, 1)
    side = padded[2:, 1:-1] + padded[:-2, 1:-1]
    side = side + padded[1:-1, 2:] + padded[1:-1, :-2]
    lane = lax.broadcasted_iota(jnp.int32, core.shape, 2) % NZ
    zeros = jnp.zeros(core.shape[:2] + (1,), core.dtype)
    upper = jnp.where(lane == NZ - 1, 0.0, jnp.concatenate([core[..., 1:], zeros], axis=2))
    lower = jnp.where(lane == 0, 0.0, jnp.concatenate([zeros, core[..., :-1]], axis=2))
    side = side + upper + lower
    return -side / 6.0


def widen_one(field):
    return extended(field, (("sx", 0), ("sy", 1)), 1)


def potential(density):
    t_prev = density
    t_cur = screened(widen_one(density))
    total = cheb_coeffs[0] * t_prev + cheb_coeffs[1] * t_cur
    for order in range(2, DEGREE + 1):
        t_next = 2.0 * screened(widen_one(t_cur)) - t_prev
        total = total + cheb_coeffs[order] * t_next
        t_prev, t_cur = (t_cur, t_next)
    return total


def own_block(orbitals, slot):
    rows_x, rows_y, _ = orbitals.shape
    block = lax.dynamic_slice_in_dim(orbitals, slot * NZ, NZ, 2)
    return block.reshape(rows_x, rows_y * NZ)


def fetch_single(orbitals, owner, slot):
    rows_x, rows_y, _ = orbitals.shape
    got = spread_2(own_block(orbitals, slot), "orb", owner)
    return got.reshape(rows_x, rows_y, NZ)


def fetch_sources(orbitals, src_owner, src_slot, rnd):
    return [
        fetch_single(orbitals, src_owner[rnd, place], src_slot[rnd, place]) for place in range(SRC)
    ]


def body(orbitals, src_owner, src_slot):
    rows_x, rows_y, width = orbitals.shape
    held = width // NZ
    exchange_field = jnp.zeros(orbitals.shape, jnp.float32)
    own = orbitals.astype(jnp.float32)
    for rnd in range(ROUNDS):
        sources = fetch_sources(orbitals, src_owner, src_slot, rnd)
        tiled = [jnp.tile(source.astype(jnp.float32), (1, 1, held)) for source in sources]
        density = jnp.concatenate([own * spread for spread in tiled], axis=2)
        total = potential(density)
        for place in range(SRC):
            exchange_field = (
                exchange_field - total[..., place * width : (place + 1) * width] * tiled[place]
            )
    return exchange_field


def solution(mesh):
    in_specs = (P("sx", "sy", "orb"), P(), P())
    out_specs = P("sx", "sy", "orb")
    return jax.shard_map(body, mesh=mesh, in_specs=in_specs, out_specs=out_specs, check_vma=False)
```

profile of v0, /device:TPU:30, one launch (start us, length us, event | category | flops | bytes accessed | tf_op | source)
XLA Modules:
  0.0 117.5 jit_solution(2591254254019798334)
XLA Ops:
  0.0 1.5 %fusion.111 = (s32[1,1]{1,0:T(1,128)}, s32[1,1]{1,0:T(1,128)}, s32[1,1]{1,0:T(1,128)}, s32[1,1]{1,0:T(1,128)}) fusion(s32[2,2]{1,0:T(2,128)} %param.5), kind=kLoop, calls=%fused_computation.242 | loop fusion | bytes 32 | tf_op jit(solution)/shard_map/slice | solution.py:85
  4.0 1.5 %fusion.110 = (s32[1,1]{1,0:T(1,128)}, s32[1,1]{1,0:T(1,128)}, s32[1,1]{1,0:T(1,128)}, s32[1,1]{1,0:T(1,128)}) fusion(s32[2,2]{1,0:T(2,128)} %param.4), kind=kLoop, calls=%fused_computation.241 | loop fusion | bytes 32 | tf_op jit(solution)/shard_map/slice | solution.py:85
  8.9 11.0 %all-reduce.16 = (bf16[8,8,32]{2,1,0:T(8,128)(2,1)S(1)}, bf16[8,8,32]{2,1,0:T(8,128)(2,1)S(1)}, bf16[8,8,32]{2,1,0:T(8,128)(2,1)S(1)}, bf16[8,8,32]{2,1,0:T(8,128)(2,1)S(1)}) all-reduce(bf16[8,8,32]{2,1,0:T(8,128)(2,1)S(1)} %get-tuple-element.67, ...), channel_id=1, replica_groups=mesh['orb'=4,'sx'=2,'sy'=4] {'orb'}, use_global_device_ids=true, to_apply=%region_0.1 | all-reduce | flops 8192 | bytes 32768 | tf_op jit(solution)/shard_map/psum | solution.py:37
  22.3 1.7 %tile.41 = f32[8,8,2048]{2,1,0:T(8,128)} reshape(f32[8,8,64,32]{3,2,1,0:T(8,128)S(1)} %tile.40) | data formatting | bytes 1048576 | tf_op jit(solution)/shard_map/tile | solution.py:96
  24.1 1.8 %tile.17 = f32[8,8,2048]{2,1,0:T(8,128)} reshape(f32[8,8,64,32]{3,2,1,0:T(8,128)S(1)} %tile.16) | data formatting | bytes 1048576 | tf_op jit(solution)/shard_map/tile | solution.py:96
  25.9 1.4 %convert_multiply_fusion.2 = (f32[8,8,2048]{2,1,0:T(8,128)S(1)}, f32[8,8,2048]{2,1,0:T(8,128)S(1)}, f32[8,8,2048]{2,1,0:T(8,128)S(1)}, f32[8,8,2048]{2,1,0:T(8,128)S(1)}) fusion(f32[8,8,2048]{2,1,0:T(8,128)S(1)} %tile.19, bf16[8,8,2048]{2,1,0:T(8,128)(2,1)S(1)} %copy-done.2, f32[8,8,2048]{2,1,0:T(8,128)} %tile.41, f32[8,8,2048]{2,1,0:T(8,128)S(1)} %tile.43, ...), kind=kLoop, calls=%fused_computation.178 | loop fusion | flops 655360 | bytes 4456448 | tf_op jit(solution)/shard_map/mul | solution.py:97
  27.9 1.5 %collective-permute-start.17 = (f32[1,8,4096]{2,1,0:T(8,128)S(1)}, f32[1,8,4096]{2,1,0:T(8,128)S(1)}, u32[]{:S(2)}, u32[]{:S(2)}) collective-permute-start(f32[1,8,4096]{2,1,0:T(8,128)S(1)} %get-tuple-element.57), channel_id=1, source_target_pairs={{0,4},{4,0},{1,5},{5,1},{2,6},{6,2},{3,7},{7,3},{8,12},{12,8},{9,1... | collective-permute-start | bytes 393224 | tf_op jit(solution)/shard_map/ppermute | solution.py:27
  30.0 1.5 %collective-permute-start.1 = (f32[1,8,4096]{2,1,0:T(8,128)S(1)}, f32[1,8,4096]{2,1,0:T(8,128)S(1)}, u32[]{:S(2)}, u32[]{:S(2)}) collective-permute-start(f32[1,8,4096]{2,1,0:T(8,128)S(1)} %get-tuple-element.41), channel_id=1, source_target_pairs={{0,4},{4,0},{1,5},{5,1},{2,6},{6,2},{3,7},{7,3},{8,12},{12,8},{9,1... | collective-permute-start | bytes 393224 | tf_op jit(solution)/shard_map/ppermute | solution.py:27
  32.3 1.4 %collective-permute-done.16 = f32[1,8,4096]{2,1,0:T(8,128)S(1)} collective-permute-done((f32[1,8,4096]{2,1,0:T(8,128)S(1)}, f32[1,8,4096]{2,1,0:T(8,128)S(1)}, u32[]{:S(2)}, u32[]{:S(2)}) %collective-permute-start.16) | collective-permute-done | bytes 131104 | tf_op jit(solution)/shard_map/ppermute | solution.py:30
  33.8 2.8 %collective-permute-done.17 = f32[1,8,4096]{2,1,0:T(8,128)S(1)} collective-permute-done((f32[1,8,4096]{2,1,0:T(8,128)S(1)}, f32[1,8,4096]{2,1,0:T(8,128)S(1)}, u32[]{:S(2)}, u32[]{:S(2)}) %collective-permute-start.17) | collective-permute-done | bytes 131104 | tf_op jit(solution)/shard_map/ppermute | solution.py:27
  37.1 1.8 %collective-permute-start.18 = (f32[10,1,4096]{2,1,0:T(1,128)S(1)}, f32[10,1,4096]{2,1,0:T(1,128)S(1)}, u32[]{:S(2)}, u32[]{:S(2)}) collective-permute-start(f32[10,1,4096]{2,1,0:T(1,128)S(1)} %get-tuple-element.27), channel_id=1, source_target_pairs={{1,0},{2,1},{3,2},{0,3},{5,4},{6,5},{7,6},{4,7},{9,8},{10,9},{11,1... | collective-permute-start | bytes 491528 | tf_op jit(solution)/shard_map/ppermute | solution.py:30
  39.4 2.0 %collective-permute-done.1 = f32[1,8,4096]{2,1,0:T(8,128)S(1)} collective-permute-done((f32[1,8,4096]{2,1,0:T(8,128)S(1)}, f32[1,8,4096]{2,1,0:T(8,128)S(1)}, u32[]{:S(2)}, u32[]{:S(2)}) %collective-permute-start.1) | collective-permute-done | bytes 131104 | tf_op jit(solution)/shard_map/ppermute | solution.py:27
  41.9 1.8 %collective-permute-start.2 = (f32[10,1,4096]{2,1,0:T(1,128)S(1)}, f32[10,1,4096]{2,1,0:T(1,128)S(1)}, u32[]{:S(2)}, u32[]{:S(2)}) collective-permute-start(f32[10,1,4096]{2,1,0:T(1,128)S(1)} %get-tuple-element.19), channel_id=1, source_target_pairs={{1,0},{2,1},{3,2},{0,3},{5,4},{6,5},{7,6},{4,7},{9,8},{10,9},{11,1... | collective-permute-start | bytes 491528 | tf_op jit(solution)/shard_map/ppermute | solution.py:30
  43.7 3.0 %collective-permute-done.18 = f32[10,1,4096]{2,1,0:T(1,128)S(1)} collective-permute-done((f32[10,1,4096]{2,1,0:T(1,128)S(1)}, f32[10,1,4096]{2,1,0:T(1,128)S(1)}, u32[]{:S(2)}, u32[]{:S(2)}) %collective-permute-start.18) | collective-permute-done | bytes 163872 | tf_op jit(solution)/shard_map/ppermute | solution.py:30
  48.4 1.5 %collective-permute-start.21 = (f32[1,8,4096]{2,1,0:T(8,128)S(1)}, f32[1,8,4096]{2,1,0:T(8,128)S(1)}, u32[]{:S(2)}, u32[]{:S(2)}) collective-permute-start(f32[1,8,4096]{2,1,0:T(8,128)S(1)} %get-tuple-element.55), channel_id=1, source_target_pairs={{0,4},{4,0},{1,5},{5,1},{2,6},{6,2},{3,7},{7,3},{8,12},{12,8},{9,1... | collective-permute-start | bytes 393224 | tf_op jit(solution)/shard_map/ppermute | solution.py:27
  50.0 2.3 %collective-permute-done.3 = f32[10,1,4096]{2,1,0:T(1,128)S(1)} collective-permute-done((f32[10,1,4096]{2,1,0:T(1,128)S(1)}, f32[10,1,4096]{2,1,0:T(1,128)S(1)}, u32[]{:S(2)}, u32[]{:S(2)}) %collective-permute-start.3) | collective-permute-done | bytes 163872 | tf_op jit(solution)/shard_map/ppermute | solution.py:27
  53.9 1.5 %collective-permute-start.5 = (f32[1,8,4096]{2,1,0:T(8,128)S(1)}, f32[1,8,4096]{2,1,0:T(8,128)S(1)}, u32[]{:S(2)}, u32[]{:S(2)}) collective-permute-start(f32[1,8,4096]{2,1,0:T(8,128)S(1)} %get-tuple-element.39), channel_id=1, source_target_pairs={{0,4},{4,0},{1,5},{5,1},{2,6},{6,2},{3,7},{7,3},{8,12},{12,8},{9,1... | collective-permute-start | bytes 393224 | tf_op jit(solution)/shard_map/ppermute | solution.py:27
  55.7 3.3 %collective-permute-start.23 = (f32[10,1,4096]{2,1,0:T(1,128)S(1)}, f32[10,1,4096]{2,1,0:T(1,128)S(1)}, u32[]{:S(2)}, u32[]{:S(2)}) collective-permute-start(f32[10,1,4096]{2,1,0:T(1,128)S(1)} %get-tuple-element.26), channel_id=1, source_target_pairs={{0,1},{1,2},{2,3},{3,0},{4,5},{5,6},{6,7},{7,4},{8,9},{9,10},{10,1... | collective-permute-start | bytes 491528 | tf_op jit(solution)/shard_map/ppermute | solution.py:27
  60.2 3.4 %collective-permute-start.7 = (f32[10,1,4096]{2,1,0:T(1,128)S(1)}, f32[10,1,4096]{2,1,0:T(1,128)S(1)}, u32[]{:S(2)}, u32[]{:S(2)}) collective-permute-start(f32[10,1,4096]{2,1,0:T(1,128)S(1)} %get-tuple-element.18), channel_id=1, source_target_pairs={{0,1},{1,2},{2,3},{3,0},{4,5},{5,6},{6,7},{7,4},{8,9},{9,10},{10,1... | collective-permute-start | bytes 491528 | tf_op jit(solution)/shard_map/ppermute | solution.py:27
  64.1 6.0 %collective-permute-done.22 = f32[10,1,4096]{2,1,0:T(1,128)S(1)} collective-permute-done((f32[10,1,4096]{2,1,0:T(1,128)S(1)}, f32[10,1,4096]{2,1,0:T(1,128)S(1)}, u32[]{:S(2)}, u32[]{:S(2)}) %collective-permute-start.22) | collective-permute-done | bytes 163872 | tf_op jit(solution)/shard_map/ppermute | solution.py:30
  71.9 1.4 %collective-permute-start.25 = (f32[1,8,4096]{2,1,0:T(8,128)S(1)}, f32[1,8,4096]{2,1,0:T(8,128)S(1)}, u32[]{:S(2)}, u32[]{:S(2)}) collective-permute-start(f32[1,8,4096]{2,1,0:T(8,128)S(1)} %get-tuple-element.51), channel_id=1, source_target_pairs={{0,4},{4,0},{1,5},{5,1},{2,6},{6,2},{3,7},{7,3},{8,12},{12,8},{9,1... | collective-permute-start | bytes 393224 | tf_op jit(solution)/shard_map/ppermute | solution.py:27
  75.8 1.5 %collective-permute-start.9 = (f32[1,8,4096]{2,1,0:T(8,128)S(1)}, f32[1,8,4096]{2,1,0:T(8,128)S(1)}, u32[]{:S(2)}, u32[]{:S(2)}) collective-permute-start(f32[1,8,4096]{2,1,0:T(8,128)S(1)} %get-tuple-element.35), channel_id=1, source_target_pairs={{0,4},{4,0},{1,5},{5,1},{2,6},{6,2},{3,7},{7,3},{8,12},{12,8},{9,1... | collective-permute-start | bytes 393224 | tf_op jit(solution)/shard_map/ppermute | solution.py:27
  77.7 2.6 %collective-permute-done.25 = f32[1,8,4096]{2,1,0:T(8,128)S(1)} collective-permute-done((f32[1,8,4096]{2,1,0:T(8,128)S(1)}, f32[1,8,4096]{2,1,0:T(8,128)S(1)}, u32[]{:S(2)}, u32[]{:S(2)}) %collective-permute-start.25) | collective-permute-done | bytes 131104 | tf_op jit(solution)/shard_map/ppermute | solution.py:27
  80.5 2.7 %collective-permute-start.27 = (f32[10,1,4096]{2,1,0:T(1,128)S(1)}, f32[10,1,4096]{2,1,0:T(1,128)S(1)}, u32[]{:S(2)}, u32[]{:S(2)}) collective-permute-start(f32[10,1,4096]{2,1,0:T(1,128)S(1)} %get-tuple-element.24), channel_id=1, source_target_pairs={{0,1},{1,2},{2,3},{3,0},{4,5},{5,6},{6,7},{7,4},{8,9},{9,10},{10,1... | collective-permute-start | bytes 491528 | tf_op jit(solution)/shard_map/ppermute | solution.py:27
  83.5 3.9 %collective-permute-start.11 = (f32[10,1,4096]{2,1,0:T(1,128)S(1)}, f32[10,1,4096]{2,1,0:T(1,128)S(1)}, u32[]{:S(2)}, u32[]{:S(2)}) collective-permute-start(f32[10,1,4096]{2,1,0:T(1,128)S(1)} %get-tuple-element.16), channel_id=1, source_target_pairs={{0,1},{1,2},{2,3},{3,0},{4,5},{5,6},{6,7},{7,4},{8,9},{9,10},{10,1... | collective-permute-start | bytes 491528 | tf_op jit(solution)/shard_map/ppermute | solution.py:27
  87.8 3.0 %collective-permute-done.26 = f32[10,1,4096]{2,1,0:T(1,128)S(1)} collective-permute-done((f32[10,1,4096]{2,1,0:T(1,128)S(1)}, f32[10,1,4096]{2,1,0:T(1,128)S(1)}, u32[]{:S(2)}, u32[]{:S(2)}) %collective-permute-start.26) | collective-permute-done | bytes 163872 | tf_op jit(solution)/shard_map/ppermute | solution.py:30
  99.1 1.4 %collective-permute-start.31 = (f32[10,1,4096]{2,1,0:T(1,128)S(1)}, f32[10,1,4096]{2,1,0:T(1,128)S(1)}, u32[]{:S(2)}, u32[]{:S(2)}) collective-permute-start(f32[10,1,4096]{2,1,0:T(1,128)S(1)} %get-tuple-element.22), channel_id=1, source_target_pairs={{0,1},{1,2},{2,3},{3,0},{4,5},{5,6},{6,7},{7,4},{8,9},{9,10},{10,1... | collective-permute-start | bytes 491528 | tf_op jit(solution)/shard_map/ppermute | solution.py:27
  102.4 2.4 %collective-permute-start.15 = (f32[10,1,4096]{2,1,0:T(1,128)S(1)}, f32[10,1,4096]{2,1,0:T(1,128)S(1)}, u32[]{:S(2)}, u32[]{:S(2)}) collective-permute-start(f32[10,1,4096]{2,1,0:T(1,128)S(1)} %get-tuple-element.14), channel_id=1, source_target_pairs={{0,1},{1,2},{2,3},{3,0},{4,5},{5,6},{6,7},{7,4},{8,9},{9,10},{10,1... | collective-permute-start | bytes 491528 | tf_op jit(solution)/shard_map/ppermute | solution.py:27
  105.1 6.3 %collective-permute-done.30 = f32[10,1,4096]{2,1,0:T(1,128)S(1)} collective-permute-done((f32[10,1,4096]{2,1,0:T(1,128)S(1)}, f32[10,1,4096]{2,1,0:T(1,128)S(1)}, u32[]{:S(2)}, u32[]{:S(2)}) %collective-permute-start.30) | collective-permute-done | bytes 163872 | tf_op jit(solution)/shard_map/ppermute | solution.py:30
  111.4 1.5 %fusion.47 = f32[8,8,4096]{2,1,0:T(8,128)S(1)} fusion(f32[8,8,4096]{2,1,0:T(8,128)S(1)} %fusion.37, f32[10,1,4096]{2,1,0:T(1,128)S(1)} %collective-permute-done.31, f32[1,8,4096]{2,1,0:T(8,128)S(1)} %collective-permute-done.28, f32[8,8,4096]{2,1,0:T(8,128)S(1)} %fusion.41, f32[1,8,4096]{2,1,0:T(8,128)S(1)} %collective-permute-done.29, ...), kind=kLoop, calls=%fused_computation.67 | loop fusion | flops 8126464 | bytes 7966208 | tf_op jit(solution)/shard_map/add | solution.py:66
  112.9 2.0 %collective-permute-done.14 = f32[10,1,4096]{2,1,0:T(1,128)S(1)} collective-permute-done((f32[10,1,4096]{2,1,0:T(1,128)S(1)}, f32[10,1,4096]{2,1,0:T(1,128)S(1)}, u32[]{:S(2)}, u32[]{:S(2)}) %collective-permute-start.14) | collective-permute-done | bytes 163872 | tf_op jit(solution)/shard_map/ppermute | solution.py:30
  114.9 1.5 %fusion.31 = f32[8,8,4096]{2,1,0:T(8,128)S(1)} fusion(f32[8,8,4096]{2,1,0:T(8,128)S(1)} %fusion.21, f32[10,1,4096]{2,1,0:T(1,128)S(1)} %collective-permute-done.15, f32[1,8,4096]{2,1,0:T(8,128)S(1)} %collective-permute-done.12, f32[8,8,4096]{2,1,0:T(8,128)S(1)} %fusion.25, f32[1,8,4096]{2,1,0:T(8,128)S(1)} %collective-permute-done.13, ...), kind=kLoop, calls=%fused_computation.51 | loop fusion | flops 8126464 | bytes 7966208 | tf_op jit(solution)/shard_map/add | solution.py:66
  (86 shorter events, 29.5 us)
Async XLA Ops:
  27.4 6.4 %collective-permute-start.16 = (f32[1,8,4096]{2,1,0:T(8,128)S(1)}, f32[1,8,4096]{2,1,0:T(8,128)S(1)}, u32[]{:S(2)}, u32[]{:S(2)}) collective-permute-start(f32[1,8,4096]{2,1,0:T(8,128)S(1)} %get-tuple-element.58), channel_id=1, source_target_pairs={{4,0},{0,4},{5,1},{1,5},{6,2},{2,6},{7,3},{3,7},{12,8},{8,12},{13,... | collective-permute-start | bytes 393224 | tf_op jit(solution)/shard_map/ppermute | solution.py:30
  27.9 8.7 %collective-permute-start.17 = (f32[1,8,4096]{2,1,0:T(8,128)S(1)}, f32[1,8,4096]{2,1,0:T(8,128)S(1)}, u32[]{:S(2)}, u32[]{:S(2)}) collective-permute-start(f32[1,8,4096]{2,1,0:T(8,128)S(1)} %get-tuple-element.57), channel_id=1, source_target_pairs={{0,4},{4,0},{1,5},{5,1},{2,6},{6,2},{3,7},{7,3},{8,12},{12,8},{9,1... | collective-permute-start | bytes 393224 | tf_op jit(solution)/shard_map/ppermute | solution.py:27
  29.5 9.9 %collective-permute-start = (f32[1,8,4096]{2,1,0:T(8,128)S(1)}, f32[1,8,4096]{2,1,0:T(8,128)S(1)}, u32[]{:S(2)}, u32[]{:S(2)}) collective-permute-start(f32[1,8,4096]{2,1,0:T(8,128)S(1)} %get-tuple-element.42), channel_id=1, source_target_pairs={{4,0},{0,4},{5,1},{1,5},{6,2},{2,6},{7,3},{3,7},{12,8},{8,12},{13,... | collective-permute-start | bytes 393224 | tf_op jit(solution)/shard_map/ppermute | solution.py:30
  30.0 11.3 %collective-permute-start.1 = (f32[1,8,4096]{2,1,0:T(8,128)S(1)}, f32[1,8,4096]{2,1,0:T(8,128)S(1)}, u32[]{:S(2)}, u32[]{:S(2)}) collective-permute-start(f32[1,8,4096]{2,1,0:T(8,128)S(1)} %get-tuple-element.41), channel_id=1, source_target_pairs={{0,4},{4,0},{1,5},{5,1},{2,6},{6,2},{3,7},{7,3},{8,12},{12,8},{9,1... | collective-permute-start | bytes 393224 | tf_op jit(solution)/shard_map/ppermute | solution.py:27
  36.8 6.9 %collective-permute-start.19 = (f32[10,1,4096]{2,1,0:T(1,128)S(1)}, f32[10,1,4096]{2,1,0:T(1,128)S(1)}, u32[]{:S(2)}, u32[]{:S(2)}) collective-permute-start(f32[10,1,4096]{2,1,0:T(1,128)S(1)} %get-tuple-element.28), channel_id=1, source_target_pairs={{0,1},{1,2},{2,3},{3,0},{4,5},{5,6},{6,7},{7,4},{8,9},{9,10},{10,1... | collective-permute-start | bytes 491528 | tf_op jit(solution)/shard_map/ppermute | solution.py:27
  37.1 9.6 %collective-permute-start.18 = (f32[10,1,4096]{2,1,0:T(1,128)S(1)}, f32[10,1,4096]{2,1,0:T(1,128)S(1)}, u32[]{:S(2)}, u32[]{:S(2)}) collective-permute-start(f32[10,1,4096]{2,1,0:T(1,128)S(1)} %get-tuple-element.27), channel_id=1, source_target_pairs={{1,0},{2,1},{3,2},{0,3},{5,4},{6,5},{7,6},{4,7},{9,8},{10,9},{11,1... | collective-permute-start | bytes 491528 | tf_op jit(solution)/shard_map/ppermute | solution.py:30
  41.6 10.6 %collective-permute-start.3 = (f32[10,1,4096]{2,1,0:T(1,128)S(1)}, f32[10,1,4096]{2,1,0:T(1,128)S(1)}, u32[]{:S(2)}, u32[]{:S(2)}) collective-permute-start(f32[10,1,4096]{2,1,0:T(1,128)S(1)} %get-tuple-element.20), channel_id=1, source_target_pairs={{0,1},{1,2},{2,3},{3,0},{4,5},{5,6},{6,7},{7,4},{8,9},{9,10},{10,1... | collective-permute-start | bytes 491528 | tf_op jit(solution)/shard_map/ppermute | solution.py:27
  41.9 10.3 %collective-permute-start.2 = (f32[10,1,4096]{2,1,0:T(1,128)S(1)}, f32[10,1,4096]{2,1,0:T(1,128)S(1)}, u32[]{:S(2)}, u32[]{:S(2)}) collective-permute-start(f32[10,1,4096]{2,1,0:T(1,128)S(1)} %get-tuple-element.19), channel_id=1, source_target_pairs={{1,0},{2,1},{3,2},{0,3},{5,4},{6,5},{7,6},{4,7},{9,8},{10,9},{11,1... | collective-permute-start | bytes 491528 | tf_op jit(solution)/shard_map/ppermute | solution.py:30
  47.9 7.6 %collective-permute-start.20 = (f32[1,8,4096]{2,1,0:T(8,128)S(1)}, f32[1,8,4096]{2,1,0:T(8,128)S(1)}, u32[]{:S(2)}, u32[]{:S(2)}) collective-permute-start(f32[1,8,4096]{2,1,0:T(8,128)S(1)} %get-tuple-element.56), channel_id=1, source_target_pairs={{4,0},{0,4},{5,1},{1,5},{6,2},{2,6},{7,3},{3,7},{12,8},{8,12},{13,... | collective-permute-start | bytes 393224 | tf_op jit(solution)/shard_map/ppermute | solution.py:30
  48.4 7.0 %collective-permute-start.21 = (f32[1,8,4096]{2,1,0:T(8,128)S(1)}, f32[1,8,4096]{2,1,0:T(8,128)S(1)}, u32[]{:S(2)}, u32[]{:S(2)}) collective-permute-start(f32[1,8,4096]{2,1,0:T(8,128)S(1)} %get-tuple-element.55), channel_id=1, source_target_pairs={{0,4},{4,0},{1,5},{5,1},{2,6},{6,2},{3,7},{7,3},{8,12},{12,8},{9,1... | collective-permute-start | bytes 393224 | tf_op jit(solution)/shard_map/ppermute | solution.py:27
  53.4 5.7 %collective-permute-start.4 = (f32[1,8,4096]{2,1,0:T(8,128)S(1)}, f32[1,8,4096]{2,1,0:T(8,128)S(1)}, u32[]{:S(2)}, u32[]{:S(2)}) collective-permute-start(f32[1,8,4096]{2,1,0:T(8,128)S(1)} %get-tuple-element.40), channel_id=1, source_target_pairs={{4,0},{0,4},{5,1},{1,5},{6,2},{2,6},{7,3},{3,7},{12,8},{8,12},{13,... | collective-permute-start | bytes 393224 | tf_op jit(solution)/shard_map/ppermute | solution.py:30
  53.9 6.0 %collective-permute-start.5 = (f32[1,8,4096]{2,1,0:T(8,128)S(1)}, f32[1,8,4096]{2,1,0:T(8,128)S(1)}, u32[]{:S(2)}, u32[]{:S(2)}) collective-permute-start(f32[1,8,4096]{2,1,0:T(8,128)S(1)} %get-tuple-element.39), channel_id=1, source_target_pairs={{0,4},{4,0},{1,5},{5,1},{2,6},{6,2},{3,7},{7,3},{8,12},{12,8},{9,1... | collective-permute-start | bytes 393224 | tf_op jit(solution)/shard_map/ppermute | solution.py:27
  55.7 8.4 %collective-permute-start.23 = (f32[10,1,4096]{2,1,0:T(1,128)S(1)}, f32[10,1,4096]{2,1,0:T(1,128)S(1)}, u32[]{:S(2)}, u32[]{:S(2)}) collective-permute-start(f32[10,1,4096]{2,1,0:T(1,128)S(1)} %get-tuple-element.26), channel_id=1, source_target_pairs={{0,1},{1,2},{2,3},{3,0},{4,5},{5,6},{6,7},{7,4},{8,9},{9,10},{10,1... | collective-permute-start | bytes 491528 | tf_op jit(solution)/shard_map/ppermute | solution.py:27
  59.1 11.0 %collective-permute-start.22 = (f32[10,1,4096]{2,1,0:T(1,128)S(1)}, f32[10,1,4096]{2,1,0:T(1,128)S(1)}, u32[]{:S(2)}, u32[]{:S(2)}) collective-permute-start(f32[10,1,4096]{2,1,0:T(1,128)S(1)} %get-tuple-element.25), channel_id=1, source_target_pairs={{1,0},{2,1},{3,2},{0,3},{5,4},{6,5},{7,6},{4,7},{9,8},{10,9},{11,1... | collective-permute-start | bytes 491528 | tf_op jit(solution)/shard_map/ppermute | solution.py:30
  60.2 13.1 %collective-permute-start.7 = (f32[10,1,4096]{2,1,0:T(1,128)S(1)}, f32[10,1,4096]{2,1,0:T(1,128)S(1)}, u32[]{:S(2)}, u32[]{:S(2)}) collective-permute-start(f32[10,1,4096]{2,1,0:T(1,128)S(1)} %get-tuple-element.18), channel_id=1, source_target_pairs={{0,1},{1,2},{2,3},{3,0},{4,5},{5,6},{6,7},{7,4},{8,9},{9,10},{10,1... | collective-permute-start | bytes 491528 | tf_op jit(solution)/shard_map/ppermute | solution.py:27
  63.6 10.5 %collective-permute-start.6 = (f32[10,1,4096]{2,1,0:T(1,128)S(1)}, f32[10,1,4096]{2,1,0:T(1,128)S(1)}, u32[]{:S(2)}, u32[]{:S(2)}) collective-permute-start(f32[10,1,4096]{2,1,0:T(1,128)S(1)} %get-tuple-element.17), channel_id=1, source_target_pairs={{1,0},{2,1},{3,2},{0,3},{5,4},{6,5},{7,6},{4,7},{9,8},{10,9},{11,1... | collective-permute-start | bytes 491528 | tf_op jit(solution)/shard_map/ppermute | solution.py:30
  71.2 6.4 %collective-permute-start.24 = (f32[1,8,4096]{2,1,0:T(8,128)S(1)}, f32[1,8,4096]{2,1,0:T(8,128)S(1)}, u32[]{:S(2)}, u32[]{:S(2)}) collective-permute-start(f32[1,8,4096]{2,1,0:T(8,128)S(1)} %get-tuple-element.52), channel_id=1, source_target_pairs={{4,0},{0,4},{5,1},{1,5},{6,2},{2,6},{7,3},{3,7},{12,8},{8,12},{13,... | collective-permute-start | bytes 393224 | tf_op jit(solution)/shard_map/ppermute | solution.py:30
  71.9 8.3 %collective-permute-start.25 = (f32[1,8,4096]{2,1,0:T(8,128)S(1)}, f32[1,8,4096]{2,1,0:T(8,128)S(1)}, u32[]{:S(2)}, u32[]{:S(2)}) collective-permute-start(f32[1,8,4096]{2,1,0:T(8,128)S(1)} %get-tuple-element.51), channel_id=1, source_target_pairs={{0,4},{4,0},{1,5},{5,1},{2,6},{6,2},{3,7},{7,3},{8,12},{12,8},{9,1... | collective-permute-start | bytes 393224 | tf_op jit(solution)/shard_map/ppermute | solution.py:27
  75.2 8.0 %collective-permute-start.8 = (f32[1,8,4096]{2,1,0:T(8,128)S(1)}, f32[1,8,4096]{2,1,0:T(8,128)S(1)}, u32[]{:S(2)}, u32[]{:S(2)}) collective-permute-start(f32[1,8,4096]{2,1,0:T(8,128)S(1)} %get-tuple-element.36), channel_id=1, source_target_pairs={{4,0},{0,4},{5,1},{1,5},{6,2},{2,6},{7,3},{3,7},{12,8},{8,12},{13,... | collective-permute-start | bytes 393224 | tf_op jit(solution)/shard_map/ppermute | solution.py:30
  75.8 7.4 %collective-permute-start.9 = (f32[1,8,4096]{2,1,0:T(8,128)S(1)}, f32[1,8,4096]{2,1,0:T(8,128)S(1)}, u32[]{:S(2)}, u32[]{:S(2)}) collective-permute-start(f32[1,8,4096]{2,1,0:T(8,128)S(1)} %get-tuple-element.35), channel_id=1, source_target_pairs={{0,4},{4,0},{1,5},{5,1},{2,6},{6,2},{3,7},{7,3},{8,12},{12,8},{9,1... | collective-permute-start | bytes 393224 | tf_op jit(solution)/shard_map/ppermute | solution.py:27
  80.5 7.3 %collective-permute-start.27 = (f32[10,1,4096]{2,1,0:T(1,128)S(1)}, f32[10,1,4096]{2,1,0:T(1,128)S(1)}, u32[]{:S(2)}, u32[]{:S(2)}) collective-permute-start(f32[10,1,4096]{2,1,0:T(1,128)S(1)} %get-tuple-element.24), channel_id=1, source_target_pairs={{0,1},{1,2},{2,3},{3,0},{4,5},{5,6},{6,7},{7,4},{8,9},{9,10},{10,1... | collective-permute-start | bytes 491528 | tf_op jit(solution)/shard_map/ppermute | solution.py:27
  83.2 7.6 %collective-permute-start.26 = (f32[10,1,4096]{2,1,0:T(1,128)S(1)}, f32[10,1,4096]{2,1,0:T(1,128)S(1)}, u32[]{:S(2)}, u32[]{:S(2)}) collective-permute-start(f32[10,1,4096]{2,1,0:T(1,128)S(1)} %get-tuple-element.23), channel_id=1, source_target_pairs={{1,0},{2,1},{3,2},{0,3},{5,4},{6,5},{7,6},{4,7},{9,8},{10,9},{11,1... | collective-permute-start | bytes 491528 | tf_op jit(solution)/shard_map/ppermute | solution.py:30
  83.5 10.6 %collective-permute-start.11 = (f32[10,1,4096]{2,1,0:T(1,128)S(1)}, f32[10,1,4096]{2,1,0:T(1,128)S(1)}, u32[]{:S(2)}, u32[]{:S(2)}) collective-permute-start(f32[10,1,4096]{2,1,0:T(1,128)S(1)} %get-tuple-element.16), channel_id=1, source_target_pairs={{0,1},{1,2},{2,3},{3,0},{4,5},{5,6},{6,7},{7,4},{8,9},{9,10},{10,1... | collective-permute-start | bytes 491528 | tf_op jit(solution)/shard_map/ppermute | solution.py:27
  87.3 7.1 %collective-permute-start.10 = (f32[10,1,4096]{2,1,0:T(1,128)S(1)}, f32[10,1,4096]{2,1,0:T(1,128)S(1)}, u32[]{:S(2)}, u32[]{:S(2)}) collective-permute-start(f32[10,1,4096]{2,1,0:T(1,128)S(1)} %get-tuple-element.15), channel_id=1, source_target_pairs={{1,0},{2,1},{3,2},{0,3},{5,4},{6,5},{7,6},{4,7},{9,8},{10,9},{11,1... | collective-permute-start | bytes 491528 | tf_op jit(solution)/shard_map/ppermute | solution.py:30
  92.0 5.7 %collective-permute-start.28 = (f32[1,8,4096]{2,1,0:T(8,128)S(1)}, f32[1,8,4096]{2,1,0:T(8,128)S(1)}, u32[]{:S(2)}, u32[]{:S(2)}) collective-permute-start(f32[1,8,4096]{2,1,0:T(8,128)S(1)} %get-tuple-element.48), channel_id=1, source_target_pairs={{4,0},{0,4},{5,1},{1,5},{6,2},{2,6},{7,3},{3,7},{12,8},{8,12},{13,... | collective-permute-start | bytes 393224 | tf_op jit(solution)/shard_map/ppermute | solution.py:30
  92.9 6.0 %collective-permute-start.29 = (f32[1,8,4096]{2,1,0:T(8,128)S(1)}, f32[1,8,4096]{2,1,0:T(8,128)S(1)}, u32[]{:S(2)}, u32[]{:S(2)}) collective-permute-start(f32[1,8,4096]{2,1,0:T(8,128)S(1)} %get-tuple-element.47), channel_id=1, source_target_pairs={{0,4},{4,0},{1,5},{5,1},{2,6},{6,2},{3,7},{7,3},{8,12},{12,8},{9,1... | collective-permute-start | bytes 393224 | tf_op jit(solution)/shard_map/ppermute | solution.py:27
  95.6 6.0 %collective-permute-start.12 = (f32[1,8,4096]{2,1,0:T(8,128)S(1)}, f32[1,8,4096]{2,1,0:T(8,128)S(1)}, u32[]{:S(2)}, u32[]{:S(2)}) collective-permute-start(f32[1,8,4096]{2,1,0:T(8,128)S(1)} %get-tuple-element.32), channel_id=1, source_target_pairs={{4,0},{0,4},{5,1},{1,5},{6,2},{2,6},{7,3},{3,7},{12,8},{8,12},{13,... | collective-permute-start | bytes 393224 | tf_op jit(solution)/shard_map/ppermute | solution.py:30
  96.5 5.5 %collective-permute-start.13 = (f32[1,8,4096]{2,1,0:T(8,128)S(1)}, f32[1,8,4096]{2,1,0:T(8,128)S(1)}, u32[]{:S(2)}, u32[]{:S(2)}) collective-permute-start(f32[1,8,4096]{2,1,0:T(8,128)S(1)} %get-tuple-element.31), channel_id=1, source_target_pairs={{0,4},{4,0},{1,5},{5,1},{2,6},{6,2},{3,7},{7,3},{8,12},{12,8},{9,1... | collective-permute-start | bytes 393224 | tf_op jit(solution)/shard_map/ppermute | solution.py:27
  99.1 6.0 %collective-permute-start.31 = (f32[10,1,4096]{2,1,0:T(1,128)S(1)}, f32[10,1,4096]{2,1,0:T(1,128)S(1)}, u32[]{:S(2)}, u32[]{:S(2)}) collective-permute-start(f32[10,1,4096]{2,1,0:T(1,128)S(1)} %get-tuple-element.22), channel_id=1, source_target_pairs={{0,1},{1,2},{2,3},{3,0},{4,5},{5,6},{6,7},{7,4},{8,9},{9,10},{10,1... | collective-permute-start | bytes 491528 | tf_op jit(solution)/shard_map/ppermute | solution.py:27
  100.6 10.8 %collective-permute-start.30 = (f32[10,1,4096]{2,1,0:T(1,128)S(1)}, f32[10,1,4096]{2,1,0:T(1,128)S(1)}, u32[]{:S(2)}, u32[]{:S(2)}) collective-permute-start(f32[10,1,4096]{2,1,0:T(1,128)S(1)} %get-tuple-element.21), channel_id=1, source_target_pairs={{1,0},{2,1},{3,2},{0,3},{5,4},{6,5},{7,6},{4,7},{9,8},{10,9},{11,1... | collective-permute-start | bytes 491528 | tf_op jit(solution)/shard_map/ppermute | solution.py:30
  102.4 10.5 %collective-permute-start.15 = (f32[10,1,4096]{2,1,0:T(1,128)S(1)}, f32[10,1,4096]{2,1,0:T(1,128)S(1)}, u32[]{:S(2)}, u32[]{:S(2)}) collective-permute-start(f32[10,1,4096]{2,1,0:T(1,128)S(1)} %get-tuple-element.14), channel_id=1, source_target_pairs={{0,1},{1,2},{2,3},{3,0},{4,5},{5,6},{6,7},{7,4},{8,9},{9,10},{10,1... | collective-permute-start | bytes 491528 | tf_op jit(solution)/shard_map/ppermute | solution.py:27
  104.7 10.1 %collective-permute-start.14 = (f32[10,1,4096]{2,1,0:T(1,128)S(1)}, f32[10,1,4096]{2,1,0:T(1,128)S(1)}, u32[]{:S(2)}, u32[]{:S(2)}) collective-permute-start(f32[10,1,4096]{2,1,0:T(1,128)S(1)} %get-tuple-element.13), channel_id=1, source_target_pairs={{1,0},{2,1},{3,2},{0,3},{5,4},{6,5},{7,6},{4,7},{9,8},{10,9},{11,1... | collective-permute-start | bytes 491528 | tf_op jit(solution)/shard_map/ppermute | solution.py:30
  (3 other events, 4.9 us)
where the time goes:
time: 118 us; the launch traced here: 117 us
  starting transfers between devices  39 us (33%)
  waiting for transfers between devices  37.2 us (32%)
  other arithmetic  13.8 us (12%)
  local copies, waits for them, and re-layouts  11.1 us (9%)
  blocking collectives  11 us (9%)
  between operations  5.41 us (5%)
    ppermute x16, starting transfers between devices, extended(): lax.ppermute(lax.slice_in_dim(block, block.shape[dim] - width, None, axis...  28.9 us
    ppermute x16, waiting for transfers between devices, extended(): lax.ppermute(lax.slice_in_dim(block, 0, width, axis=dim), axis, backward)  23.6 us
    ppermute x16, waiting for transfers between devices, extended(): lax.ppermute(lax.slice_in_dim(block, block.shape[dim] - width, None, axis...  13.6 us
    psum x1, blocking collectives, spread_2(): return lax.psum(block, axis)  11 us
    ppermute x16, starting transfers between devices, extended(): lax.ppermute(lax.slice_in_dim(block, 0, width, axis=dim), axis, backward)  10.1 us
    another operation x8, local copies, waits for them, and re-layouts, body(): jnp.tile(source.astype(jnp.float32), (1, 1, held))  5.96 us
    sub x4, other arithmetic, potential(): t_next = 2.0 * screened(widen_one(t_cur)) - t_prev  3.11 us
    add x2, other arithmetic, potential(): total = total + cheb_coeffs[order] * t_next  2.93 us
  transfers between devices with their start and end apart: 32, of which 20 were waited for; matrix products, arithmetic and copies ran while one was open for 9% of the time, Pallas kernels for 0%

commit v1 on v0

v1 whole, which is shorter than its diff:
```python
import functools

import jax
import jax.numpy as jnp
from jax import lax
from jax.experimental import pallas as pl
from jax.experimental.pallas import tpu as pltpu
from jax.sharding import PartitionSpec as P

NZ = 32
LANES = 128
SUB = 8
DEGREE = 4
HALO = DEGREE
EDGE = 8

CHEB = (
    1.021021021021021,
    -1.7357357357357357,
    1.4753753753753753,
    -1.254069069069069,
    1.0659587087087088,
)


def power_coeffs():
    c0, c1, c2, c3, c4 = CHEB
    return (
        c0 - c2 + c4,
        -(c1 - 3.0 * c3) / 6.0,
        (2.0 * c2 - 8.0 * c4) / 36.0,
        -4.0 * c3 / 216.0,
        8.0 * c4 / 1296.0,
    )


CORNER_LOW = ((0, 5, 3), (1, 6, 2), (2, 7, 1), (5, 7, 1), (6, 6, 2), (7, 5, 3))
CORNER_HIGH = tuple((row, 0, count) for row, _, count in CORNER_LOW)


def ring(axis, step):
    count = lax.axis_size(axis)
    return [(i, (i + step) % count) for i in range(count)]


def diagonal(step_x, step_y):
    count_x, count_y = lax.axis_size("sx"), lax.axis_size("sy")
    return [
        (i * count_y + j, (i + step_x) % count_x * count_y + (j + step_y) % count_y)
        for i in range(count_x)
        for j in range(count_y)
    ]


def pack(block, corners):
    return jnp.concatenate(
        [block[row, first : first + count] for row, first, count in corners], axis=0
    )


def halos(block):
    last, first = block[:, EDGE - HALO :], block[:, :HALO]
    if lax.axis_size("sx") == 2:
        across = lax.ppermute(block, "sx", ring("sx", 1))
    else:
        across = jnp.concatenate(
            [
                lax.ppermute(block[:HALO], "sx", ring("sx", -1)),
                lax.ppermute(block[EDGE - HALO :], "sx", ring("sx", 1)),
            ],
            axis=0,
        )
    below = lax.ppermute(last, "sy", ring("sy", 1))
    above = lax.ppermute(first, "sy", ring("sy", -1))
    both = ("sx", "sy")
    corners = []
    for cells, step_y in ((CORNER_LOW, 1), (CORNER_HIGH, -1)):
        if lax.axis_size("sx") == 2:
            corners.append(lax.ppermute(pack(block, cells), both, diagonal(1, step_y)))
        else:
            corners.append(
                jnp.concatenate(
                    [
                        lax.ppermute(pack(block, cells[:3]), both, diagonal(-1, step_y)),
                        lax.ppermute(pack(block, cells[3:]), both, diagonal(1, step_y)),
                    ],
                    axis=0,
                )
            )
    return block, across, below, above, corners[0], corners[1]


def candidates(orbitals, src_slot):
    slots = src_slot.reshape(-1)
    return jnp.concatenate(
        [lax.dynamic_slice_in_dim(orbitals, slots[i] * NZ, NZ, 2) for i in range(slots.shape[0])],
        axis=2,
    )


def pick_sources(mine, src_owner):
    count = lax.axis_size("orb")
    owner = jnp.repeat(src_owner.reshape(-1), NZ)
    me = lax.axis_index("orb")
    picked = mine
    for step in range(1, count):
        theirs = lax.ppermute(mine, "orb", ring("orb", step))
        picked = jnp.where(owner == (me + count - step) % count, theirs, picked)
    return picked


def fill(dst, own, across, below, above, corner_low, corner_high, groups):
    size = 2 * HALO + EDGE

    def put(x, y, rows, group, values):
        start = y * groups + group
        if groups == 1:
            dst[x, pl.ds(start, rows), :] = values
        else:
            dst[x, pl.ds(start, rows, stride=groups), :] = values

    def one(group):
        lanes = pl.ds(group * LANES, LANES)
        for row in range(EDGE):
            put(HALO + row, HALO, EDGE, group, own[row, :, lanes].astype(jnp.float32))
            outer = row - EDGE if row >= HALO else row + EDGE
            put(HALO + outer, HALO, EDGE, group, across[row, :, lanes].astype(jnp.float32))
            put(HALO + row, 0, HALO, group, below[row, :, lanes].astype(jnp.float32))
            put(HALO + row, HALO + EDGE, HALO, group, above[row, :, lanes].astype(jnp.float32))
        for ref, cells, shift in (
            (corner_low, CORNER_LOW, HALO - EDGE),
            (corner_high, CORNER_HIGH, HALO + EDGE),
        ):
            values = ref[:, lanes].astype(jnp.float32)
            at = 0
            for row, first, count in cells:
                outer = row - EDGE if row >= HALO else row + EDGE
                put(HALO + outer, first + shift, count, group, values[at : at + count])
                at += count

    for group in range(groups):
        one(group)


def reach(x, y):
    out_x = max(HALO - x, x - (HALO + EDGE - 1), 0)
    out_y = max(HALO - y, y - (HALO + EDGE - 1), 0)
    return out_x + out_y


def kernel(count, *refs):
    block, source = refs[0:6], refs[6:12]
    out, cells, src_rows, src, dens, work_a, work_b, acc = refs[12:]
    groups = block[0].shape[2] // LANES
    size = 2 * HALO + EDGE
    p0, p1, p2, p3, p4 = power_coeffs()
    tail = (p3 / p4, p2 / p4, p1 / p4, p0 / p4)

    fill(src_rows, *source, 1)
    lane = lax.broadcasted_iota(jnp.int32, (SUB, LANES), 1)
    for x in range(size):
        for y in range(0, size, SUB):
            rows = src_rows[x, pl.ds(y, SUB), :]
            for place in range(count):
                one = jnp.where(lane // NZ == place, rows, 0.0)
                one = one + pltpu.roll(one, NZ, 1)
                src[place, x, pl.ds(y, SUB), :] = one + pltpu.roll(one, 2 * NZ, 1)
    fill(cells, *block, groups)

    inner = lane % NZ
    not_first, not_last = inner != 0, inner != NZ - 1

    def z_sum(v):
        lower = jnp.where(not_first, pltpu.roll(v, 1, 1), 0.0)
        upper = jnp.where(not_last, pltpu.roll(v, LANES - 1, 1), 0.0)
        return lower + upper

    spots = [
        [(x, y) for x in range(size) for y in range(size) if reach(x, y) <= radius]
        for radius in range(HALO + 1)
    ]

    def one_pass(index, carry):
        place, half = index // (groups // SUB), index % (groups // SUB)
        base = half * SUB

        def spread(x, y):
            row = src[place, x, pl.ds(y, 1), :]
            return jnp.broadcast_to(row, (SUB, LANES))

        for x, y in spots[HALO]:
            value = cells[x, pl.ds(pl.multiple_of(y * groups + base, SUB), SUB), :]
            dens[x, y] = value * spread(x, y)
        old = dens
        for step in range(DEGREE):
            new = (work_a, work_b, work_a, None)[step]
            radius = HALO - 1 - step
            targets = set(spots[radius])
            pair_prev = {}
            for x in range(size):
                pair = {}
                for y in range(size):
                    if (x, y) in targets or (x + 1, y + 1) in targets:
                        pair[y] = old[x + 1, y] + old[x, y + 1]
                for y in range(size):
                    if (x, y) not in targets:
                        continue
                    total = pair[y] + pair_prev[y - 1]
                    total = total + z_sum(old[x, y])
                    total = total + tail[step] * dens[x, y]
                    if new is not None:
                        new[x, y] = total
                    else:
                        total = total * spread(x, y)
                        at = pl.multiple_of((y - HALO) * groups + base, SUB)
                        row = acc.at[x - HALO, pl.ds(at, SUB), :]
                        row[...] = row[...] + total
                pair_prev = pair
            old = new
        return carry

    acc[...] = jnp.zeros(acc.shape, jnp.float32)
    lax.fori_loop(0, count * (groups // SUB), one_pass, 0)
    for x in range(EDGE):
        for group in range(groups):
            tile = acc[x, pl.ds(group, EDGE, stride=groups), :]
            out[x, :, pl.ds(group * LANES, LANES)] = tile * (-p4)


def fields(block, source, count):
    rows_x, rows_y, width = block[0].shape
    groups = width // LANES
    size = 2 * HALO + EDGE
    vmem = pl.BlockSpec(memory_space=pltpu.VMEM)
    plane = pltpu.VMEM((size, size, SUB, LANES), jnp.float32)
    return pl.pallas_call(
        functools.partial(kernel, count),
        out_shape=jax.ShapeDtypeStruct((rows_x, rows_y, width), jnp.float32),
        in_specs=[vmem] * 12,
        out_specs=vmem,
        scratch_shapes=[
            pltpu.VMEM((size, size * groups, LANES), jnp.float32),
            pltpu.VMEM((size, size, LANES), jnp.float32),
            pltpu.VMEM((count, size, size, LANES), jnp.float32),
            plane,
            plane,
            plane,
            pltpu.VMEM((rows_x, rows_y * groups, LANES), jnp.float32),
        ],
        compiler_params=pltpu.CompilerParams(vmem_limit_bytes=40 * 2**20),
        name="fields",
    )(*block, *source)


def body(orbitals, src_owner, src_slot):
    mine = candidates(orbitals, src_slot)
    block = halos(orbitals)
    source = halos(pick_sources(mine, src_owner))
    return fields(block, source, src_slot.size)


def solution(mesh):
    in_specs = (P("sx", "sy", "orb"), P(), P())
    out_specs = P("sx", "sy", "orb")
    return jax.shard_map(body, mesh=mesh, in_specs=in_specs, out_specs=out_specs, check_vma=False)
```

time: 118 us -> 52.9 us (0.45)
  the two profiles are of different devices: /device:TPU:30 before, /device:TPU:0 now
where the time goes in v1:
time: 52.9 us; the launch traced here: 52.7 us
  starting transfers between devices  20.4 us (39%)
  Pallas kernels  14.2 us (27%)
  waiting for transfers between devices  10.4 us (20%)
  local copies, waits for them, and re-layouts  4.75 us (9%)
  between operations  2.87 us (5%)
    pallas_call x1, Pallas kernels, fields(): pl.pallas_call(functools.partial(kernel, count), out_shape=jax.ShapeDtype...  14.2 us
    ppermute x4, starting transfers between devices, halos(): corners.append(lax.ppermute(pack(block, cells), both, diagonal(1, step_y)))  9.51 us
    ppermute x2, waiting for transfers between devices, halos(): below = lax.ppermute(last, 'sy', ring('sy', 1))  4.96 us
    ppermute x3, starting transfers between devices, pick_sources(): theirs = lax.ppermute(mine, 'orb', ring('orb', step))  4.46 us
    ppermute x2, starting transfers between devices, halos(): above = lax.ppermute(first, 'sy', ring('sy', -1))  3.66 us
    ppermute x4, waiting for transfers between devices, halos(): corners.append(lax.ppermute(pack(block, cells), both, diagonal(1, step_y)))  3.61 us
    ppermute x2, starting transfers between devices, halos(): across = lax.ppermute(block, 'sx', ring('sx', 1))  2.03 us
    ppermute x2, waiting for transfers between devices, halos(): above = lax.ppermute(first, 'sy', ring('sy', -1))  1.82 us
  transfers between devices with their start and end apart: 13, of which 4 were waited for; matrix products, arithmetic and copies ran while one was open for 3% of the time, Pallas kernels for 0%

profile of v1, /device:TPU:0, one launch (start us, length us, event | category | flops | bytes accessed | tf_op | source)
XLA Modules:
  0.0 52.7 jit_solution(1134656440860430987)
XLA Ops:
  0.0 0.8 %reshape.25 = s32[4]{0:T(128)S(1)} reshape(s32[2,2]{1,0:T(2,128)} %param.5) | data formatting | bytes 32 | tf_op jit(solution)/shard_map/reshape | solution.py:94
  0.8 0.7 %fusion.2 = (s32[1]{0:T(128)}, s32[1]{0:T(128)}, s32[1]{0:T(128)}, s32[1]{0:T(128)}) fusion(s32[4]{0:T(128)S(1)} %reshape.25), kind=kLoop, calls=%fused_computation.35 | loop fusion | bytes 32 | tf_op jit(solution)/shard_map/slice | solution.py:96
  4.2 0.9 %constant_dynamic-slice_fusion.3 = (bf16[8,8,32]{2,1,0:T(8,128)(2,1)S(1)}, bf16[8,8,32]{2,1,0:T(8,128)(2,1)S(1)}, bf16[8,8,32]{2,1,0:T(8,128)(2,1)S(1)}, bf16[8,8,32]{2,1,0:T(8,128)(2,1)S(1)}) fusion(bf16[8,8,2048]{2,1,0:T(8,128)(2,1)} %refs_0_.1, s32[]{:T(128)S(6)} %select_n.38, s32[]{:T(128)S(6)} %select_n.40, s32[]{:T(128)S(6)} %select_n.39, s32[]{:T(128)S(6)} %select_n.41), kind=kLoop, calls=%fused_computation.21 | loop fusion | bytes 32784 | tf_op jit(solution)/shard_map/dynamic_slice | solution.py:96
  5.1 0.1 pad_maximum_fusion
  5.2 0.5 collective-permute-start.7
  5.7 2.6 %collective-permute-start.6 = (bf16[8,8,128]{2,1,0:T(8,128)(2,1)S(1)}, bf16[8,8,128]{2,1,0:T(8,128)(2,1)S(1)}, u32[]{:S(2)}, u32[]{:S(2)}) collective-permute-start(bf16[8,8,128]{2,1,0:T(8,128)(2,1)S(1)} %pad_maximum_fusion), channel_id=1, source_target_pairs={{0,16},{8,24},{16,0},{24,8},{1,17},{9,25},{17,1},{25,9},{2,18},{10... | collective-permute-start | bytes 49160 | tf_op jit(solution)/shard_map/ppermute | solution.py:107
  8.3 1.4 %collective-permute-start.5 = (bf16[8,8,128]{2,1,0:T(8,128)(2,1)S(1)}, bf16[8,8,128]{2,1,0:T(8,128)(2,1)S(1)}, u32[]{:S(2)}, u32[]{:S(2)}) collective-permute-start(bf16[8,8,128]{2,1,0:T(8,128)(2,1)S(1)} %pad_maximum_fusion), channel_id=1, source_target_pairs={{0,24},{8,0},{16,8},{24,16},{1,25},{9,1},{17,9},{25,17},{2,26},{10... | collective-permute-start | bytes 49160 | tf_op jit(solution)/shard_map/ppermute | solution.py:107
  9.6 1.5 %collective-permute-start = (bf16[8,8,2048]{2,1,0:T(8,128)(2,1)S(1)}, bf16[8,8,2048]{2,1,0:T(8,128)(2,1)S(1)}, u32[]{:S(2)}, u32[]{:S(2)}) collective-permute-start(bf16[8,8,2048]{2,1,0:T(8,128)(2,1)S(1)} %copy-done), channel_id=1, source_target_pairs={{0,4},{4,0},{1,5},{5,1},{2,6},{6,2},{3,7},{7,3},{8,12},{12,8},{9,1... | collective-permute-start | bytes 786440 | tf_op jit(solution)/shard_map/ppermute | solution.py:64
  11.2 0.1 fusion
  11.3 3.7 %collective-permute-start.2 = (bf16[8,4,2048]{2,1,0:T(4,128)(2,1)S(1)}, bf16[8,4,2048]{2,1,0:T(4,128)(2,1)S(1)}, u32[]{:S(2)}, u32[]{:S(2)}) collective-permute-start(bf16[8,4,2048]{2,1,0:T(4,128)(2,1)S(1)} %get-tuple-element.21), channel_id=1, source_target_pairs={{0,3},{1,0},{2,1},{3,2},{4,7},{5,4},{6,5},{7,6},{8,11},{9,8},{10,9... | collective-permute-start | bytes 393224 | tf_op jit(solution)/shard_map/ppermute | solution.py:74
  15.0 0.7 %copy-done.1 = s32[2,2]{1,0:T(2,128)S(1)} copy-done((s32[2,2]{1,0:T(2,128)S(1)}, s32[2,2]{1,0:T(2,128)}, u32[]{:S(2)}) %copy-start.1) | copy-done | bytes 40
  15.7 0.1 eq.45
  15.8 0.1 broadcast_in_dim.17
  15.8 0.1 eq.46
  15.9 0.1 eq.53
  16.0 0.1 broadcast_in_dim.21
  16.1 0.1 eq.54
  16.2 0.1 eq.49
  16.3 0.1 eq.50
  16.5 0.1 concatenate.18
  16.7 0.1 concatenate.19
  16.9 4.7 %collective-permute-start.12 = (bf16[12,128]{1,0:T(8,128)(2,1)S(1)}, bf16[12,128]{1,0:T(8,128)(2,1)S(1)}, u32[]{:S(2)}, u32[]{:S(2)}) collective-permute-start(bf16[12,128]{1,0:T(8,128)(2,1)S(1)} %concatenate.19), channel_id=1, source_target_pairs={{0,7},{1,4},{2,5},{3,6},{4,3},{5,0},{6,1},{7,2},{8,15},{9,12},{10,... | collective-permute-start | bytes 9224 | tf_op jit(solution)/shard_map/ppermute | solution.py:79
  21.6 1.4 %collective-permute-done.11.refs_10_ = bf16[12,128]{1,0:T(8,128)(2,1)S(1)} collective-permute-done((bf16[12,128]{1,0:T(8,128)(2,1)S(1)}, bf16[12,128]{1,0:T(8,128)(2,1)S(1)}, u32[]{:S(2)}, u32[]{:S(2)}) %collective-permute-start.11) | collective-permute-done | bytes 3104 | tf_op jit(solution)/shard_map/ppermute | solution.py:79
  23.0 0.7 %collective-permute-start.1 = (bf16[8,4,2048]{2,1,0:T(4,128)(2,1)S(1)}, bf16[8,4,2048]{2,1,0:T(4,128)(2,1)S(1)}, u32[]{:S(2)}, u32[]{:S(2)}) collective-permute-start(bf16[8,4,2048]{2,1,0:T(4,128)(2,1)S(1)} %get-tuple-element.22), channel_id=1, source_target_pairs={{0,1},{1,2},{2,3},{3,0},{4,5},{5,6},{6,7},{7,4},{8,9},{9,10},{10,1... | collective-permute-start | bytes 393224 | tf_op jit(solution)/shard_map/ppermute | solution.py:73
  23.7 0.5 collective-permute-start.8
  24.2 1.8 %collective-permute-done.10.refs_9_ = bf16[8,4,128]{2,1,0:T(4,128)(2,1)S(1)} collective-permute-done((bf16[8,4,128]{2,1,0:T(4,128)(2,1)S(1)}, bf16[8,4,128]{2,1,0:T(4,128)(2,1)S(1)}, u32[]{:S(2)}, u32[]{:S(2)}) %collective-permute-start.10) | collective-permute-done | bytes 8224 | tf_op jit(solution)/shard_map/ppermute | solution.py:74
  26.1 0.2 concatenate.16
  26.3 0.2 concatenate.15
  26.6 5.0 %collective-permute-done.9.refs_8_ = bf16[8,4,128]{2,1,0:T(4,128)(2,1)S(1)} collective-permute-done((bf16[8,4,128]{2,1,0:T(4,128)(2,1)S(1)}, bf16[8,4,128]{2,1,0:T(4,128)(2,1)S(1)}, u32[]{:S(2)}, u32[]{:S(2)}) %collective-permute-start.9) | collective-permute-done | bytes 8224 | tf_op jit(solution)/shard_map/ppermute | solution.py:73
  31.5 4.7 %collective-permute-start.4 = (bf16[12,2048]{1,0:T(8,128)(2,1)S(1)}, bf16[12,2048]{1,0:T(8,128)(2,1)S(1)}, u32[]{:S(2)}, u32[]{:S(2)}) collective-permute-start(bf16[12,2048]{1,0:T(8,128)(2,1)S(1)} %concatenate.16), channel_id=1, source_target_pairs={{0,7},{1,4},{2,5},{3,6},{4,3},{5,0},{6,1},{7,2},{8,15},{9,12},{10,... | collective-permute-start | bytes 147464 | tf_op jit(solution)/shard_map/ppermute | solution.py:79
  36.2 2.2 %collective-permute-done.3.refs_4_ = bf16[12,2048]{1,0:T(8,128)(2,1)S(1)} collective-permute-done((bf16[12,2048]{1,0:T(8,128)(2,1)S(1)}, bf16[12,2048]{1,0:T(8,128)(2,1)S(1)}, u32[]{:S(2)}, u32[]{:S(2)}) %collective-permute-start.3) | collective-permute-done | bytes 49184 | tf_op jit(solution)/shard_map/ppermute | solution.py:79
  38.5 14.2 %fields.1 = f32[8,8,2048]{2,1,0:T(8,128)} custom-call(bf16[8,8,2048]{2,1,0:T(8,128)(2,1)S(1)} %copy-done, bf16[8,8,2048]{2,1,0:T(8,128)(2,1)S(1)} %collective-permute-done.refs_1_, bf16[8,4,2048]{2,1,0:T(4,128)(2,1)S(1)} %collective-permute-done.1.refs_2_, bf16[8,4,2048]{2,1,0:T(4,128)(2,1)S(1)} %collective-permute-done.2.refs_3_, ...), custom_call_target="tpu_custom_call" | custom-call | tf_op jit(solution)/shard_map/fields/pallas_call | solution.py:236
  (26 shorter events, 0.3 us)
Async XLA Ops:
  0.0 9.6 %copy-start = (bf16[8,8,2048]{2,1,0:T(8,128)(2,1)S(1)}, bf16[8,8,2048]{2,1,0:T(8,128)(2,1)}, u32[]{:S(2)}) copy-start(bf16[8,8,2048]{2,1,0:T(8,128)(2,1)} %refs_0_.1) | copy-start | bytes 786436
  5.2 11.3 %collective-permute-start.7 = (bf16[8,8,128]{2,1,0:T(8,128)(2,1)S(1)}, bf16[8,8,128]{2,1,0:T(8,128)(2,1)S(1)}, u32[]{:S(2)}, u32[]{:S(2)}) collective-permute-start(bf16[8,8,128]{2,1,0:T(8,128)(2,1)S(1)} %pad_maximum_fusion), channel_id=1, source_target_pairs={{0,8},{8,16},{16,24},{24,0},{1,9},{9,17},{17,25},{25,1},{2,10},{10... | collective-permute-start | bytes 49160 | tf_op jit(solution)/shard_map/ppermute | solution.py:107
  5.7 10.8 %collective-permute-start.6 = (bf16[8,8,128]{2,1,0:T(8,128)(2,1)S(1)}, bf16[8,8,128]{2,1,0:T(8,128)(2,1)S(1)}, u32[]{:S(2)}, u32[]{:S(2)}) collective-permute-start(bf16[8,8,128]{2,1,0:T(8,128)(2,1)S(1)} %pad_maximum_fusion), channel_id=1, source_target_pairs={{0,16},{8,24},{16,0},{24,8},{1,17},{9,25},{17,1},{25,9},{2,18},{10... | collective-permute-start | bytes 49160 | tf_op jit(solution)/shard_map/ppermute | solution.py:107
  8.3 8.2 %collective-permute-start.5 = (bf16[8,8,128]{2,1,0:T(8,128)(2,1)S(1)}, bf16[8,8,128]{2,1,0:T(8,128)(2,1)S(1)}, u32[]{:S(2)}, u32[]{:S(2)}) collective-permute-start(bf16[8,8,128]{2,1,0:T(8,128)(2,1)S(1)} %pad_maximum_fusion), channel_id=1, source_target_pairs={{0,24},{8,0},{16,8},{24,16},{1,25},{9,1},{17,9},{25,17},{2,26},{10... | collective-permute-start | bytes 49160 | tf_op jit(solution)/shard_map/ppermute | solution.py:107
  9.6 28.9 %collective-permute-start = (bf16[8,8,2048]{2,1,0:T(8,128)(2,1)S(1)}, bf16[8,8,2048]{2,1,0:T(8,128)(2,1)S(1)}, u32[]{:S(2)}, u32[]{:S(2)}) collective-permute-start(bf16[8,8,2048]{2,1,0:T(8,128)(2,1)S(1)} %copy-done), channel_id=1, source_target_pairs={{0,4},{4,0},{1,5},{5,1},{2,6},{6,2},{3,7},{7,3},{8,12},{12,8},{9,1... | collective-permute-start | bytes 786440 | tf_op jit(solution)/shard_map/ppermute | solution.py:64
  11.3 27.2 %collective-permute-start.2 = (bf16[8,4,2048]{2,1,0:T(4,128)(2,1)S(1)}, bf16[8,4,2048]{2,1,0:T(4,128)(2,1)S(1)}, u32[]{:S(2)}, u32[]{:S(2)}) collective-permute-start(bf16[8,4,2048]{2,1,0:T(4,128)(2,1)S(1)} %get-tuple-element.21), channel_id=1, source_target_pairs={{0,3},{1,0},{2,1},{3,2},{4,7},{5,4},{6,5},{7,6},{8,11},{9,8},{10,9... | collective-permute-start | bytes 393224 | tf_op jit(solution)/shard_map/ppermute | solution.py:74
  15.0 0.7 %copy-start.1 = (s32[2,2]{1,0:T(2,128)S(1)}, s32[2,2]{1,0:T(2,128)}, u32[]{:S(2)}) copy-start(s32[2,2]{1,0:T(2,128)} %param.4) | copy-start | bytes 52
  16.7 6.3 %collective-permute-start.11 = (bf16[12,128]{1,0:T(8,128)(2,1)S(1)}, bf16[12,128]{1,0:T(8,128)(2,1)S(1)}, u32[]{:S(2)}, u32[]{:S(2)}) collective-permute-start(bf16[12,128]{1,0:T(8,128)(2,1)S(1)} %concatenate.18), channel_id=1, source_target_pairs={{0,5},{1,6},{2,7},{3,4},{4,1},{5,2},{6,3},{7,0},{8,13},{9,14},{10,... | collective-permute-start | bytes 9224 | tf_op jit(solution)/shard_map/ppermute | solution.py:79
  16.9 6.9 %collective-permute-start.12 = (bf16[12,128]{1,0:T(8,128)(2,1)S(1)}, bf16[12,128]{1,0:T(8,128)(2,1)S(1)}, u32[]{:S(2)}, u32[]{:S(2)}) collective-permute-start(bf16[12,128]{1,0:T(8,128)(2,1)S(1)} %concatenate.19), channel_id=1, source_target_pairs={{0,7},{1,4},{2,5},{3,6},{4,3},{5,0},{6,1},{7,2},{8,15},{9,12},{10,... | collective-permute-start | bytes 9224 | tf_op jit(solution)/shard_map/ppermute | solution.py:79
  21.6 4.4 %collective-permute-start.10 = (bf16[8,4,128]{2,1,0:T(4,128)(2,1)S(1)}, bf16[8,4,128]{2,1,0:T(4,128)(2,1)S(1)}, u32[]{:S(2)}, u32[]{:S(2)}) collective-permute-start(bf16[8,4,128]{2,1,0:T(4,128)(2,1)S(1)} %get-tuple-element.35), channel_id=1, source_target_pairs={{0,3},{1,0},{2,1},{3,2},{4,7},{5,4},{6,5},{7,6},{8,11},{9,8},{10,9... | collective-permute-start | bytes 24584 | tf_op jit(solution)/shard_map/ppermute | solution.py:74
  23.0 15.5 %collective-permute-start.1 = (bf16[8,4,2048]{2,1,0:T(4,128)(2,1)S(1)}, bf16[8,4,2048]{2,1,0:T(4,128)(2,1)S(1)}, u32[]{:S(2)}, u32[]{:S(2)}) collective-permute-start(bf16[8,4,2048]{2,1,0:T(4,128)(2,1)S(1)} %get-tuple-element.22), channel_id=1, source_target_pairs={{0,1},{1,2},{2,3},{3,0},{4,5},{5,6},{6,7},{7,4},{8,9},{9,10},{10,1... | collective-permute-start | bytes 393224 | tf_op jit(solution)/shard_map/ppermute | solution.py:73
  23.7 7.8 %collective-permute-start.8 = (bf16[8,8,128]{2,1,0:T(8,128)(2,1)S(1)}, bf16[8,8,128]{2,1,0:T(8,128)(2,1)S(1)}, u32[]{:S(2)}, u32[]{:S(2)}) collective-permute-start(bf16[8,8,128]{2,1,0:T(8,128)(2,1)S(1)} %select_select_fusion.refs_6_), channel_id=1, source_target_pairs={{0,4},{4,0},{1,5},{5,1},{2,6},{6,2},{3,7},{7,3},{8,12},{12,8},{9,1... | collective-permute-start | bytes 49160 | tf_op jit(solution)/shard_map/ppermute | solution.py:64
  26.1 5.5 %collective-permute-start.9 = (bf16[8,4,128]{2,1,0:T(4,128)(2,1)S(1)}, bf16[8,4,128]{2,1,0:T(4,128)(2,1)S(1)}, u32[]{:S(2)}, u32[]{:S(2)}) collective-permute-start(bf16[8,4,128]{2,1,0:T(4,128)(2,1)S(1)} %get-tuple-element.36), channel_id=1, source_target_pairs={{0,1},{1,2},{2,3},{3,0},{4,5},{5,6},{6,7},{7,4},{8,9},{9,10},{10,1... | collective-permute-start | bytes 24584 | tf_op jit(solution)/shard_map/ppermute | solution.py:73
  31.5 7.0 %collective-permute-start.3 = (bf16[12,2048]{1,0:T(8,128)(2,1)S(1)}, bf16[12,2048]{1,0:T(8,128)(2,1)S(1)}, u32[]{:S(2)}, u32[]{:S(2)}) collective-permute-start(bf16[12,2048]{1,0:T(8,128)(2,1)S(1)} %concatenate.15), channel_id=1, source_target_pairs={{0,5},{1,6},{2,7},{3,4},{4,1},{5,2},{6,3},{7,0},{8,13},{9,14},{10,... | collective-permute-start | bytes 147464 | tf_op jit(solution)/shard_map/ppermute | solution.py:79
  31.5 7.0 %collective-permute-start.4 = (bf16[12,2048]{1,0:T(8,128)(2,1)S(1)}, bf16[12,2048]{1,0:T(8,128)(2,1)S(1)}, u32[]{:S(2)}, u32[]{:S(2)}) collective-permute-start(bf16[12,2048]{1,0:T(8,128)(2,1)S(1)} %concatenate.16), channel_id=1, source_target_pairs={{0,7},{1,4},{2,5},{3,6},{4,3},{5,0},{6,1},{7,2},{8,15},{9,12},{10,... | collective-permute-start | bytes 147464 | tf_op jit(solution)/shard_map/ppermute | solution.py:79

commit v2 on v1

v2 whole, which is shorter than its diff:
```python
import functools

import jax
import jax.numpy as jnp
from jax import lax
from jax.experimental import pallas as pl
from jax.experimental.pallas import tpu as pltpu
from jax.sharding import PartitionSpec as P

NZ = 32
LANES = 128
SUB = 8
DEGREE = 4
HALO = DEGREE
EDGE = 8

CHEB = (
    1.021021021021021,
    -1.7357357357357357,
    1.4753753753753753,
    -1.254069069069069,
    1.0659587087087088,
)


def power_coeffs():
    c0, c1, c2, c3, c4 = CHEB
    return (
        c0 - c2 + c4,
        -(c1 - 3.0 * c3) / 6.0,
        (2.0 * c2 - 8.0 * c4) / 36.0,
        -4.0 * c3 / 216.0,
        8.0 * c4 / 1296.0,
    )


CORNER_LOW = ((0, 5, 3), (1, 6, 2), (2, 7, 1), (5, 7, 1), (6, 6, 2), (7, 5, 3))
CORNER_HIGH = tuple((row, 0, count) for row, _, count in CORNER_LOW)


def ring(axis, step):
    count = lax.axis_size(axis)
    return [(i, (i + step) % count) for i in range(count)]


def diagonal(step_x, step_y):
    count_x, count_y = lax.axis_size("sx"), lax.axis_size("sy")
    return [
        (i * count_y + j, (i + step_x) % count_x * count_y + (j + step_y) % count_y)
        for i in range(count_x)
        for j in range(count_y)
    ]


def candidates_kernel(slots, orbitals, out):
    lane = lax.broadcasted_iota(jnp.int32, (EDGE, LANES), 1)
    per_tile = LANES // NZ
    rounds, places = slots.shape
    for row in range(EDGE):
        packed = jnp.zeros((EDGE, LANES), jnp.float32)
        for index in range(rounds * places):
            slot = slots[index // places, index % places]
            first = pl.multiple_of(slot // per_tile * LANES, LANES)
            tile = orbitals[row, :, pl.ds(first, LANES)].astype(jnp.float32)
            shift = (index - slot % per_tile + per_tile) % per_tile * NZ
            packed = jnp.where(lane // NZ == index, pltpu.roll(tile, shift, 1), packed)
        out[row] = packed.astype(jnp.bfloat16)


def candidates(orbitals, src_slot):
    vmem = pl.BlockSpec(memory_space=pltpu.VMEM)
    return pl.pallas_call(
        candidates_kernel,
        out_shape=jax.ShapeDtypeStruct(orbitals.shape[:2] + (LANES,), jnp.bfloat16),
        in_specs=[pl.BlockSpec(memory_space=pltpu.SMEM), vmem],
        out_specs=vmem,
        name="candidates",
    )(src_slot, orbitals)


def messages_kernel(count, owner, orbitals, *refs):
    offered, (block, last, first, corner_low, corner_high) = refs[:count], refs[count:]
    groups = orbitals.shape[2] // LANES
    me = lax.axis_index("orb")
    lane = lax.broadcasted_iota(jnp.int32, (EDGE, LANES), 1)
    rounds, places = owner.shape
    wanted = jnp.zeros((EDGE, LANES), jnp.int32)
    for index in range(rounds * places):
        wanted = jnp.where(lane // NZ == index, owner[index // places, index % places], wanted)
    for group in range(groups + 1):
        lanes = pl.ds(group * LANES, LANES)
        tiles = []
        for row in range(EDGE):
            if group < groups:
                tile = orbitals[row, :, lanes].astype(jnp.float32)
            else:
                tile = offered[0][row].astype(jnp.float32)
                for step in range(1, count):
                    theirs = offered[step][row].astype(jnp.float32)
                    tile = jnp.where(wanted == lax.rem(me + count - step, count), theirs, tile)
            tiles.append(tile)
            block[row, :, lanes] = tile.astype(jnp.bfloat16)
            last[row, :, lanes] = tile[EDGE - HALO :].astype(jnp.bfloat16)
            first[row, :, lanes] = tile[:HALO].astype(jnp.bfloat16)
        for ref, cells in ((corner_low, CORNER_LOW), (corner_high, CORNER_HIGH)):
            parts = [tiles[row][start : start + rows] for row, start, rows in cells]
            ref[:, lanes] = jnp.concatenate(parts, axis=0).astype(jnp.bfloat16)


def messages(orbitals, mine, src_owner):
    count = lax.axis_size("orb")
    offered = [mine] + [lax.ppermute(mine, "orb", ring("orb", step)) for step in range(1, count)]
    width = orbitals.shape[2] + LANES
    corners = sum(rows for _, _, rows in CORNER_LOW)
    shapes = [(EDGE, EDGE, width)] + [(EDGE, HALO, width)] * 2 + [(corners, width)] * 2
    vmem = pl.BlockSpec(memory_space=pltpu.VMEM)
    return pl.pallas_call(
        functools.partial(messages_kernel, count),
        out_shape=[jax.ShapeDtypeStruct(shape, jnp.bfloat16) for shape in shapes],
        in_specs=[pl.BlockSpec(memory_space=pltpu.SMEM)] + [vmem] * (1 + count),
        out_specs=[vmem] * 5,
        name="messages",
    )(src_owner, orbitals, *offered)


def exchange(block, last, first, corner_low, corner_high):
    both = ("sx", "sy")
    if lax.axis_size("sx") == 2:
        low = lax.ppermute(corner_low, both, diagonal(1, 1))
        high = lax.ppermute(corner_high, both, diagonal(1, -1))
        across = lax.ppermute(block, "sx", ring("sx", 1))
    else:
        half = corner_low.shape[0] // 2

        def split(cells, step_y):
            return jnp.concatenate(
                [
                    lax.ppermute(cells[:half], both, diagonal(-1, step_y)),
                    lax.ppermute(cells[half:], both, diagonal(1, step_y)),
                ],
                axis=0,
            )

        low, high = split(corner_low, 1), split(corner_high, -1)
        across = jnp.concatenate(
            [
                lax.ppermute(block[:HALO], "sx", ring("sx", -1)),
                lax.ppermute(block[EDGE - HALO :], "sx", ring("sx", 1)),
            ],
            axis=0,
        )
    below = lax.ppermute(last, "sy", ring("sy", 1))
    above = lax.ppermute(first, "sy", ring("sy", -1))
    return across, below, above, low, high


def fill(cells, sources, own, across, below, above, corner_low, corner_high):
    groups = own.shape[2] // LANES - 1
    pitch = cells.shape[1] // (2 * HALO + EDGE)

    def put(x, y, rows, group, values):
        if group == groups:
            sources[x, pl.ds(y, rows), :] = values
        else:
            cells[x, pl.ds(y * pitch + group, rows, stride=pitch), :] = values

    for group in range(groups + 1):
        lanes = pl.ds(group * LANES, LANES)
        for row in range(EDGE):
            outer = row - EDGE if row >= HALO else row + EDGE
            put(HALO + row, HALO, EDGE, group, own[row, :, lanes].astype(jnp.float32))
            put(HALO + outer, HALO, EDGE, group, across[row, :, lanes].astype(jnp.float32))
            put(HALO + row, 0, HALO, group, below[row, :, lanes].astype(jnp.float32))
            put(HALO + row, HALO + EDGE, HALO, group, above[row, :, lanes].astype(jnp.float32))
        for ref, spots, shift in (
            (corner_low, CORNER_LOW, HALO - EDGE),
            (corner_high, CORNER_HIGH, HALO + EDGE),
        ):
            values = ref[:, lanes].astype(jnp.float32)
            at = 0
            for row, first, count in spots:
                outer = row - EDGE if row >= HALO else row + EDGE
                put(HALO + outer, first + shift, count, group, values[at : at + count])
                at += count


def reach(x, y):
    out_x = max(HALO - x, x - (HALO + EDGE - 1), 0)
    out_y = max(HALO - y, y - (HALO + EDGE - 1), 0)
    return out_x + out_y


def kernel(count, *refs):
    halo, (out, cells, rows_of, src, dens, work_a, work_b, acc) = refs[:6], refs[6:]
    groups = halo[0].shape[2] // LANES - 1
    size = 2 * HALO + EDGE
    pitch = cells.shape[1] // size
    halves = groups // SUB
    p0, p1, p2, p3, p4 = power_coeffs()
    tail = (p3 / p4, p2 / p4, p1 / p4, p0 / p4)

    fill(cells, rows_of, *halo)
    spots = [
        [[y for y in range(size) if reach(x, y) <= radius] for x in range(size)]
        for radius in range(HALO + 1)
    ]
    lane = lax.broadcasted_iota(jnp.int32, (SUB, LANES), 1)
    for x in range(size):
        for y in range(0, size, SUB):
            rows = rows_of[x, pl.ds(y, SUB), :]
            for place in range(count):
                one = jnp.where(lane // NZ == place, rows, 0.0)
                one = one + pltpu.roll(one, NZ, 1)
                one = one + pltpu.roll(one, 2 * NZ, 1)
                for step in range(SUB):
                    if y + step in spots[HALO][x]:
                        src[place, x, y + step] = jnp.broadcast_to(
                            one[step : step + 1], (SUB, LANES)
                        )

    inner = lane % NZ
    not_first, not_last = inner != 0, inner != NZ - 1

    def z_sum(v):
        lower = jnp.where(not_first, pltpu.roll(v, 1, 1), 0.0)
        upper = jnp.where(not_last, pltpu.roll(v, LANES - 1, 1), 0.0)
        return lower + upper

    def one_pass(index, carry):
        place, half = index // halves, index % halves
        base = half * SUB

        for x in range(size):
            row = spots[HALO][x]
            values = [cells[x, pl.ds(y * pitch + base, SUB), :] for y in row]
            spread = [src[place, x, y] for y in row]
            for y, value, other in zip(row, values, spread):
                dens[x, y] = value * other
        old = dens
        for step in range(DEGREE):
            new = (work_a, work_b, work_a, None)[step]
            targets = spots[HALO - 1 - step]
            known = spots[HALO - step]
            here, pair_prev = {y: old[0, y] for y in known[0]}, {}
            for x in range(size - 1):
                ahead = {y: old[x + 1, y] for y in known[x + 1]}
                pair = {}
                for y in range(size - 1):
                    if y in targets[x] or y + 1 in targets[x + 1]:
                        pair[y] = ahead[y] + here[y + 1]
                extra = [dens[x, y] for y in targets[x]]
                totals = []
                for y, density in zip(targets[x], extra):
                    total = pair[y] + pair_prev[y - 1] + z_sum(here[y])
                    totals.append(total + tail[step] * density)
                if new is not None:
                    for y, total in zip(targets[x], totals):
                        new[x, y] = total
                elif totals:
                    spread = [src[place, x, y] for y in targets[x]]
                    at = [((y - HALO) * pitch + base) for y in targets[x]]
                    before = [acc[x - HALO, pl.ds(start, SUB), :] for start in at]
                    for i, start in enumerate(at):
                        acc[x - HALO, pl.ds(start, SUB), :] = before[i] + totals[i] * spread[i]
                here, pair_prev = ahead, pair
            old = new
        return carry

    acc[...] = jnp.zeros(acc.shape, jnp.float32)
    lax.fori_loop(0, count * halves, one_pass, 0)
    for x in range(EDGE):
        for group in range(groups):
            tile = acc[x, pl.ds(group, EDGE, stride=pitch), :]
            out[x, :, pl.ds(group * LANES, LANES)] = tile * (-p4)


def fields(halo, count):
    rows_x, rows_y, width = halo[0].shape
    width = width - LANES
    size = 2 * HALO + EDGE
    pitch = width // LANES + 1
    vmem = pl.BlockSpec(memory_space=pltpu.VMEM)
    plane = pltpu.VMEM((size, size, SUB, LANES), jnp.float32)
    return pl.pallas_call(
        functools.partial(kernel, count),
        out_shape=jax.ShapeDtypeStruct((rows_x, rows_y, width), jnp.float32),
        in_specs=[vmem] * 6,
        out_specs=vmem,
        scratch_shapes=[
            pltpu.VMEM((size, size * pitch, LANES), jnp.float32),
            pltpu.VMEM((size, size, LANES), jnp.float32),
            pltpu.VMEM((count, size, size, SUB, LANES), jnp.float32),
            plane,
            plane,
            plane,
            pltpu.VMEM((rows_x, rows_y * pitch, LANES), jnp.float32),
        ],
        compiler_params=pltpu.CompilerParams(vmem_limit_bytes=40 * 2**20),
        name="fields",
    )(*halo)


def body(orbitals, src_owner, src_slot):
    packed = messages(orbitals, candidates(orbitals, src_slot), src_owner)
    return fields((packed[0], *exchange(*packed)), src_slot.size)


def solution(mesh):
    in_specs = (P("sx", "sy", "orb"), P(), P())
    out_specs = P("sx", "sy", "orb")
    return jax.shard_map(body, mesh=mesh, in_specs=in_specs, out_specs=out_specs, check_vma=False)
```

time: 52.9 us -> 37.3 us (0.71)
  starting transfers between devices: 20.4 us -> 13.2 us
  waiting for transfers between devices: 10.4 us -> 6.01 us
  between operations: 2.87 us -> 0.03 us
  local copies, waits for them, and re-layouts: 4.75 us -> 2.15 us
  Pallas kernels: 14.2 us -> 15.7 us
    ppermute x13 -> x8, starting transfers between devices: 20.4 us -> 13.2 us  [the longest x1 4.72 us: exchange(): high = lax.ppermute(corner_high, both, diagonal(1, -1))]
    ppermute x13 -> x8, waiting for transfers between devices: 10.4 us -> 6.01 us  [the longest x3 3.32 us: messages(): lax.ppermute(mine, 'orb', ring('orb', step))]
    pallas_call x0 -> x2, Pallas kernels: none -> 3.64 us  [the longest x1 1.97 us: messages(): pl.pallas_call(functools.partial(messages_kernel, count), out_shape=[jax....]
    pallas_call x1, Pallas kernels: 14.2 us -> 12.1 us  [fields(): pl.pallas_call(functools.partial(kernel, count), out_shape=jax.ShapeDtype...]
    unnamed x4 -> x8, local copies, waits for them, and re-layouts: 0.67 us -> 2.15 us
    dynamic_slice x1 -> x0, local copies, waits for them, and re-layouts: 0.89 us -> none  [candidates(): lax.dynamic_slice_in_dim(orbitals, slots[i] * NZ, NZ, 2)]
    reshape x1 -> x0, local copies, waits for them, and re-layouts: 0.8 us -> none  [candidates(): slots = src_slot.reshape(-1)]
    slice x3 -> x0, local copies, waits for them, and re-layouts: 0.79 us -> none  [the longest x1 0.67 us: candidates(): slots[i] * NZ]
  transfers between devices with their start and end apart: 13 -> 8, of which waited for: 4 -> 3; matrix products, arithmetic and copies ran while one was open for 3% -> 0% of each run, Pallas kernels for 0% -> 0%
where the time goes in v2:
time: 37.3 us; the launch traced here: 37.1 us
  Pallas kernels  15.7 us (42%)
  starting transfers between devices  13.2 us (35%)
  waiting for transfers between devices  6.01 us (16%)
  local copies, waits for them, and re-layouts  2.15 us (6%)
    pallas_call x1, Pallas kernels, fields(): pl.pallas_call(functools.partial(kernel, count), out_shape=jax.ShapeDtype...  12.1 us
    ppermute x1, starting transfers between devices, exchange(): high = lax.ppermute(corner_high, both, diagonal(1, -1))  4.72 us
    ppermute x3, waiting for transfers between devices, messages(): lax.ppermute(mine, 'orb', ring('orb', step))  3.32 us
    ppermute x3, starting transfers between devices, messages(): lax.ppermute(mine, 'orb', ring('orb', step))  3.17 us
    ppermute x1, waiting for transfers between devices, exchange(): low = lax.ppermute(corner_low, both, diagonal(1, 1))  2.64 us
    ppermute x1, starting transfers between devices, exchange(): above = lax.ppermute(first, 'sy', ring('sy', -1))  2.25 us
    unnamed x8, local copies, waits for them, and re-layouts  2.15 us
    pallas_call x1, Pallas kernels, messages(): pl.pallas_call(functools.partial(messages_kernel, count), out_shape=[jax....  1.97 us
  transfers between devices with their start and end apart: 8, of which 3 were waited for; matrix products, arithmetic and copies ran while one was open for 0% of the time, Pallas kernels for 0%

profile of v2, /device:TPU:0, one launch (start us, length us, event | category | flops | bytes accessed | tf_op | source)
XLA Modules:
  0.0 37.1 jit_solution(3734384348423920681)
XLA Ops:
  0.0 1.7 %candidates.1.refs_0_ = bf16[8,8,128]{2,1,0:T(8,128)(2,1)} custom-call(s32[2,2]{1,0:T(2,128)} %slots.1, bf16[8,8,2048]{2,1,0:T(8,128)(2,1)} %orbitals.3), custom_call_target="tpu_custom_call" | custom-call | tf_op jit(solution)/shard_map/candidates/pallas_call | solution.py:72
  1.7 2.4 %collective-permute-start.2 = (bf16[8,8,128]{2,1,0:T(8,128)(2,1)}, bf16[8,8,128]{2,1,0:T(8,128)(2,1)S(1)}, u32[]{:S(2)}, u32[]{:S(2)}) collective-permute-start(bf16[8,8,128]{2,1,0:T(8,128)(2,1)} %candidates.1.refs_0_), channel_id=1, source_target_pairs={{0,24},{8,0},{16,8},{24,16},{1,25},{9,1},{17,9},{25,17},{2,26},{10... | collective-permute-start | bytes 49160 | tf_op jit(solution)/shard_map/ppermute | solution.py:112
  4.1 0.6 %collective-permute-start.1 = (bf16[8,8,128]{2,1,0:T(8,128)(2,1)}, bf16[8,8,128]{2,1,0:T(8,128)(2,1)S(1)}, u32[]{:S(2)}, u32[]{:S(2)}) collective-permute-start(bf16[8,8,128]{2,1,0:T(8,128)(2,1)} %candidates.1.refs_0_), channel_id=1, source_target_pairs={{0,16},{8,24},{16,0},{24,8},{1,17},{9,25},{17,1},{25,9},{2,18},{10... | collective-permute-start | bytes 49160 | tf_op jit(solution)/shard_map/ppermute | solution.py:112
  4.6 0.2 collective-permute-start
  4.8 0.9 %collective-permute-done.2.refs_3_ = bf16[8,8,128]{2,1,0:T(8,128)(2,1)S(1)} collective-permute-done((bf16[8,8,128]{2,1,0:T(8,128)(2,1)}, bf16[8,8,128]{2,1,0:T(8,128)(2,1)S(1)}, u32[]{:S(2)}, u32[]{:S(2)}) %collective-permute-start.2) | collective-permute-done | bytes 16416 | tf_op jit(solution)/shard_map/ppermute | solution.py:112
  5.7 0.0 copy-start.1
  5.7 2.5 %collective-permute-done.1.refs_2_ = bf16[8,8,128]{2,1,0:T(8,128)(2,1)S(1)} collective-permute-done((bf16[8,8,128]{2,1,0:T(8,128)(2,1)}, bf16[8,8,128]{2,1,0:T(8,128)(2,1)S(1)}, u32[]{:S(2)}, u32[]{:S(2)}) %collective-permute-start.1) | collective-permute-done | bytes 16416 | tf_op jit(solution)/shard_map/ppermute | solution.py:112
  8.2 0.0 copy-start.2
  8.2 0.0 collective-permute-done.refs_1_
  8.2 0.0 copy-done.1
  8.2 0.6 %copy-done.2 = bf16[8,8,128]{2,1,0:T(8,128)(2,1)} copy-done((bf16[8,8,128]{2,1,0:T(8,128)(2,1)}, bf16[8,8,128]{2,1,0:T(8,128)(2,1)S(1)}, u32[]{:S(2)}) %copy-start.2) | copy-done | bytes 16408
  8.8 0.0 copy-start.3
  8.8 0.6 %copy-done.3 = bf16[8,8,128]{2,1,0:T(8,128)(2,1)} copy-done((bf16[8,8,128]{2,1,0:T(8,128)(2,1)}, bf16[8,8,128]{2,1,0:T(8,128)(2,1)S(1)}, u32[]{:S(2)}) %copy-start.3) | copy-done | bytes 16408
  9.4 2.0 %messages.1 = (bf16[8,8,2176]{2,1,0:T(8,128)(2,1)}, bf16[8,4,2176]{2,1,0:T(4,128)(2,1)}, bf16[8,4,2176]{2,1,0:T(4,128)(2,1)}, bf16[12,2176]{1,0:T(8,128)(2,1)}, bf16[12,2176]{1,0:T(8,128)(2,1)}) custom-call(s32[2,2]{1,0:T(2,128)} %owner.1, bf16[8,8,2048]{2,1,0:T(8,128)(2,1)} %orbitals.3, bf16[8,8,128]{2,1,0:T(8,128)(2,1)} %candidates.1.refs_0_, ...), custom_call_target="tpu_custom_call" | custom-call | tf_op jit(solution)/shard_map/messages/pallas_call | solution.py:117
  11.3 1.5 %collective-permute-start.3 = (bf16[8,8,2176]{2,1,0:T(8,128)(2,1)}, bf16[8,8,2176]{2,1,0:T(8,128)(2,1)S(1)}, u32[]{:S(2)}, u32[]{:S(2)}) collective-permute-start(bf16[8,8,2176]{2,1,0:T(8,128)(2,1)} %get-tuple-element.10.refs_0_), channel_id=1, source_target_pairs={{0,4},{4,0},{1,5},{5,1},{2,6},{6,2},{3,7},{7,3},{8,12},{12,8},{9,1... | collective-permute-start | bytes 835592 | tf_op jit(solution)/shard_map/ppermute | solution.py:131
  12.9 1.6 %collective-permute-start.4 = (bf16[8,4,2176]{2,1,0:T(4,128)(2,1)}, bf16[8,4,2176]{2,1,0:T(4,128)(2,1)S(1)}, u32[]{:S(2)}, u32[]{:S(2)}) collective-permute-start(bf16[8,4,2176]{2,1,0:T(4,128)(2,1)} %get-tuple-element.11), channel_id=1, source_target_pairs={{0,1},{1,2},{2,3},{3,0},{4,5},{5,6},{6,7},{7,4},{8,9},{9,10},{10,1... | collective-permute-start | bytes 417800 | tf_op jit(solution)/shard_map/ppermute | solution.py:152
  14.4 2.2 %collective-permute-start.5 = (bf16[8,4,2176]{2,1,0:T(4,128)(2,1)}, bf16[8,4,2176]{2,1,0:T(4,128)(2,1)S(1)}, u32[]{:S(2)}, u32[]{:S(2)}) collective-permute-start(bf16[8,4,2176]{2,1,0:T(4,128)(2,1)} %get-tuple-element.12), channel_id=1, source_target_pairs={{0,3},{1,0},{2,1},{3,2},{4,7},{5,4},{6,5},{7,6},{8,11},{9,8},{10,9... | collective-permute-start | bytes 417800 | tf_op jit(solution)/shard_map/ppermute | solution.py:153
  16.7 0.0 collective-permute-start.6
  16.7 4.7 %collective-permute-start.7 = (bf16[12,2176]{1,0:T(8,128)(2,1)}, bf16[12,2176]{1,0:T(8,128)(2,1)S(1)}, u32[]{:S(2)}, u32[]{:S(2)}) collective-permute-start(bf16[12,2176]{1,0:T(8,128)(2,1)} %get-tuple-element.14), channel_id=1, source_target_pairs={{0,7},{1,4},{2,5},{3,6},{4,3},{5,0},{6,1},{7,2},{8,15},{9,12},{10,... | collective-permute-start | bytes 156680 | tf_op jit(solution)/shard_map/ppermute | solution.py:130
  21.4 2.6 %collective-permute-done.6.refs_4_ = bf16[12,2176]{1,0:T(8,128)(2,1)S(1)} collective-permute-done((bf16[12,2176]{1,0:T(8,128)(2,1)}, bf16[12,2176]{1,0:T(8,128)(2,1)S(1)}, u32[]{:S(2)}, u32[]{:S(2)}) %collective-permute-start.6) | collective-permute-done | bytes 52256 | tf_op jit(solution)/shard_map/ppermute | solution.py:129
  24.0 0.0 collective-permute-done.7.refs_5_
  24.1 0.0 collective-permute-done.4.refs_2_
  24.1 0.0 collective-permute-done.5.refs_3_
  24.1 0.0 collective-permute-done.3.refs_1_
  24.1 0.0 copy-start
  24.1 0.9 %copy-done = bf16[8,8,2176]{2,1,0:T(8,128)(2,1)S(1)} copy-done((bf16[8,8,2176]{2,1,0:T(8,128)(2,1)S(1)}, bf16[8,8,2176]{2,1,0:T(8,128)(2,1)}, u32[]{:S(2)}) %copy-start) | copy-done | bytes 278552
  25.1 12.1 %fields.1 = f32[8,8,2048]{2,1,0:T(8,128)} custom-call(bf16[8,8,2176]{2,1,0:T(8,128)(2,1)S(1)} %copy-done, bf16[8,8,2176]{2,1,0:T(8,128)(2,1)S(1)} %collective-permute-done.3.refs_1_, bf16[8,4,2176]{2,1,0:T(4,128)(2,1)S(1)} %collective-permute-done.4.refs_2_, bf16[8,4,2176]{2,1,0:T(4,128)(2,1)S(1)} %collective-permute-done.5.refs_3_, ...), custom_call_target="tpu_custom_call" | custom-call | tf_op jit(solution)/shard_map/fields/pallas_call | solution.py:284
Async XLA Ops:
  1.7 4.0 %collective-permute-start.2 = (bf16[8,8,128]{2,1,0:T(8,128)(2,1)}, bf16[8,8,128]{2,1,0:T(8,128)(2,1)S(1)}, u32[]{:S(2)}, u32[]{:S(2)}) collective-permute-start(bf16[8,8,128]{2,1,0:T(8,128)(2,1)} %candidates.1.refs_0_), channel_id=1, source_target_pairs={{0,24},{8,0},{16,8},{24,16},{1,25},{9,1},{17,9},{25,17},{2,26},{10... | collective-permute-start | bytes 49160 | tf_op jit(solution)/shard_map/ppermute | solution.py:112
  4.1 4.1 %collective-permute-start.1 = (bf16[8,8,128]{2,1,0:T(8,128)(2,1)}, bf16[8,8,128]{2,1,0:T(8,128)(2,1)S(1)}, u32[]{:S(2)}, u32[]{:S(2)}) collective-permute-start(bf16[8,8,128]{2,1,0:T(8,128)(2,1)} %candidates.1.refs_0_), channel_id=1, source_target_pairs={{0,16},{8,24},{16,0},{24,8},{1,17},{9,25},{17,1},{25,9},{2,18},{10... | collective-permute-start | bytes 49160 | tf_op jit(solution)/shard_map/ppermute | solution.py:112
  4.6 3.6 %collective-permute-start = (bf16[8,8,128]{2,1,0:T(8,128)(2,1)}, bf16[8,8,128]{2,1,0:T(8,128)(2,1)S(1)}, u32[]{:S(2)}, u32[]{:S(2)}) collective-permute-start(bf16[8,8,128]{2,1,0:T(8,128)(2,1)} %candidates.1.refs_0_), channel_id=1, source_target_pairs={{0,8},{8,16},{16,24},{24,0},{1,9},{9,17},{17,25},{25,1},{2,10},{10... | collective-permute-start | bytes 49160 | tf_op jit(solution)/shard_map/ppermute | solution.py:112
  5.7 2.5 %copy-start.1 = (bf16[8,8,128]{2,1,0:T(8,128)(2,1)}, bf16[8,8,128]{2,1,0:T(8,128)(2,1)S(1)}, u32[]{:S(2)}) copy-start(bf16[8,8,128]{2,1,0:T(8,128)(2,1)S(1)} %collective-permute-done.2.refs_3_) | copy-start | bytes 49156
  8.2 0.6 %copy-start.2 = (bf16[8,8,128]{2,1,0:T(8,128)(2,1)}, bf16[8,8,128]{2,1,0:T(8,128)(2,1)S(1)}, u32[]{:S(2)}) copy-start(bf16[8,8,128]{2,1,0:T(8,128)(2,1)S(1)} %collective-permute-done.1.refs_2_) | copy-start | bytes 49156
  8.8 0.6 %copy-start.3 = (bf16[8,8,128]{2,1,0:T(8,128)(2,1)}, bf16[8,8,128]{2,1,0:T(8,128)(2,1)S(1)}, u32[]{:S(2)}) copy-start(bf16[8,8,128]{2,1,0:T(8,128)(2,1)S(1)} %collective-permute-done.refs_1_) | copy-start | bytes 49156
  11.3 12.8 %collective-permute-start.3 = (bf16[8,8,2176]{2,1,0:T(8,128)(2,1)}, bf16[8,8,2176]{2,1,0:T(8,128)(2,1)S(1)}, u32[]{:S(2)}, u32[]{:S(2)}) collective-permute-start(bf16[8,8,2176]{2,1,0:T(8,128)(2,1)} %get-tuple-element.10.refs_0_), channel_id=1, source_target_pairs={{0,4},{4,0},{1,5},{5,1},{2,6},{6,2},{3,7},{7,3},{8,12},{12,8},{9,1... | collective-permute-start | bytes 835592 | tf_op jit(solution)/shard_map/ppermute | solution.py:131
  12.9 11.2 %collective-permute-start.4 = (bf16[8,4,2176]{2,1,0:T(4,128)(2,1)}, bf16[8,4,2176]{2,1,0:T(4,128)(2,1)S(1)}, u32[]{:S(2)}, u32[]{:S(2)}) collective-permute-start(bf16[8,4,2176]{2,1,0:T(4,128)(2,1)} %get-tuple-element.11), channel_id=1, source_target_pairs={{0,1},{1,2},{2,3},{3,0},{4,5},{5,6},{6,7},{7,4},{8,9},{9,10},{10,1... | collective-permute-start | bytes 417800 | tf_op jit(solution)/shard_map/ppermute | solution.py:152
  14.4 9.7 %collective-permute-start.5 = (bf16[8,4,2176]{2,1,0:T(4,128)(2,1)}, bf16[8,4,2176]{2,1,0:T(4,128)(2,1)S(1)}, u32[]{:S(2)}, u32[]{:S(2)}) collective-permute-start(bf16[8,4,2176]{2,1,0:T(4,128)(2,1)} %get-tuple-element.12), channel_id=1, source_target_pairs={{0,3},{1,0},{2,1},{3,2},{4,7},{5,4},{6,5},{7,6},{8,11},{9,8},{10,9... | collective-permute-start | bytes 417800 | tf_op jit(solution)/shard_map/ppermute | solution.py:153
  16.7 7.4 %collective-permute-start.6 = (bf16[12,2176]{1,0:T(8,128)(2,1)}, bf16[12,2176]{1,0:T(8,128)(2,1)S(1)}, u32[]{:S(2)}, u32[]{:S(2)}) collective-permute-start(bf16[12,2176]{1,0:T(8,128)(2,1)} %get-tuple-element.13), channel_id=1, source_target_pairs={{0,5},{1,6},{2,7},{3,4},{4,1},{5,2},{6,3},{7,0},{8,13},{9,14},{10,... | collective-permute-start | bytes 156680 | tf_op jit(solution)/shard_map/ppermute | solution.py:129
  16.7 7.4 %collective-permute-start.7 = (bf16[12,2176]{1,0:T(8,128)(2,1)}, bf16[12,2176]{1,0:T(8,128)(2,1)S(1)}, u32[]{:S(2)}, u32[]{:S(2)}) collective-permute-start(bf16[12,2176]{1,0:T(8,128)(2,1)} %get-tuple-element.14), channel_id=1, source_target_pairs={{0,7},{1,4},{2,5},{3,6},{4,3},{5,0},{6,1},{7,2},{8,15},{9,12},{10,... | collective-permute-start | bytes 156680 | tf_op jit(solution)/shard_map/ppermute | solution.py:130
  24.1 1.0 %copy-start = (bf16[8,8,2176]{2,1,0:T(8,128)(2,1)S(1)}, bf16[8,8,2176]{2,1,0:T(8,128)(2,1)}, u32[]{:S(2)}) copy-start(bf16[8,8,2176]{2,1,0:T(8,128)(2,1)} %get-tuple-element.10.refs_0_) | copy-start | bytes 835588

commit v3 on v2

v3 whole, which is shorter than its diff:
```python
import functools

import jax
import jax.numpy as jnp
from jax import lax
from jax.experimental import pallas as pl
from jax.experimental.pallas import tpu as pltpu
from jax.sharding import PartitionSpec as P

NZ = 32
LANES = 128
SUB = 8
ROWS = 16
DEGREE = 4
HALO = DEGREE
EDGE = 8

CHEB = (
    1.021021021021021,
    -1.7357357357357357,
    1.4753753753753753,
    -1.254069069069069,
    1.0659587087087088,
)


def power_coeffs():
    c0, c1, c2, c3, c4 = CHEB
    return (
        c0 - c2 + c4,
        -(c1 - 3.0 * c3) / 6.0,
        (2.0 * c2 - 8.0 * c4) / 36.0,
        -4.0 * c3 / 216.0,
        8.0 * c4 / 1296.0,
    )


CORNER_LOW = tuple(
    (x, y)
    for x in range(EDGE)
    for y in range(EDGE - HALO, EDGE)
    if min(x + 1, EDGE - x) + EDGE - y <= DEGREE
)
CORNER_HIGH = tuple((x, EDGE - 1 - y) for x, y in CORNER_LOW)
SPLIT = len(CORNER_LOW) // 2


def ring(axis, step):
    count = lax.axis_size(axis)
    return [(i, (i + step) % count) for i in range(count)]


def diagonal(step_x, step_y):
    count_x, count_y = lax.axis_size("sx"), lax.axis_size("sy")
    return [
        (i * count_y + j, (i + step_x) % count_x * count_y + (j + step_y) % count_y)
        for i in range(count_x)
        for j in range(count_y)
    ]


VMEM = pl.BlockSpec(memory_space=pltpu.VMEM)
SMEM = pl.BlockSpec(memory_space=pltpu.SMEM)
SMALL = pltpu.CompilerParams(vmem_limit_bytes=8 * 2**20)


def candidates_kernel(slots, orbitals, out):
    lane = lax.broadcasted_iota(jnp.int32, (EDGE, LANES), 1)
    per_tile = LANES // NZ
    rounds, places = slots.shape
    chosen = [slots[index // places, index % places] for index in range(rounds * places)]
    firsts = [pl.multiple_of(slot // per_tile * LANES, LANES) for slot in chosen]
    shifts = [
        (index - slot % per_tile + per_tile) % per_tile * NZ for index, slot in enumerate(chosen)
    ]
    rows = []
    for row in range(EDGE):
        packed = jnp.zeros((EDGE, LANES), jnp.float32)
        for index, (first, shift) in enumerate(zip(firsts, shifts)):
            tile = orbitals[row, :, pl.ds(first, LANES)].astype(jnp.float32)
            packed = jnp.where(lane // NZ == index, pltpu.roll(tile, shift, 1), packed)
        rows.append(packed)
    for tile in range(EDGE // 2):
        out[tile] = jnp.concatenate(rows[2 * tile : 2 * tile + 2], axis=0).astype(jnp.bfloat16)


def candidates(orbitals, src_slot):
    return pl.pallas_call(
        candidates_kernel,
        out_shape=jax.ShapeDtypeStruct((EDGE * EDGE // ROWS, ROWS, LANES), jnp.bfloat16),
        in_specs=[SMEM, VMEM],
        out_specs=VMEM,
        compiler_params=SMALL,
        name="candidates",
    )(src_slot, orbitals)


def cells_kernel(orbitals, out, scratch):
    for row in range(EDGE):
        for group in range(ROWS):
            tile = orbitals[row, :, pl.ds(group * LANES, LANES)].astype(jnp.float32)
            scratch[row, pl.ds(group, EDGE, stride=ROWS + 1), :] = tile
    for row in range(EDGE):
        for y in range(EDGE):
            tile = scratch[row, pl.ds(y * (ROWS + 1), ROWS), :]
            out[row * EDGE + y] = tile.astype(jnp.bfloat16)


def cells_of(orbitals):
    return pl.pallas_call(
        cells_kernel,
        out_shape=jax.ShapeDtypeStruct((EDGE * EDGE, ROWS, LANES), jnp.bfloat16),
        in_specs=[VMEM],
        out_specs=VMEM,
        scratch_shapes=[pltpu.VMEM((EDGE, EDGE * (ROWS + 1), LANES), jnp.float32)],
        compiler_params=SMALL,
        cost_estimate=pl.CostEstimate(flops=0, bytes_accessed=4 * 2**20, transcendentals=0),
        name="cells",
    )(orbitals)


def messages_kernel(count, owner, cells, *refs):
    offered, (block, last, first, corner_low, corner_high) = refs[:count], refs[count:]
    me = lax.axis_index("orb")
    lane = lax.broadcasted_iota(jnp.int32, (ROWS, LANES), 1)
    rounds, places = owner.shape
    wanted = jnp.zeros((ROWS, LANES), jnp.int32)
    for index in range(rounds * places):
        wanted = jnp.where(lane // NZ == index, owner[index // places, index % places], wanted)
    picked = []
    for tile in range(EDGE * EDGE // ROWS):
        value = offered[0][tile].astype(jnp.float32)
        for step in range(1, count):
            theirs = offered[step][tile].astype(jnp.float32)
            value = jnp.where(wanted == lax.rem(me + count - step, count), theirs, value)
        picked.append(value)

    def pack(ref, spots):
        for at, (x, y) in enumerate(spots):
            ref[at] = cells[x * EDGE + y]
        used = len(spots)
        runs = []
        for x, y in spots:
            if runs and runs[-1][0] == x and runs[-1][2] == y:
                runs[-1][2] = y + 1
            else:
                runs.append([x, y, y + 1])
        parts = [
            picked[x * EDGE // ROWS][x * EDGE % ROWS + low : x * EDGE % ROWS + high]
            for x, low, high in runs
        ]
        if used % ROWS:
            parts.append(jnp.zeros((ROWS - used % ROWS, LANES), jnp.float32))
        rows = jnp.concatenate(parts, axis=0).astype(jnp.bfloat16)
        for tile in range(rows.shape[0] // ROWS):
            ref[used + tile] = rows[tile * ROWS : (tile + 1) * ROWS]

    pack(block, [(x, y) for x in range(EDGE) for y in range(EDGE)])
    pack(last, [(x, y) for x in range(EDGE) for y in range(EDGE - HALO, EDGE)])
    pack(first, [(x, y) for x in range(EDGE) for y in range(HALO)])
    pack(corner_low, CORNER_LOW)
    pack(corner_high, CORNER_HIGH)


def tiles(spots):
    return spots + -(-spots // ROWS)


def messages(orbitals, mine, src_owner):
    count = lax.axis_size("orb")
    offered = [mine] + [lax.ppermute(mine, "orb", ring("orb", step)) for step in range(1, count)]
    lengths = [EDGE * EDGE] + [EDGE * HALO] * 2 + [len(CORNER_LOW)] * 2
    return pl.pallas_call(
        functools.partial(messages_kernel, count),
        out_shape=[
            jax.ShapeDtypeStruct((tiles(length), ROWS, LANES), jnp.bfloat16) for length in lengths
        ],
        in_specs=[SMEM] + [VMEM] * (1 + count),
        out_specs=[VMEM] * 5,
        compiler_params=SMALL,
        name="messages",
    )(src_owner, cells_of(orbitals), *offered)


def exchange(block, last, first, corner_low, corner_high):
    both = ("sx", "sy")
    if lax.axis_size("sx") == 2:
        low = lax.ppermute(corner_low, both, diagonal(1, 1))
        high = lax.ppermute(corner_high, both, diagonal(1, -1))
        across = lax.ppermute(block, "sx", ring("sx", 1))
    else:
        def two_ways(cells, half, axes, down, up, merge):
            end = 2 * half
            back = lax.ppermute(jnp.concatenate([cells[:half], cells[end:]]), axes, down)
            ahead = lax.ppermute(jnp.concatenate([cells[half:end], cells[end:]]), axes, up)
            return jnp.concatenate([back[:half], ahead[:half], merge(back[half:], ahead[half:])])

        def halves(back, ahead):
            return jnp.concatenate([back[: back.shape[0] // 2], ahead[ahead.shape[0] // 2 :]])

        def rows(back, ahead):
            return jnp.concatenate([back[:, :SPLIT], ahead[:, SPLIT:]], axis=1)

        low = two_ways(corner_low, SPLIT, both, diagonal(-1, 1), diagonal(1, 1), rows)
        high = two_ways(corner_high, SPLIT, both, diagonal(-1, -1), diagonal(1, -1), rows)
        across = two_ways(block, EDGE * HALO, "sx", ring("sx", -1), ring("sx", 1), halves)
    below = lax.ppermute(last, "sy", ring("sy", 1))
    above = lax.ppermute(first, "sy", ring("sy", -1))
    return across, below, above, low, high


def place_of(x, y):
    row, core_x = (x - HALO) % EDGE, HALO <= x < HALO + EDGE
    if HALO <= y < HALO + EDGE:
        return (0 if core_x else 1), row * EDGE + y - HALO
    if y < HALO:
        return (2, row * HALO + y) if core_x else (4, CORNER_LOW.index((row, y + EDGE - HALO)))
    y = y - HALO - EDGE
    return (3, row * HALO + y) if core_x else (5, CORNER_HIGH.index((row, y)))


def reach(x, y):
    out_x = max(HALO - x, x - (HALO + EDGE - 1), 0)
    out_y = max(HALO - y, y - (HALO + EDGE - 1), 0)
    return out_x + out_y


def kernel(count, *refs):
    halo, (out, rows_of, dens, work_a, work_b, acc) = refs[:6], refs[6:]
    size = 2 * HALO + EDGE
    pitch = ROWS + 1
    p0, p1, p2, p3, p4 = power_coeffs()
    tail = (p3 / p4, p2 / p4, p1 / p4, p0 / p4)
    spots = [
        [[y for y in range(size) if reach(x, y) <= radius] for x in range(size)]
        for radius in range(HALO + 1)
    ]

    shape = (LANES, LANES)
    lane = lax.broadcasted_iota(jnp.int32, shape, 1) % NZ
    line = lax.broadcasted_iota(jnp.int32, shape, 0)
    first_row = []
    total = 0
    for ref in halo:
        used = ref.shape[0] * ROWS // (ROWS + 1)
        packed = ref[used:].reshape(-1, LANES)
        first_row.append(total)
        for place in range(count):
            repeat = (line == lane + place * NZ).astype(jnp.bfloat16)
            rows_of[place, pl.ds(total, packed.shape[0]), :] = jnp.dot(
                packed, repeat, preferred_element_type=jnp.float32
            )
        total += packed.shape[0]

    def spread(place, x, y):
        which, at = place_of(x, y)
        row = rows_of[place, pl.ds(first_row[which] + at, 1), :]
        return jnp.broadcast_to(row, (SUB, LANES))

    inner = lax.broadcasted_iota(jnp.int32, (SUB, LANES), 1) % NZ
    not_first, not_last = inner != 0, inner != NZ - 1

    def z_sum(v):
        lower = jnp.where(not_first, pltpu.roll(v, 1, 1), 0.0)
        upper = jnp.where(not_last, pltpu.roll(v, LANES - 1, 1), 0.0)
        return lower + upper

    def one_half(place, half):
        base = half * SUB
        old = dens.at[half]
        for step in range(DEGREE):
            new = (work_a, work_b, work_a, None)[step]
            targets = spots[HALO - 1 - step]
            known = spots[HALO - step]
            here, pair_prev = {y: old[0, y] for y in known[0]}, {}
            for x in range(size - 1):
                ahead = {y: old[x + 1, y] for y in known[x + 1]}
                pair = {}
                for y in range(size - 1):
                    if y in targets[x] or y + 1 in targets[x + 1]:
                        pair[y] = ahead[y] + here[y + 1]
                extra = [dens[half, x, y] for y in targets[x]]
                totals = []
                for y, density in zip(targets[x], extra):
                    value = pair[y] + pair_prev[y - 1] + z_sum(here[y])
                    totals.append(value + tail[step] * density)
                if new is not None:
                    for y, value in zip(targets[x], totals):
                        new[x, y] = value
                elif totals:
                    others = [spread(place, x, y) for y in targets[x]]
                    at = [((y - HALO) * pitch + base) for y in targets[x]]
                    before = [acc[x - HALO, pl.ds(start, SUB), :] for start in at]
                    for i, start in enumerate(at):
                        acc[x - HALO, pl.ds(start, SUB), :] = before[i] + totals[i] * others[i]
                here, pair_prev = ahead, pair
            old = new

    def one_source(place, carry):
        for x in range(size):
            row = spots[HALO][x]
            values = []
            for y in row:
                which, at = place_of(x, y)
                values.append(halo[which][at].astype(jnp.float32))
            others = [spread(place, x, y) for y in row]
            for y, value, other in zip(row, values, others):
                for half in range(ROWS // SUB):
                    dens[half, x, y] = value[half * SUB : (half + 1) * SUB] * other

        def inner_loop(half, carry):
            one_half(place, half)
            return carry

        return lax.fori_loop(0, ROWS // SUB, inner_loop, carry)

    acc[...] = jnp.zeros(acc.shape, jnp.float32)
    lax.fori_loop(0, count, one_source, 0)
    for x in range(EDGE):
        for group in range(ROWS):
            tile = acc[x, pl.ds(group, EDGE, stride=pitch), :]
            out[x, :, pl.ds(group * LANES, LANES)] = tile * (-p4)


def fields(halo, count):
    size = 2 * HALO + EDGE
    plane = pltpu.VMEM((size, size, SUB, LANES), jnp.float32)
    rows = sum(array.shape[0] * ROWS // (ROWS + 1) + ROWS for array in halo)
    return pl.pallas_call(
        functools.partial(kernel, count),
        out_shape=jax.ShapeDtypeStruct((EDGE, EDGE, ROWS * LANES), jnp.float32),
        in_specs=[VMEM] * 6,
        out_specs=VMEM,
        scratch_shapes=[
            pltpu.VMEM((count, rows, LANES), jnp.float32),
            pltpu.VMEM((ROWS // SUB, size, size, SUB, LANES), jnp.float32),
            plane,
            plane,
            pltpu.VMEM((EDGE, EDGE * (ROWS + 1), LANES), jnp.float32),
        ],
        compiler_params=pltpu.CompilerParams(vmem_limit_bytes=16 * 2**20),
        name="fields",
    )(*halo)


def body(orbitals, src_owner, src_slot):
    packed = messages(orbitals, candidates(orbitals, src_slot), src_owner)
    return fields((packed[0], *exchange(*packed)), src_slot.size)


def solution(mesh):
    in_specs = (P("sx", "sy", "orb"), P(), P())
    out_specs = P("sx", "sy", "orb")
    return jax.shard_map(body, mesh=mesh, in_specs=in_specs, out_specs=out_specs, check_vma=False)
```

time: 37.3 us -> 32.3 us (0.87)
  Pallas kernels: 15.7 us -> 11.6 us
  local copies, waits for them, and re-layouts: 2.15 us -> 1.63 us
  waiting for transfers between devices: 6.01 us -> 5.51 us
    pallas_call x1, Pallas kernels: 12.1 us -> 10.2 us  [fields(): pl.pallas_call(functools.partial(kernel, count), out_shape=jax.ShapeDtype...]
    pallas_call x1, Pallas kernels: 1.97 us -> 0.64 us  [messages(): pl.pallas_call(functools.partial(messages_kernel, count), out_shape=[jax....]
    pallas_call x1 -> x2, Pallas kernels: 1.67 us -> 0.72 us  [the longest x1 0.66 us: candidates(): pl.pallas_call(candidates_kernel, out_shape=jax.ShapeDtypeStruct((EDGE *...]
    unnamed x8 -> x6, local copies, waits for them, and re-layouts: 2.15 us -> 1.63 us
  transfers between devices with their start and end apart: 8 -> 8, of which waited for: 3 -> 4; matrix products, arithmetic and copies ran while one was open for 0% -> 0% of each run, Pallas kernels for 0% -> 0%
where the time goes in v3:
time: 32.3 us; the launch traced here: 32.1 us
  starting transfers between devices  13.4 us (41%)
  Pallas kernels  11.6 us (36%)
  waiting for transfers between devices  5.51 us (17%)
  local copies, waits for them, and re-layouts  1.63 us (5%)
    pallas_call x1, Pallas kernels, fields(): pl.pallas_call(functools.partial(kernel, count), out_shape=jax.ShapeDtype...  10.2 us
    ppermute x1, starting transfers between devices, exchange(): high = lax.ppermute(corner_high, both, diagonal(1, -1))  4.72 us
    ppermute x3, starting transfers between devices, messages(): lax.ppermute(mine, 'orb', ring('orb', step))  3.23 us
    ppermute x3, waiting for transfers between devices, messages(): lax.ppermute(mine, 'orb', ring('orb', step))  3.05 us
    ppermute x1, waiting for transfers between devices, exchange(): low = lax.ppermute(corner_low, both, diagonal(1, 1))  2.44 us
    ppermute x1, starting transfers between devices, exchange(): above = lax.ppermute(first, 'sy', ring('sy', -1))  2.25 us
    unnamed x6, local copies, waits for them, and re-layouts  1.63 us
    ppermute x1, starting transfers between devices, exchange(): across = lax.ppermute(block, 'sx', ring('sx', 1))  1.58 us
  transfers between devices with their start and end apart: 8, of which 4 were waited for; matrix products, arithmetic and copies ran while one was open for 0% of the time, Pallas kernels for 0%

profile of v3, /device:TPU:0, one launch (start us, length us, event | category | flops | bytes accessed | tf_op | source)
XLA Modules:
  0.0 32.1 jit_solution(14662741677621118405)
XLA Ops:
  0.0 0.0 copy-start
  0.0 0.9 %copy-done = bf16[8,8,2048]{2,1,0:T(8,128)(2,1)S(1)} copy-done((bf16[8,8,2048]{2,1,0:T(8,128)(2,1)S(1)}, bf16[8,8,2048]{2,1,0:T(8,128)(2,1)}, u32[]{:S(2)}) %copy-start) | copy-done | bytes 262168
  1.0 0.0 copy-start.1
  1.0 0.7 %copy-done.1 = s32[2,2]{1,0:T(2,128)S(1)} copy-done((s32[2,2]{1,0:T(2,128)S(1)}, s32[2,2]{1,0:T(2,128)}, u32[]{:S(2)}) %copy-start.1) | copy-done | bytes 40
  1.6 0.7 %candidates.1.refs_0_ = bf16[4,16,128]{2,1,0:T(8,128)(2,1)S(1)} custom-call(s32[2,2]{1,0:T(2,128)S(1)} %copy-done.1, bf16[8,8,2048]{2,1,0:T(8,128)(2,1)S(1)} %copy-done), custom_call_target="tpu_custom_call" | custom-call | tf_op jit(solution)/shard_map/candidates/pallas_call | solution.py:88
  2.3 0.0 copy-start.2
  2.3 2.4 %collective-permute-start.2 = (bf16[4,16,128]{2,1,0:T(8,128)(2,1)S(1)}, bf16[4,16,128]{2,1,0:T(8,128)(2,1)S(1)}, u32[]{:S(2)}, u32[]{:S(2)}) collective-permute-start(bf16[4,16,128]{2,1,0:T(8,128)(2,1)S(1)} %candidates.1.refs_0_), channel_id=1, source_target_pairs={{0,24},{8,0},{16,8},{24,16},{1,25},{9,1},{17,9},{25,17},{2,26},{10... | collective-permute-start | bytes 49160 | tf_op jit(solution)/shard_map/ppermute | solution.py:171
  4.7 0.6 %collective-permute-start.1 = (bf16[4,16,128]{2,1,0:T(8,128)(2,1)S(1)}, bf16[4,16,128]{2,1,0:T(8,128)(2,1)S(1)}, u32[]{:S(2)}, u32[]{:S(2)}) collective-permute-start(bf16[4,16,128]{2,1,0:T(8,128)(2,1)S(1)} %candidates.1.refs_0_), channel_id=1, source_target_pairs={{0,16},{8,24},{16,0},{24,8},{1,17},{9,25},{17,1},{25,9},{2,18},{10... | collective-permute-start | bytes 49160 | tf_op jit(solution)/shard_map/ppermute | solution.py:171
  5.4 0.2 collective-permute-start
  5.5 0.1 cells.1
  5.6 0.6 %collective-permute-done.2.refs_3_ = bf16[4,16,128]{2,1,0:T(8,128)(2,1)S(1)} collective-permute-done((bf16[4,16,128]{2,1,0:T(8,128)(2,1)S(1)}, bf16[4,16,128]{2,1,0:T(8,128)(2,1)S(1)}, u32[]{:S(2)}, u32[]{:S(2)}) %collective-permute-start.2) | collective-permute-done | bytes 16416 | tf_op jit(solution)/shard_map/ppermute | solution.py:171
  6.2 2.4 %collective-permute-done.1.refs_2_ = bf16[4,16,128]{2,1,0:T(8,128)(2,1)S(1)} collective-permute-done((bf16[4,16,128]{2,1,0:T(8,128)(2,1)S(1)}, bf16[4,16,128]{2,1,0:T(8,128)(2,1)S(1)}, u32[]{:S(2)}, u32[]{:S(2)}) %collective-permute-start.1) | collective-permute-done | bytes 16416 | tf_op jit(solution)/shard_map/ppermute | solution.py:171
  8.6 0.1 collective-permute-done.refs_1_
  8.7 0.0 copy-done.2
  8.7 0.6 %messages.1 = (bf16[68,16,128]{2,1,0:T(8,128)(2,1)S(1)}, bf16[34,16,128]{2,1,0:T(8,128)(2,1)S(1)}, bf16[34,16,128]{2,1,0:T(8,128)(2,1)S(1)}, bf16[13,16,128]{2,1,0:T(8,128)(2,1)S(1)}, bf16[13,16,128]{2,1,0:T(8,128)(2,1)S(1)}) custom-call(s32[2,2]{1,0:T(2,128)S(1)} %copy-done.2, bf16[64,16,128]{2,1,0:T(8,128)(2,1)S(1)} %cells.1, ...), custom_call_target="tpu_custom_call" | custom-call | tf_op jit(solution)/shard_map/messages/pallas_call | solution.py:173
  9.3 1.6 %collective-permute-start.3 = (bf16[68,16,128]{2,1,0:T(8,128)(2,1)S(1)}, bf16[68,16,128]{2,1,0:T(8,128)(2,1)S(1)}, u32[]{:S(2)}, u32[]{:S(2)}) collective-permute-start(bf16[68,16,128]{2,1,0:T(8,128)(2,1)S(1)} %get-tuple-element.10.refs_0_), channel_id=1, source_target_pairs={{0,4},{4,0},{1,5},{5,1},{2,6},{6,2},{3,7},{7,3},{8,12},{12,8},{9,1... | collective-permute-start | bytes 835592 | tf_op jit(solution)/shard_map/ppermute | solution.py:190
  10.9 1.6 %collective-permute-start.4 = (bf16[34,16,128]{2,1,0:T(8,128)(2,1)S(1)}, bf16[34,16,128]{2,1,0:T(8,128)(2,1)S(1)}, u32[]{:S(2)}, u32[]{:S(2)}) collective-permute-start(bf16[34,16,128]{2,1,0:T(8,128)(2,1)S(1)} %get-tuple-element.11), channel_id=1, source_target_pairs={{0,1},{1,2},{2,3},{3,0},{4,5},{5,6},{6,7},{7,4},{8,9},{9,10},{10,1... | collective-permute-start | bytes 417800 | tf_op jit(solution)/shard_map/ppermute | solution.py:207
  12.5 2.2 %collective-permute-start.5 = (bf16[34,16,128]{2,1,0:T(8,128)(2,1)S(1)}, bf16[34,16,128]{2,1,0:T(8,128)(2,1)S(1)}, u32[]{:S(2)}, u32[]{:S(2)}) collective-permute-start(bf16[34,16,128]{2,1,0:T(8,128)(2,1)S(1)} %get-tuple-element.12), channel_id=1, source_target_pairs={{0,3},{1,0},{2,1},{3,2},{4,7},{5,4},{6,5},{7,6},{8,11},{9,8},{10,9... | collective-permute-start | bytes 417800 | tf_op jit(solution)/shard_map/ppermute | solution.py:208
  14.7 0.0 collective-permute-start.6
  14.7 4.7 %collective-permute-start.7 = (bf16[13,16,128]{2,1,0:T(8,128)(2,1)S(1)}, bf16[13,16,128]{2,1,0:T(8,128)(2,1)S(1)}, u32[]{:S(2)}, u32[]{:S(2)}) collective-permute-start(bf16[13,16,128]{2,1,0:T(8,128)(2,1)S(1)} %get-tuple-element.14), channel_id=1, source_target_pairs={{0,7},{1,4},{2,5},{3,6},{4,3},{5,0},{6,1},{7,2},{8,15},{9,12},{10,... | collective-permute-start | bytes 159752 | tf_op jit(solution)/shard_map/ppermute | solution.py:189
  19.4 2.4 %collective-permute-done.6.refs_4_ = bf16[13,16,128]{2,1,0:T(8,128)(2,1)S(1)} collective-permute-done((bf16[13,16,128]{2,1,0:T(8,128)(2,1)S(1)}, bf16[13,16,128]{2,1,0:T(8,128)(2,1)S(1)}, u32[]{:S(2)}, u32[]{:S(2)}) %collective-permute-start.6) | collective-permute-done | bytes 53280 | tf_op jit(solution)/shard_map/ppermute | solution.py:188
  21.9 0.0 collective-permute-done.7.refs_5_
  21.9 0.0 collective-permute-done.4.refs_2_
  21.9 0.0 collective-permute-done.5.refs_3_
  21.9 0.0 collective-permute-done.3.refs_1_
  21.9 10.2 %fields.1 = f32[8,8,2048]{2,1,0:T(8,128)} custom-call(bf16[68,16,128]{2,1,0:T(8,128)(2,1)S(1)} %get-tuple-element.10.refs_0_, bf16[68,16,128]{2,1,0:T(8,128)(2,1)S(1)} %collective-permute-done.3.refs_1_, bf16[34,16,128]{2,1,0:T(8,128)(2,1)S(1)} %collective-permute-done.4.refs_2_, bf16[34,16,128]{2,1,0:T(8,128)(2,1)S(1)} %collective-permute-done.5.refs_3_, ...), custom_call_target="tpu_custom_call" | custom-call | tf_op jit(solution)/shard_map/fields/pallas_call | solution.py:329
Async XLA Ops:
  0.0 0.9 %copy-start = (bf16[8,8,2048]{2,1,0:T(8,128)(2,1)S(1)}, bf16[8,8,2048]{2,1,0:T(8,128)(2,1)}, u32[]{:S(2)}) copy-start(bf16[8,8,2048]{2,1,0:T(8,128)(2,1)} %orbitals.3) | copy-start | bytes 786436
  1.0 0.7 %copy-start.1 = (s32[2,2]{1,0:T(2,128)S(1)}, s32[2,2]{1,0:T(2,128)}, u32[]{:S(2)}) copy-start(s32[2,2]{1,0:T(2,128)} %slots.1) | copy-start | bytes 52
  2.3 6.4 %copy-start.2 = (s32[2,2]{1,0:T(2,128)S(1)}, s32[2,2]{1,0:T(2,128)}, u32[]{:S(2)}) copy-start(s32[2,2]{1,0:T(2,128)} %owner.1) | copy-start | bytes 52
  2.3 3.9 %collective-permute-start.2 = (bf16[4,16,128]{2,1,0:T(8,128)(2,1)S(1)}, bf16[4,16,128]{2,1,0:T(8,128)(2,1)S(1)}, u32[]{:S(2)}, u32[]{:S(2)}) collective-permute-start(bf16[4,16,128]{2,1,0:T(8,128)(2,1)S(1)} %candidates.1.refs_0_), channel_id=1, source_target_pairs={{0,24},{8,0},{16,8},{24,16},{1,25},{9,1},{17,9},{25,17},{2,26},{10... | collective-permute-start | bytes 49160 | tf_op jit(solution)/shard_map/ppermute | solution.py:171
  4.7 3.8 %collective-permute-start.1 = (bf16[4,16,128]{2,1,0:T(8,128)(2,1)S(1)}, bf16[4,16,128]{2,1,0:T(8,128)(2,1)S(1)}, u32[]{:S(2)}, u32[]{:S(2)}) collective-permute-start(bf16[4,16,128]{2,1,0:T(8,128)(2,1)S(1)} %candidates.1.refs_0_), channel_id=1, source_target_pairs={{0,16},{8,24},{16,0},{24,8},{1,17},{9,25},{17,1},{25,9},{2,18},{10... | collective-permute-start | bytes 49160 | tf_op jit(solution)/shard_map/ppermute | solution.py:171
  5.4 3.3 %collective-permute-start = (bf16[4,16,128]{2,1,0:T(8,128)(2,1)S(1)}, bf16[4,16,128]{2,1,0:T(8,128)(2,1)S(1)}, u32[]{:S(2)}, u32[]{:S(2)}) collective-permute-start(bf16[4,16,128]{2,1,0:T(8,128)(2,1)S(1)} %candidates.1.refs_0_), channel_id=1, source_target_pairs={{0,8},{8,16},{16,24},{24,0},{1,9},{9,17},{17,25},{25,1},{2,10},{10... | collective-permute-start | bytes 49160 | tf_op jit(solution)/shard_map/ppermute | solution.py:171
  9.3 12.6 %collective-permute-start.3 = (bf16[68,16,128]{2,1,0:T(8,128)(2,1)S(1)}, bf16[68,16,128]{2,1,0:T(8,128)(2,1)S(1)}, u32[]{:S(2)}, u32[]{:S(2)}) collective-permute-start(bf16[68,16,128]{2,1,0:T(8,128)(2,1)S(1)} %get-tuple-element.10.refs_0_), channel_id=1, source_target_pairs={{0,4},{4,0},{1,5},{5,1},{2,6},{6,2},{3,7},{7,3},{8,12},{12,8},{9,1... | collective-permute-start | bytes 835592 | tf_op jit(solution)/shard_map/ppermute | solution.py:190
  10.9 11.0 %collective-permute-start.4 = (bf16[34,16,128]{2,1,0:T(8,128)(2,1)S(1)}, bf16[34,16,128]{2,1,0:T(8,128)(2,1)S(1)}, u32[]{:S(2)}, u32[]{:S(2)}) collective-permute-start(bf16[34,16,128]{2,1,0:T(8,128)(2,1)S(1)} %get-tuple-element.11), channel_id=1, source_target_pairs={{0,1},{1,2},{2,3},{3,0},{4,5},{5,6},{6,7},{7,4},{8,9},{9,10},{10,1... | collective-permute-start | bytes 417800 | tf_op jit(solution)/shard_map/ppermute | solution.py:207
  12.5 9.4 %collective-permute-start.5 = (bf16[34,16,128]{2,1,0:T(8,128)(2,1)S(1)}, bf16[34,16,128]{2,1,0:T(8,128)(2,1)S(1)}, u32[]{:S(2)}, u32[]{:S(2)}) collective-permute-start(bf16[34,16,128]{2,1,0:T(8,128)(2,1)S(1)} %get-tuple-element.12), channel_id=1, source_target_pairs={{0,3},{1,0},{2,1},{3,2},{4,7},{5,4},{6,5},{7,6},{8,11},{9,8},{10,9... | collective-permute-start | bytes 417800 | tf_op jit(solution)/shard_map/ppermute | solution.py:208
  14.7 7.2 %collective-permute-start.6 = (bf16[13,16,128]{2,1,0:T(8,128)(2,1)S(1)}, bf16[13,16,128]{2,1,0:T(8,128)(2,1)S(1)}, u32[]{:S(2)}, u32[]{:S(2)}) collective-permute-start(bf16[13,16,128]{2,1,0:T(8,128)(2,1)S(1)} %get-tuple-element.13), channel_id=1, source_target_pairs={{0,5},{1,6},{2,7},{3,4},{4,1},{5,2},{6,3},{7,0},{8,13},{9,14},{10,... | collective-permute-start | bytes 159752 | tf_op jit(solution)/shard_map/ppermute | solution.py:188
  14.7 7.2 %collective-permute-start.7 = (bf16[13,16,128]{2,1,0:T(8,128)(2,1)S(1)}, bf16[13,16,128]{2,1,0:T(8,128)(2,1)S(1)}, u32[]{:S(2)}, u32[]{:S(2)}) collective-permute-start(bf16[13,16,128]{2,1,0:T(8,128)(2,1)S(1)} %get-tuple-element.14), channel_id=1, source_target_pairs={{0,7},{1,4},{2,5},{3,6},{4,3},{5,0},{6,1},{7,2},{8,15},{9,12},{10,... | collective-permute-start | bytes 159752 | tf_op jit(solution)/shard_map/ppermute | solution.py:189

commit v4 on v3

--- a/solution.py
+++ b/solution.py
@@ -2,6 +2,8 @@
 
 import jax
 import jax.numpy as jnp
+import ml_dtypes
+import numpy as np
 from jax import lax
 from jax.experimental import pallas as pl
 from jax.experimental.pallas import tpu as pltpu
@@ -61,23 +63,35 @@
 
 VMEM = pl.BlockSpec(memory_space=pltpu.VMEM)
 SMEM = pl.BlockSpec(memory_space=pltpu.SMEM)
+HBM = pl.BlockSpec(memory_space=pltpu.HBM)
 SMALL = pltpu.CompilerParams(vmem_limit_bytes=8 * 2**20)
 
 
-def candidates_kernel(slots, orbitals, out):
+def candidates_kernel(slots, orbitals, out, chosen, tiles_of, slot_sem, tile_sems):
+    copy = pltpu.make_async_copy(slots, chosen, slot_sem)
+    copy.start()
+    copy.wait()
     lane = lax.broadcasted_iota(jnp.int32, (EDGE, LANES), 1)
     per_tile = LANES // NZ
     rounds, places = slots.shape
-    chosen = [slots[index // places, index % places] for index in range(rounds * places)]
-    firsts = [pl.multiple_of(slot // per_tile * LANES, LANES) for slot in chosen]
-    shifts = [
-        (index - slot % per_tile + per_tile) % per_tile * NZ for index, slot in enumerate(chosen)
-    ]
+    copies, shifts = [], []
+    for index in range(rounds * places):
+        slot = chosen[index // places, index % places]
+        lanes = pl.ds(pl.multiple_of(slot // per_tile * LANES, LANES), LANES)
+        copies.append(
+            pltpu.make_async_copy(
+                orbitals.at[:, :, lanes], tiles_of.at[index], tile_sems.at[index]
+            )
+        )
+        copies[-1].start()
+        shifts.append((index - slot % per_tile + per_tile) % per_tile * NZ)
+    for copy in copies:
+        copy.wait()
     rows = []
     for row in range(EDGE):
         packed = jnp.zeros((EDGE, LANES), jnp.float32)
-        for index, (first, shift) in enumerate(zip(firsts, shifts)):
-            tile = orbitals[row, :, pl.ds(first, LANES)].astype(jnp.float32)
+        for index, shift in enumerate(shifts):
+            tile = tiles_of[index, row].astype(jnp.float32)
             packed = jnp.where(lane // NZ == index, pltpu.roll(tile, shift, 1), packed)
         rows.append(packed)
     for tile in range(EDGE // 2):
@@ -85,17 +99,30 @@
 
 
 def candidates(orbitals, src_slot):
+    count = src_slot.size
     return pl.pallas_call(
         candidates_kernel,
         out_shape=jax.ShapeDtypeStruct((EDGE * EDGE // ROWS, ROWS, LANES), jnp.bfloat16),
-        in_specs=[SMEM, VMEM],
+        in_specs=[HBM, HBM],
         out_specs=VMEM,
+        scratch_shapes=[
+            pltpu.SMEM(src_slot.shape, jnp.int32),
+            pltpu.VMEM((count, EDGE, EDGE, LANES), jnp.bfloat16),
+            pltpu.SemaphoreType.DMA,
+            pltpu.SemaphoreType.DMA((count,)),
+        ],
         compiler_params=SMALL,
         name="candidates",
     )(src_slot, orbitals)
 
 
-def cells_kernel(orbitals, out, scratch):
+def cells_kernel(owner, orbitals, out, wanted, scratch):
+    lane = lax.broadcasted_iota(jnp.int32, (ROWS, LANES), 1)
+    rounds, places = owner.shape
+    owners = jnp.zeros((ROWS, LANES), jnp.int32)
+    for index in range(rounds * places):
+        owners = jnp.where(lane // NZ == index, owner[index // places, index % places], owners)
+    wanted[...] = owners
     for row in range(EDGE):
         for group in range(ROWS):
             tile = orbitals[row, :, pl.ds(group * LANES, LANES)].astype(jnp.float32)
@@ -106,27 +133,26 @@
             out[row * EDGE + y] = tile.astype(jnp.bfloat16)
 
 
-def cells_of(orbitals):
+def cells_of(orbitals, src_owner):
     return pl.pallas_call(
         cells_kernel,
-        out_shape=jax.ShapeDtypeStruct((EDGE * EDGE, ROWS, LANES), jnp.bfloat16),
-        in_specs=[VMEM],
-        out_specs=VMEM,
+        out_shape=[
+            jax.ShapeDtypeStruct((EDGE * EDGE, ROWS, LANES), jnp.bfloat16),
+            jax.ShapeDtypeStruct((ROWS, LANES), jnp.int32),
+        ],
+        in_specs=[SMEM, VMEM],
+        out_specs=[VMEM, VMEM],
         scratch_shapes=[pltpu.VMEM((EDGE, EDGE * (ROWS + 1), LANES), jnp.float32)],
         compiler_params=SMALL,
         cost_estimate=pl.CostEstimate(flops=0, bytes_accessed=4 * 2**20, transcendentals=0),
         name="cells",
-    )(orbitals)
-
-
-def messages_kernel(count, owner, cells, *refs):
+    )(src_owner, orbitals)
+
+
+def messages_kernel(count, cells, owners, *refs):
     offered, (block, last, first, corner_low, corner_high) = refs[:count], refs[count:]
     me = lax.axis_index("orb")
-    lane = lax.broadcasted_iota(jnp.int32, (ROWS, LANES), 1)
-    rounds, places = owner.shape
-    wanted = jnp.zeros((ROWS, LANES), jnp.int32)
-    for index in range(rounds * places):
-        wanted = jnp.where(lane // NZ == index, owner[index // places, index % places], wanted)
+    wanted = owners[...]
     picked = []
     for tile in range(EDGE * EDGE // ROWS):
         value = offered[0][tile].astype(jnp.float32)
@@ -175,11 +201,11 @@
         out_shape=[
             jax.ShapeDtypeStruct((tiles(length), ROWS, LANES), jnp.bfloat16) for length in lengths
         ],
-        in_specs=[SMEM] + [VMEM] * (1 + count),
+        in_specs=[VMEM] * (2 + count),
         out_specs=[VMEM] * 5,
         compiler_params=SMALL,
         name="messages",
-    )(src_owner, cells_of(orbitals), *offered)
+    )(*cells_of(orbitals, src_owner), *offered)
 
 
 def exchange(block, last, first, corner_low, corner_high):
@@ -225,16 +251,42 @@
     return out_x + out_y
 
 
+def z_modes():
+    index = np.arange(1, NZ + 1)
+    modes = np.sqrt(2.0 / (NZ + 1)) * np.sin(np.pi * np.outer(index, index) / (NZ + 1))
+    modes = np.kron(np.eye(LANES // NZ), modes)
+    high = modes.astype(ml_dtypes.bfloat16)
+    low = (modes - high.astype(np.float64)).astype(ml_dtypes.bfloat16)
+    both = np.concatenate([high, low], axis=1)
+    value = np.tile(2.0 * np.cos(np.pi * index / (NZ + 1)), LANES // NZ)
+    p0, p1, p2, p3, p4 = power_coeffs()
+    a3, a2, a1, a0 = p3 / p4, p2 / p4, p1 / p4, p0 / p4
+    tail = [
+        4.0 * value + a3,
+        6.0 * value**2 + 3.0 * a3 * value + a2,
+        4.0 * value**3 + 3.0 * a3 * value**2 + 2.0 * a2 * value + a1,
+        value**4 + a3 * value**3 + a2 * value**2 + a1 * value + a0,
+    ]
+    tail = np.repeat(np.stack(tail)[:, None, :], SUB, axis=1).astype(np.float32)
+    return np.concatenate([both, both], axis=0), tail
+
+
+SIZE = 2 * HALO + EDGE
+
+
+def within(radius):
+    return [[y for y in range(SIZE) if reach(x, y) <= radius] for x in range(SIZE)]
+
+
+CELLS = [(x, y) for x in range(SIZE) for y in within(HALO)[x]]
+CORE = [(x, y) for x in range(HALO, HALO + EDGE) for y in range(HALO, HALO + EDGE)]
+
+
 def kernel(count, *refs):
-    halo, (out, rows_of, dens, work_a, work_b, acc) = refs[:6], refs[6:]
-    size = 2 * HALO + EDGE
+    halo, modes, tails = refs[:6], refs[6], refs[7]
+    out, rows_of, parts, hat, work_a, work_b, last, acc = refs[8:]
     pitch = ROWS + 1
-    p0, p1, p2, p3, p4 = power_coeffs()
-    tail = (p3 / p4, p2 / p4, p1 / p4, p0 / p4)
-    spots = [
-        [[y for y in range(size) if reach(x, y) <= radius] for x in range(size)]
-        for radius in range(HALO + 1)
-    ]
+    number = {cell: at for at, cell in enumerate(CELLS)}
 
     shape = (LANES, LANES)
     lane = lax.broadcasted_iota(jnp.int32, shape, 1) % NZ
@@ -255,92 +307,106 @@
     def spread(place, x, y):
         which, at = place_of(x, y)
         row = rows_of[place, pl.ds(first_row[which] + at, 1), :]
-        return jnp.broadcast_to(row, (SUB, LANES))
-
-    inner = lax.broadcasted_iota(jnp.int32, (SUB, LANES), 1) % NZ
-    not_first, not_last = inner != 0, inner != NZ - 1
-
-    def z_sum(v):
-        lower = jnp.where(not_first, pltpu.roll(v, 1, 1), 0.0)
-        upper = jnp.where(not_last, pltpu.roll(v, LANES - 1, 1), 0.0)
-        return lower + upper
-
-    def one_half(place, half):
-        base = half * SUB
-        old = dens.at[half]
+        return jnp.broadcast_to(row, (ROWS, LANES))
+
+    def keep(at, value):
+        high = value.astype(jnp.bfloat16)
+        low = (value - high.astype(jnp.float32)).astype(jnp.bfloat16)
+        parts[at, :, :LANES] = high
+        parts[at, :, LANES:] = low
+
+    def turned(cells):
+        rows = parts[:cells].reshape(cells * ROWS, 2 * LANES)
+        both = jnp.dot(rows, modes[...], preferred_element_type=jnp.float32)
+        return (both[:, :LANES] + both[:, LANES:]).reshape(cells, ROWS, LANES)
+
+    def one_half(half):
+        rows = pl.ds(pl.multiple_of(half * SUB, SUB), SUB)
+
+        def start(x, y):
+            return hat[number[x, y], rows, :]
+
         for step in range(DEGREE):
             new = (work_a, work_b, work_a, None)[step]
-            targets = spots[HALO - 1 - step]
-            known = spots[HALO - step]
-            here, pair_prev = {y: old[0, y] for y in known[0]}, {}
-            for x in range(size - 1):
-                ahead = {y: old[x + 1, y] for y in known[x + 1]}
+            old = (None, work_a, work_b, work_a)[step]
+            targets, known = within(HALO - 1 - step), within(HALO - step)
+
+            def load(x):
+                return {y: start(x, y) if old is None else old[x, y] for y in known[x]}
+
+            here, pair_prev = load(0), {}
+            for x in range(SIZE - 1):
+                ahead = load(x + 1)
                 pair = {}
-                for y in range(size - 1):
+                for y in range(SIZE - 1):
                     if y in targets[x] or y + 1 in targets[x + 1]:
                         pair[y] = ahead[y] + here[y + 1]
-                extra = [dens[half, x, y] for y in targets[x]]
-                totals = []
-                for y, density in zip(targets[x], extra):
-                    value = pair[y] + pair_prev[y - 1] + z_sum(here[y])
-                    totals.append(value + tail[step] * density)
-                if new is not None:
-                    for y, value in zip(targets[x], totals):
+                extra = [here[y] if old is None else start(x, y) for y in targets[x]]
+                totals = [
+                    pair[y] + pair_prev[y - 1] + tails[step] * density
+                    for y, density in zip(targets[x], extra)
+                ]
+                for y, value in zip(targets[x], totals):
+                    if new is not None:
                         new[x, y] = value
-                elif totals:
-                    others = [spread(place, x, y) for y in targets[x]]
-                    at = [((y - HALO) * pitch + base) for y in targets[x]]
-                    before = [acc[x - HALO, pl.ds(start, SUB), :] for start in at]
-                    for i, start in enumerate(at):
-                        acc[x - HALO, pl.ds(start, SUB), :] = before[i] + totals[i] * others[i]
+                    else:
+                        last[CORE.index((x, y)), rows, :] = value
                 here, pair_prev = ahead, pair
-            old = new
 
     def one_source(place, carry):
-        for x in range(size):
-            row = spots[HALO][x]
+        for x in range(SIZE):
+            row = within(HALO)[x]
             values = []
             for y in row:
                 which, at = place_of(x, y)
                 values.append(halo[which][at].astype(jnp.float32))
             others = [spread(place, x, y) for y in row]
             for y, value, other in zip(row, values, others):
-                for half in range(ROWS // SUB):
-                    dens[half, x, y] = value[half * SUB : (half + 1) * SUB] * other
+                keep(number[x, y], value * other)
+        hat[...] = turned(len(CELLS))
 
         def inner_loop(half, carry):
-            one_half(place, half)
+            one_half(half)
             return carry
 
-        return lax.fori_loop(0, ROWS // SUB, inner_loop, carry)
+        lax.fori_loop(0, ROWS // SUB, inner_loop, 0)
+        for at in range(len(CORE)):
+            keep(at, last[at])
+        back = turned(len(CORE))
+        for at, (x, y) in enumerate(CORE):
+            rows = pl.ds((y - HALO) * pitch, ROWS)
+            acc[x - HALO, rows, :] = acc[x - HALO, rows, :] + back[at] * spread(place, x, y)
+        return carry
 
     acc[...] = jnp.zeros(acc.shape, jnp.float32)
     lax.fori_loop(0, count, one_source, 0)
     for x in range(EDGE):
         for group in range(ROWS):
             tile = acc[x, pl.ds(group, EDGE, stride=pitch), :]
-            out[x, :, pl.ds(group * LANES, LANES)] = tile * (-p4)
+            out[x, :, pl.ds(group * LANES, LANES)] = tile * (-power_coeffs()[-1])
 
 
 def fields(halo, count):
-    size = 2 * HALO + EDGE
-    plane = pltpu.VMEM((size, size, SUB, LANES), jnp.float32)
+    plane = pltpu.VMEM((SIZE, SIZE, SUB, LANES), jnp.float32)
     rows = sum(array.shape[0] * ROWS // (ROWS + 1) + ROWS for array in halo)
+    modes, tails = z_modes()
     return pl.pallas_call(
         functools.partial(kernel, count),
         out_shape=jax.ShapeDtypeStruct((EDGE, EDGE, ROWS * LANES), jnp.float32),
-        in_specs=[VMEM] * 6,
+        in_specs=[VMEM] * 8,
         out_specs=VMEM,
         scratch_shapes=[
             pltpu.VMEM((count, rows, LANES), jnp.float32),
-            pltpu.VMEM((ROWS // SUB, size, size, SUB, LANES), jnp.float32),
+            pltpu.VMEM((len(CELLS), ROWS, 2 * LANES), jnp.bfloat16),
+            pltpu.VMEM((len(CELLS), ROWS, LANES), jnp.float32),
             plane,
             plane,
+            pltpu.VMEM((len(CORE), ROWS, LANES), jnp.float32),
             pltpu.VMEM((EDGE, EDGE * (ROWS + 1), LANES), jnp.float32),
         ],
-        compiler_params=pltpu.CompilerParams(vmem_limit_bytes=16 * 2**20),
+        compiler_params=pltpu.CompilerParams(vmem_limit_bytes=24 * 2**20),
         name="fields",
-    )(*halo)
+    )(*halo, modes, tails)
 
 
 def body(orbitals, src_owner, src_slot):

time: 32.3 us -> 29.9 us (0.926)
  Pallas kernels: 11.6 us -> 9.69 us
  waiting for transfers between devices: 5.51 us -> 4.95 us
    pallas_call x1, Pallas kernels: 10.2 us -> 8.23 us  [fields(): pl.pallas_call(functools.partial(kernel, count), out_shape=jax.ShapeDtype...]
    ppermute x3, waiting for transfers between devices: 3.05 us -> 2.49 us  [messages(): lax.ppermute(mine, 'orb', ring('orb', step))]
    pallas_call x1, Pallas kernels: 0.05 us -> 0.6 us  [cells_of(): pl.pallas_call(cells_kernel, out_shape=[jax.ShapeDtypeStruct((EDGE * EDGE...]
    pallas_call x1, Pallas kernels: 0.64 us -> 0.09 us  [messages(): pl.pallas_call(functools.partial(messages_kernel, count), out_shape=[jax....]
    unnamed x6 -> x12, local copies, waits for them, and re-layouts: 1.63 us -> 1.64 us
  transfers between devices with their start and end apart: 8 -> 8, of which waited for: 4 -> 3; matrix products, arithmetic and copies ran while one was open for 0% -> 0% of each run, Pallas kernels for 0% -> 2%
where the time goes in v4:
time: 29.9 us; the launch traced here: 29.7 us
  starting transfers between devices  13.4 us (45%)
  Pallas kernels  9.69 us (32%)
  waiting for transfers between devices  4.95 us (17%)
  local copies, waits for them, and re-layouts  1.64 us (5%)
    pallas_call x1, Pallas kernels, fields(): pl.pallas_call(functools.partial(kernel, count), out_shape=jax.ShapeDtype...  8.23 us
    ppermute x1, starting transfers between devices, exchange(): high = lax.ppermute(corner_high, both, diagonal(1, -1))  4.72 us
    ppermute x3, starting transfers between devices, messages(): lax.ppermute(mine, 'orb', ring('orb', step))  3.23 us
    ppermute x3, waiting for transfers between devices, messages(): lax.ppermute(mine, 'orb', ring('orb', step))  2.49 us
    ppermute x1, waiting for transfers between devices, exchange(): low = lax.ppermute(corner_low, both, diagonal(1, 1))  2.44 us
    ppermute x1, starting transfers between devices, exchange(): above = lax.ppermute(first, 'sy', ring('sy', -1))  2.25 us
    unnamed x12, local copies, waits for them, and re-layouts  1.64 us
    ppermute x1, starting transfers between devices, exchange(): across = lax.ppermute(block, 'sx', ring('sx', 1))  1.58 us
  transfers between devices with their start and end apart: 8, of which 3 were waited for; matrix products, arithmetic and copies ran while one was open for 0% of the time, Pallas kernels for 2%

profile of v4, /device:TPU:0, one launch (start us, length us, event | category | flops | bytes accessed | tf_op | source)
XLA Modules:
  0.0 29.7 jit_solution(8831278660881271960)
XLA Ops:
  0.0 0.0 copy-start
  0.0 0.9 %copy-done = bf16[8,8,2048]{2,1,0:T(8,128)(2,1)S(1)} copy-done((bf16[8,8,2048]{2,1,0:T(8,128)(2,1)S(1)}, bf16[8,8,2048]{2,1,0:T(8,128)(2,1)}, u32[]{:S(2)}) %copy-start) | copy-done | bytes 262168
  1.0 0.0 copy-start.4
  1.0 0.7 %copy-done.4 = s32[2,2]{1,0:T(2,128)S(1)} copy-done((s32[2,2]{1,0:T(2,128)S(1)}, s32[2,2]{1,0:T(2,128)}, u32[]{:S(2)}) %copy-start.4) | copy-done | bytes 40
  1.6 0.0 copy-start.1
  1.6 0.0 copy-start.5
  1.6 0.8 %candidates.1.refs_0_ = bf16[4,16,128]{2,1,0:T(8,128)(2,1)S(1)} custom-call(s32[2,2]{1,0:T(2,128)S(1)} %copy-done.4, bf16[8,8,2048]{2,1,0:T(8,128)(2,1)S(1)} %copy-done), custom_call_target="tpu_custom_call" | custom-call | tf_op jit(solution)/shard_map/candidates/pallas_call | solution.py:103
  2.4 2.4 %collective-permute-start.2 = (bf16[4,16,128]{2,1,0:T(8,128)(2,1)S(1)}, bf16[4,16,128]{2,1,0:T(8,128)(2,1)S(1)}, u32[]{:S(2)}, u32[]{:S(2)}) collective-permute-start(bf16[4,16,128]{2,1,0:T(8,128)(2,1)S(1)} %candidates.1.refs_0_), channel_id=1, source_target_pairs={{0,24},{8,0},{16,8},{24,16},{1,25},{9,1},{17,9},{25,17},{2,26},{10... | collective-permute-start | bytes 49160 | tf_op jit(solution)/shard_map/ppermute | solution.py:197
  4.8 0.6 %collective-permute-start.1 = (bf16[4,16,128]{2,1,0:T(8,128)(2,1)S(1)}, bf16[4,16,128]{2,1,0:T(8,128)(2,1)S(1)}, u32[]{:S(2)}, u32[]{:S(2)}) collective-permute-start(bf16[4,16,128]{2,1,0:T(8,128)(2,1)S(1)} %candidates.1.refs_0_), channel_id=1, source_target_pairs={{0,16},{8,24},{16,0},{24,8},{1,17},{9,25},{17,1},{25,9},{2,18},{10... | collective-permute-start | bytes 49160 | tf_op jit(solution)/shard_map/ppermute | solution.py:197
  5.5 0.2 collective-permute-start
  5.6 0.0 copy-done.1
  5.6 0.0 copy-done.5
  5.6 0.6 %cells.1 = (bf16[64,16,128]{2,1,0:T(8,128)(2,1)S(1)}, s32[16,128]{1,0:T(8,128)S(1)}) custom-call(s32[2,2]{1,0:T(2,128)S(1)} %copy-done.5, bf16[8,8,2048]{2,1,0:T(8,128)(2,1)S(1)} %copy-done.1), custom_call_target="tpu_custom_call" | custom-call | bytes 4194304 | tf_op jit(solution)/shard_map/cells/pallas_call | solution.py:137
  6.3 0.0 collective-permute-done.2.refs_3_
  6.3 2.4 %collective-permute-done.1.refs_2_ = bf16[4,16,128]{2,1,0:T(8,128)(2,1)S(1)} collective-permute-done((bf16[4,16,128]{2,1,0:T(8,128)(2,1)S(1)}, bf16[4,16,128]{2,1,0:T(8,128)(2,1)S(1)}, u32[]{:S(2)}, u32[]{:S(2)}) %collective-permute-start.1) | collective-permute-done | bytes 16416 | tf_op jit(solution)/shard_map/ppermute | solution.py:197
  8.7 0.1 collective-permute-done.refs_1_
  8.7 0.0 copy-start.2
  8.8 0.0 copy-start.3
  8.8 0.1 messages.1
  8.8 1.6 %collective-permute-start.3 = (bf16[68,16,128]{2,1,0:T(8,128)(2,1)S(1)}, bf16[68,16,128]{2,1,0:T(8,128)(2,1)S(1)}, u32[]{:S(2)}, u32[]{:S(2)}) collective-permute-start(bf16[68,16,128]{2,1,0:T(8,128)(2,1)S(1)} %get-tuple-element.14.refs_0_), channel_id=1, source_target_pairs={{0,4},{4,0},{1,5},{5,1},{2,6},{6,2},{3,7},{7,3},{8,12},{12,8},{9,1... | collective-permute-start | bytes 835592 | tf_op jit(solution)/shard_map/ppermute | solution.py:216
  10.4 1.6 %collective-permute-start.4 = (bf16[34,16,128]{2,1,0:T(8,128)(2,1)S(1)}, bf16[34,16,128]{2,1,0:T(8,128)(2,1)S(1)}, u32[]{:S(2)}, u32[]{:S(2)}) collective-permute-start(bf16[34,16,128]{2,1,0:T(8,128)(2,1)S(1)} %get-tuple-element.15), channel_id=1, source_target_pairs={{0,1},{1,2},{2,3},{3,0},{4,5},{5,6},{6,7},{7,4},{8,9},{9,10},{10,1... | collective-permute-start | bytes 417800 | tf_op jit(solution)/shard_map/ppermute | solution.py:233
  12.0 2.2 %collective-permute-start.5 = (bf16[34,16,128]{2,1,0:T(8,128)(2,1)S(1)}, bf16[34,16,128]{2,1,0:T(8,128)(2,1)S(1)}, u32[]{:S(2)}, u32[]{:S(2)}) collective-permute-start(bf16[34,16,128]{2,1,0:T(8,128)(2,1)S(1)} %get-tuple-element.16), channel_id=1, source_target_pairs={{0,3},{1,0},{2,1},{3,2},{4,7},{5,4},{6,5},{7,6},{8,11},{9,8},{10,9... | collective-permute-start | bytes 417800 | tf_op jit(solution)/shard_map/ppermute | solution.py:234
  14.3 0.0 collective-permute-start.6
  14.3 4.7 %collective-permute-start.7 = (bf16[13,16,128]{2,1,0:T(8,128)(2,1)S(1)}, bf16[13,16,128]{2,1,0:T(8,128)(2,1)S(1)}, u32[]{:S(2)}, u32[]{:S(2)}) collective-permute-start(bf16[13,16,128]{2,1,0:T(8,128)(2,1)S(1)} %get-tuple-element.18), channel_id=1, source_target_pairs={{0,7},{1,4},{2,5},{3,6},{4,3},{5,0},{6,1},{7,2},{8,15},{9,12},{10,... | collective-permute-start | bytes 159752 | tf_op jit(solution)/shard_map/ppermute | solution.py:215
  19.0 2.4 %collective-permute-done.6.refs_4_ = bf16[13,16,128]{2,1,0:T(8,128)(2,1)S(1)} collective-permute-done((bf16[13,16,128]{2,1,0:T(8,128)(2,1)S(1)}, bf16[13,16,128]{2,1,0:T(8,128)(2,1)S(1)}, u32[]{:S(2)}, u32[]{:S(2)}) %collective-permute-start.6) | collective-permute-done | bytes 53280 | tf_op jit(solution)/shard_map/ppermute | solution.py:214
  21.4 0.0 collective-permute-done.7.refs_5_
  21.4 0.0 collective-permute-done.4.refs_2_
  21.4 0.0 collective-permute-done.5.refs_3_
  21.4 0.0 collective-permute-done.3.refs_1_
  21.4 0.0 copy-done.2
  21.5 0.0 copy-done.3
  21.5 8.2 %fields.1 = f32[8,8,2048]{2,1,0:T(8,128)} custom-call(bf16[68,16,128]{2,1,0:T(8,128)(2,1)S(1)} %get-tuple-element.14.refs_0_, bf16[68,16,128]{2,1,0:T(8,128)(2,1)S(1)} %collective-permute-done.3.refs_1_, bf16[34,16,128]{2,1,0:T(8,128)(2,1)S(1)} %collective-permute-done.4.refs_2_, bf16[34,16,128]{2,1,0:T(8,128)(2,1)S(1)} %collective-permute-done.5.refs_3_, ...), custom_call_target="tpu_custom_call" | custom-call | tf_op jit(solution)/shard_map/fields/pallas_call | solution.py:393
Async XLA Ops:
  0.0 0.9 %copy-start = (bf16[8,8,2048]{2,1,0:T(8,128)(2,1)S(1)}, bf16[8,8,2048]{2,1,0:T(8,128)(2,1)}, u32[]{:S(2)}) copy-start(bf16[8,8,2048]{2,1,0:T(8,128)(2,1)} %orbitals.3) | copy-start | bytes 786436
  1.0 0.7 %copy-start.4 = (s32[2,2]{1,0:T(2,128)S(1)}, s32[2,2]{1,0:T(2,128)}, u32[]{:S(2)}) copy-start(s32[2,2]{1,0:T(2,128)} %slots.1) | copy-start | bytes 52
  1.6 4.0 %copy-start.1 = (bf16[8,8,2048]{2,1,0:T(8,128)(2,1)S(1)}, bf16[8,8,2048]{2,1,0:T(8,128)(2,1)}, u32[]{:S(2)}) copy-start(bf16[8,8,2048]{2,1,0:T(8,128)(2,1)} %orbitals.3) | copy-start | bytes 786436
  1.6 4.0 %copy-start.5 = (s32[2,2]{1,0:T(2,128)S(1)}, s32[2,2]{1,0:T(2,128)}, u32[]{:S(2)}) copy-start(s32[2,2]{1,0:T(2,128)} %owner.1) | copy-start | bytes 52
  2.4 3.9 %collective-permute-start.2 = (bf16[4,16,128]{2,1,0:T(8,128)(2,1)S(1)}, bf16[4,16,128]{2,1,0:T(8,128)(2,1)S(1)}, u32[]{:S(2)}, u32[]{:S(2)}) collective-permute-start(bf16[4,16,128]{2,1,0:T(8,128)(2,1)S(1)} %candidates.1.refs_0_), channel_id=1, source_target_pairs={{0,24},{8,0},{16,8},{24,16},{1,25},{9,1},{17,9},{25,17},{2,26},{10... | collective-permute-start | bytes 49160 | tf_op jit(solution)/shard_map/ppermute | solution.py:197
  4.8 3.8 %collective-permute-start.1 = (bf16[4,16,128]{2,1,0:T(8,128)(2,1)S(1)}, bf16[4,16,128]{2,1,0:T(8,128)(2,1)S(1)}, u32[]{:S(2)}, u32[]{:S(2)}) collective-permute-start(bf16[4,16,128]{2,1,0:T(8,128)(2,1)S(1)} %candidates.1.refs_0_), channel_id=1, source_target_pairs={{0,16},{8,24},{16,0},{24,8},{1,17},{9,25},{17,1},{25,9},{2,18},{10... | collective-permute-start | bytes 49160 | tf_op jit(solution)/shard_map/ppermute | solution.py:197
  5.5 3.3 %collective-permute-start = (bf16[4,16,128]{2,1,0:T(8,128)(2,1)S(1)}, bf16[4,16,128]{2,1,0:T(8,128)(2,1)S(1)}, u32[]{:S(2)}, u32[]{:S(2)}) collective-permute-start(bf16[4,16,128]{2,1,0:T(8,128)(2,1)S(1)} %candidates.1.refs_0_), channel_id=1, source_target_pairs={{0,8},{8,16},{16,24},{24,0},{1,9},{9,17},{17,25},{25,1},{2,10},{10... | collective-permute-start | bytes 49160 | tf_op jit(solution)/shard_map/ppermute | solution.py:197
  8.7 12.7 %copy-start.2 = (bf16[256,256]{1,0:T(8,128)(2,1)S(1)}, bf16[256,256]{1,0:T(8,128)(2,1)}, u32[]{:S(2)}) copy-start(bf16[256,256]{1,0:T(8,128)(2,1)} %constant.4.clone.refs_6_) | copy-start | bytes 393220
  8.8 12.7 %copy-start.3 = (f32[4,8,128]{2,1,0:T(8,128)S(1)}, f32[4,8,128]{2,1,0:T(8,128)}, u32[]{:S(2)}) copy-start(f32[4,8,128]{2,1,0:T(8,128)} %constant.5.clone.refs_7_) | copy-start | bytes 49156
  8.8 12.6 %collective-permute-start.3 = (bf16[68,16,128]{2,1,0:T(8,128)(2,1)S(1)}, bf16[68,16,128]{2,1,0:T(8,128)(2,1)S(1)}, u32[]{:S(2)}, u32[]{:S(2)}) collective-permute-start(bf16[68,16,128]{2,1,0:T(8,128)(2,1)S(1)} %get-tuple-element.14.refs_0_), channel_id=1, source_target_pairs={{0,4},{4,0},{1,5},{5,1},{2,6},{6,2},{3,7},{7,3},{8,12},{12,8},{9,1... | collective-permute-start | bytes 835592 | tf_op jit(solution)/shard_map/ppermute | solution.py:216
  10.4 11.0 %collective-permute-start.4 = (bf16[34,16,128]{2,1,0:T(8,128)(2,1)S(1)}, bf16[34,16,128]{2,1,0:T(8,128)(2,1)S(1)}, u32[]{:S(2)}, u32[]{:S(2)}) collective-permute-start(bf16[34,16,128]{2,1,0:T(8,128)(2,1)S(1)} %get-tuple-element.15), channel_id=1, source_target_pairs={{0,1},{1,2},{2,3},{3,0},{4,5},{5,6},{6,7},{7,4},{8,9},{9,10},{10,1... | collective-permute-start | bytes 417800 | tf_op jit(solution)/shard_map/ppermute | solution.py:233
  12.0 9.4 %collective-permute-start.5 = (bf16[34,16,128]{2,1,0:T(8,128)(2,1)S(1)}, bf16[34,16,128]{2,1,0:T(8,128)(2,1)S(1)}, u32[]{:S(2)}, u32[]{:S(2)}) collective-permute-start(bf16[34,16,128]{2,1,0:T(8,128)(2,1)S(1)} %get-tuple-element.16), channel_id=1, source_target_pairs={{0,3},{1,0},{2,1},{3,2},{4,7},{5,4},{6,5},{7,6},{8,11},{9,8},{10,9... | collective-permute-start | bytes 417800 | tf_op jit(solution)/shard_map/ppermute | solution.py:234
  14.3 7.2 %collective-permute-start.6 = (bf16[13,16,128]{2,1,0:T(8,128)(2,1)S(1)}, bf16[13,16,128]{2,1,0:T(8,128)(2,1)S(1)}, u32[]{:S(2)}, u32[]{:S(2)}) collective-permute-start(bf16[13,16,128]{2,1,0:T(8,128)(2,1)S(1)} %get-tuple-element.17), channel_id=1, source_target_pairs={{0,5},{1,6},{2,7},{3,4},{4,1},{5,2},{6,3},{7,0},{8,13},{9,14},{10,... | collective-permute-start | bytes 159752 | tf_op jit(solution)/shard_map/ppermute | solution.py:214
  14.3 7.2 %collective-permute-start.7 = (bf16[13,16,128]{2,1,0:T(8,128)(2,1)S(1)}, bf16[13,16,128]{2,1,0:T(8,128)(2,1)S(1)}, u32[]{:S(2)}, u32[]{:S(2)}) collective-permute-start(bf16[13,16,128]{2,1,0:T(8,128)(2,1)S(1)} %get-tuple-element.18), channel_id=1, source_target_pairs={{0,7},{1,4},{2,5},{3,6},{4,3},{5,0},{6,1},{7,2},{8,15},{9,12},{10,... | collective-permute-start | bytes 159752 | tf_op jit(solution)/shard_map/ppermute | solution.py:215

commit v5 on v4

v5 whole, which is shorter than its diff:
```python
import functools

import jax
import jax.numpy as jnp
import ml_dtypes
import numpy as np
from jax import lax
from jax.experimental import pallas as pl
from jax.experimental.pallas import tpu as pltpu
from jax.sharding import PartitionSpec as P

NZ = 32
LANES = 128
SUB = 8
ROWS = 16
DEGREE = 4
HALO = DEGREE
EDGE = 8

CHEB = (
    1.021021021021021,
    -1.7357357357357357,
    1.4753753753753753,
    -1.254069069069069,
    1.0659587087087088,
)


def power_coeffs():
    c0, c1, c2, c3, c4 = CHEB
    return (
        c0 - c2 + c4,
        -(c1 - 3.0 * c3) / 6.0,
        (2.0 * c2 - 8.0 * c4) / 36.0,
        -4.0 * c3 / 216.0,
        8.0 * c4 / 1296.0,
    )


CORNER_LOW = tuple(
    (x, y)
    for x in range(EDGE)
    for y in range(EDGE - HALO, EDGE)
    if min(x + 1, EDGE - x) + EDGE - y <= DEGREE
)
CORNER_HIGH = tuple((x, EDGE - 1 - y) for x, y in CORNER_LOW)
SPLIT = len(CORNER_LOW) // 2


def ring(axis, step):
    count = lax.axis_size(axis)
    return [(i, (i + step) % count) for i in range(count)]


def diagonal(step_x, step_y):
    count_x, count_y = lax.axis_size("sx"), lax.axis_size("sy")
    return [
        (i * count_y + j, (i + step_x) % count_x * count_y + (j + step_y) % count_y)
        for i in range(count_x)
        for j in range(count_y)
    ]


VMEM = pl.BlockSpec(memory_space=pltpu.VMEM)
HBM = pl.BlockSpec(memory_space=pltpu.HBM)
SMALL = pltpu.CompilerParams(vmem_limit_bytes=8 * 2**20)


def candidates_kernel(
    owner, slots, orbitals, out, wanted, holders, chosen, tiles_of, small_sems, tile_sems
):
    owner_copy = pltpu.make_async_copy(owner, holders, small_sems.at[0])
    slot_copy = pltpu.make_async_copy(slots, chosen, small_sems.at[1])
    owner_copy.start()
    slot_copy.start()
    slot_copy.wait()
    lane = lax.broadcasted_iota(jnp.int32, (EDGE, LANES), 1)
    per_tile = LANES // NZ
    rounds, places = slots.shape
    copies, shifts = [], []
    for index in range(rounds * places):
        slot = chosen[index // places, index % places]
        lanes = pl.ds(pl.multiple_of(slot // per_tile * LANES, LANES), LANES)
        copies.append(
            pltpu.make_async_copy(
                orbitals.at[:, :, lanes], tiles_of.at[index], tile_sems.at[index]
            )
        )
        copies[-1].start()
        shifts.append((index - slot % per_tile + per_tile) % per_tile * NZ)
    owner_copy.wait()
    seat = lax.broadcasted_iota(jnp.int32, (ROWS, LANES), 1) // NZ
    owners = jnp.zeros((ROWS, LANES), jnp.int32)
    for index in range(rounds * places):
        owners = jnp.where(seat == index, holders[index // places, index % places], owners)
    wanted[...] = owners
    for copy in copies:
        copy.wait()
    rows = []
    for row in range(EDGE):
        packed = jnp.zeros((EDGE, LANES), jnp.float32)
        for index, shift in enumerate(shifts):
            tile = tiles_of[index, row].astype(jnp.float32)
            packed = jnp.where(lane // NZ == index, pltpu.roll(tile, shift, 1), packed)
        rows.append(packed)
    for tile in range(EDGE // 2):
        out[tile] = jnp.concatenate(rows[2 * tile : 2 * tile + 2], axis=0).astype(jnp.bfloat16)


def candidates(orbitals, src_owner, src_slot):
    count = src_slot.size
    return pl.pallas_call(
        candidates_kernel,
        out_shape=[
            jax.ShapeDtypeStruct((EDGE * EDGE // ROWS, ROWS, LANES), jnp.bfloat16),
            jax.ShapeDtypeStruct((ROWS, LANES), jnp.int32),
        ],
        in_specs=[HBM] * 3,
        out_specs=[VMEM] * 2,
        scratch_shapes=[
            pltpu.SMEM(src_owner.shape, jnp.int32),
            pltpu.SMEM(src_slot.shape, jnp.int32),
            pltpu.VMEM((count, EDGE, EDGE, LANES), jnp.bfloat16),
            pltpu.SemaphoreType.DMA((2,)),
            pltpu.SemaphoreType.DMA((count,)),
        ],
        compiler_params=pltpu.CompilerParams(vmem_limit_bytes=60 * 2**20),
        name="candidates",
    )(src_owner, src_slot, orbitals)


def cells_kernel(orbitals, out, last, first, scratch):
    for row in range(EDGE):
        for group in range(ROWS):
            tile = orbitals[row, :, pl.ds(group * LANES, LANES)].astype(jnp.float32)
            scratch[row, pl.ds(group, EDGE, stride=ROWS + 1), :] = tile
    for row in range(EDGE):
        for y in range(EDGE):
            tile = scratch[row, pl.ds(y * (ROWS + 1), ROWS), :].astype(jnp.bfloat16)
            out[row * EDGE + y] = tile
            if y < HALO:
                first[row * HALO + y] = tile
            if y >= EDGE - HALO:
                last[row * HALO + y + HALO - EDGE] = tile


def cells_of(orbitals):
    lengths = (EDGE * EDGE, EDGE * HALO, EDGE * HALO)
    return pl.pallas_call(
        cells_kernel,
        out_shape=[jax.ShapeDtypeStruct((length, ROWS, LANES), jnp.bfloat16) for length in lengths],
        in_specs=[VMEM],
        out_specs=[VMEM] * 3,
        scratch_shapes=[pltpu.VMEM((EDGE, EDGE * (ROWS + 1), LANES), jnp.float32)],
        compiler_params=SMALL,
        name="cells",
    )(orbitals)


def sources_kernel(count, cells, owners, *refs):
    offered, (block, last, first, corner_low, corner_high) = refs[:count], refs[count:]
    me = lax.axis_index("orb")
    wanted = owners[...]
    picked = []
    for tile in range(EDGE * EDGE // ROWS):
        value = offered[0][tile].astype(jnp.float32)
        for step in range(1, count):
            theirs = offered[step][tile].astype(jnp.float32)
            value = jnp.where(wanted == lax.rem(me + count - step, count), theirs, value)
        picked.append(value)
        block[tile] = value.astype(jnp.bfloat16)

    def pack(ref, used, spots):
        runs = []
        for x, y in spots:
            if runs and runs[-1][0] == x and runs[-1][2] == y:
                runs[-1][2] = y + 1
            else:
                runs.append([x, y, y + 1])
        parts = [
            picked[x * EDGE // ROWS][x * EDGE % ROWS + low : x * EDGE % ROWS + high]
            for x, low, high in runs
        ]
        if len(spots) % ROWS:
            parts.append(jnp.zeros((ROWS - len(spots) % ROWS, LANES), jnp.float32))
        rows = jnp.concatenate(parts, axis=0).astype(jnp.bfloat16)
        for tile in range(rows.shape[0] // ROWS):
            ref[used + tile] = rows[tile * ROWS : (tile + 1) * ROWS]

    pack(last, 0, [(x, y) for x in range(EDGE) for y in range(EDGE - HALO, EDGE)])
    pack(first, 0, [(x, y) for x in range(EDGE) for y in range(HALO)])
    for ref, spots in ((corner_low, CORNER_LOW), (corner_high, CORNER_HIGH)):
        for at, (x, y) in enumerate(spots):
            ref[at] = cells[x * EDGE + y]
        pack(ref, len(spots), spots)


def sources_of(cells, owners, offered):
    corner = len(CORNER_LOW) + 1
    lengths = (EDGE * EDGE // ROWS,) + (EDGE * HALO // ROWS,) * 2 + (corner,) * 2
    return pl.pallas_call(
        functools.partial(sources_kernel, len(offered)),
        out_shape=[jax.ShapeDtypeStruct((length, ROWS, LANES), jnp.bfloat16) for length in lengths],
        in_specs=[VMEM] * (2 + len(offered)),
        out_specs=[VMEM] * 5,
        compiler_params=SMALL,
        name="sources",
    )(cells, owners, *offered)


def across_x(block):
    if lax.axis_size("sx") == 2:
        return lax.ppermute(block, "sx", ring("sx", 1))
    half = block.shape[0] // 2
    low = lax.ppermute(block[:half], "sx", ring("sx", -1))
    return jnp.concatenate([low, lax.ppermute(block[half:], "sx", ring("sx", 1))], axis=0)


def across_corner(cells, step_y):
    both = ("sx", "sy")
    if lax.axis_size("sx") == 2:
        return lax.ppermute(cells, both, diagonal(1, step_y))
    low = lax.ppermute(cells[:SPLIT], both, diagonal(-1, step_y))
    high = lax.ppermute(cells[SPLIT : 2 * SPLIT], both, diagonal(1, step_y))
    rows = [lax.ppermute(cells[2 * SPLIT :], both, diagonal(step_x, step_y)) for step_x in (-1, 1)]
    rows = jnp.concatenate([rows[0][:, :SPLIT], rows[1][:, SPLIT:]], axis=1)
    return jnp.concatenate([low, high, rows], axis=0)


def across_y(last, first):
    return lax.ppermute(last, "sy", ring("sy", 1)), lax.ppermute(first, "sy", ring("sy", -1))


def place_of(x, y):
    row, core_x = (x - HALO) % EDGE, HALO <= x < HALO + EDGE
    if HALO <= y < HALO + EDGE:
        return (0 if core_x else 1), row * EDGE + y - HALO
    if y < HALO:
        return (2, row * HALO + y) if core_x else (4, CORNER_LOW.index((row, y + EDGE - HALO)))
    y = y - HALO - EDGE
    return (3, row * HALO + y) if core_x else (5, CORNER_HIGH.index((row, y)))


def reach(x, y):
    out_x = max(HALO - x, x - (HALO + EDGE - 1), 0)
    out_y = max(HALO - y, y - (HALO + EDGE - 1), 0)
    return out_x + out_y


def z_modes():
    index = np.arange(1, NZ + 1)
    modes = np.sqrt(2.0 / (NZ + 1)) * np.sin(np.pi * np.outer(index, index) / (NZ + 1))
    modes = np.kron(np.eye(LANES // NZ), modes)
    high = modes.astype(ml_dtypes.bfloat16)
    low = (modes - high.astype(np.float64)).astype(ml_dtypes.bfloat16)
    both = np.concatenate([high, low], axis=1)
    value = np.tile(2.0 * np.cos(np.pi * index / (NZ + 1)), LANES // NZ)
    p0, p1, p2, p3, p4 = power_coeffs()
    a3, a2, a1, a0 = p3 / p4, p2 / p4, p1 / p4, p0 / p4
    tail = [
        4.0 * value + a3,
        6.0 * value**2 + 3.0 * a3 * value + a2,
        4.0 * value**3 + 3.0 * a3 * value**2 + 2.0 * a2 * value + a1,
        value**4 + a3 * value**3 + a2 * value**2 + a1 * value + a0,
    ]
    tail = np.repeat(np.stack(tail)[:, None, :], SUB, axis=1).astype(np.float32)
    return np.concatenate([both, both], axis=0), tail


SIZE = 2 * HALO + EDGE


def within(radius):
    return [[y for y in range(SIZE) if reach(x, y) <= radius] for x in range(SIZE)]


CELLS = [(x, y) for x in range(SIZE) for y in within(HALO)[x]]
CORE = [(x, y) for x in range(HALO, HALO + EDGE) for y in range(HALO, HALO + EDGE)]


def kernel(count, *refs):
    halo, sources, modes, tails = refs[:6], refs[6:10], refs[10], refs[11]
    out, rows_of, parts, hat, work_a, work_b, last, acc = refs[12:]
    pitch = ROWS + 1
    number = {cell: at for at, cell in enumerate(CELLS)}

    shape = (LANES, LANES)
    lane = lax.broadcasted_iota(jnp.int32, shape, 1) % NZ
    line = lax.broadcasted_iota(jnp.int32, shape, 0)
    repeats = [(line == lane + place * NZ).astype(jnp.bfloat16) for place in range(count)]
    first_row = []
    total, edges = 0, ROWS * sum(ref.shape[0] for ref in sources)
    for ref in (*sources, *halo[4:]):
        packed = (ref[len(CORNER_LOW) :] if total >= edges else ref[...]).reshape(-1, LANES)
        first_row.append(total)
        for place, repeat in enumerate(repeats):
            rows_of[place, pl.ds(total, packed.shape[0]), :] = jnp.dot(
                packed, repeat, preferred_element_type=jnp.float32
            )
        total += packed.shape[0]

    def spread(place, x, y):
        which, at = place_of(x, y)
        row = rows_of[place, pl.ds(first_row[which] + at, 1), :]
        return jnp.broadcast_to(row, (ROWS, LANES))

    def keep(at, value):
        high = value.astype(jnp.bfloat16)
        low = (value - high.astype(jnp.float32)).astype(jnp.bfloat16)
        parts[at, :, :LANES] = high
        parts[at, :, LANES:] = low

    def turned(first, end):
        cells = end - first
        rows = parts[first:end].reshape(cells * ROWS, 2 * LANES)
        both = jnp.dot(rows, modes[...], preferred_element_type=jnp.float32)
        return (both[:, :LANES] + both[:, LANES:]).reshape(cells, ROWS, LANES)

    def one_half(half):
        rows = pl.ds(half * SUB, SUB)

        def start(x, y):
            return hat[number[x, y], rows, :]

        for step in range(DEGREE):
            new = (work_a, work_b, work_a, None)[step]
            old = (None, work_a, work_b, work_a)[step]
            targets, known = within(HALO - 1 - step), within(HALO - step)

            def load(x):
                return {y: start(x, y) if old is None else old[x, y] for y in known[x]}

            here, pair_prev = load(0), {}
            for x in range(SIZE - 1):
                ahead = load(x + 1)
                pair = {}
                for y in range(SIZE - 1):
                    if y in targets[x] or y + 1 in targets[x + 1]:
                        pair[y] = ahead[y] + here[y + 1]
                    if y in targets[x]:
                        density = here[y] if old is None else start(x, y)
                        value = pair[y] + pair_prev[y - 1] + tails[step] * density
                        if new is not None:
                            new[x, y] = value
                        else:
                            last[CORE.index((x, y)), rows, :] = value
                here, pair_prev = ahead, pair

    def one_source(place, carry):
        chunk = len(CELLS) // 4
        for first in range(0, len(CELLS), chunk):
            end = min(first + chunk, len(CELLS))
            for at in range(first, end):
                which, spot = place_of(*CELLS[at])
                keep(at, halo[which][spot].astype(jnp.float32) * spread(place, *CELLS[at]))
            hat[first:end] = turned(first, end)
        for half in range(ROWS // SUB):
            one_half(half)
        for at in range(len(CORE)):
            keep(at, last[at])
        back = turned(0, len(CORE))
        for at, (x, y) in enumerate(CORE):
            rows = pl.ds((y - HALO) * pitch, ROWS)
            acc[x - HALO, rows, :] = acc[x - HALO, rows, :] + back[at] * spread(place, x, y)
        return carry

    acc[...] = jnp.zeros(acc.shape, jnp.float32)
    lax.fori_loop(0, count, one_source, 0)
    for x in range(EDGE):
        for group in range(ROWS):
            tile = acc[x, pl.ds(group, EDGE, stride=pitch), :]
            out[x, :, pl.ds(group * LANES, LANES)] = tile * (-power_coeffs()[-1])


def fields(halo, sources, count):
    plane = pltpu.VMEM((SIZE, SIZE, SUB, LANES), jnp.float32)
    rows = ROWS * (sum(array.shape[0] for array in sources) + 2)
    modes, tails = z_modes()
    return pl.pallas_call(
        functools.partial(kernel, count),
        out_shape=jax.ShapeDtypeStruct((EDGE, EDGE, ROWS * LANES), jnp.float32),
        in_specs=[VMEM] * 12,
        out_specs=VMEM,
        scratch_shapes=[
            pltpu.VMEM((count, rows, LANES), jnp.float32),
            pltpu.VMEM((len(CELLS), ROWS, 2 * LANES), jnp.bfloat16),
            pltpu.VMEM((len(CELLS), ROWS, LANES), jnp.float32),
            plane,
            plane,
            pltpu.VMEM((len(CORE), ROWS, LANES), jnp.float32),
            pltpu.VMEM((EDGE, EDGE * (ROWS + 1), LANES), jnp.float32),
        ],
        compiler_params=pltpu.CompilerParams(vmem_limit_bytes=24 * 2**20),
        name="fields",
    )(*halo, *sources, modes, tails)


def body(orbitals, src_owner, src_slot):
    mine, owners = candidates(orbitals, src_owner, src_slot)
    cells, last, first = cells_of(orbitals)
    block = (cells, across_x(cells), *across_y(last, first))
    offered = [
        mine if step == 0 else lax.ppermute(mine, "orb", ring("orb", step))
        for step in range(lax.axis_size("orb"))
    ]
    picked, last, first, low, high = sources_of(cells, owners, offered)
    sources = (picked, across_x(picked), *across_y(last, first))
    corners = (across_corner(low, 1), across_corner(high, -1))
    return fields(block + corners, sources, src_slot.size)


def solution(mesh):
    in_specs = (P("sx", "sy", "orb"), P(), P())
    out_specs = P("sx", "sy", "orb")
    return jax.shard_map(body, mesh=mesh, in_specs=in_specs, out_specs=out_specs, check_vma=False)
```

time: 29.9 us -> 39.8 us (1.33)
  waiting for transfers between devices: 4.95 us -> 13 us
  starting transfers between devices: 13.4 us -> 15.4 us
  Pallas kernels: 9.69 us -> 8.65 us
  local copies, waits for them, and re-layouts: 1.64 us -> 2.37 us
    ppermute x8 -> x11, waiting for transfers between devices: 4.95 us -> 13 us  [the longest x2 4.87 us: across_y(): lax.ppermute(last, 'sy', ring('sy', 1))]
    ppermute x8 -> x11, starting transfers between devices: 13.4 us -> 15.4 us  [the longest x2 4.72 us: across_corner(): return lax.ppermute(cells, both, diagonal(1, step_y))]
    pallas_call x1, Pallas kernels: 8.23 us -> 6.3 us  [fields(): pl.pallas_call(functools.partial(kernel, count), out_shape=jax.ShapeDtype...]
    pallas_call x3, Pallas kernels: 1.45 us -> 2.34 us  [the longest x1 2.24 us: candidates(): pl.pallas_call(candidates_kernel, out_shape=[jax.ShapeDtypeStruct((EDGE *...]
    unnamed x12 -> x10, local copies, waits for them, and re-layouts: 1.64 us -> 2.37 us
  transfers between devices with their start and end apart: 8 -> 11, of which waited for: 3 -> 6; matrix products, arithmetic and copies ran while one was open for 0% -> 0% of each run, Pallas kernels for 2% -> 6%
where the time goes in v5:
time: 39.8 us; the launch traced here: 39.4 us
  starting transfers between devices  15.4 us (39%)
  waiting for transfers between devices  13 us (33%)
  Pallas kernels  8.65 us (22%)
  local copies, waits for them, and re-layouts  2.37 us (6%)
    pallas_call x1, Pallas kernels, fields(): pl.pallas_call(functools.partial(kernel, count), out_shape=jax.ShapeDtype...  6.3 us
    ppermute x2, waiting for transfers between devices, across_y(): lax.ppermute(last, 'sy', ring('sy', 1))  4.87 us
    ppermute x2, starting transfers between devices, across_corner(): return lax.ppermute(cells, both, diagonal(1, step_y))  4.72 us
    ppermute x2, waiting for transfers between devices, across_y(): lax.ppermute(first, 'sy', ring('sy', -1))  3.65 us
    ppermute x2, starting transfers between devices, across_x(): return lax.ppermute(block, 'sx', ring('sx', 1))  3.6 us
    ppermute x3, starting transfers between devices, body(): lax.ppermute(mine, 'orb', ring('orb', step))  3.16 us
    unnamed x10, local copies, waits for them, and re-layouts  2.37 us
    ppermute x3, waiting for transfers between devices, body(): lax.ppermute(mine, 'orb', ring('orb', step))  2.34 us
  transfers between devices with their start and end apart: 11, of which 6 were waited for; matrix products, arithmetic and copies ran while one was open for 0% of the time, Pallas kernels for 6%

profile of v5, /device:TPU:0, one launch (start us, length us, event | category | flops | bytes accessed | tf_op | source)
XLA Modules:
  0.0 39.4 jit_solution(9658469314766136661)
XLA Ops:
  0.0 0.0 copy-start
  0.0 0.9 %copy-done = bf16[8,8,2048]{2,1,0:T(8,128)(2,1)S(1)} copy-done((bf16[8,8,2048]{2,1,0:T(8,128)(2,1)S(1)}, bf16[8,8,2048]{2,1,0:T(8,128)(2,1)}, u32[]{:S(2)}) %copy-start) | copy-done | bytes 262168
  1.0 0.1 cells.1
  1.0 3.0 %collective-permute-start = (bf16[64,16,128]{2,1,0:T(8,128)(2,1)S(1)}, bf16[64,16,128]{2,1,0:T(8,128)(2,1)S(1)}, u32[]{:S(2)}, u32[]{:S(2)}) collective-permute-start(bf16[64,16,128]{2,1,0:T(8,128)(2,1)S(1)} %get-tuple-element.15.cells.refs_0_), channel_id=1, source_target_pairs={{0,4},{4,0},{1,5},{5,1},{2,6},{6,2},{3,7},{7,3},{8,12},{12,8},{9,1... | collective-permute-start | bytes 786440 | tf_op jit(solution)/shard_map/ppermute | solution.py:213
  4.1 1.6 %collective-permute-start.1 = (bf16[32,16,128]{2,1,0:T(8,128)(2,1)S(1)}, bf16[32,16,128]{2,1,0:T(8,128)(2,1)S(1)}, u32[]{:S(2)}, u32[]{:S(2)}) collective-permute-start(bf16[32,16,128]{2,1,0:T(8,128)(2,1)S(1)} %get-tuple-element.16), channel_id=1, source_target_pairs={{0,1},{1,2},{2,3},{3,0},{4,5},{5,6},{6,7},{7,4},{8,9},{9,10},{10,1... | collective-permute-start | bytes 393224 | tf_op jit(solution)/shard_map/ppermute | solution.py:231
  5.6 2.2 %collective-permute-start.2 = (bf16[32,16,128]{2,1,0:T(8,128)(2,1)S(1)}, bf16[32,16,128]{2,1,0:T(8,128)(2,1)S(1)}, u32[]{:S(2)}, u32[]{:S(2)}) collective-permute-start(bf16[32,16,128]{2,1,0:T(8,128)(2,1)S(1)} %get-tuple-element.17), channel_id=1, source_target_pairs={{0,3},{1,0},{2,1},{3,2},{4,7},{5,4},{6,5},{7,6},{8,11},{9,8},{10,9... | collective-permute-start | bytes 393224 | tf_op jit(solution)/shard_map/ppermute | solution.py:231
  7.9 2.2 %candidates.1 = (bf16[4,16,128]{2,1,0:T(8,128)(2,1)}, s32[16,128]{1,0:T(8,128)}) custom-call(s32[2,2]{1,0:T(2,128)} %owner.1, s32[2,2]{1,0:T(2,128)} %slots.1, bf16[8,8,2048]{2,1,0:T(8,128)(2,1)} %orbitals.3), custom_call_target="tpu_custom_call" | custom-call | tf_op jit(solution)/shard_map/candidates/pallas_call | solution.py:112
  10.1 0.2 collective-permute-start.5
  10.3 1.4 %collective-permute-start.4 = (bf16[4,16,128]{2,1,0:T(8,128)(2,1)}, bf16[4,16,128]{2,1,0:T(8,128)(2,1)S(1)}, u32[]{:S(2)}, u32[]{:S(2)}) collective-permute-start(bf16[4,16,128]{2,1,0:T(8,128)(2,1)} %get-tuple-element.19.refs_0_), channel_id=1, source_target_pairs={{0,16},{8,24},{16,0},{24,8},{1,17},{9,25},{17,1},{25,9},{2,18},{10... | collective-permute-start | bytes 49160 | tf_op jit(solution)/shard_map/ppermute | solution.py:403
  11.8 0.2 collective-permute-done.5.refs_3_
  12.0 1.5 %collective-permute-start.3 = (bf16[4,16,128]{2,1,0:T(8,128)(2,1)}, bf16[4,16,128]{2,1,0:T(8,128)(2,1)S(1)}, u32[]{:S(2)}, u32[]{:S(2)}) collective-permute-start(bf16[4,16,128]{2,1,0:T(8,128)(2,1)} %get-tuple-element.19.refs_0_), channel_id=1, source_target_pairs={{0,8},{8,16},{16,24},{24,0},{1,9},{9,17},{17,25},{25,1},{2,10},{10... | collective-permute-start | bytes 49160 | tf_op jit(solution)/shard_map/ppermute | solution.py:403
  13.5 0.8 %collective-permute-done.4.refs_2_ = bf16[4,16,128]{2,1,0:T(8,128)(2,1)S(1)} collective-permute-done((bf16[4,16,128]{2,1,0:T(8,128)(2,1)}, bf16[4,16,128]{2,1,0:T(8,128)(2,1)S(1)}, u32[]{:S(2)}, u32[]{:S(2)}) %collective-permute-start.4) | collective-permute-done | bytes 16416 | tf_op jit(solution)/shard_map/ppermute | solution.py:403
  14.3 1.3 %collective-permute-done.3.refs_1_ = bf16[4,16,128]{2,1,0:T(8,128)(2,1)S(1)} collective-permute-done((bf16[4,16,128]{2,1,0:T(8,128)(2,1)}, bf16[4,16,128]{2,1,0:T(8,128)(2,1)S(1)}, u32[]{:S(2)}, u32[]{:S(2)}) %collective-permute-start.3) | collective-permute-done | bytes 16416 | tf_op jit(solution)/shard_map/ppermute | solution.py:403
  15.6 0.0 copy-start.3
  15.6 0.7 %copy-done.3 = bf16[4,16,128]{2,1,0:T(8,128)(2,1)S(1)} copy-done((bf16[4,16,128]{2,1,0:T(8,128)(2,1)S(1)}, bf16[4,16,128]{2,1,0:T(8,128)(2,1)}, u32[]{:S(2)}) %copy-start.3) | copy-done | bytes 16408
  16.4 0.7 %copy-done.4 = s32[16,128]{1,0:T(8,128)S(1)} copy-done((s32[16,128]{1,0:T(8,128)S(1)}, s32[16,128]{1,0:T(8,128)}, u32[]{:S(2)}) %copy-start.4) | copy-done | bytes 8216
  17.1 0.1 collective-permute-start.9
  17.2 0.6 %collective-permute-start.8 = (bf16[4,16,128]{2,1,0:T(8,128)(2,1)S(1)}, bf16[4,16,128]{2,1,0:T(8,128)(2,1)S(1)}, u32[]{:S(2)}, u32[]{:S(2)}) collective-permute-start(bf16[4,16,128]{2,1,0:T(8,128)(2,1)S(1)} %get-tuple-element.22.refs_6_), channel_id=1, source_target_pairs={{0,4},{4,0},{1,5},{5,1},{2,6},{6,2},{3,7},{7,3},{8,12},{12,8},{9,1... | collective-permute-start | bytes 49160 | tf_op jit(solution)/shard_map/ppermute | solution.py:213
  17.7 4.9 %collective-permute-done.9.refs_8_ = bf16[2,16,128]{2,1,0:T(8,128)(2,1)S(1)} collective-permute-done((bf16[2,16,128]{2,1,0:T(8,128)(2,1)S(1)}, bf16[2,16,128]{2,1,0:T(8,128)(2,1)S(1)}, u32[]{:S(2)}, u32[]{:S(2)}) %collective-permute-start.9) | collective-permute-done | bytes 8224 | tf_op jit(solution)/shard_map/ppermute | solution.py:231
  22.6 0.0 collective-permute-start.10
  22.6 3.6 %collective-permute-done.10.refs_9_ = bf16[2,16,128]{2,1,0:T(8,128)(2,1)S(1)} collective-permute-done((bf16[2,16,128]{2,1,0:T(8,128)(2,1)S(1)}, bf16[2,16,128]{2,1,0:T(8,128)(2,1)S(1)}, u32[]{:S(2)}, u32[]{:S(2)}) %collective-permute-start.10) | collective-permute-done | bytes 8224 | tf_op jit(solution)/shard_map/ppermute | solution.py:231
  26.2 0.0 collective-permute-start.6
  26.2 0.0 collective-permute-done.8.refs_7_
  26.2 4.7 %collective-permute-start.7 = (bf16[13,16,128]{2,1,0:T(8,128)(2,1)S(1)}, bf16[13,16,128]{2,1,0:T(8,128)(2,1)S(1)}, u32[]{:S(2)}, u32[]{:S(2)}) collective-permute-start(bf16[13,16,128]{2,1,0:T(8,128)(2,1)S(1)} %get-tuple-element.21), channel_id=1, source_target_pairs={{0,7},{1,4},{2,5},{3,6},{4,3},{5,0},{6,1},{7,2},{8,15},{9,12},{10,... | collective-permute-start | bytes 159752 | tf_op jit(solution)/shard_map/ppermute | solution.py:222
  31.0 2.1 %collective-permute-done.6.refs_4_ = bf16[13,16,128]{2,1,0:T(8,128)(2,1)S(1)} collective-permute-done((bf16[13,16,128]{2,1,0:T(8,128)(2,1)S(1)}, bf16[13,16,128]{2,1,0:T(8,128)(2,1)S(1)}, u32[]{:S(2)}, u32[]{:S(2)}) %collective-permute-start.6) | collective-permute-done | bytes 53280 | tf_op jit(solution)/shard_map/ppermute | solution.py:222
  33.1 0.0 collective-permute-done.7.refs_5_
  33.1 0.0 collective-permute-done.1.refs_2_
  33.1 0.0 collective-permute-done.2.refs_3_
  33.1 0.0 collective-permute-done.refs_1_
  33.1 0.0 copy-done.1
  33.1 0.0 copy-done.2
  33.1 6.3 %fields.1 = f32[8,8,2048]{2,1,0:T(8,128)} custom-call(bf16[64,16,128]{2,1,0:T(8,128)(2,1)S(1)} %get-tuple-element.15.cells.refs_0_, bf16[64,16,128]{2,1,0:T(8,128)(2,1)S(1)} %collective-permute-done.refs_1_, bf16[32,16,128]{2,1,0:T(8,128)(2,1)S(1)} %collective-permute-done.1.refs_2_, bf16[32,16,128]{2,1,0:T(8,128)(2,1)S(1)} %collective-permute-done.2.refs_3_, ...), custom_call_target="tpu_custom_call" | custom-call | tf_op jit(solution)/shard_map/fields/pallas_call | solution.py:379
  (4 shorter events, 0.0 us)
Async XLA Ops:
  0.0 0.9 %copy-start = (bf16[8,8,2048]{2,1,0:T(8,128)(2,1)S(1)}, bf16[8,8,2048]{2,1,0:T(8,128)(2,1)}, u32[]{:S(2)}) copy-start(bf16[8,8,2048]{2,1,0:T(8,128)(2,1)} %orbitals.3) | copy-start | bytes 786436
  1.0 32.1 %collective-permute-start = (bf16[64,16,128]{2,1,0:T(8,128)(2,1)S(1)}, bf16[64,16,128]{2,1,0:T(8,128)(2,1)S(1)}, u32[]{:S(2)}, u32[]{:S(2)}) collective-permute-start(bf16[64,16,128]{2,1,0:T(8,128)(2,1)S(1)} %get-tuple-element.15.cells.refs_0_), channel_id=1, source_target_pairs={{0,4},{4,0},{1,5},{5,1},{2,6},{6,2},{3,7},{7,3},{8,12},{12,8},{9,1... | collective-permute-start | bytes 786440 | tf_op jit(solution)/shard_map/ppermute | solution.py:213
  4.1 29.0 %collective-permute-start.1 = (bf16[32,16,128]{2,1,0:T(8,128)(2,1)S(1)}, bf16[32,16,128]{2,1,0:T(8,128)(2,1)S(1)}, u32[]{:S(2)}, u32[]{:S(2)}) collective-permute-start(bf16[32,16,128]{2,1,0:T(8,128)(2,1)S(1)} %get-tuple-element.16), channel_id=1, source_target_pairs={{0,1},{1,2},{2,3},{3,0},{4,5},{5,6},{6,7},{7,4},{8,9},{9,10},{10,1... | collective-permute-start | bytes 393224 | tf_op jit(solution)/shard_map/ppermute | solution.py:231
  5.6 27.4 %collective-permute-start.2 = (bf16[32,16,128]{2,1,0:T(8,128)(2,1)S(1)}, bf16[32,16,128]{2,1,0:T(8,128)(2,1)S(1)}, u32[]{:S(2)}, u32[]{:S(2)}) collective-permute-start(bf16[32,16,128]{2,1,0:T(8,128)(2,1)S(1)} %get-tuple-element.17), channel_id=1, source_target_pairs={{0,3},{1,0},{2,1},{3,2},{4,7},{5,4},{6,5},{7,6},{8,11},{9,8},{10,9... | collective-permute-start | bytes 393224 | tf_op jit(solution)/shard_map/ppermute | solution.py:231
  10.1 1.9 %collective-permute-start.5 = (bf16[4,16,128]{2,1,0:T(8,128)(2,1)}, bf16[4,16,128]{2,1,0:T(8,128)(2,1)S(1)}, u32[]{:S(2)}, u32[]{:S(2)}) collective-permute-start(bf16[4,16,128]{2,1,0:T(8,128)(2,1)} %get-tuple-element.19.refs_0_), channel_id=1, source_target_pairs={{0,24},{8,0},{16,8},{24,16},{1,25},{9,1},{17,9},{25,17},{2,26},{10... | collective-permute-start | bytes 49160 | tf_op jit(solution)/shard_map/ppermute | solution.py:403
  10.3 4.0 %collective-permute-start.4 = (bf16[4,16,128]{2,1,0:T(8,128)(2,1)}, bf16[4,16,128]{2,1,0:T(8,128)(2,1)S(1)}, u32[]{:S(2)}, u32[]{:S(2)}) collective-permute-start(bf16[4,16,128]{2,1,0:T(8,128)(2,1)} %get-tuple-element.19.refs_0_), channel_id=1, source_target_pairs={{0,16},{8,24},{16,0},{24,8},{1,17},{9,25},{17,1},{25,9},{2,18},{10... | collective-permute-start | bytes 49160 | tf_op jit(solution)/shard_map/ppermute | solution.py:403
  12.0 3.6 %collective-permute-start.3 = (bf16[4,16,128]{2,1,0:T(8,128)(2,1)}, bf16[4,16,128]{2,1,0:T(8,128)(2,1)S(1)}, u32[]{:S(2)}, u32[]{:S(2)}) collective-permute-start(bf16[4,16,128]{2,1,0:T(8,128)(2,1)} %get-tuple-element.19.refs_0_), channel_id=1, source_target_pairs={{0,8},{8,16},{16,24},{24,0},{1,9},{9,17},{17,25},{25,1},{2,10},{10... | collective-permute-start | bytes 49160 | tf_op jit(solution)/shard_map/ppermute | solution.py:403
  15.6 0.7 %copy-start.3 = (bf16[4,16,128]{2,1,0:T(8,128)(2,1)S(1)}, bf16[4,16,128]{2,1,0:T(8,128)(2,1)}, u32[]{:S(2)}) copy-start(bf16[4,16,128]{2,1,0:T(8,128)(2,1)} %get-tuple-element.19.refs_0_) | copy-start | bytes 49156
  16.4 0.7 %copy-start.4 = (s32[16,128]{1,0:T(8,128)S(1)}, s32[16,128]{1,0:T(8,128)}, u32[]{:S(2)}) copy-start(s32[16,128]{1,0:T(8,128)} %get-tuple-element.18.owners) | copy-start | bytes 24580
  17.1 16.0 %copy-start.1 = (bf16[256,256]{1,0:T(8,128)(2,1)S(1)}, bf16[256,256]{1,0:T(8,128)(2,1)}, u32[]{:S(2)}) copy-start(bf16[256,256]{1,0:T(8,128)(2,1)} %constant.4.clone.refs_10_) | copy-start | bytes 393220
  17.1 16.1 %copy-start.2 = (f32[4,8,128]{2,1,0:T(8,128)S(1)}, f32[4,8,128]{2,1,0:T(8,128)}, u32[]{:S(2)}) copy-start(f32[4,8,128]{2,1,0:T(8,128)} %constant.5.clone.refs_11_) | copy-start | bytes 49156
  17.1 5.5 %collective-permute-start.9 = (bf16[2,16,128]{2,1,0:T(8,128)(2,1)S(1)}, bf16[2,16,128]{2,1,0:T(8,128)(2,1)S(1)}, u32[]{:S(2)}, u32[]{:S(2)}) collective-permute-start(bf16[2,16,128]{2,1,0:T(8,128)(2,1)S(1)} %get-tuple-element.23), channel_id=1, source_target_pairs={{0,1},{1,2},{2,3},{3,0},{4,5},{5,6},{6,7},{7,4},{8,9},{9,10},{10,1... | collective-permute-start | bytes 24584 | tf_op jit(solution)/shard_map/ppermute | solution.py:231
  17.2 9.1 %collective-permute-start.8 = (bf16[4,16,128]{2,1,0:T(8,128)(2,1)S(1)}, bf16[4,16,128]{2,1,0:T(8,128)(2,1)S(1)}, u32[]{:S(2)}, u32[]{:S(2)}) collective-permute-start(bf16[4,16,128]{2,1,0:T(8,128)(2,1)S(1)} %get-tuple-element.22.refs_6_), channel_id=1, source_target_pairs={{0,4},{4,0},{1,5},{5,1},{2,6},{6,2},{3,7},{7,3},{8,12},{12,8},{9,1... | collective-permute-start | bytes 49160 | tf_op jit(solution)/shard_map/ppermute | solution.py:213
  22.6 3.7 %collective-permute-start.10 = (bf16[2,16,128]{2,1,0:T(8,128)(2,1)S(1)}, bf16[2,16,128]{2,1,0:T(8,128)(2,1)S(1)}, u32[]{:S(2)}, u32[]{:S(2)}) collective-permute-start(bf16[2,16,128]{2,1,0:T(8,128)(2,1)S(1)} %get-tuple-element.24), channel_id=1, source_target_pairs={{0,3},{1,0},{2,1},{3,2},{4,7},{5,4},{6,5},{7,6},{8,11},{9,8},{10,9... | collective-permute-start | bytes 24584 | tf_op jit(solution)/shard_map/ppermute | solution.py:231
  26.2 6.8 %collective-permute-start.6 = (bf16[13,16,128]{2,1,0:T(8,128)(2,1)S(1)}, bf16[13,16,128]{2,1,0:T(8,128)(2,1)S(1)}, u32[]{:S(2)}, u32[]{:S(2)}) collective-permute-start(bf16[13,16,128]{2,1,0:T(8,128)(2,1)S(1)} %get-tuple-element.20), channel_id=1, source_target_pairs={{0,5},{1,6},{2,7},{3,4},{4,1},{5,2},{6,3},{7,0},{8,13},{9,14},{10,... | collective-permute-start | bytes 159752 | tf_op jit(solution)/shard_map/ppermute | solution.py:222
  26.2 6.8 %collective-permute-start.7 = (bf16[13,16,128]{2,1,0:T(8,128)(2,1)S(1)}, bf16[13,16,128]{2,1,0:T(8,128)(2,1)S(1)}, u32[]{:S(2)}, u32[]{:S(2)}) collective-permute-start(bf16[13,16,128]{2,1,0:T(8,128)(2,1)S(1)} %get-tuple-element.21), channel_id=1, source_target_pairs={{0,7},{1,4},{2,5},{3,6},{4,3},{5,0},{6,1},{7,2},{8,15},{9,12},{10,... | collective-permute-start | bytes 159752 | tf_op jit(solution)/shard_map/ppermute | solution.py:222

commit v6 on v4

--- a/solution.py
+++ b/solution.py
@@ -62,67 +62,57 @@
 
 
 VMEM = pl.BlockSpec(memory_space=pltpu.VMEM)
-SMEM = pl.BlockSpec(memory_space=pltpu.SMEM)
-HBM = pl.BlockSpec(memory_space=pltpu.HBM)
 SMALL = pltpu.CompilerParams(vmem_limit_bytes=8 * 2**20)
 
 
-def candidates_kernel(slots, orbitals, out, chosen, tiles_of, slot_sem, tile_sems):
-    copy = pltpu.make_async_copy(slots, chosen, slot_sem)
-    copy.start()
-    copy.wait()
+def spread_out(values):
+    return lax.broadcast_in_dim(values, values.shape + (ROWS, LANES), (0, 1))
+
+
+def by_seat(entries):
+    rounds, places, rows, lanes = entries.shape
+    seat = lax.broadcasted_iota(jnp.int32, (rows, lanes), 1) // NZ
+    value = entries[0, 0]
+    for index in range(1, rounds * places):
+        value = jnp.where(seat == index, entries[index // places, index % places], value)
+    return value
+
+
+def candidates_kernel(slots, orbitals, out):
+    per_tile = LANES // NZ
+    slot = by_seat(slots)[:EDGE]
     lane = lax.broadcasted_iota(jnp.int32, (EDGE, LANES), 1)
-    per_tile = LANES // NZ
-    rounds, places = slots.shape
-    copies, shifts = [], []
-    for index in range(rounds * places):
-        slot = chosen[index // places, index % places]
-        lanes = pl.ds(pl.multiple_of(slot // per_tile * LANES, LANES), LANES)
-        copies.append(
-            pltpu.make_async_copy(
-                orbitals.at[:, :, lanes], tiles_of.at[index], tile_sems.at[index]
-            )
-        )
-        copies[-1].start()
-        shifts.append((index - slot % per_tile + per_tile) % per_tile * NZ)
-    for copy in copies:
-        copy.wait()
+    group, turn = slot // per_tile, (lane // NZ - slot % per_tile + per_tile) % per_tile
+    asked = [pltpu.roll(group, LANES - step * NZ, 1) if step else group for step in range(per_tile)]
+    found = [[jnp.zeros((EDGE, LANES), jnp.float32)] * EDGE for _ in range(per_tile)]
+    for number in range(ROWS):
+        lanes = pl.ds(number * LANES, LANES)
+        tiles = [orbitals[row, :, lanes].astype(jnp.float32) for row in range(EDGE)]
+        for step in range(per_tile):
+            here = asked[step] == number
+            found[step] = [jnp.where(here, tile, old) for tile, old in zip(tiles, found[step])]
     rows = []
     for row in range(EDGE):
-        packed = jnp.zeros((EDGE, LANES), jnp.float32)
-        for index, shift in enumerate(shifts):
-            tile = tiles_of[index, row].astype(jnp.float32)
-            packed = jnp.where(lane // NZ == index, pltpu.roll(tile, shift, 1), packed)
+        packed = found[0][row]
+        for step in range(1, per_tile):
+            packed = jnp.where(turn == step, pltpu.roll(found[step][row], step * NZ, 1), packed)
         rows.append(packed)
     for tile in range(EDGE // 2):
         out[tile] = jnp.concatenate(rows[2 * tile : 2 * tile + 2], axis=0).astype(jnp.bfloat16)
 
 
-def candidates(orbitals, src_slot):
-    count = src_slot.size
+def candidates(slots, orbitals):
     return pl.pallas_call(
         candidates_kernel,
         out_shape=jax.ShapeDtypeStruct((EDGE * EDGE // ROWS, ROWS, LANES), jnp.bfloat16),
-        in_specs=[HBM, HBM],
+        in_specs=[VMEM] * 2,
         out_specs=VMEM,
-        scratch_shapes=[
-            pltpu.SMEM(src_slot.shape, jnp.int32),
-            pltpu.VMEM((count, EDGE, EDGE, LANES), jnp.bfloat16),
-            pltpu.SemaphoreType.DMA,
-            pltpu.SemaphoreType.DMA((count,)),
-        ],
         compiler_params=SMALL,
         name="candidates",
-    )(src_slot, orbitals)
-
-
-def cells_kernel(owner, orbitals, out, wanted, scratch):
-    lane = lax.broadcasted_iota(jnp.int32, (ROWS, LANES), 1)
-    rounds, places = owner.shape
-    owners = jnp.zeros((ROWS, LANES), jnp.int32)
-    for index in range(rounds * places):
-        owners = jnp.where(lane // NZ == index, owner[index // places, index % places], owners)
-    wanted[...] = owners
+    )(slots, orbitals)
+
+
+def cells_kernel(orbitals, out, scratch):
     for row in range(EDGE):
         for group in range(ROWS):
             tile = orbitals[row, :, pl.ds(group * LANES, LANES)].astype(jnp.float32)
@@ -133,33 +123,64 @@
             out[row * EDGE + y] = tile.astype(jnp.bfloat16)
 
 
-def cells_of(orbitals, src_owner):
+def cells_of(orbitals):
     return pl.pallas_call(
         cells_kernel,
-        out_shape=[
-            jax.ShapeDtypeStruct((EDGE * EDGE, ROWS, LANES), jnp.bfloat16),
-            jax.ShapeDtypeStruct((ROWS, LANES), jnp.int32),
-        ],
-        in_specs=[SMEM, VMEM],
-        out_specs=[VMEM, VMEM],
+        out_shape=jax.ShapeDtypeStruct((EDGE * EDGE, ROWS, LANES), jnp.bfloat16),
+        in_specs=[VMEM],
+        out_specs=VMEM,
         scratch_shapes=[pltpu.VMEM((EDGE, EDGE * (ROWS + 1), LANES), jnp.float32)],
         compiler_params=SMALL,
         cost_estimate=pl.CostEstimate(flops=0, bytes_accessed=4 * 2**20, transcendentals=0),
         name="cells",
-    )(src_owner, orbitals)
-
-
-def messages_kernel(count, cells, owners, *refs):
-    offered, (block, last, first, corner_low, corner_high) = refs[:count], refs[count:]
-    me = lax.axis_index("orb")
-    wanted = owners[...]
+    )(orbitals)
+
+
+def chosen(owners, mine, others, bit):
+    owner, me = by_seat(owners), lax.axis_index("orb")
+    count = lax.axis_size("orb")
     picked = []
-    for tile in range(EDGE * EDGE // ROWS):
-        value = offered[0][tile].astype(jnp.float32)
-        for step in range(1, count):
-            theirs = offered[step][tile].astype(jnp.float32)
-            value = jnp.where(wanted == lax.rem(me + count - step, count), theirs, value)
+    for tile in range(mine.shape[0]):
+        value = mine[tile].astype(jnp.float32)
+        for step, other in enumerate(others, 1):
+            if bit is None:
+                here = owner == lax.rem(me + count - step, count)
+            else:
+                here = (owner >> bit & 1) != (me >> bit & 1)
+            value = jnp.where(here, other[tile].astype(jnp.float32), value)
         picked.append(value)
+    return picked
+
+
+def nearer_kernel(bit, owners, mine, other, out):
+    for tile, value in enumerate(chosen(owners, mine, [other], bit)):
+        out[tile] = value.astype(jnp.bfloat16)
+
+
+def gathered(owners, mine):
+    count = lax.axis_size("orb")
+    if count & (count - 1):
+        others = [lax.ppermute(mine, "orb", ring("orb", step)) for step in range(1, count)]
+        return mine, others, None
+    bits = count.bit_length() - 1
+    for bit in range(bits):
+        other = lax.ppermute(mine, "orb", [(i, i ^ 1 << bit) for i in range(count)])
+        if bit == bits - 1:
+            return mine, [other], bit
+        mine = pl.pallas_call(
+            functools.partial(nearer_kernel, bit),
+            out_shape=jax.ShapeDtypeStruct(mine.shape, mine.dtype),
+            in_specs=[VMEM] * 3,
+            out_specs=VMEM,
+            compiler_params=SMALL,
+            name="nearer",
+        )(owners, mine, other)
+    return mine, [], None
+
+
+def messages_kernel(bit, owners, cells, mine, *refs):
+    others, (block, last, first, corner_low, corner_high) = refs[:-5], refs[-5:]
+    picked = chosen(owners, mine, others, bit)
 
     def pack(ref, spots):
         for at, (x, y) in enumerate(spots):
@@ -192,20 +213,20 @@
     return spots + -(-spots // ROWS)
 
 
-def messages(orbitals, mine, src_owner):
-    count = lax.axis_size("orb")
-    offered = [mine] + [lax.ppermute(mine, "orb", ring("orb", step)) for step in range(1, count)]
+def messages(orbitals, src_owner, src_slot):
+    owners = spread_out(src_owner)
+    mine, others, bit = gathered(owners, candidates(spread_out(src_slot), orbitals))
     lengths = [EDGE * EDGE] + [EDGE * HALO] * 2 + [len(CORNER_LOW)] * 2
     return pl.pallas_call(
-        functools.partial(messages_kernel, count),
+        functools.partial(messages_kernel, bit),
         out_shape=[
             jax.ShapeDtypeStruct((tiles(length), ROWS, LANES), jnp.bfloat16) for length in lengths
         ],
-        in_specs=[VMEM] * (2 + count),
+        in_specs=[VMEM] * (3 + len(others)),
         out_specs=[VMEM] * 5,
         compiler_params=SMALL,
         name="messages",
-    )(*cells_of(orbitals, src_owner), *offered)
+    )(owners, cells_of(orbitals), mine, *others)
 
 
 def exchange(block, last, first, corner_low, corner_high):
@@ -291,14 +312,13 @@
     shape = (LANES, LANES)
     lane = lax.broadcasted_iota(jnp.int32, shape, 1) % NZ
     line = lax.broadcasted_iota(jnp.int32, shape, 0)
+    repeats = [(line == lane + place * NZ).astype(jnp.bfloat16) for place in range(count)]
     first_row = []
     total = 0
     for ref in halo:
-        used = ref.shape[0] * ROWS // (ROWS + 1)
-        packed = ref[used:].reshape(-1, LANES)
+        packed = ref[ref.shape[0] * ROWS // (ROWS + 1) :].reshape(-1, LANES)
         first_row.append(total)
-        for place in range(count):
-            repeat = (line == lane + place * NZ).astype(jnp.bfloat16)
+        for place, repeat in enumerate(repeats):
             rows_of[place, pl.ds(total, packed.shape[0]), :] = jnp.dot(
                 packed, repeat, preferred_element_type=jnp.float32
             )
@@ -315,13 +335,14 @@
         parts[at, :, :LANES] = high
         parts[at, :, LANES:] = low
 
-    def turned(cells):
-        rows = parts[:cells].reshape(cells * ROWS, 2 * LANES)
+    def turned(first, end):
+        cells = end - first
+        rows = parts[first:end].reshape(cells * ROWS, 2 * LANES)
         both = jnp.dot(rows, modes[...], preferred_element_type=jnp.float32)
         return (both[:, :LANES] + both[:, LANES:]).reshape(cells, ROWS, LANES)
 
     def one_half(half):
-        rows = pl.ds(pl.multiple_of(half * SUB, SUB), SUB)
+        rows = pl.ds(half * SUB, SUB)
 
         def start(x, y):
             return hat[number[x, y], rows, :]
@@ -341,38 +362,28 @@
                 for y in range(SIZE - 1):
                     if y in targets[x] or y + 1 in targets[x + 1]:
                         pair[y] = ahead[y] + here[y + 1]
-                extra = [here[y] if old is None else start(x, y) for y in targets[x]]
-                totals = [
-                    pair[y] + pair_prev[y - 1] + tails[step] * density
-                    for y, density in zip(targets[x], extra)
-                ]
-                for y, value in zip(targets[x], totals):
-                    if new is not None:
-                        new[x, y] = value
-                    else:
-                        last[CORE.index((x, y)), rows, :] = value
+                    if y in targets[x]:
+                        density = here[y] if old is None else start(x, y)
+                        value = pair[y] + pair_prev[y - 1] + tails[step] * density
+                        if new is not None:
+                            new[x, y] = value
+                        else:
+                            last[CORE.index((x, y)), rows, :] = value
                 here, pair_prev = ahead, pair
 
     def one_source(place, carry):
-        for x in range(SIZE):
-            row = within(HALO)[x]
-            values = []
-            for y in row:
-                which, at = place_of(x, y)
-                values.append(halo[which][at].astype(jnp.float32))
-            others = [spread(place, x, y) for y in row]
-            for y, value, other in zip(row, values, others):
-                keep(number[x, y], value * other)
-        hat[...] = turned(len(CELLS))
-
-        def inner_loop(half, carry):
+        chunk = len(CELLS) // 4
+        for first in range(0, len(CELLS), chunk):
+            end = min(first + chunk, len(CELLS))
+            for at in range(first, end):
+                which, spot = place_of(*CELLS[at])
+                keep(at, halo[which][spot].astype(jnp.float32) * spread(place, *CELLS[at]))
+            hat[first:end] = turned(first, end)
+        for half in range(ROWS // SUB):
             one_half(half)
-            return carry
-
-        lax.fori_loop(0, ROWS // SUB, inner_loop, 0)
         for at in range(len(CORE)):
             keep(at, last[at])
-        back = turned(len(CORE))
+        back = turned(0, len(CORE))
         for at, (x, y) in enumerate(CORE):
             rows = pl.ds((y - HALO) * pitch, ROWS)
             acc[x - HALO, rows, :] = acc[x - HALO, rows, :] + back[at] * spread(place, x, y)
@@ -410,7 +421,7 @@
 
 
 def body(orbitals, src_owner, src_slot):
-    packed = messages(orbitals, candidates(orbitals, src_slot), src_owner)
+    packed = messages(orbitals, src_owner, src_slot)
     return fields((packed[0], *exchange(*packed)), src_slot.size)
 
 

time: 29.9 us -> 27.7 us (0.926)
  Pallas kernels: 9.69 us -> 6.8 us
  starting transfers between devices: 13.4 us -> 14.1 us
    pallas_call x1, Pallas kernels: 8.23 us -> 6.42 us  [fields(): pl.pallas_call(functools.partial(kernel, count), out_shape=jax.ShapeDtype...]
    broadcast_in_dim x0 -> x2, local copies, waits for them, and re-layouts: none -> 0.82 us  [spread_out(): return lax.broadcast_in_dim(values, values.shape + (ROWS, LANES), (0, 1))]
    unnamed x12 -> x10, local copies, waits for them, and re-layouts: 1.64 us -> 0.97 us
    pallas_call x1, Pallas kernels: 0.76 us -> 0.22 us  [candidates(): pl.pallas_call(candidates_kernel, out_shape=jax.ShapeDtypeStruct((EDGE *...]
    pallas_call x2 -> x3, Pallas kernels: 0.69 us -> 0.16 us  [the longest x1 0.09 us: messages(): pl.pallas_call(functools.partial(messages_kernel, bit), out_shape=[jax.Sh...]
    ppermute x1, starting transfers between devices: 1.58 us -> 2.11 us  [exchange(): across = lax.ppermute(block, 'sx', ring('sx', 1))]
    ppermute x3 -> x2, starting transfers between devices: 3.23 us -> 3.41 us  [gathered(): other = lax.ppermute(mine, 'orb', [(i, i ^ 1 << bit) for i in range(count)])]
    ppermute x3 -> x2, waiting for transfers between devices: 2.49 us -> 2.48 us  [gathered(): other = lax.ppermute(mine, 'orb', [(i, i ^ 1 << bit) for i in range(count)])]
  transfers between devices with their start and end apart: 8 -> 7, of which waited for: 3 -> 3; matrix products, arithmetic and copies ran while one was open for 0% -> 0% of each run, Pallas kernels for 2% -> 0%
where the time goes in v6:
time: 27.7 us; the launch traced here: 27.6 us
  starting transfers between devices  14.1 us (51%)
  Pallas kernels  6.8 us (25%)
  waiting for transfers between devices  4.86 us (18%)
  local copies, waits for them, and re-layouts  1.79 us (6%)
    pallas_call x1, Pallas kernels, fields(): pl.pallas_call(functools.partial(kernel, count), out_shape=jax.ShapeDtype...  6.42 us
    ppermute x1, starting transfers between devices, exchange(): high = lax.ppermute(corner_high, both, diagonal(1, -1))  4.72 us
    ppermute x2, starting transfers between devices, gathered(): other = lax.ppermute(mine, 'orb', [(i, i ^ 1 << bit) for i in range(count)])  3.41 us
    ppermute x2, waiting for transfers between devices, gathered(): other = lax.ppermute(mine, 'orb', [(i, i ^ 1 << bit) for i in range(count)])  2.48 us
    ppermute x1, waiting for transfers between devices, exchange(): low = lax.ppermute(corner_low, both, diagonal(1, 1))  2.36 us
    ppermute x1, starting transfers between devices, exchange(): above = lax.ppermute(first, 'sy', ring('sy', -1))  2.25 us
    ppermute x1, starting transfers between devices, exchange(): across = lax.ppermute(block, 'sx', ring('sx', 1))  2.11 us
    ppermute x1, starting transfers between devices, exchange(): below = lax.ppermute(last, 'sy', ring('sy', 1))  1.58 us
  transfers between devices with their start and end apart: 7, of which 3 were waited for; matrix products, arithmetic and copies ran while one was open for 0% of the time, Pallas kernels for 0%

profile of v6, /device:TPU:0, one launch (start us, length us, event | category | flops | bytes accessed | tf_op | source)
XLA Modules:
  0.0 27.6 jit_solution(13693592223220658619)
XLA Ops:
  0.0 0.7 %broadcast_in_dim.7.slots = s32[2,2,16,128]{3,2,1,0:T(8,128)S(1)} broadcast(s32[2,2]{1,0:T(2,128)} %param.7), dimensions={0,1} | broadcast | bytes 32784 | tf_op jit(solution)/shard_map/broadcast_in_dim | solution.py:69
  0.7 0.0 copy-start
  0.8 0.9 %copy-done = bf16[8,8,2048]{2,1,0:T(8,128)(2,1)S(1)} copy-done((bf16[8,8,2048]{2,1,0:T(8,128)(2,1)S(1)}, bf16[8,8,2048]{2,1,0:T(8,128)(2,1)}, u32[]{:S(2)}) %copy-start) | copy-done | bytes 262168
  1.7 0.0 copy-start.4
  1.7 0.0 copy-start.1
  1.7 0.2 candidates.1.mine
  1.9 0.5 %collective-permute-start = (bf16[4,16,128]{2,1,0:T(8,128)(2,1)S(1)}, bf16[4,16,128]{2,1,0:T(8,128)(2,1)S(1)}, u32[]{:S(2)}, u32[]{:S(2)}) collective-permute-start(bf16[4,16,128]{2,1,0:T(8,128)(2,1)S(1)} %candidates.1.mine), channel_id=1, source_target_pairs={{0,8},{8,0},{16,24},{24,16},{1,9},{9,1},{17,25},{25,17},{2,10},{10... | collective-permute-start | bytes 49160 | tf_op jit(solution)/shard_map/ppermute | solution.py:167
  2.4 0.8 %collective-permute-done.other = bf16[4,16,128]{2,1,0:T(8,128)(2,1)S(1)} collective-permute-done((bf16[4,16,128]{2,1,0:T(8,128)(2,1)S(1)}, bf16[4,16,128]{2,1,0:T(8,128)(2,1)S(1)}, u32[]{:S(2)}, u32[]{:S(2)}) %collective-permute-start) | collective-permute-done | bytes 16416 | tf_op jit(solution)/shard_map/ppermute | solution.py:167
  3.3 0.0 copy-done.4
  3.3 0.1 broadcast_in_dim.6.owners
  3.4 2.9 %collective-permute-start.1 = (bf16[4,16,128]{2,1,0:T(8,128)(2,1)S(1)}, bf16[4,16,128]{2,1,0:T(8,128)(2,1)S(1)}, u32[]{:S(2)}, u32[]{:S(2)}) collective-permute-start(bf16[4,16,128]{2,1,0:T(8,128)(2,1)S(1)} %nearer.1.mine), channel_id=1, source_target_pairs={{0,16},{8,24},{16,0},{24,8},{1,17},{9,25},{17,1},{25,9},{2,18},{10... | collective-permute-start | bytes 49160 | tf_op jit(solution)/shard_map/ppermute | solution.py:167
  6.3 0.0 copy-done.1
  6.3 0.1 cells.1
  6.3 0.0 copy-start.2
  6.3 1.6 %collective-permute-done.1.refs_0_ = bf16[4,16,128]{2,1,0:T(8,128)(2,1)S(1)} collective-permute-done((bf16[4,16,128]{2,1,0:T(8,128)(2,1)S(1)}, bf16[4,16,128]{2,1,0:T(8,128)(2,1)S(1)}, u32[]{:S(2)}, u32[]{:S(2)}) %collective-permute-start.1) | collective-permute-done | bytes 16416 | tf_op jit(solution)/shard_map/ppermute | solution.py:167
  8.0 0.0 copy-start.3
  8.0 0.1 messages.1
  8.1 2.1 %collective-permute-start.2 = (bf16[68,16,128]{2,1,0:T(8,128)(2,1)S(1)}, bf16[68,16,128]{2,1,0:T(8,128)(2,1)S(1)}, u32[]{:S(2)}, u32[]{:S(2)}) collective-permute-start(bf16[68,16,128]{2,1,0:T(8,128)(2,1)S(1)} %get-tuple-element.10.refs_0_), channel_id=1, source_target_pairs={{0,4},{4,0},{1,5},{5,1},{2,6},{6,2},{3,7},{7,3},{8,12},{12,8},{9,1... | collective-permute-start | bytes 835592 | tf_op jit(solution)/shard_map/ppermute | solution.py:237
  10.2 1.6 %collective-permute-start.3 = (bf16[34,16,128]{2,1,0:T(8,128)(2,1)S(1)}, bf16[34,16,128]{2,1,0:T(8,128)(2,1)S(1)}, u32[]{:S(2)}, u32[]{:S(2)}) collective-permute-start(bf16[34,16,128]{2,1,0:T(8,128)(2,1)S(1)} %get-tuple-element.11), channel_id=1, source_target_pairs={{0,1},{1,2},{2,3},{3,0},{4,5},{5,6},{6,7},{7,4},{8,9},{9,10},{10,1... | collective-permute-start | bytes 417800 | tf_op jit(solution)/shard_map/ppermute | solution.py:254
  11.8 2.2 %collective-permute-start.4 = (bf16[34,16,128]{2,1,0:T(8,128)(2,1)S(1)}, bf16[34,16,128]{2,1,0:T(8,128)(2,1)S(1)}, u32[]{:S(2)}, u32[]{:S(2)}) collective-permute-start(bf16[34,16,128]{2,1,0:T(8,128)(2,1)S(1)} %get-tuple-element.12), channel_id=1, source_target_pairs={{0,3},{1,0},{2,1},{3,2},{4,7},{5,4},{6,5},{7,6},{8,11},{9,8},{10,9... | collective-permute-start | bytes 417800 | tf_op jit(solution)/shard_map/ppermute | solution.py:255
  14.0 0.0 collective-permute-start.5
  14.0 4.7 %collective-permute-start.6 = (bf16[13,16,128]{2,1,0:T(8,128)(2,1)S(1)}, bf16[13,16,128]{2,1,0:T(8,128)(2,1)S(1)}, u32[]{:S(2)}, u32[]{:S(2)}) collective-permute-start(bf16[13,16,128]{2,1,0:T(8,128)(2,1)S(1)} %get-tuple-element.14), channel_id=1, source_target_pairs={{0,7},{1,4},{2,5},{3,6},{4,3},{5,0},{6,1},{7,2},{8,15},{9,12},{10,... | collective-permute-start | bytes 159752 | tf_op jit(solution)/shard_map/ppermute | solution.py:236
  18.7 2.4 %collective-permute-done.5.refs_4_ = bf16[13,16,128]{2,1,0:T(8,128)(2,1)S(1)} collective-permute-done((bf16[13,16,128]{2,1,0:T(8,128)(2,1)S(1)}, bf16[13,16,128]{2,1,0:T(8,128)(2,1)S(1)}, u32[]{:S(2)}, u32[]{:S(2)}) %collective-permute-start.5) | collective-permute-done | bytes 53280 | tf_op jit(solution)/shard_map/ppermute | solution.py:235
  21.1 0.0 collective-permute-done.6.refs_5_
  21.1 0.0 collective-permute-done.3.refs_2_
  21.1 0.0 collective-permute-done.4.refs_3_
  21.1 0.0 collective-permute-done.2.refs_1_
  21.1 0.0 copy-done.2
  21.1 0.0 copy-done.3
  21.2 6.4 %fields.1 = f32[8,8,2048]{2,1,0:T(8,128)} custom-call(bf16[68,16,128]{2,1,0:T(8,128)(2,1)S(1)} %get-tuple-element.10.refs_0_, bf16[68,16,128]{2,1,0:T(8,128)(2,1)S(1)} %collective-permute-done.2.refs_1_, bf16[34,16,128]{2,1,0:T(8,128)(2,1)S(1)} %collective-permute-done.3.refs_2_, bf16[34,16,128]{2,1,0:T(8,128)(2,1)S(1)} %collective-permute-done.4.refs_3_, ...), custom_call_target="tpu_custom_call" | custom-call | tf_op jit(solution)/shard_map/fields/pallas_call | solution.py:404
  (1 shorter events, 0.0 us)
Async XLA Ops:
  0.7 1.0 %copy-start = (bf16[8,8,2048]{2,1,0:T(8,128)(2,1)S(1)}, bf16[8,8,2048]{2,1,0:T(8,128)(2,1)}, u32[]{:S(2)}) copy-start(bf16[8,8,2048]{2,1,0:T(8,128)(2,1)} %orbitals.3) | copy-start | bytes 786436
  1.7 1.6 %copy-start.4 = (s32[2,2]{1,0:T(2,128)S(1)}, s32[2,2]{1,0:T(2,128)}, u32[]{:S(2)}) copy-start(s32[2,2]{1,0:T(2,128)} %param.6) | copy-start | bytes 52
  1.7 4.6 %copy-start.1 = (bf16[8,8,2048]{2,1,0:T(8,128)(2,1)S(1)}, bf16[8,8,2048]{2,1,0:T(8,128)(2,1)}, u32[]{:S(2)}) copy-start(bf16[8,8,2048]{2,1,0:T(8,128)(2,1)} %orbitals.3) | copy-start | bytes 786436
  1.9 1.4 %collective-permute-start = (bf16[4,16,128]{2,1,0:T(8,128)(2,1)S(1)}, bf16[4,16,128]{2,1,0:T(8,128)(2,1)S(1)}, u32[]{:S(2)}, u32[]{:S(2)}) collective-permute-start(bf16[4,16,128]{2,1,0:T(8,128)(2,1)S(1)} %candidates.1.mine), channel_id=1, source_target_pairs={{0,8},{8,0},{16,24},{24,16},{1,9},{9,1},{17,25},{25,17},{2,10},{10... | collective-permute-start | bytes 49160 | tf_op jit(solution)/shard_map/ppermute | solution.py:167
  3.4 4.6 %collective-permute-start.1 = (bf16[4,16,128]{2,1,0:T(8,128)(2,1)S(1)}, bf16[4,16,128]{2,1,0:T(8,128)(2,1)S(1)}, u32[]{:S(2)}, u32[]{:S(2)}) collective-permute-start(bf16[4,16,128]{2,1,0:T(8,128)(2,1)S(1)} %nearer.1.mine), channel_id=1, source_target_pairs={{0,16},{8,24},{16,0},{24,8},{1,17},{9,25},{17,1},{25,9},{2,18},{10... | collective-permute-start | bytes 49160 | tf_op jit(solution)/shard_map/ppermute | solution.py:167
  6.3 14.8 %copy-start.2 = (bf16[256,256]{1,0:T(8,128)(2,1)S(1)}, bf16[256,256]{1,0:T(8,128)(2,1)}, u32[]{:S(2)}) copy-start(bf16[256,256]{1,0:T(8,128)(2,1)} %constant.4.clone.refs_6_) | copy-start | bytes 393220
  8.0 13.2 %copy-start.3 = (f32[4,8,128]{2,1,0:T(8,128)S(1)}, f32[4,8,128]{2,1,0:T(8,128)}, u32[]{:S(2)}) copy-start(f32[4,8,128]{2,1,0:T(8,128)} %constant.5.clone.refs_7_) | copy-start | bytes 49156
  8.1 13.0 %collective-permute-start.2 = (bf16[68,16,128]{2,1,0:T(8,128)(2,1)S(1)}, bf16[68,16,128]{2,1,0:T(8,128)(2,1)S(1)}, u32[]{:S(2)}, u32[]{:S(2)}) collective-permute-start(bf16[68,16,128]{2,1,0:T(8,128)(2,1)S(1)} %get-tuple-element.10.refs_0_), channel_id=1, source_target_pairs={{0,4},{4,0},{1,5},{5,1},{2,6},{6,2},{3,7},{7,3},{8,12},{12,8},{9,1... | collective-permute-start | bytes 835592 | tf_op jit(solution)/shard_map/ppermute | solution.py:237
  10.2 10.9 %collective-permute-start.3 = (bf16[34,16,128]{2,1,0:T(8,128)(2,1)S(1)}, bf16[34,16,128]{2,1,0:T(8,128)(2,1)S(1)}, u32[]{:S(2)}, u32[]{:S(2)}) collective-permute-start(bf16[34,16,128]{2,1,0:T(8,128)(2,1)S(1)} %get-tuple-element.11), channel_id=1, source_target_pairs={{0,1},{1,2},{2,3},{3,0},{4,5},{5,6},{6,7},{7,4},{8,9},{9,10},{10,1... | collective-permute-start | bytes 417800 | tf_op jit(solution)/shard_map/ppermute | solution.py:254
  11.8 9.3 %collective-permute-start.4 = (bf16[34,16,128]{2,1,0:T(8,128)(2,1)S(1)}, bf16[34,16,128]{2,1,0:T(8,128)(2,1)S(1)}, u32[]{:S(2)}, u32[]{:S(2)}) collective-permute-start(bf16[34,16,128]{2,1,0:T(8,128)(2,1)S(1)} %get-tuple-element.12), channel_id=1, source_target_pairs={{0,3},{1,0},{2,1},{3,2},{4,7},{5,4},{6,5},{7,6},{8,11},{9,8},{10,9... | collective-permute-start | bytes 417800 | tf_op jit(solution)/shard_map/ppermute | solution.py:255
  14.0 7.1 %collective-permute-start.5 = (bf16[13,16,128]{2,1,0:T(8,128)(2,1)S(1)}, bf16[13,16,128]{2,1,0:T(8,128)(2,1)S(1)}, u32[]{:S(2)}, u32[]{:S(2)}) collective-permute-start(bf16[13,16,128]{2,1,0:T(8,128)(2,1)S(1)} %get-tuple-element.13), channel_id=1, source_target_pairs={{0,5},{1,6},{2,7},{3,4},{4,1},{5,2},{6,3},{7,0},{8,13},{9,14},{10,... | collective-permute-start | bytes 159752 | tf_op jit(solution)/shard_map/ppermute | solution.py:235
  14.0 7.1 %collective-permute-start.6 = (bf16[13,16,128]{2,1,0:T(8,128)(2,1)S(1)}, bf16[13,16,128]{2,1,0:T(8,128)(2,1)S(1)}, u32[]{:S(2)}, u32[]{:S(2)}) collective-permute-start(bf16[13,16,128]{2,1,0:T(8,128)(2,1)S(1)} %get-tuple-element.14), channel_id=1, source_target_pairs={{0,7},{1,4},{2,5},{3,6},{4,3},{5,0},{6,1},{7,2},{8,15},{9,12},{10,... | collective-permute-start | bytes 159752 | tf_op jit(solution)/shard_map/ppermute | solution.py:236

commit v7 on v6

--- a/solution.py
+++ b/solution.py
@@ -213,6 +213,10 @@
     return spots + -(-spots // ROWS)
 
 
+def spots_of(length):
+    return length * ROWS // (ROWS + 1)
+
+
 def messages(orbitals, src_owner, src_slot):
     owners = spread_out(src_owner)
     mine, others, bit = gathered(owners, candidates(spread_out(src_slot), orbitals))
@@ -299,53 +303,110 @@
     return [[y for y in range(SIZE) if reach(x, y) <= radius] for x in range(SIZE)]
 
 
-CELLS = [(x, y) for x in range(SIZE) for y in within(HALO)[x]]
 CORE = [(x, y) for x in range(HALO, HALO + EDGE) for y in range(HALO, HALO + EDGE)]
 
 
-def kernel(count, *refs):
-    halo, modes, tails = refs[:6], refs[6], refs[7]
-    out, rows_of, parts, hat, work_a, work_b, last, acc = refs[8:]
-    pitch = ROWS + 1
-    number = {cell: at for at, cell in enumerate(CELLS)}
-
+def source_rows(ref, out, first):
     shape = (LANES, LANES)
     lane = lax.broadcasted_iota(jnp.int32, shape, 1) % NZ
     line = lax.broadcasted_iota(jnp.int32, shape, 0)
-    repeats = [(line == lane + place * NZ).astype(jnp.bfloat16) for place in range(count)]
-    first_row = []
-    total = 0
+    packed = ref[spots_of(ref.shape[0]) :].reshape(-1, LANES)
+    for place in range(out.shape[0]):
+        repeat = (line == lane + place * NZ).astype(jnp.bfloat16)
+        out[place, pl.ds(first, packed.shape[0]), :] = jnp.dot(
+            packed, repeat, preferred_element_type=jnp.float32
+        )
+    return first + packed.shape[0]
+
+
+def keep(parts, at, value):
+    high = value.astype(jnp.bfloat16)
+    low = (value - high.astype(jnp.float32)).astype(jnp.bfloat16)
+    parts[at, :, :LANES] = high
+    parts[at, :, LANES:] = low
+
+
+def turned(parts, first, end, modes):
+    cells = end - first
+    rows = parts[first:end].reshape(cells * ROWS, 2 * LANES)
+    both = jnp.dot(rows, modes[...], preferred_element_type=jnp.float32)
+    return (both[:, :LANES] + both[:, LANES:]).reshape(cells, ROWS, LANES)
+
+
+def densities(refs, rows, firsts, place, parts, modes, put):
+    cells = [(ref, at, first + at) for ref, first in zip(refs, firsts) for at in range(spots_of(ref.shape[0]))]
+    chunk = 48
+    for start in range(0, len(cells), chunk):
+        end = min(start + chunk, len(cells))
+        for number in range(start, end):
+            ref, at, row = cells[number]
+            other = jnp.broadcast_to(rows[place, pl.ds(row, 1), :], (ROWS, LANES))
+            keep(parts, number, ref[at].astype(jnp.float32) * other)
+        put(start, end, turned(parts, start, end, modes))
+
+
+def modes_kernel(count, *refs):
+    halo, modes, (hat, own_rows, rows, parts) = refs[:4], refs[4], refs[5:]
+    firsts = [0]
     for ref in halo:
-        packed = ref[ref.shape[0] * ROWS // (ROWS + 1) :].reshape(-1, LANES)
-        first_row.append(total)
-        for place, repeat in enumerate(repeats):
-            rows_of[place, pl.ds(total, packed.shape[0]), :] = jnp.dot(
-                packed, repeat, preferred_element_type=jnp.float32
-            )
-        total += packed.shape[0]
-
-    def spread(place, x, y):
-        which, at = place_of(x, y)
-        row = rows_of[place, pl.ds(first_row[which] + at, 1), :]
-        return jnp.broadcast_to(row, (ROWS, LANES))
-
-    def keep(at, value):
-        high = value.astype(jnp.bfloat16)
-        low = (value - high.astype(jnp.float32)).astype(jnp.bfloat16)
-        parts[at, :, :LANES] = high
-        parts[at, :, LANES:] = low
-
-    def turned(first, end):
-        cells = end - first
-        rows = parts[first:end].reshape(cells * ROWS, 2 * LANES)
-        both = jnp.dot(rows, modes[...], preferred_element_type=jnp.float32)
-        return (both[:, :LANES] + both[:, LANES:]).reshape(cells, ROWS, LANES)
-
-    def one_half(half):
+        firsts.append(source_rows(ref, rows, firsts[-1]))
+    own_rows[...] = rows[:, : own_rows.shape[1], :]
+
+    def one_source(place, carry):
+        def put(start, end, value):
+            hat[place, start:end] = value
+
+        densities(halo, rows, firsts, place, parts, modes, put)
+        return carry
+
+    lax.fori_loop(0, count, one_source, 0)
+
+
+def modes_of(halo, modes, count):
+    cells = sum(spots_of(array.shape[0]) for array in halo)
+    return pl.pallas_call(
+        functools.partial(modes_kernel, count),
+        out_shape=[
+            jax.ShapeDtypeStruct((count, cells, ROWS, LANES), jnp.float32),
+            jax.ShapeDtypeStruct((count, len(CORE), LANES), jnp.float32),
+        ],
+        in_specs=[VMEM] * 5,
+        out_specs=[VMEM] * 2,
+        scratch_shapes=[
+            pltpu.VMEM((count, cells, LANES), jnp.float32),
+            pltpu.VMEM((cells, ROWS, 2 * LANES), jnp.bfloat16),
+        ],
+        compiler_params=pltpu.CompilerParams(vmem_limit_bytes=20 * 2**20),
+        cost_estimate=pl.CostEstimate(flops=0, bytes_accessed=8 * 2**20, transcendentals=0),
+        name="modes",
+    )(*halo, modes)
+
+
+def fields_kernel(count, beside, own_rows, low, high, modes, tails, *refs):
+    out, rows, parts, corners, work_a, work_b, last, acc = refs
+    pitch = ROWS + 1
+    offset = (0, EDGE * EDGE, 2 * EDGE * EDGE, 2 * EDGE * EDGE + EDGE * HALO)
+
+    firsts = [0, source_rows(low, rows, 0)]
+    source_rows(high, rows, firsts[1])
+    for place in range(count):
+
+        def put(start, end, value, place=place):
+            corners[place, start:end] = value
+
+        densities((low, high), rows, firsts, place, parts, modes, put)
+
+    def spread(place, at):
+        return jnp.broadcast_to(own_rows[place, pl.ds(at, 1), :], (ROWS, LANES))
+
+    def one_half(place, half):
         rows = pl.ds(half * SUB, SUB)
 
         def start(x, y):
-            return hat[number[x, y], rows, :]
+            which, at = place_of(x, y)
+            if which < 4:
+                return beside[place, offset[which] + at, rows, :]
+            return corners[place, (which - 4) * len(CORNER_LOW) + at, rows, :]
 
         for step in range(DEGREE):
             new = (work_a, work_b, work_a, None)[step]
@@ -372,21 +433,14 @@
                 here, pair_prev = ahead, pair
 
     def one_source(place, carry):
-        chunk = len(CELLS) // 4
-        for first in range(0, len(CELLS), chunk):
-            end = min(first + chunk, len(CELLS))
-            for at in range(first, end):
-                which, spot = place_of(*CELLS[at])
-                keep(at, halo[which][spot].astype(jnp.float32) * spread(place, *CELLS[at]))
-            hat[first:end] = turned(first, end)
         for half in range(ROWS // SUB):
-            one_half(half)
+            one_half(place, half)
         for at in range(len(CORE)):
-            keep(at, last[at])
-        back = turned(0, len(CORE))
+            keep(parts, at, last[at])
+        back = turned(parts, 0, len(CORE), modes)
         for at, (x, y) in enumerate(CORE):
             rows = pl.ds((y - HALO) * pitch, ROWS)
-            acc[x - HALO, rows, :] = acc[x - HALO, rows, :] + back[at] * spread(place, x, y)
+            acc[x - HALO, rows, :] = acc[x - HALO, rows, :] + back[at] * spread(place, at)
         return carry
 
     acc[...] = jnp.zeros(acc.shape, jnp.float32)
@@ -399,17 +453,18 @@
 
 def fields(halo, count):
     plane = pltpu.VMEM((SIZE, SIZE, SUB, LANES), jnp.float32)
-    rows = sum(array.shape[0] * ROWS // (ROWS + 1) + ROWS for array in halo)
     modes, tails = z_modes()
+    beside, own_rows = modes_of(halo[:4], modes, count)
+    corners = 2 * len(CORNER_LOW)
     return pl.pallas_call(
-        functools.partial(kernel, count),
+        functools.partial(fields_kernel, count),
         out_shape=jax.ShapeDtypeStruct((EDGE, EDGE, ROWS * LANES), jnp.float32),
-        in_specs=[VMEM] * 8,
+        in_specs=[VMEM] * 6,
         out_specs=VMEM,
         scratch_shapes=[
-            pltpu.VMEM((count, rows, LANES), jnp.float32),
-            pltpu.VMEM((len(CELLS), ROWS, 2 * LANES), jnp.bfloat16),
-            pltpu.VMEM((len(CELLS), ROWS, LANES), jnp.float32),
+            pltpu.VMEM((count, 2 * ROWS, LANES), jnp.float32),
+            pltpu.VMEM((len(CORE), ROWS, 2 * LANES), jnp.bfloat16),
+            pltpu.VMEM((count, corners, ROWS, LANES), jnp.float32),
             plane,
             plane,
             pltpu.VMEM((len(CORE), ROWS, LANES), jnp.float32),
@@ -417,7 +472,7 @@
         ],
         compiler_params=pltpu.CompilerParams(vmem_limit_bytes=24 * 2**20),
         name="fields",
-    )(*halo, modes, tails)
+    )(beside, own_rows, *halo[4:], modes, tails)
 
 
 def body(orbitals, src_owner, src_slot):

time: 27.7 us -> 30 us (1.083)
  local copies, waits for them, and re-layouts: 1.79 us -> 5.01 us
  waiting for transfers between devices: 4.86 us -> 2.74 us
  Pallas kernels: 6.8 us -> 7.83 us
    unnamed x10 -> x8, local copies, waits for them, and re-layouts: 0.97 us -> 3.52 us
    ppermute x1, waiting for transfers between devices: 2.36 us -> 0.01 us  [exchange(): low = lax.ppermute(corner_low, both, diagonal(1, 1))]
    ppermute x1, waiting for transfers between devices: 0.01 us -> 1.18 us  [exchange(): above = lax.ppermute(first, 'sy', ring('sy', -1))]
    pallas_call x1 -> x2, Pallas kernels: 6.42 us -> 7.45 us  [the longest x1 4.88 us: fields(): pl.pallas_call(functools.partial(fields_kernel, count), out_shape=jax.Sha...]
    ppermute x2, waiting for transfers between devices: 2.48 us -> 1.55 us  [gathered(): other = lax.ppermute(mine, 'orb', [(i, i ^ 1 << bit) for i in range(count)])]
    broadcast_in_dim x2, local copies, waits for them, and re-layouts: 0.82 us -> 1.5 us  [spread_out(): return lax.broadcast_in_dim(values, values.shape + (ROWS, LANES), (0, 1))]
  transfers between devices with their start and end apart: 7 -> 7, of which waited for: 3 -> 3; matrix products, arithmetic and copies ran while one was open for 0% -> 0% of each run, Pallas kernels for 0% -> 9%
where the time goes in v7:
time: 30 us; the launch traced here: 29.7 us
  starting transfers between devices  14.1 us (47%)
  Pallas kernels  7.83 us (26%)
  local copies, waits for them, and re-layouts  5.01 us (17%)
  waiting for transfers between devices  2.74 us (9%)
    pallas_call x1, Pallas kernels, fields(): pl.pallas_call(functools.partial(fields_kernel, count), out_shape=jax.Sha...  4.88 us
    ppermute x1, starting transfers between devices, exchange(): high = lax.ppermute(corner_high, both, diagonal(1, -1))  4.72 us
    unnamed x8, local copies, waits for them, and re-layouts  3.52 us
    ppermute x2, starting transfers between devices, gathered(): other = lax.ppermute(mine, 'orb', [(i, i ^ 1 << bit) for i in range(count)])  3.41 us
    pallas_call x1, Pallas kernels, modes_of(): pl.pallas_call(functools.partial(modes_kernel, count), out_shape=[jax.Sha...  2.57 us
    ppermute x1, starting transfers between devices, exchange(): above = lax.ppermute(first, 'sy', ring('sy', -1))  2.25 us
    ppermute x1, starting transfers between devices, exchange(): across = lax.ppermute(block, 'sx', ring('sx', 1))  2.11 us
    ppermute x1, starting transfers between devices, exchange(): below = lax.ppermute(last, 'sy', ring('sy', 1))  1.58 us
  transfers between devices with their start and end apart: 7, of which 3 were waited for; matrix products, arithmetic and copies ran while one was open for 0% of the time, Pallas kernels for 9%

profile of v7, /device:TPU:0, one launch (start us, length us, event | category | flops | bytes accessed | tf_op | source)
XLA Modules:
  0.0 29.7 jit_solution(3083682710801298852)
XLA Ops:
  0.0 0.7 %broadcast_in_dim.7.slots = s32[2,2,16,128]{3,2,1,0:T(8,128)S(1)} broadcast(s32[2,2]{1,0:T(2,128)} %param.7), dimensions={0,1} | broadcast | bytes 32784 | tf_op jit(solution)/shard_map/broadcast_in_dim | solution.py:69
  0.7 0.0 copy-start
  0.8 0.9 %copy-done = bf16[8,8,2048]{2,1,0:T(8,128)(2,1)S(1)} copy-done((bf16[8,8,2048]{2,1,0:T(8,128)(2,1)S(1)}, bf16[8,8,2048]{2,1,0:T(8,128)(2,1)}, u32[]{:S(2)}) %copy-start) | copy-done | bytes 262168
  1.7 0.2 candidates.1.mine
  1.9 0.5 %collective-permute-start = (bf16[4,16,128]{2,1,0:T(8,128)(2,1)S(1)}, bf16[4,16,128]{2,1,0:T(8,128)(2,1)S(1)}, u32[]{:S(2)}, u32[]{:S(2)}) collective-permute-start(bf16[4,16,128]{2,1,0:T(8,128)(2,1)S(1)} %candidates.1.mine), channel_id=1, source_target_pairs={{0,8},{8,0},{16,24},{24,16},{1,9},{9,1},{17,25},{25,17},{2,10},{10... | collective-permute-start | bytes 49160 | tf_op jit(solution)/shard_map/ppermute | solution.py:167
  2.4 0.8 %collective-permute-done.other = bf16[4,16,128]{2,1,0:T(8,128)(2,1)S(1)} collective-permute-done((bf16[4,16,128]{2,1,0:T(8,128)(2,1)S(1)}, bf16[4,16,128]{2,1,0:T(8,128)(2,1)S(1)}, u32[]{:S(2)}, u32[]{:S(2)}) %collective-permute-start) | collective-permute-done | bytes 16416 | tf_op jit(solution)/shard_map/ppermute | solution.py:167
  3.3 0.7 %broadcast_in_dim.6.owners = s32[2,2,16,128]{3,2,1,0:T(8,128)S(1)} broadcast(s32[2,2]{1,0:T(2,128)} %param.6), dimensions={0,1} | broadcast | bytes 32784 | tf_op jit(solution)/shard_map/broadcast_in_dim | solution.py:69
  4.0 2.9 %collective-permute-start.1 = (bf16[4,16,128]{2,1,0:T(8,128)(2,1)S(1)}, bf16[4,16,128]{2,1,0:T(8,128)(2,1)S(1)}, u32[]{:S(2)}, u32[]{:S(2)}) collective-permute-start(bf16[4,16,128]{2,1,0:T(8,128)(2,1)S(1)} %nearer.1.mine), channel_id=1, source_target_pairs={{0,16},{8,24},{16,0},{24,8},{1,17},{9,25},{17,1},{25,9},{2,18},{10... | collective-permute-start | bytes 49160 | tf_op jit(solution)/shard_map/ppermute | solution.py:167
  6.9 0.0 copy-start.1
  6.9 0.9 %copy-done.1 = bf16[8,8,2048]{2,1,0:T(8,128)(2,1)S(1)} copy-done((bf16[8,8,2048]{2,1,0:T(8,128)(2,1)S(1)}, bf16[8,8,2048]{2,1,0:T(8,128)(2,1)}, u32[]{:S(2)}) %copy-start.1) | copy-done | bytes 262168
  7.9 0.1 cells.1
  7.9 0.7 %collective-permute-done.1.refs_0_ = bf16[4,16,128]{2,1,0:T(8,128)(2,1)S(1)} collective-permute-done((bf16[4,16,128]{2,1,0:T(8,128)(2,1)S(1)}, bf16[4,16,128]{2,1,0:T(8,128)(2,1)S(1)}, u32[]{:S(2)}, u32[]{:S(2)}) %collective-permute-start.1) | collective-permute-done | bytes 16416 | tf_op jit(solution)/shard_map/ppermute | solution.py:167
  8.7 0.1 messages.1
  8.8 2.1 %collective-permute-start.2 = (bf16[68,16,128]{2,1,0:T(8,128)(2,1)S(1)}, bf16[68,16,128]{2,1,0:T(8,128)(2,1)S(1)}, u32[]{:S(2)}, u32[]{:S(2)}) collective-permute-start(bf16[68,16,128]{2,1,0:T(8,128)(2,1)S(1)} %get-tuple-element.12.refs_0_), channel_id=1, source_target_pairs={{0,4},{4,0},{1,5},{5,1},{2,6},{6,2},{3,7},{7,3},{8,12},{12,8},{9,1... | collective-permute-start | bytes 835592 | tf_op jit(solution)/shard_map/ppermute | solution.py:241
  10.9 1.6 %collective-permute-start.3 = (bf16[34,16,128]{2,1,0:T(8,128)(2,1)S(1)}, bf16[34,16,128]{2,1,0:T(8,128)(2,1)S(1)}, u32[]{:S(2)}, u32[]{:S(2)}) collective-permute-start(bf16[34,16,128]{2,1,0:T(8,128)(2,1)S(1)} %get-tuple-element.13), channel_id=1, source_target_pairs={{0,1},{1,2},{2,3},{3,0},{4,5},{5,6},{6,7},{7,4},{8,9},{9,10},{10,1... | collective-permute-start | bytes 417800 | tf_op jit(solution)/shard_map/ppermute | solution.py:258
  12.4 2.2 %collective-permute-start.4 = (bf16[34,16,128]{2,1,0:T(8,128)(2,1)S(1)}, bf16[34,16,128]{2,1,0:T(8,128)(2,1)S(1)}, u32[]{:S(2)}, u32[]{:S(2)}) collective-permute-start(bf16[34,16,128]{2,1,0:T(8,128)(2,1)S(1)} %get-tuple-element.14), channel_id=1, source_target_pairs={{0,3},{1,0},{2,1},{3,2},{4,7},{5,4},{6,5},{7,6},{8,11},{9,8},{10,9... | collective-permute-start | bytes 417800 | tf_op jit(solution)/shard_map/ppermute | solution.py:259
  14.7 0.0 collective-permute-start.5
  14.7 4.7 %collective-permute-start.6 = (bf16[13,16,128]{2,1,0:T(8,128)(2,1)S(1)}, bf16[13,16,128]{2,1,0:T(8,128)(2,1)S(1)}, u32[]{:S(2)}, u32[]{:S(2)}) collective-permute-start(bf16[13,16,128]{2,1,0:T(8,128)(2,1)S(1)} %get-tuple-element.18), channel_id=1, source_target_pairs={{0,7},{1,4},{2,5},{3,6},{4,3},{5,0},{6,1},{7,2},{8,15},{9,12},{10,... | collective-permute-start | bytes 159752 | tf_op jit(solution)/shard_map/ppermute | solution.py:240
  19.4 0.0 collective-permute-done.3.refs_2_
  19.4 1.2 %collective-permute-done.4.refs_3_ = bf16[34,16,128]{2,1,0:T(8,128)(2,1)S(1)} collective-permute-done((bf16[34,16,128]{2,1,0:T(8,128)(2,1)S(1)}, bf16[34,16,128]{2,1,0:T(8,128)(2,1)S(1)}, u32[]{:S(2)}, u32[]{:S(2)}) %collective-permute-start.4) | collective-permute-done | bytes 139296 | tf_op jit(solution)/shard_map/ppermute | solution.py:259
  20.6 0.0 collective-permute-done.2.refs_1_
  20.6 0.0 copy-start.2
  20.6 0.9 %copy-done.2 = bf16[256,256]{1,0:T(8,128)(2,1)S(1)} copy-done((bf16[256,256]{1,0:T(8,128)(2,1)S(1)}, bf16[256,256]{1,0:T(8,128)(2,1)}, u32[]{:S(2)}) %copy-start.2) | copy-done | bytes 131096
  21.5 2.6 %modes.2 = (f32[4,192,16,128]{3,2,1,0:T(8,128)S(1)}, f32[4,64,128]{2,1,0:T(8,128)S(1)}) custom-call(bf16[68,16,128]{2,1,0:T(8,128)(2,1)S(1)} %get-tuple-element.12.refs_0_, bf16[68,16,128]{2,1,0:T(8,128)(2,1)S(1)} %collective-permute-done.2.refs_1_, bf16[34,16,128]{2,1,0:T(8,128)(2,1)S(1)} %collective-permute-done.3.refs_2_, ...), custom_call_target="tpu_custom_call" | custom-call | bytes 8388608 | tf_op jit(solution)/shard_map/modes/pallas_call | solution.py:367
  24.1 0.0 collective-permute-done.5.low
  24.1 0.0 collective-permute-done.6.high
  24.1 0.0 copy-start.3
  24.1 0.7 %copy-done.3 = f32[4,8,128]{2,1,0:T(8,128)S(1)} copy-done((f32[4,8,128]{2,1,0:T(8,128)S(1)}, f32[4,8,128]{2,1,0:T(8,128)}, u32[]{:S(2)}) %copy-start.3) | copy-done | bytes 16408
  24.8 4.9 %fields.1 = f32[8,8,2048]{2,1,0:T(8,128)} custom-call(f32[4,192,16,128]{3,2,1,0:T(8,128)S(1)} %get-tuple-element.15.beside, f32[4,64,128]{2,1,0:T(8,128)S(1)} %get-tuple-element.16.own_rows, bf16[13,16,128]{2,1,0:T(8,128)(2,1)S(1)} %collective-permute-done.5.low, bf16[13,16,128]{2,1,0:T(8,128)(2,1)S(1)} %collective-permute-done.6.high, ...), custom_call_target="tpu_custom_call" | custom-call | tf_op jit(solution)/shard_map/fields/pallas_call | solution.py:459
  (1 shorter events, 0.0 us)
Async XLA Ops:
  0.7 1.0 %copy-start = (bf16[8,8,2048]{2,1,0:T(8,128)(2,1)S(1)}, bf16[8,8,2048]{2,1,0:T(8,128)(2,1)}, u32[]{:S(2)}) copy-start(bf16[8,8,2048]{2,1,0:T(8,128)(2,1)} %orbitals.3) | copy-start | bytes 786436
  1.9 1.4 %collective-permute-start = (bf16[4,16,128]{2,1,0:T(8,128)(2,1)S(1)}, bf16[4,16,128]{2,1,0:T(8,128)(2,1)S(1)}, u32[]{:S(2)}, u32[]{:S(2)}) collective-permute-start(bf16[4,16,128]{2,1,0:T(8,128)(2,1)S(1)} %candidates.1.mine), channel_id=1, source_target_pairs={{0,8},{8,0},{16,24},{24,16},{1,9},{9,1},{17,25},{25,17},{2,10},{10... | collective-permute-start | bytes 49160 | tf_op jit(solution)/shard_map/ppermute | solution.py:167
  4.0 4.6 %collective-permute-start.1 = (bf16[4,16,128]{2,1,0:T(8,128)(2,1)S(1)}, bf16[4,16,128]{2,1,0:T(8,128)(2,1)S(1)}, u32[]{:S(2)}, u32[]{:S(2)}) collective-permute-start(bf16[4,16,128]{2,1,0:T(8,128)(2,1)S(1)} %nearer.1.mine), channel_id=1, source_target_pairs={{0,16},{8,24},{16,0},{24,8},{1,17},{9,25},{17,1},{25,9},{2,18},{10... | collective-permute-start | bytes 49160 | tf_op jit(solution)/shard_map/ppermute | solution.py:167
  6.9 0.9 %copy-start.1 = (bf16[8,8,2048]{2,1,0:T(8,128)(2,1)S(1)}, bf16[8,8,2048]{2,1,0:T(8,128)(2,1)}, u32[]{:S(2)}) copy-start(bf16[8,8,2048]{2,1,0:T(8,128)(2,1)} %orbitals.3) | copy-start | bytes 786436
  8.8 11.9 %collective-permute-start.2 = (bf16[68,16,128]{2,1,0:T(8,128)(2,1)S(1)}, bf16[68,16,128]{2,1,0:T(8,128)(2,1)S(1)}, u32[]{:S(2)}, u32[]{:S(2)}) collective-permute-start(bf16[68,16,128]{2,1,0:T(8,128)(2,1)S(1)} %get-tuple-element.12.refs_0_), channel_id=1, source_target_pairs={{0,4},{4,0},{1,5},{5,1},{2,6},{6,2},{3,7},{7,3},{8,12},{12,8},{9,1... | collective-permute-start | bytes 835592 | tf_op jit(solution)/shard_map/ppermute | solution.py:241
  10.9 8.6 %collective-permute-start.3 = (bf16[34,16,128]{2,1,0:T(8,128)(2,1)S(1)}, bf16[34,16,128]{2,1,0:T(8,128)(2,1)S(1)}, u32[]{:S(2)}, u32[]{:S(2)}) collective-permute-start(bf16[34,16,128]{2,1,0:T(8,128)(2,1)S(1)} %get-tuple-element.13), channel_id=1, source_target_pairs={{0,1},{1,2},{2,3},{3,0},{4,5},{5,6},{6,7},{7,4},{8,9},{9,10},{10,1... | collective-permute-start | bytes 417800 | tf_op jit(solution)/shard_map/ppermute | solution.py:258
  12.4 8.2 %collective-permute-start.4 = (bf16[34,16,128]{2,1,0:T(8,128)(2,1)S(1)}, bf16[34,16,128]{2,1,0:T(8,128)(2,1)S(1)}, u32[]{:S(2)}, u32[]{:S(2)}) collective-permute-start(bf16[34,16,128]{2,1,0:T(8,128)(2,1)S(1)} %get-tuple-element.14), channel_id=1, source_target_pairs={{0,3},{1,0},{2,1},{3,2},{4,7},{5,4},{6,5},{7,6},{8,11},{9,8},{10,9... | collective-permute-start | bytes 417800 | tf_op jit(solution)/shard_map/ppermute | solution.py:259
  14.7 9.4 %collective-permute-start.5 = (bf16[13,16,128]{2,1,0:T(8,128)(2,1)S(1)}, bf16[13,16,128]{2,1,0:T(8,128)(2,1)S(1)}, u32[]{:S(2)}, u32[]{:S(2)}) collective-permute-start(bf16[13,16,128]{2,1,0:T(8,128)(2,1)S(1)} %get-tuple-element.17), channel_id=1, source_target_pairs={{0,5},{1,6},{2,7},{3,4},{4,1},{5,2},{6,3},{7,0},{8,13},{9,14},{10,... | collective-permute-start | bytes 159752 | tf_op jit(solution)/shard_map/ppermute | solution.py:239
  14.7 9.4 %collective-permute-start.6 = (bf16[13,16,128]{2,1,0:T(8,128)(2,1)S(1)}, bf16[13,16,128]{2,1,0:T(8,128)(2,1)S(1)}, u32[]{:S(2)}, u32[]{:S(2)}) collective-permute-start(bf16[13,16,128]{2,1,0:T(8,128)(2,1)S(1)} %get-tuple-element.18), channel_id=1, source_target_pairs={{0,7},{1,4},{2,5},{3,6},{4,3},{5,0},{6,1},{7,2},{8,15},{9,12},{10,... | collective-permute-start | bytes 159752 | tf_op jit(solution)/shard_map/ppermute | solution.py:240
  20.6 0.9 %copy-start.2 = (bf16[256,256]{1,0:T(8,128)(2,1)S(1)}, bf16[256,256]{1,0:T(8,128)(2,1)}, u32[]{:S(2)}) copy-start(bf16[256,256]{1,0:T(8,128)(2,1)} %constant.4.clone.refs_4_.modes) | copy-start | bytes 393220
  24.1 0.7 %copy-start.3 = (f32[4,8,128]{2,1,0:T(8,128)S(1)}, f32[4,8,128]{2,1,0:T(8,128)}, u32[]{:S(2)}) copy-start(f32[4,8,128]{2,1,0:T(8,128)} %constant.5.clone.tails) | copy-start | bytes 49156

commit v8 on v6

--- a/solution.py
+++ b/solution.py
@@ -98,13 +98,15 @@
             packed = jnp.where(turn == step, pltpu.roll(found[step][row], step * NZ, 1), packed)
         rows.append(packed)
     for tile in range(EDGE // 2):
-        out[tile] = jnp.concatenate(rows[2 * tile : 2 * tile + 2], axis=0).astype(jnp.bfloat16)
-
-
-def candidates(slots, orbitals):
+        pair = jnp.concatenate(rows[2 * tile : 2 * tile + 2], axis=0).astype(jnp.bfloat16)
+        for target in range(out.shape[0]):
+            out[target, tile] = pair
+
+
+def candidates(slots, orbitals, count):
     return pl.pallas_call(
         candidates_kernel,
-        out_shape=jax.ShapeDtypeStruct((EDGE * EDGE // ROWS, ROWS, LANES), jnp.bfloat16),
+        out_shape=jax.ShapeDtypeStruct((count, EDGE * EDGE // ROWS, ROWS, LANES), jnp.bfloat16),
         in_specs=[VMEM] * 2,
         out_specs=VMEM,
         compiler_params=SMALL,
@@ -136,51 +138,19 @@
     )(orbitals)
 
 
-def chosen(owners, mine, others, bit):
-    owner, me = by_seat(owners), lax.axis_index("orb")
-    count = lax.axis_size("orb")
+def chosen(owners, offered):
+    owner = by_seat(owners)
     picked = []
-    for tile in range(mine.shape[0]):
-        value = mine[tile].astype(jnp.float32)
-        for step, other in enumerate(others, 1):
-            if bit is None:
-                here = owner == lax.rem(me + count - step, count)
-            else:
-                here = (owner >> bit & 1) != (me >> bit & 1)
-            value = jnp.where(here, other[tile].astype(jnp.float32), value)
+    for tile in range(offered.shape[1]):
+        value = offered[0, tile].astype(jnp.float32)
+        for holder in range(1, offered.shape[0]):
+            value = jnp.where(owner == holder, offered[holder, tile].astype(jnp.float32), value)
         picked.append(value)
     return picked
 
 
-def nearer_kernel(bit, owners, mine, other, out):
-    for tile, value in enumerate(chosen(owners, mine, [other], bit)):
-        out[tile] = value.astype(jnp.bfloat16)
-
-
-def gathered(owners, mine):
-    count = lax.axis_size("orb")
-    if count & (count - 1):
-        others = [lax.ppermute(mine, "orb", ring("orb", step)) for step in range(1, count)]
-        return mine, others, None
-    bits = count.bit_length() - 1
-    for bit in range(bits):
-        other = lax.ppermute(mine, "orb", [(i, i ^ 1 << bit) for i in range(count)])
-        if bit == bits - 1:
-            return mine, [other], bit
-        mine = pl.pallas_call(
-            functools.partial(nearer_kernel, bit),
-            out_shape=jax.ShapeDtypeStruct(mine.shape, mine.dtype),
-            in_specs=[VMEM] * 3,
-            out_specs=VMEM,
-            compiler_params=SMALL,
-            name="nearer",
-        )(owners, mine, other)
-    return mine, [], None
-
-
-def messages_kernel(bit, owners, cells, mine, *refs):
-    others, (block, last, first, corner_low, corner_high) = refs[:-5], refs[-5:]
-    picked = chosen(owners, mine, others, bit)
+def messages_kernel(owners, cells, offered, block, last, first, corner_low, corner_high):
+    picked = chosen(owners, offered)
 
     def pack(ref, spots):
         for at, (x, y) in enumerate(spots):
@@ -214,19 +184,20 @@
 
 
 def messages(orbitals, src_owner, src_slot):
-    owners = spread_out(src_owner)
-    mine, others, bit = gathered(owners, candidates(spread_out(src_slot), orbitals))
+    count = lax.axis_size("orb")
+    mine = candidates(spread_out(src_slot), orbitals, count)
+    offered = lax.all_to_all(mine, "orb", 0, 0, tiled=True)
     lengths = [EDGE * EDGE] + [EDGE * HALO] * 2 + [len(CORNER_LOW)] * 2
     return pl.pallas_call(
-        functools.partial(messages_kernel, bit),
+        messages_kernel,
         out_shape=[
             jax.ShapeDtypeStruct((tiles(length), ROWS, LANES), jnp.bfloat16) for length in lengths
         ],
-        in_specs=[VMEM] * (3 + len(others)),
+        in_specs=[VMEM] * 3,
         out_specs=[VMEM] * 5,
         compiler_params=SMALL,
         name="messages",
-    )(owners, cells_of(orbitals), mine, *others)
+    )(spread_out(src_owner), cells_of(orbitals), offered)
 
 
 def exchange(block, last, first, corner_low, corner_high):

time: 27.7 us -> 31.4 us (1.13)
  waiting for transfers between devices: 4.86 us -> 7.06 us
  starting transfers between devices: 14.1 us -> 14.8 us
  Pallas kernels: 6.8 us -> 7.42 us
    all_to_all x0 -> x1, starting transfers between devices: none -> 4.21 us  [messages(): offered = lax.all_to_all(mine, 'orb', 0, 0, tiled=True)]
    all_to_all x0 -> x1, waiting for transfers between devices: none -> 4.06 us  [messages(): offered = lax.all_to_all(mine, 'orb', 0, 0, tiled=True)]
    ppermute x2 -> x0, starting transfers between devices: 3.41 us -> none  [gathered(): other = lax.ppermute(mine, 'orb', [(i, i ^ 1 << bit) for i in range(count)])]
    ppermute x2 -> x0, waiting for transfers between devices: 2.48 us -> none  [gathered(): other = lax.ppermute(mine, 'orb', [(i, i ^ 1 << bit) for i in range(count)])]
    ppermute x1, waiting for transfers between devices: 2.36 us -> 2.99 us  [exchange(): low = lax.ppermute(corner_low, both, diagonal(1, 1))]
    pallas_call x3 -> x2, Pallas kernels: 0.32 us -> 0.94 us  [the longest x1 0.85 us: candidates(): pl.pallas_call(candidates_kernel, out_shape=jax.ShapeDtypeStruct((count,...]
  transfers between devices with their start and end apart: 7 -> 6, of which waited for: 3 -> 2; matrix products, arithmetic and copies ran while one was open for 0% -> 0% of each run, Pallas kernels for 0% -> 0%
where the time goes in v8:
time: 31.4 us; the launch traced here: 31.1 us
  starting transfers between devices  14.8 us (47%)
  Pallas kernels  7.42 us (24%)
  waiting for transfers between devices  7.06 us (22%)
  local copies, waits for them, and re-layouts  1.78 us (6%)
    pallas_call x1, Pallas kernels, fields(): pl.pallas_call(functools.partial(kernel, count), out_shape=jax.ShapeDtype...  6.42 us
    ppermute x1, starting transfers between devices, exchange(): high = lax.ppermute(corner_high, both, diagonal(1, -1))  4.72 us
    all_to_all x1, starting transfers between devices, messages(): offered = lax.all_to_all(mine, 'orb', 0, 0, tiled=True)  4.21 us
    all_to_all x1, waiting for transfers between devices, messages(): offered = lax.all_to_all(mine, 'orb', 0, 0, tiled=True)  4.06 us
    ppermute x1, waiting for transfers between devices, exchange(): low = lax.ppermute(corner_low, both, diagonal(1, 1))  2.99 us
    ppermute x1, starting transfers between devices, exchange(): above = lax.ppermute(first, 'sy', ring('sy', -1))  2.25 us
    ppermute x1, starting transfers between devices, exchange(): across = lax.ppermute(block, 'sx', ring('sx', 1))  2.08 us
    ppermute x1, starting transfers between devices, exchange(): below = lax.ppermute(last, 'sy', ring('sy', 1))  1.58 us
  transfers between devices with their start and end apart: 6, of which 2 were waited for; matrix products, arithmetic and copies ran while one was open for 0% of the time, Pallas kernels for 0%

profile of v8, /device:TPU:0, one launch (start us, length us, event | category | flops | bytes accessed | tf_op | source)
XLA Modules:
  0.0 31.1 jit_solution(1852644080977943241)
XLA Ops:
  0.0 0.7 %broadcast_in_dim.7.slots = s32[2,2,16,128]{3,2,1,0:T(8,128)S(1)} broadcast(s32[2,2]{1,0:T(2,128)} %param.7), dimensions={0,1} | broadcast | bytes 32784 | tf_op jit(solution)/shard_map/broadcast_in_dim | solution.py:69
  0.7 0.0 copy-start
  0.8 0.9 %copy-done = bf16[8,8,2048]{2,1,0:T(8,128)(2,1)S(1)} copy-done((bf16[8,8,2048]{2,1,0:T(8,128)(2,1)S(1)}, bf16[8,8,2048]{2,1,0:T(8,128)(2,1)}, u32[]{:S(2)}) %copy-start) | copy-done | bytes 262168
  1.7 0.0 copy-start.1
  1.7 0.9 %candidates.1 = bf16[4,4,16,128]{3,2,1,0:T(8,128)(2,1)} custom-call(s32[2,2,16,128]{3,2,1,0:T(8,128)S(1)} %broadcast_in_dim.7.slots, bf16[8,8,2048]{2,1,0:T(8,128)(2,1)S(1)} %copy-done), custom_call_target="tpu_custom_call" | custom-call | tf_op jit(solution)/shard_map/candidates/pallas_call | solution.py:107
  2.6 4.2 %all-to-all-start = ((bf16[4,4,16,128]{3,2,1,0:T(8,128)(2,1)}), bf16[4,4,16,128]{3,2,1,0:T(8,128)(2,1)S(1)}, u32[]{:S(2)}, u32[]{:S(2)}) async-start(bf16[4,4,16,128]{3,2,1,0:T(8,128)(2,1)} %candidates.1), calls=%async_computation | async-start | bytes 131072 | tf_op jit(solution)/shard_map/all_to_all | solution.py:189
  6.8 0.0 copy-done.1
  6.8 0.0 copy-start.4
  6.8 0.1 cells.1
  6.8 4.1 %all-to-all-done.offered = bf16[4,4,16,128]{3,2,1,0:T(8,128)(2,1)S(1)} async-done(((bf16[4,4,16,128]{3,2,1,0:T(8,128)(2,1)}), bf16[4,4,16,128]{3,2,1,0:T(8,128)(2,1)S(1)}, u32[]{:S(2)}, u32[]{:S(2)}) %all-to-all-start) | async-done | bytes 65568 | tf_op jit(solution)/shard_map/all_to_all | solution.py:189
  10.9 0.0 copy-done.4
  10.9 0.1 broadcast_in_dim.6.owners
  11.0 0.0 copy-start.2
  11.0 0.0 copy-start.3
  11.0 0.1 messages.1
  11.1 2.1 %collective-permute-start = (bf16[68,16,128]{2,1,0:T(8,128)(2,1)S(1)}, bf16[68,16,128]{2,1,0:T(8,128)(2,1)S(1)}, u32[]{:S(2)}, u32[]{:S(2)}) collective-permute-start(bf16[68,16,128]{2,1,0:T(8,128)(2,1)S(1)} %get-tuple-element.10.refs_0_), channel_id=1, source_target_pairs={{0,4},{4,0},{1,5},{5,1},{2,6},{6,2},{3,7},{7,3},{8,12},{12,8},{9,1... | collective-permute-start | bytes 835592 | tf_op jit(solution)/shard_map/ppermute | solution.py:208
  13.1 1.6 %collective-permute-start.1 = (bf16[34,16,128]{2,1,0:T(8,128)(2,1)S(1)}, bf16[34,16,128]{2,1,0:T(8,128)(2,1)S(1)}, u32[]{:S(2)}, u32[]{:S(2)}) collective-permute-start(bf16[34,16,128]{2,1,0:T(8,128)(2,1)S(1)} %get-tuple-element.11), channel_id=1, source_target_pairs={{0,1},{1,2},{2,3},{3,0},{4,5},{5,6},{6,7},{7,4},{8,9},{9,10},{10,1... | collective-permute-start | bytes 417800 | tf_op jit(solution)/shard_map/ppermute | solution.py:225
  14.7 2.2 %collective-permute-start.2 = (bf16[34,16,128]{2,1,0:T(8,128)(2,1)S(1)}, bf16[34,16,128]{2,1,0:T(8,128)(2,1)S(1)}, u32[]{:S(2)}, u32[]{:S(2)}) collective-permute-start(bf16[34,16,128]{2,1,0:T(8,128)(2,1)S(1)} %get-tuple-element.12), channel_id=1, source_target_pairs={{0,3},{1,0},{2,1},{3,2},{4,7},{5,4},{6,5},{7,6},{8,11},{9,8},{10,9... | collective-permute-start | bytes 417800 | tf_op jit(solution)/shard_map/ppermute | solution.py:226
  17.0 0.0 collective-permute-start.3
  17.0 4.7 %collective-permute-start.4 = (bf16[13,16,128]{2,1,0:T(8,128)(2,1)S(1)}, bf16[13,16,128]{2,1,0:T(8,128)(2,1)S(1)}, u32[]{:S(2)}, u32[]{:S(2)}) collective-permute-start(bf16[13,16,128]{2,1,0:T(8,128)(2,1)S(1)} %get-tuple-element.14), channel_id=1, source_target_pairs={{0,7},{1,4},{2,5},{3,6},{4,3},{5,0},{6,1},{7,2},{8,15},{9,12},{10,... | collective-permute-start | bytes 159752 | tf_op jit(solution)/shard_map/ppermute | solution.py:207
  21.7 3.0 %collective-permute-done.3.refs_4_ = bf16[13,16,128]{2,1,0:T(8,128)(2,1)S(1)} collective-permute-done((bf16[13,16,128]{2,1,0:T(8,128)(2,1)S(1)}, bf16[13,16,128]{2,1,0:T(8,128)(2,1)S(1)}, u32[]{:S(2)}, u32[]{:S(2)}) %collective-permute-start.3) | collective-permute-done | bytes 53280 | tf_op jit(solution)/shard_map/ppermute | solution.py:206
  24.7 0.0 collective-permute-done.4.refs_5_
  24.7 0.0 collective-permute-done.1.refs_2_
  24.7 0.0 collective-permute-done.2.refs_3_
  24.7 0.0 collective-permute-done.refs_1_
  24.7 0.0 copy-done.2
  24.7 0.0 copy-done.3
  24.7 6.4 %fields.1 = f32[8,8,2048]{2,1,0:T(8,128)} custom-call(bf16[68,16,128]{2,1,0:T(8,128)(2,1)S(1)} %get-tuple-element.10.refs_0_, bf16[68,16,128]{2,1,0:T(8,128)(2,1)S(1)} %collective-permute-done.refs_1_, bf16[34,16,128]{2,1,0:T(8,128)(2,1)S(1)} %collective-permute-done.1.refs_2_, bf16[34,16,128]{2,1,0:T(8,128)(2,1)S(1)} %collective-permute-done.2.refs_3_, ...), custom_call_target="tpu_custom_call" | custom-call | tf_op jit(solution)/shard_map/fields/pallas_call | solution.py:375
Async XLA Ops:
  0.7 1.0 %copy-start = (bf16[8,8,2048]{2,1,0:T(8,128)(2,1)S(1)}, bf16[8,8,2048]{2,1,0:T(8,128)(2,1)}, u32[]{:S(2)}) copy-start(bf16[8,8,2048]{2,1,0:T(8,128)(2,1)} %orbitals.3) | copy-start | bytes 786436
  1.7 5.1 %copy-start.1 = (bf16[8,8,2048]{2,1,0:T(8,128)(2,1)S(1)}, bf16[8,8,2048]{2,1,0:T(8,128)(2,1)}, u32[]{:S(2)}) copy-start(bf16[8,8,2048]{2,1,0:T(8,128)(2,1)} %orbitals.3) | copy-start | bytes 786436
  2.6 8.3 %all-to-all-start = ((bf16[4,4,16,128]{3,2,1,0:T(8,128)(2,1)}), bf16[4,4,16,128]{3,2,1,0:T(8,128)(2,1)S(1)}, u32[]{:S(2)}, u32[]{:S(2)}) async-start(bf16[4,4,16,128]{3,2,1,0:T(8,128)(2,1)} %candidates.1), calls=%async_computation | async-start | bytes 131072 | tf_op jit(solution)/shard_map/all_to_all | solution.py:189
  6.8 4.1 %copy-start.4 = (s32[2,2]{1,0:T(2,128)S(1)}, s32[2,2]{1,0:T(2,128)}, u32[]{:S(2)}) copy-start(s32[2,2]{1,0:T(2,128)} %param.6) | copy-start | bytes 52
  11.0 13.7 %copy-start.2 = (bf16[256,256]{1,0:T(8,128)(2,1)S(1)}, bf16[256,256]{1,0:T(8,128)(2,1)}, u32[]{:S(2)}) copy-start(bf16[256,256]{1,0:T(8,128)(2,1)} %constant.4.clone.refs_6_) | copy-start | bytes 393220
  11.0 13.8 %copy-start.3 = (f32[4,8,128]{2,1,0:T(8,128)S(1)}, f32[4,8,128]{2,1,0:T(8,128)}, u32[]{:S(2)}) copy-start(f32[4,8,128]{2,1,0:T(8,128)} %constant.5.clone.refs_7_) | copy-start | bytes 49156
  11.1 13.6 %collective-permute-start = (bf16[68,16,128]{2,1,0:T(8,128)(2,1)S(1)}, bf16[68,16,128]{2,1,0:T(8,128)(2,1)S(1)}, u32[]{:S(2)}, u32[]{:S(2)}) collective-permute-start(bf16[68,16,128]{2,1,0:T(8,128)(2,1)S(1)} %get-tuple-element.10.refs_0_), channel_id=1, source_target_pairs={{0,4},{4,0},{1,5},{5,1},{2,6},{6,2},{3,7},{7,3},{8,12},{12,8},{9,1... | collective-permute-start | bytes 835592 | tf_op jit(solution)/shard_map/ppermute | solution.py:208
  13.1 11.5 %collective-permute-start.1 = (bf16[34,16,128]{2,1,0:T(8,128)(2,1)S(1)}, bf16[34,16,128]{2,1,0:T(8,128)(2,1)S(1)}, u32[]{:S(2)}, u32[]{:S(2)}) collective-permute-start(bf16[34,16,128]{2,1,0:T(8,128)(2,1)S(1)} %get-tuple-element.11), channel_id=1, source_target_pairs={{0,1},{1,2},{2,3},{3,0},{4,5},{5,6},{6,7},{7,4},{8,9},{9,10},{10,1... | collective-permute-start | bytes 417800 | tf_op jit(solution)/shard_map/ppermute | solution.py:225
  14.7 10.0 %collective-permute-start.2 = (bf16[34,16,128]{2,1,0:T(8,128)(2,1)S(1)}, bf16[34,16,128]{2,1,0:T(8,128)(2,1)S(1)}, u32[]{:S(2)}, u32[]{:S(2)}) collective-permute-start(bf16[34,16,128]{2,1,0:T(8,128)(2,1)S(1)} %get-tuple-element.12), channel_id=1, source_target_pairs={{0,3},{1,0},{2,1},{3,2},{4,7},{5,4},{6,5},{7,6},{8,11},{9,8},{10,9... | collective-permute-start | bytes 417800 | tf_op jit(solution)/shard_map/ppermute | solution.py:226
  17.0 7.7 %collective-permute-start.3 = (bf16[13,16,128]{2,1,0:T(8,128)(2,1)S(1)}, bf16[13,16,128]{2,1,0:T(8,128)(2,1)S(1)}, u32[]{:S(2)}, u32[]{:S(2)}) collective-permute-start(bf16[13,16,128]{2,1,0:T(8,128)(2,1)S(1)} %get-tuple-element.13), channel_id=1, source_target_pairs={{0,5},{1,6},{2,7},{3,4},{4,1},{5,2},{6,3},{7,0},{8,13},{9,14},{10,... | collective-permute-start | bytes 159752 | tf_op jit(solution)/shard_map/ppermute | solution.py:206
  17.0 7.7 %collective-permute-start.4 = (bf16[13,16,128]{2,1,0:T(8,128)(2,1)S(1)}, bf16[13,16,128]{2,1,0:T(8,128)(2,1)S(1)}, u32[]{:S(2)}, u32[]{:S(2)}) collective-permute-start(bf16[13,16,128]{2,1,0:T(8,128)(2,1)S(1)} %get-tuple-element.14), channel_id=1, source_target_pairs={{0,7},{1,4},{2,5},{3,6},{4,3},{5,0},{6,1},{7,2},{8,15},{9,12},{10,... | collective-permute-start | bytes 159752 | tf_op jit(solution)/shard_map/ppermute | solution.py:207

commit v9 on v7

--- a/solution.py
+++ b/solution.py
@@ -1,9 +1,8 @@
 import functools
+import math
 
 import jax
 import jax.numpy as jnp
-import ml_dtypes
-import numpy as np
 from jax import lax
 from jax.experimental import pallas as pl
 from jax.experimental.pallas import tpu as pltpu
@@ -66,7 +65,9 @@
 
 
 def spread_out(values):
-    return lax.broadcast_in_dim(values, values.shape + (ROWS, LANES), (0, 1))
+    return lax.broadcast_in_dim(
+        values, values.shape + (ROWS, LANES), tuple(range(values.ndim))
+    )
 
 
 def by_seat(entries):
@@ -78,9 +79,9 @@
     return value
 
 
-def candidates_kernel(slots, orbitals, out):
+def prepare_kernel(entries, orbitals, out, cells, scratch):
     per_tile = LANES // NZ
-    slot = by_seat(slots)[:EDGE]
+    slot = by_seat(entries[0])[:EDGE]
     lane = lax.broadcasted_iota(jnp.int32, (EDGE, LANES), 1)
     group, turn = slot // per_tile, (lane // NZ - slot % per_tile + per_tile) % per_tile
     asked = [pltpu.roll(group, LANES - step * NZ, 1) if step else group for step in range(per_tile)]
@@ -99,20 +100,6 @@
         rows.append(packed)
     for tile in range(EDGE // 2):
         out[tile] = jnp.concatenate(rows[2 * tile : 2 * tile + 2], axis=0).astype(jnp.bfloat16)
-
-
-def candidates(slots, orbitals):
-    return pl.pallas_call(
-        candidates_kernel,
-        out_shape=jax.ShapeDtypeStruct((EDGE * EDGE // ROWS, ROWS, LANES), jnp.bfloat16),
-        in_specs=[VMEM] * 2,
-        out_specs=VMEM,
-        compiler_params=SMALL,
-        name="candidates",
-    )(slots, orbitals)
-
-
-def cells_kernel(orbitals, out, scratch):
     for row in range(EDGE):
         for group in range(ROWS):
             tile = orbitals[row, :, pl.ds(group * LANES, LANES)].astype(jnp.float32)
@@ -120,24 +107,24 @@
     for row in range(EDGE):
         for y in range(EDGE):
             tile = scratch[row, pl.ds(y * (ROWS + 1), ROWS), :]
-            out[row * EDGE + y] = tile.astype(jnp.bfloat16)
-
-
-def cells_of(orbitals):
+            cells[row * EDGE + y] = tile.astype(jnp.bfloat16)
+
+
+def prepare(entries, orbitals):
+    lengths = (EDGE * EDGE // ROWS, EDGE * EDGE)
     return pl.pallas_call(
-        cells_kernel,
-        out_shape=jax.ShapeDtypeStruct((EDGE * EDGE, ROWS, LANES), jnp.bfloat16),
-        in_specs=[VMEM],
-        out_specs=VMEM,
+        prepare_kernel,
+        out_shape=[jax.ShapeDtypeStruct((length, ROWS, LANES), jnp.bfloat16) for length in lengths],
+        in_specs=[VMEM] * 2,
+        out_specs=[VMEM] * 2,
         scratch_shapes=[pltpu.VMEM((EDGE, EDGE * (ROWS + 1), LANES), jnp.float32)],
         compiler_params=SMALL,
-        cost_estimate=pl.CostEstimate(flops=0, bytes_accessed=4 * 2**20, transcendentals=0),
-        name="cells",
-    )(orbitals)
-
-
-def chosen(owners, mine, others, bit):
-    owner, me = by_seat(owners), lax.axis_index("orb")
+        name="prepare",
+    )(entries, orbitals)
+
+
+def chosen(entries, mine, others, bit):
+    owner, me = by_seat(entries[1]), lax.axis_index("orb")
     count = lax.axis_size("orb")
     picked = []
     for tile in range(mine.shape[0]):
@@ -152,12 +139,12 @@
     return picked
 
 
-def nearer_kernel(bit, owners, mine, other, out):
-    for tile, value in enumerate(chosen(owners, mine, [other], bit)):
+def nearer_kernel(bit, entries, mine, other, out):
+    for tile, value in enumerate(chosen(entries, mine, [other], bit)):
         out[tile] = value.astype(jnp.bfloat16)
 
 
-def gathered(owners, mine):
+def gathered(entries, mine):
     count = lax.axis_size("orb")
     if count & (count - 1):
         others = [lax.ppermute(mine, "orb", ring("orb", step)) for step in range(1, count)]
@@ -174,13 +161,13 @@
             out_specs=VMEM,
             compiler_params=SMALL,
             name="nearer",
-        )(owners, mine, other)
+        )(entries, mine, other)
     return mine, [], None
 
 
-def messages_kernel(bit, owners, cells, mine, *refs):
+def messages_kernel(bit, entries, cells, mine, *refs):
     others, (block, last, first, corner_low, corner_high) = refs[:-5], refs[-5:]
-    picked = chosen(owners, mine, others, bit)
+    picked = chosen(entries, mine, others, bit)
 
     def pack(ref, spots):
         for at, (x, y) in enumerate(spots):
@@ -218,8 +205,9 @@
 
 
 def messages(orbitals, src_owner, src_slot):
-    owners = spread_out(src_owner)
-    mine, others, bit = gathered(owners, candidates(spread_out(src_slot), orbitals))
+    entries = spread_out(jnp.stack([src_slot, src_owner]))
+    mine, cells = prepare(entries, orbitals)
+    mine, others, bit = gathered(entries, mine)
     lengths = [EDGE * EDGE] + [EDGE * HALO] * 2 + [len(CORNER_LOW)] * 2
     return pl.pallas_call(
         functools.partial(messages_kernel, bit),
@@ -230,7 +218,7 @@
         out_specs=[VMEM] * 5,
         compiler_params=SMALL,
         name="messages",
-    )(owners, cells_of(orbitals), mine, *others)
+    )(entries, cells, mine, *others)
 
 
 def exchange(block, last, first, corner_low, corner_high):
@@ -276,24 +264,32 @@
     return out_x + out_y
 
 
-def z_modes():
-    index = np.arange(1, NZ + 1)
-    modes = np.sqrt(2.0 / (NZ + 1)) * np.sin(np.pi * np.outer(index, index) / (NZ + 1))
-    modes = np.kron(np.eye(LANES // NZ), modes)
-    high = modes.astype(ml_dtypes.bfloat16)
-    low = (modes - high.astype(np.float64)).astype(ml_dtypes.bfloat16)
-    both = np.concatenate([high, low], axis=1)
-    value = np.tile(2.0 * np.cos(np.pi * index / (NZ + 1)), LANES // NZ)
+def z_modes(out):
+    shape = (LANES, LANES)
+    row, col = (lax.broadcasted_iota(jnp.int32, shape, axis) for axis in range(2))
+    product = ((row % NZ + 1) * (col % NZ + 1)).astype(jnp.float32)
+    period = 2.0 * (NZ + 1)
+    turn = product - period * jnp.floor((product + 0.5) / period)
+    value = math.sqrt(2.0 / (NZ + 1)) * jnp.sin(turn * (math.pi / (NZ + 1)))
+    value = jnp.where(row // NZ == col // NZ, value, 0.0)
+    high = value.astype(jnp.bfloat16)
+    low = (value - high.astype(jnp.float32)).astype(jnp.bfloat16)
+    for first in (0, LANES):
+        out[pl.ds(first, LANES), pl.ds(0, LANES)] = high
+        out[pl.ds(first, LANES), pl.ds(LANES, LANES)] = low
+
+
+def z_tails():
+    lane = lax.broadcasted_iota(jnp.int32, (SUB, LANES), 1) % NZ
+    value = 2.0 * jnp.cos((lane + 1).astype(jnp.float32) * (math.pi / (NZ + 1)))
     p0, p1, p2, p3, p4 = power_coeffs()
     a3, a2, a1, a0 = p3 / p4, p2 / p4, p1 / p4, p0 / p4
-    tail = [
+    return (
         4.0 * value + a3,
-        6.0 * value**2 + 3.0 * a3 * value + a2,
-        4.0 * value**3 + 3.0 * a3 * value**2 + 2.0 * a2 * value + a1,
-        value**4 + a3 * value**3 + a2 * value**2 + a1 * value + a0,
-    ]
-    tail = np.repeat(np.stack(tail)[:, None, :], SUB, axis=1).astype(np.float32)
-    return np.concatenate([both, both], axis=0), tail
+        (6.0 * value + 3.0 * a3) * value + a2,
+        ((4.0 * value + 3.0 * a3) * value + 2.0 * a2) * value + a1,
+        (((value + a3) * value + a2) * value + a1) * value + a0,
+    )
 
 
 SIZE = 2 * HALO + EDGE
@@ -334,10 +330,14 @@
 
 
 def densities(refs, rows, firsts, place, parts, modes, put):
-    cells = [(ref, at, first + at) for ref, first in zip(refs, firsts) for at in range(spots_of(ref.shape[0]))]
-    chunk = 48
-    for start in range(0, len(cells), chunk):
-        end = min(start + chunk, len(cells))
+    cells = [
+        (ref, at, first + at)
+        for ref, first in zip(refs, firsts)
+        for at in range(spots_of(ref.shape[0]))
+    ]
+    pieces = -(-len(cells) // 48)
+    for piece in range(pieces):
+        start, end = (len(cells) * at // pieces for at in (piece, piece + 1))
         for number in range(start, end):
             ref, at, row = cells[number]
             other = jnp.broadcast_to(rows[place, pl.ds(row, 1), :], (ROWS, LANES))
@@ -345,70 +345,89 @@
         put(start, end, turned(parts, start, end, modes))
 
 
-def modes_kernel(count, *refs):
-    halo, modes, (hat, own_rows, rows, parts) = refs[:4], refs[4], refs[5:]
+def all_rows(refs, rows):
     firsts = [0]
-    for ref in halo:
+    for ref in refs:
         firsts.append(source_rows(ref, rows, firsts[-1]))
+    return firsts
+
+
+def modes_kernel(own, across, hat, own_rows, modes, rows, parts):
+    z_modes(modes)
+    firsts = all_rows((own, across), rows)
     own_rows[...] = rows[:, : own_rows.shape[1], :]
 
     def one_source(place, carry):
         def put(start, end, value):
             hat[place, start:end] = value
 
-        densities(halo, rows, firsts, place, parts, modes, put)
+        densities((own, across), rows, firsts, place, parts, modes, put)
         return carry
 
-    lax.fori_loop(0, count, one_source, 0)
-
-
-def modes_of(halo, modes, count):
-    cells = sum(spots_of(array.shape[0]) for array in halo)
+    lax.fori_loop(0, hat.shape[0], one_source, 0)
+
+
+def modes_of(own, across, count):
+    cells = 2 * len(CORE)
     return pl.pallas_call(
-        functools.partial(modes_kernel, count),
+        modes_kernel,
         out_shape=[
             jax.ShapeDtypeStruct((count, cells, ROWS, LANES), jnp.float32),
             jax.ShapeDtypeStruct((count, len(CORE), LANES), jnp.float32),
+            jax.ShapeDtypeStruct((2 * LANES, 2 * LANES), jnp.bfloat16),
         ],
-        in_specs=[VMEM] * 5,
-        out_specs=[VMEM] * 2,
+        in_specs=[VMEM] * 2,
+        out_specs=[VMEM] * 3,
         scratch_shapes=[
             pltpu.VMEM((count, cells, LANES), jnp.float32),
             pltpu.VMEM((cells, ROWS, 2 * LANES), jnp.bfloat16),
         ],
         compiler_params=pltpu.CompilerParams(vmem_limit_bytes=20 * 2**20),
-        cost_estimate=pl.CostEstimate(flops=0, bytes_accessed=8 * 2**20, transcendentals=0),
+        cost_estimate=pl.CostEstimate(flops=0, bytes_accessed=6 * 2**20, transcendentals=0),
         name="modes",
-    )(*halo, modes)
-
-
-def fields_kernel(count, beside, own_rows, low, high, modes, tails, *refs):
-    out, rows, parts, corners, work_a, work_b, last, acc = refs
+    )(own, across)
+
+
+def in_turn(*works):
+    works = [list(work) for work in works]
+    done = [0] * len(works)
+    for _ in range(sum(map(len, works))):
+        at = min(
+            (at for at in range(len(works)) if done[at] < len(works[at])),
+            key=lambda at: (done[at] + 0.5) / len(works[at]),
+        )
+        works[at][done[at]]()
+        done[at] += 1
+
+
+def fields_kernel(beside, own_rows, below, above, low, high, modes, *refs):
+    out, rows, parts, back, hat, work_a, work_b, last_a, last_b, acc = refs
+    count = beside.shape[0]
     pitch = ROWS + 1
-    offset = (0, EDGE * EDGE, 2 * EDGE * EDGE, 2 * EDGE * EDGE + EDGE * HALO)
-
-    firsts = [0, source_rows(low, rows, 0)]
-    source_rows(high, rows, firsts[1])
-    for place in range(count):
-
-        def put(start, end, value, place=place):
-            corners[place, start:end] = value
-
-        densities((low, high), rows, firsts, place, parts, modes, put)
-
-    def spread(place, at):
-        return jnp.broadcast_to(own_rows[place, pl.ds(at, 1), :], (ROWS, LANES))
-
-    def one_half(place, half):
-        rows = pl.ds(half * SUB, SUB)
+    tails = z_tails()
+    later = (below, above, low, high)
+    firsts = all_rows(later, rows)
+    offset = [0]
+    for ref in later:
+        offset.append(offset[-1] + spots_of(ref.shape[0]))
+
+    def one_density(place, carry):
+        def put(start, end, value):
+            hat[place, start:end] = value
+
+        densities(later, rows, firsts, place, parts, modes, put)
+        return carry
+
+    def steps(place, half, last):
+        part = pl.ds(half * SUB, SUB)
 
         def start(x, y):
             which, at = place_of(x, y)
-            if which < 4:
-                return beside[place, offset[which] + at, rows, :]
-            return corners[place, (which - 4) * len(CORNER_LOW) + at, rows, :]
-
-        for step in range(DEGREE):
+            if which < 2:
+                return beside[place, which * len(CORE) + at, part, :]
+            return hat[place, offset[which - 2] + at, part, :]
+
+        def one_row(step, x, state):
             new = (work_a, work_b, work_a, None)[step]
             old = (None, work_a, work_b, work_a)[step]
             targets, known = within(HALO - 1 - step), within(HALO - step)
@@ -416,35 +435,70 @@
             def load(x):
                 return {y: start(x, y) if old is None else old[x, y] for y in known[x]}
 
-            here, pair_prev = load(0), {}
-            for x in range(SIZE - 1):
-                ahead = load(x + 1)
-                pair = {}
-                for y in range(SIZE - 1):
-                    if y in targets[x] or y + 1 in targets[x + 1]:
-                        pair[y] = ahead[y] + here[y + 1]
-                    if y in targets[x]:
-                        density = here[y] if old is None else start(x, y)
-                        value = pair[y] + pair_prev[y - 1] + tails[step] * density
-                        if new is not None:
-                            new[x, y] = value
-                        else:
-                            last[CORE.index((x, y)), rows, :] = value
-                here, pair_prev = ahead, pair
-
-    def one_source(place, carry):
-        for half in range(ROWS // SUB):
-            one_half(place, half)
-        for at in range(len(CORE)):
-            keep(parts, at, last[at])
-        back = turned(parts, 0, len(CORE), modes)
-        for at, (x, y) in enumerate(CORE):
-            rows = pl.ds((y - HALO) * pitch, ROWS)
-            acc[x - HALO, rows, :] = acc[x - HALO, rows, :] + back[at] * spread(place, at)
+            here, pair_prev = state.get(step) or (load(x), {})
+            ahead, pair = load(x + 1), {}
+            for y in range(SIZE - 1):
+                if y in targets[x] or y + 1 in targets[x + 1]:
+                    pair[y] = ahead[y] + here[y + 1]
+                if y in targets[x]:
+                    density = here[y] if old is None else start(x, y)
+                    value = pair[y] + pair_prev[y - 1] + tails[step] * density
+                    if new is not None:
+                        new[x, y] = value
+                    else:
+                        last[CORE.index((x, y)), part, :] = value
+            state[step] = (ahead, pair)
+
+        state = {}
+        return [
+            functools.partial(one_row, step, x, state)
+            for step in range(DEGREE)
+            for x in range(step, SIZE - 1 - step)
+        ]
+
+    def way_back(place, last):
+        pieces = 2
+        size = len(CORE) // pieces
+
+        def split(at):
+            keep(back, at, last[at])
+
+        def turn(piece, held):
+            held[piece] = turned(back, piece * size, (piece + 1) * size, modes)
+
+        def add(at, held):
+            x, y = CORE[at]
+            lanes = pl.ds((y - HALO) * pitch, ROWS)
+            other = jnp.broadcast_to(own_rows[place, pl.ds(at, 1), :], (ROWS, LANES))
+            value = held[at // size][at % size] * other
+            acc[x - HALO, lanes, :] = acc[x - HALO, lanes, :] + value
+
+        held = {}
+        work = []
+        for piece in range(pieces):
+            cells = range(piece * size, (piece + 1) * size)
+            work += [functools.partial(split, at) for at in cells]
+            work.append(functools.partial(turn, piece, held))
+            work += [functools.partial(add, at, held) for at in cells]
+        return work
+
+    def two_sources(pair, carry):
+        first, second = 2 * pair, 2 * pair + 1
+        in_turn(
+            steps(first, 0, last_a) + steps(first, 1, last_a),
+            way_back(lax.max(first - 1, 0), last_b),
+        )
+        in_turn(
+            steps(second, 0, last_b) + steps(second, 1, last_b),
+            way_back(first, last_a),
+        )
         return carry
 
+    lax.fori_loop(0, count, one_density, 0)
     acc[...] = jnp.zeros(acc.shape, jnp.float32)
-    lax.fori_loop(0, count, one_source, 0)
+    last_b[...] = jnp.zeros(last_b.shape, jnp.float32)
+    lax.fori_loop(0, count // 2, two_sources, 0)
+    in_turn(way_back(count - 1, last_b))
     for x in range(EDGE):
         for group in range(ROWS):
             tile = acc[x, pl.ds(group, EDGE, stride=pitch), :]
@@ -452,27 +506,31 @@
 
 
 def fields(halo, count):
+    own, across, *later = halo
+    beside, own_rows, modes = modes_of(own, across, count)
     plane = pltpu.VMEM((SIZE, SIZE, SUB, LANES), jnp.float32)
-    modes, tails = z_modes()
-    beside, own_rows = modes_of(halo[:4], modes, count)
-    corners = 2 * len(CORNER_LOW)
+    core = pltpu.VMEM((len(CORE), ROWS, LANES), jnp.float32)
+    cells = sum(spots_of(array.shape[0]) for array in later)
+    rows = ROWS * sum(array.shape[0] - spots_of(array.shape[0]) for array in later)
     return pl.pallas_call(
-        functools.partial(fields_kernel, count),
+        fields_kernel,
         out_shape=jax.ShapeDtypeStruct((EDGE, EDGE, ROWS * LANES), jnp.float32),
-        in_specs=[VMEM] * 6,
+        in_specs=[VMEM] * 7,
         out_specs=VMEM,
         scratch_shapes=[
-            pltpu.VMEM((count, 2 * ROWS, LANES), jnp.float32),
+            pltpu.VMEM((count, rows, LANES), jnp.float32),
+            pltpu.VMEM((cells, ROWS, 2 * LANES), jnp.bfloat16),
             pltpu.VMEM((len(CORE), ROWS, 2 * LANES), jnp.bfloat16),
-            pltpu.VMEM((count, corners, ROWS, LANES), jnp.float32),
+            pltpu.VMEM((count, cells, ROWS, LANES), jnp.float32),
             plane,
             plane,
-            pltpu.VMEM((len(CORE), ROWS, LANES), jnp.float32),
+            core,
+            core,
             pltpu.VMEM((EDGE, EDGE * (ROWS + 1), LANES), jnp.float32),
         ],
         compiler_params=pltpu.CompilerParams(vmem_limit_bytes=24 * 2**20),
         name="fields",
-    )(beside, own_rows, *halo[4:], modes, tails)
+    )(beside, own_rows, *later, modes)
 
 
 def body(orbitals, src_owner, src_slot):

time: 30 us -> 27.8 us (0.927)
  local copies, waits for them, and re-layouts: 5.01 us -> 1.03 us
  Pallas kernels: 7.83 us -> 9.18 us
  other arithmetic: 0 us -> 0.7 us
    unnamed x8 -> x2, local copies, waits for them, and re-layouts: 3.52 us -> 0.95 us
    broadcast_in_dim x2 -> x1, local copies, waits for them, and re-layouts: 1.5 us -> 0.07 us  [spread_out(): lax.broadcast_in_dim(values, values.shape + (ROWS, LANES), tuple(range(va...]
    pallas_call x4 -> x3, Pallas kernels: 7.72 us -> 9.07 us  [the longest x1 6.58 us: fields(): pl.pallas_call(fields_kernel, out_shape=jax.ShapeDtypeStruct((EDGE, EDGE,...]
    ppermute x1, waiting for transfers between devices: 1.18 us -> 0.01 us  [exchange(): above = lax.ppermute(first, 'sy', ring('sy', -1))]
    ppermute x2, waiting for transfers between devices: 1.55 us -> 2.56 us  [gathered(): other = lax.ppermute(mine, 'orb', [(i, i ^ 1 << bit) for i in range(count)])]
    another operation x0 -> x1, other arithmetic: none -> 0.7 us  [messages(): entries = spread_out(jnp.stack([src_slot, src_owner]))]
  transfers between devices with their start and end apart: 7 -> 7, of which waited for: 3 -> 3; matrix products, arithmetic and copies ran while one was open for 0% -> 0% of each run, Pallas kernels for 9% -> 8%
where the time goes in v9:
time: 27.8 us; the launch traced here: 27.7 us
  starting transfers between devices  14.1 us (51%)
  Pallas kernels  9.18 us (33%)
  waiting for transfers between devices  2.65 us (10%)
  local copies, waits for them, and re-layouts  1.03 us (4%)
  other arithmetic  0.7 us (3%)
    pallas_call x1, Pallas kernels, fields(): pl.pallas_call(fields_kernel, out_shape=jax.ShapeDtypeStruct((EDGE, EDGE,...  6.58 us
    ppermute x1, starting transfers between devices, exchange(): high = lax.ppermute(corner_high, both, diagonal(1, -1))  4.72 us
    ppermute x2, starting transfers between devices, gathered(): other = lax.ppermute(mine, 'orb', [(i, i ^ 1 << bit) for i in range(count)])  3.42 us
    ppermute x2, waiting for transfers between devices, gathered(): other = lax.ppermute(mine, 'orb', [(i, i ^ 1 << bit) for i in range(count)])  2.56 us
    pallas_call x1, Pallas kernels, modes_of(): pl.pallas_call(modes_kernel, out_shape=[jax.ShapeDtypeStruct((count, cell...  2.26 us
    ppermute x1, starting transfers between devices, exchange(): above = lax.ppermute(first, 'sy', ring('sy', -1))  2.25 us
    ppermute x1, starting transfers between devices, exchange(): across = lax.ppermute(block, 'sx', ring('sx', 1))  2.11 us
    ppermute x1, starting transfers between devices, exchange(): below = lax.ppermute(last, 'sy', ring('sy', 1))  1.58 us
  transfers between devices with their start and end apart: 7, of which 3 were waited for; matrix products, arithmetic and copies ran while one was open for 0% of the time, Pallas kernels for 8%

profile of v9, /device:TPU:0, one launch (start us, length us, event | category | flops | bytes accessed | tf_op | source)
XLA Modules:
  0.0 27.7 jit_solution(13627558489434579263)
XLA Ops:
  0.0 0.7 %pad_add_fusion = s32[2,2,2]{2,1,0:T(2,128)S(1)} fusion(s32[1,2,2]{2,1,0:T(2,128)} %bitcast.2, s32[1,2,2]{2,1,0:T(2,128)} %bitcast.3), kind=kLoop, calls=%fused_computation | loop fusion | flops 8 | bytes 64 | tf_op jit(solution)/shard_map/stack | solution.py:208
  0.7 0.1 broadcast_in_dim.3.entries
  0.8 0.0 copy-start
  0.8 1.0 %copy-done = bf16[8,8,2048]{2,1,0:T(8,128)(2,1)S(1)} copy-done((bf16[8,8,2048]{2,1,0:T(8,128)(2,1)S(1)}, bf16[8,8,2048]{2,1,0:T(8,128)(2,1)}, u32[]{:S(2)}) %copy-start) | copy-done | bytes 262168
  1.7 0.2 prepare.1
  2.0 0.5 %collective-permute-start = (bf16[4,16,128]{2,1,0:T(8,128)(2,1)S(1)}, bf16[4,16,128]{2,1,0:T(8,128)(2,1)S(1)}, u32[]{:S(2)}, u32[]{:S(2)}) collective-permute-start(bf16[4,16,128]{2,1,0:T(8,128)(2,1)S(1)} %get-tuple-element.16.mine), channel_id=1, source_target_pairs={{0,8},{8,0},{16,24},{24,16},{1,9},{9,1},{17,25},{25,17},{2,10},{10... | collective-permute-start | bytes 49160 | tf_op jit(solution)/shard_map/ppermute | solution.py:154
  2.5 0.8 %collective-permute-done.other = bf16[4,16,128]{2,1,0:T(8,128)(2,1)S(1)} collective-permute-done((bf16[4,16,128]{2,1,0:T(8,128)(2,1)S(1)}, bf16[4,16,128]{2,1,0:T(8,128)(2,1)S(1)}, u32[]{:S(2)}, u32[]{:S(2)}) %collective-permute-start) | collective-permute-done | bytes 16416 | tf_op jit(solution)/shard_map/ppermute | solution.py:154
  3.3 2.9 %collective-permute-start.1 = (bf16[4,16,128]{2,1,0:T(8,128)(2,1)S(1)}, bf16[4,16,128]{2,1,0:T(8,128)(2,1)S(1)}, u32[]{:S(2)}, u32[]{:S(2)}) collective-permute-start(bf16[4,16,128]{2,1,0:T(8,128)(2,1)S(1)} %nearer.1.mine), channel_id=1, source_target_pairs={{0,16},{8,24},{16,0},{24,8},{1,17},{9,25},{17,1},{25,9},{2,18},{10... | collective-permute-start | bytes 49160 | tf_op jit(solution)/shard_map/ppermute | solution.py:154
  6.2 1.7 %collective-permute-done.1.refs_0_ = bf16[4,16,128]{2,1,0:T(8,128)(2,1)S(1)} collective-permute-done((bf16[4,16,128]{2,1,0:T(8,128)(2,1)S(1)}, bf16[4,16,128]{2,1,0:T(8,128)(2,1)S(1)}, u32[]{:S(2)}, u32[]{:S(2)}) %collective-permute-start.1) | collective-permute-done | bytes 16416 | tf_op jit(solution)/shard_map/ppermute | solution.py:154
  8.0 0.1 messages.1
  8.0 2.1 %collective-permute-start.2 = (bf16[68,16,128]{2,1,0:T(8,128)(2,1)S(1)}, bf16[68,16,128]{2,1,0:T(8,128)(2,1)S(1)}, u32[]{:S(2)}, u32[]{:S(2)}) collective-permute-start(bf16[68,16,128]{2,1,0:T(8,128)(2,1)S(1)} %get-tuple-element.17.own), channel_id=1, source_target_pairs={{0,4},{4,0},{1,5},{5,1},{2,6},{6,2},{3,7},{7,3},{8,12},{12,8},{9,1... | collective-permute-start | bytes 835592 | tf_op jit(solution)/shard_map/ppermute | solution.py:229
  10.2 1.6 %collective-permute-start.3 = (bf16[34,16,128]{2,1,0:T(8,128)(2,1)S(1)}, bf16[34,16,128]{2,1,0:T(8,128)(2,1)S(1)}, u32[]{:S(2)}, u32[]{:S(2)}) collective-permute-start(bf16[34,16,128]{2,1,0:T(8,128)(2,1)S(1)} %get-tuple-element.20), channel_id=1, source_target_pairs={{0,1},{1,2},{2,3},{3,0},{4,5},{5,6},{6,7},{7,4},{8,9},{9,10},{10,1... | collective-permute-start | bytes 417800 | tf_op jit(solution)/shard_map/ppermute | solution.py:246
  11.7 2.2 %collective-permute-start.4 = (bf16[34,16,128]{2,1,0:T(8,128)(2,1)S(1)}, bf16[34,16,128]{2,1,0:T(8,128)(2,1)S(1)}, u32[]{:S(2)}, u32[]{:S(2)}) collective-permute-start(bf16[34,16,128]{2,1,0:T(8,128)(2,1)S(1)} %get-tuple-element.21), channel_id=1, source_target_pairs={{0,3},{1,0},{2,1},{3,2},{4,7},{5,4},{6,5},{7,6},{8,11},{9,8},{10,9... | collective-permute-start | bytes 417800 | tf_op jit(solution)/shard_map/ppermute | solution.py:247
  14.0 0.0 collective-permute-start.5
  14.0 4.7 %collective-permute-start.6 = (bf16[13,16,128]{2,1,0:T(8,128)(2,1)S(1)}, bf16[13,16,128]{2,1,0:T(8,128)(2,1)S(1)}, u32[]{:S(2)}, u32[]{:S(2)}) collective-permute-start(bf16[13,16,128]{2,1,0:T(8,128)(2,1)S(1)} %get-tuple-element.23), channel_id=1, source_target_pairs={{0,7},{1,4},{2,5},{3,6},{4,3},{5,0},{6,1},{7,2},{8,15},{9,12},{10,... | collective-permute-start | bytes 159752 | tf_op jit(solution)/shard_map/ppermute | solution.py:228
  18.7 0.0 collective-permute-done.2.across
  18.7 2.3 %modes.1 = (f32[4,128,16,128]{3,2,1,0:T(8,128)S(1)}, f32[4,64,128]{2,1,0:T(8,128)S(1)}, bf16[256,256]{1,0:T(8,128)(2,1)S(1)}) custom-call(bf16[68,16,128]{2,1,0:T(8,128)(2,1)S(1)} %get-tuple-element.17.own, bf16[68,16,128]{2,1,0:T(8,128)(2,1)S(1)} %collective-permute-done.2.across), custom_call_target="tpu_custom_call" | custom-call | bytes 6291456 | tf_op jit(solution)/shard_map/modes/pallas_call | solution.py:372
  21.0 0.1 collective-permute-done.5.low
  21.1 0.0 collective-permute-done.6.high
  21.1 0.0 collective-permute-done.3.below
  21.1 0.0 collective-permute-done.4.above
  21.1 6.6 %fields.1 = f32[8,8,2048]{2,1,0:T(8,128)} custom-call(f32[4,128,16,128]{3,2,1,0:T(8,128)S(1)} %get-tuple-element.18.beside, f32[4,64,128]{2,1,0:T(8,128)S(1)} %get-tuple-element.19.own_rows, bf16[34,16,128]{2,1,0:T(8,128)(2,1)S(1)} %collective-permute-done.3.below, bf16[34,16,128]{2,1,0:T(8,128)(2,1)S(1)} %collective-permute-done.4.above, ...), custom_call_target="tpu_custom_call" | custom-call | tf_op jit(solution)/shard_map/fields/pallas_call | solution.py:515
  (1 shorter events, 0.0 us)
Async XLA Ops:
  0.8 1.0 %copy-start = (bf16[8,8,2048]{2,1,0:T(8,128)(2,1)S(1)}, bf16[8,8,2048]{2,1,0:T(8,128)(2,1)}, u32[]{:S(2)}) copy-start(bf16[8,8,2048]{2,1,0:T(8,128)(2,1)} %orbitals.1) | copy-start | bytes 786436
  2.0 1.4 %collective-permute-start = (bf16[4,16,128]{2,1,0:T(8,128)(2,1)S(1)}, bf16[4,16,128]{2,1,0:T(8,128)(2,1)S(1)}, u32[]{:S(2)}, u32[]{:S(2)}) collective-permute-start(bf16[4,16,128]{2,1,0:T(8,128)(2,1)S(1)} %get-tuple-element.16.mine), channel_id=1, source_target_pairs={{0,8},{8,0},{16,24},{24,16},{1,9},{9,1},{17,25},{25,17},{2,10},{10... | collective-permute-start | bytes 49160 | tf_op jit(solution)/shard_map/ppermute | solution.py:154
  3.3 4.6 %collective-permute-start.1 = (bf16[4,16,128]{2,1,0:T(8,128)(2,1)S(1)}, bf16[4,16,128]{2,1,0:T(8,128)(2,1)S(1)}, u32[]{:S(2)}, u32[]{:S(2)}) collective-permute-start(bf16[4,16,128]{2,1,0:T(8,128)(2,1)S(1)} %nearer.1.mine), channel_id=1, source_target_pairs={{0,16},{8,24},{16,0},{24,8},{1,17},{9,25},{17,1},{25,9},{2,18},{10... | collective-permute-start | bytes 49160 | tf_op jit(solution)/shard_map/ppermute | solution.py:154
  8.0 10.7 %collective-permute-start.2 = (bf16[68,16,128]{2,1,0:T(8,128)(2,1)S(1)}, bf16[68,16,128]{2,1,0:T(8,128)(2,1)S(1)}, u32[]{:S(2)}, u32[]{:S(2)}) collective-permute-start(bf16[68,16,128]{2,1,0:T(8,128)(2,1)S(1)} %get-tuple-element.17.own), channel_id=1, source_target_pairs={{0,4},{4,0},{1,5},{5,1},{2,6},{6,2},{3,7},{7,3},{8,12},{12,8},{9,1... | collective-permute-start | bytes 835592 | tf_op jit(solution)/shard_map/ppermute | solution.py:229
  10.2 10.9 %collective-permute-start.3 = (bf16[34,16,128]{2,1,0:T(8,128)(2,1)S(1)}, bf16[34,16,128]{2,1,0:T(8,128)(2,1)S(1)}, u32[]{:S(2)}, u32[]{:S(2)}) collective-permute-start(bf16[34,16,128]{2,1,0:T(8,128)(2,1)S(1)} %get-tuple-element.20), channel_id=1, source_target_pairs={{0,1},{1,2},{2,3},{3,0},{4,5},{5,6},{6,7},{7,4},{8,9},{9,10},{10,1... | collective-permute-start | bytes 417800 | tf_op jit(solution)/shard_map/ppermute | solution.py:246
  11.7 9.3 %collective-permute-start.4 = (bf16[34,16,128]{2,1,0:T(8,128)(2,1)S(1)}, bf16[34,16,128]{2,1,0:T(8,128)(2,1)S(1)}, u32[]{:S(2)}, u32[]{:S(2)}) collective-permute-start(bf16[34,16,128]{2,1,0:T(8,128)(2,1)S(1)} %get-tuple-element.21), channel_id=1, source_target_pairs={{0,3},{1,0},{2,1},{3,2},{4,7},{5,4},{6,5},{7,6},{8,11},{9,8},{10,9... | collective-permute-start | bytes 417800 | tf_op jit(solution)/shard_map/ppermute | solution.py:247
  14.0 7.1 %collective-permute-start.5 = (bf16[13,16,128]{2,1,0:T(8,128)(2,1)S(1)}, bf16[13,16,128]{2,1,0:T(8,128)(2,1)S(1)}, u32[]{:S(2)}, u32[]{:S(2)}) collective-permute-start(bf16[13,16,128]{2,1,0:T(8,128)(2,1)S(1)} %get-tuple-element.22), channel_id=1, source_target_pairs={{0,5},{1,6},{2,7},{3,4},{4,1},{5,2},{6,3},{7,0},{8,13},{9,14},{10,... | collective-permute-start | bytes 159752 | tf_op jit(solution)/shard_map/ppermute | solution.py:227
  14.0 7.1 %collective-permute-start.6 = (bf16[13,16,128]{2,1,0:T(8,128)(2,1)S(1)}, bf16[13,16,128]{2,1,0:T(8,128)(2,1)S(1)}, u32[]{:S(2)}, u32[]{:S(2)}) collective-permute-start(bf16[13,16,128]{2,1,0:T(8,128)(2,1)S(1)} %get-tuple-element.23), channel_id=1, source_target_pairs={{0,7},{1,4},{2,5},{3,6},{4,3},{5,0},{6,1},{7,2},{8,15},{9,12},{10,... | collective-permute-start | bytes 159752 | tf_op jit(solution)/shard_map/ppermute | solution.py:228

commit v10 on v9

--- a/solution.py
+++ b/solution.py
@@ -165,7 +165,7 @@
     return mine, [], None
 
 
-def messages_kernel(bit, entries, cells, mine, *refs):
+def messages_kernel(bit, before, entries, cells, mine, *refs):
     others, (block, last, first, corner_low, corner_high) = refs[:-5], refs[-5:]
     picked = chosen(entries, mine, others, bit)
 
@@ -209,16 +209,18 @@
     mine, cells = prepare(entries, orbitals)
     mine, others, bit = gathered(entries, mine)
     lengths = [EDGE * EDGE] + [EDGE * HALO] * 2 + [len(CORNER_LOW)] * 2
-    return pl.pallas_call(
+    modes = sines(mine)
+    packed = pl.pallas_call(
         functools.partial(messages_kernel, bit),
         out_shape=[
             jax.ShapeDtypeStruct((tiles(length), ROWS, LANES), jnp.bfloat16) for length in lengths
         ],
-        in_specs=[VMEM] * (3 + len(others)),
+        in_specs=[pl.BlockSpec(memory_space=pl.ANY)] + [VMEM] * (3 + len(others)),
         out_specs=[VMEM] * 5,
         compiler_params=SMALL,
         name="messages",
-    )(entries, cells, mine, *others)
+    )(modes, entries, cells, mine, *others)
+    return packed, modes
 
 
 def exchange(block, last, first, corner_low, corner_high):
@@ -264,7 +266,7 @@
     return out_x + out_y
 
 
-def z_modes(out):
+def sines_kernel(after, out):
     shape = (LANES, LANES)
     row, col = (lax.broadcasted_iota(jnp.int32, shape, axis) for axis in range(2))
     product = ((row % NZ + 1) * (col % NZ + 1)).astype(jnp.float32)
@@ -277,6 +279,18 @@
     for first in (0, LANES):
         out[pl.ds(first, LANES), pl.ds(0, LANES)] = high
         out[pl.ds(first, LANES), pl.ds(LANES, LANES)] = low
+
+
+def sines(after):
+    return pl.pallas_call(
+        sines_kernel,
+        out_shape=jax.ShapeDtypeStruct((2 * LANES, 2 * LANES), jnp.bfloat16),
+        in_specs=[pl.BlockSpec(memory_space=pl.ANY)],
+        out_specs=VMEM,
+        compiler_params=SMALL,
+        cost_estimate=pl.CostEstimate(flops=0, bytes_accessed=2 * 2**20, transcendentals=0),
+        name="sines",
+    )(after)
 
 
 def z_tails():
@@ -352,8 +366,7 @@
     return firsts
 
 
-def modes_kernel(own, across, hat, own_rows, modes, rows, parts):
-    z_modes(modes)
+def modes_kernel(own, across, modes, hat, own_rows, rows, parts):
     firsts = all_rows((own, across), rows)
     own_rows[...] = rows[:, : own_rows.shape[1], :]
 
@@ -367,17 +380,16 @@
     lax.fori_loop(0, hat.shape[0], one_source, 0)
 
 
-def modes_of(own, across, count):
+def modes_of(own, across, modes, count):
     cells = 2 * len(CORE)
     return pl.pallas_call(
         modes_kernel,
         out_shape=[
             jax.ShapeDtypeStruct((count, cells, ROWS, LANES), jnp.float32),
             jax.ShapeDtypeStruct((count, len(CORE), LANES), jnp.float32),
-            jax.ShapeDtypeStruct((2 * LANES, 2 * LANES), jnp.bfloat16),
         ],
-        in_specs=[VMEM] * 2,
-        out_specs=[VMEM] * 3,
+        in_specs=[VMEM] * 3,
+        out_specs=[VMEM] * 2,
         scratch_shapes=[
             pltpu.VMEM((count, cells, LANES), jnp.float32),
             pltpu.VMEM((cells, ROWS, 2 * LANES), jnp.bfloat16),
@@ -385,23 +397,11 @@
         compiler_params=pltpu.CompilerParams(vmem_limit_bytes=20 * 2**20),
         cost_estimate=pl.CostEstimate(flops=0, bytes_accessed=6 * 2**20, transcendentals=0),
         name="modes",
-    )(own, across)
-
-
-def in_turn(*works):
-    works = [list(work) for work in works]
-    done = [0] * len(works)
-    for _ in range(sum(map(len, works))):
-        at = min(
-            (at for at in range(len(works)) if done[at] < len(works[at])),
-            key=lambda at: (done[at] + 0.5) / len(works[at]),
-        )
-        works[at][done[at]]()
-        done[at] += 1
+    )(own, across, modes)
 
 
 def fields_kernel(beside, own_rows, below, above, low, high, modes, *refs):
-    out, rows, parts, back, hat, work_a, work_b, last_a, last_b, acc = refs
+    out, rows, parts, back, hat, work_a, work_b, last, acc = refs
     count = beside.shape[0]
     pitch = ROWS + 1
     tails = z_tails()
@@ -418,7 +418,7 @@
         densities(later, rows, firsts, place, parts, modes, put)
         return carry
 
-    def steps(place, half, last):
+    def steps(place, half):
         part = pl.ds(half * SUB, SUB)
 
         def start(x, y):
@@ -427,7 +427,7 @@
                 return beside[place, which * len(CORE) + at, part, :]
             return hat[place, offset[which - 2] + at, part, :]
 
-        def one_row(step, x, state):
+        for step in range(DEGREE):
             new = (work_a, work_b, work_a, None)[step]
             old = (None, work_a, work_b, work_a)[step]
             targets, known = within(HALO - 1 - step), within(HALO - step)
@@ -435,79 +435,45 @@
             def load(x):
                 return {y: start(x, y) if old is None else old[x, y] for y in known[x]}
 
-            here, pair_prev = state.get(step) or (load(x), {})
-            ahead, pair = load(x + 1), {}
-            for y in range(SIZE - 1):
-                if y in targets[x] or y + 1 in targets[x + 1]:
-                    pair[y] = ahead[y] + here[y + 1]
-                if y in targets[x]:
-                    density = here[y] if old is None else start(x, y)
-                    value = pair[y] + pair_prev[y - 1] + tails[step] * density
-                    if new is not None:
-                        new[x, y] = value
-                    else:
-                        last[CORE.index((x, y)), part, :] = value
-            state[step] = (ahead, pair)
-
-        state = {}
-        return [
-            functools.partial(one_row, step, x, state)
-            for step in range(DEGREE)
-            for x in range(step, SIZE - 1 - step)
-        ]
-
-    def way_back(place, last):
-        pieces = 2
-        size = len(CORE) // pieces
-
-        def split(at):
+            here, pair_prev = load(step), {}
+            for x in range(step, SIZE - 1 - step):
+                ahead, pair = load(x + 1), {}
+                for y in range(SIZE - 1):
+                    if y in targets[x] or y + 1 in targets[x + 1]:
+                        pair[y] = ahead[y] + here[y + 1]
+                    if y in targets[x]:
+                        density = here[y] if old is None else start(x, y)
+                        value = pair[y] + pair_prev[y - 1] + tails[step] * density
+                        if new is not None:
+                            new[x, y] = value
+                        else:
+                            last[CORE.index((x, y)), part, :] = value
+                here, pair_prev = ahead, pair
+
+    def one_source(place, carry):
+        for half in range(ROWS // SUB):
+            steps(place, half)
+        for at in range(len(CORE)):
             keep(back, at, last[at])
-
-        def turn(piece, held):
-            held[piece] = turned(back, piece * size, (piece + 1) * size, modes)
-
-        def add(at, held):
-            x, y = CORE[at]
+        result = turned(back, 0, len(CORE), modes)
+        for at, (x, y) in enumerate(CORE):
             lanes = pl.ds((y - HALO) * pitch, ROWS)
             other = jnp.broadcast_to(own_rows[place, pl.ds(at, 1), :], (ROWS, LANES))
-            value = held[at // size][at % size] * other
-            acc[x - HALO, lanes, :] = acc[x - HALO, lanes, :] + value
-
-        held = {}
-        work = []
-        for piece in range(pieces):
-            cells = range(piece * size, (piece + 1) * size)
-            work += [functools.partial(split, at) for at in cells]
-            work.append(functools.partial(turn, piece, held))
-            work += [functools.partial(add, at, held) for at in cells]
-        return work
-
-    def two_sources(pair, carry):
-        first, second = 2 * pair, 2 * pair + 1
-        in_turn(
-            steps(first, 0, last_a) + steps(first, 1, last_a),
-            way_back(lax.max(first - 1, 0), last_b),
-        )
-        in_turn(
-            steps(second, 0, last_b) + steps(second, 1, last_b),
-            way_back(first, last_a),
-        )
+            acc[x - HALO, lanes, :] = acc[x - HALO, lanes, :] + result[at] * other
         return carry
 
     lax.fori_loop(0, count, one_density, 0)
     acc[...] = jnp.zeros(acc.shape, jnp.float32)
-    last_b[...] = jnp.zeros(last_b.shape, jnp.float32)
-    lax.fori_loop(0, count // 2, two_sources, 0)
-    in_turn(way_back(count - 1, last_b))
+    lax.fori_loop(0, count, one_source, 0)
     for x in range(EDGE):
         for group in range(ROWS):
             tile = acc[x, pl.ds(group, EDGE, stride=pitch), :]
             out[x, :, pl.ds(group * LANES, LANES)] = tile * (-power_coeffs()[-1])
 
 
-def fields(halo, count):
+def fields(halo, modes, count):
     own, across, *later = halo
-    beside, own_rows, modes = modes_of(own, across, count)
+    beside, own_rows = modes_of(own, across, modes, count)
     plane = pltpu.VMEM((SIZE, SIZE, SUB, LANES), jnp.float32)
     core = pltpu.VMEM((len(CORE), ROWS, LANES), jnp.float32)
     cells = sum(spots_of(array.shape[0]) for array in later)
@@ -525,7 +491,6 @@
             plane,
             plane,
             core,
-            core,
             pltpu.VMEM((EDGE, EDGE * (ROWS + 1), LANES), jnp.float32),
         ],
         compiler_params=pltpu.CompilerParams(vmem_limit_bytes=24 * 2**20),
@@ -534,8 +499,8 @@
 
 
 def body(orbitals, src_owner, src_slot):
-    packed = messages(orbitals, src_owner, src_slot)
-    return fields((packed[0], *exchange(*packed)), src_slot.size)
+    packed, modes = messages(orbitals, src_owner, src_slot)
+    return fields((packed[0], *exchange(*packed)), modes, src_slot.size)
 
 
 def solution(mesh):

time: 27.8 us -> 27.5 us (0.989)
  Pallas kernels: 9.18 us -> 8.85 us
    pallas_call x1, Pallas kernels: 6.58 us -> 6.24 us  [fields(): pl.pallas_call(fields_kernel, out_shape=jax.ShapeDtypeStruct((EDGE, EDGE,...]
    ppermute x2, waiting for transfers between devices: 2.56 us -> 2.28 us  [gathered(): other = lax.ppermute(mine, 'orb', [(i, i ^ 1 << bit) for i in range(count)])]
where the time goes in v10:
time: 27.5 us; the launch traced here: 27.3 us
  starting transfers between devices  14.1 us (51%)
  Pallas kernels  8.85 us (32%)
  waiting for transfers between devices  2.64 us (10%)
  local copies, waits for them, and re-layouts  1.03 us (4%)
  other arithmetic  0.7 us (3%)
    pallas_call x1, Pallas kernels, fields(): pl.pallas_call(fields_kernel, out_shape=jax.ShapeDtypeStruct((EDGE, EDGE,...  6.24 us
    ppermute x1, starting transfers between devices, exchange(): high = lax.ppermute(corner_high, both, diagonal(1, -1))  4.72 us
    ppermute x2, starting transfers between devices, gathered(): other = lax.ppermute(mine, 'orb', [(i, i ^ 1 << bit) for i in range(count)])  3.42 us
    ppermute x2, waiting for transfers between devices, gathered(): other = lax.ppermute(mine, 'orb', [(i, i ^ 1 << bit) for i in range(count)])  2.28 us
    ppermute x1, starting transfers between devices, exchange(): above = lax.ppermute(first, 'sy', ring('sy', -1))  2.25 us
    ppermute x1, starting transfers between devices, exchange(): across = lax.ppermute(block, 'sx', ring('sx', 1))  2.11 us
    pallas_call x1, Pallas kernels, modes_of(): pl.pallas_call(modes_kernel, out_shape=[jax.ShapeDtypeStruct((count, cell...  1.99 us
    ppermute x1, starting transfers between devices, exchange(): below = lax.ppermute(last, 'sy', ring('sy', 1))  1.58 us
  transfers between devices with their start and end apart: 7, of which 3 were waited for; matrix products, arithmetic and copies ran while one was open for 0% of the time, Pallas kernels for 8%

profile of v10, /device:TPU:0, one launch (start us, length us, event | category | flops | bytes accessed | tf_op | source)
XLA Modules:
  0.0 27.3 jit_solution(38500265757104915)
XLA Ops:
  0.0 0.7 %pad_add_fusion = s32[2,2,2]{2,1,0:T(2,128)S(1)} fusion(s32[1,2,2]{2,1,0:T(2,128)} %bitcast.2, s32[1,2,2]{2,1,0:T(2,128)} %bitcast.3), kind=kLoop, calls=%fused_computation | loop fusion | flops 8 | bytes 64 | tf_op jit(solution)/shard_map/stack | solution.py:208
  0.7 0.1 broadcast_in_dim.3.entries
  0.8 0.0 copy-start
  0.8 1.0 %copy-done = bf16[8,8,2048]{2,1,0:T(8,128)(2,1)S(1)} copy-done((bf16[8,8,2048]{2,1,0:T(8,128)(2,1)S(1)}, bf16[8,8,2048]{2,1,0:T(8,128)(2,1)}, u32[]{:S(2)}) %copy-start) | copy-done | bytes 262168
  1.7 0.2 prepare.1
  2.0 0.5 %collective-permute-start = (bf16[4,16,128]{2,1,0:T(8,128)(2,1)S(1)}, bf16[4,16,128]{2,1,0:T(8,128)(2,1)S(1)}, u32[]{:S(2)}, u32[]{:S(2)}) collective-permute-start(bf16[4,16,128]{2,1,0:T(8,128)(2,1)S(1)} %get-tuple-element.14.mine), channel_id=1, source_target_pairs={{0,8},{8,0},{16,24},{24,16},{1,9},{9,1},{17,25},{25,17},{2,10},{10... | collective-permute-start | bytes 49160 | tf_op jit(solution)/shard_map/ppermute | solution.py:154
  2.5 0.8 %collective-permute-done.other = bf16[4,16,128]{2,1,0:T(8,128)(2,1)S(1)} collective-permute-done((bf16[4,16,128]{2,1,0:T(8,128)(2,1)S(1)}, bf16[4,16,128]{2,1,0:T(8,128)(2,1)S(1)}, u32[]{:S(2)}, u32[]{:S(2)}) %collective-permute-start) | collective-permute-done | bytes 16416 | tf_op jit(solution)/shard_map/ppermute | solution.py:154
  3.3 2.9 %collective-permute-start.1 = (bf16[4,16,128]{2,1,0:T(8,128)(2,1)S(1)}, bf16[4,16,128]{2,1,0:T(8,128)(2,1)S(1)}, u32[]{:S(2)}, u32[]{:S(2)}) collective-permute-start(bf16[4,16,128]{2,1,0:T(8,128)(2,1)S(1)} %nearer.1.after.mine), channel_id=1, source_target_pairs={{0,16},{8,24},{16,0},{24,8},{1,17},{9,25},{17,1},{25,9},{2,18},{10... | collective-permute-start | bytes 49160 | tf_op jit(solution)/shard_map/ppermute | solution.py:154
  6.2 0.3 %sines.1.before.modes = bf16[256,256]{1,0:T(8,128)(2,1)S(1)} custom-call(bf16[4,16,128]{2,1,0:T(8,128)(2,1)S(1)} %nearer.1.after.mine), custom_call_target="tpu_custom_call" | custom-call | bytes 2097152 | tf_op jit(solution)/shard_map/sines/pallas_call | solution.py:285
  6.5 1.4 %collective-permute-done.1.refs_0_ = bf16[4,16,128]{2,1,0:T(8,128)(2,1)S(1)} collective-permute-done((bf16[4,16,128]{2,1,0:T(8,128)(2,1)S(1)}, bf16[4,16,128]{2,1,0:T(8,128)(2,1)S(1)}, u32[]{:S(2)}, u32[]{:S(2)}) %collective-permute-start.1) | collective-permute-done | bytes 16416 | tf_op jit(solution)/shard_map/ppermute | solution.py:154
  8.0 0.1 messages.1
  8.0 2.1 %collective-permute-start.2 = (bf16[68,16,128]{2,1,0:T(8,128)(2,1)S(1)}, bf16[68,16,128]{2,1,0:T(8,128)(2,1)S(1)}, u32[]{:S(2)}, u32[]{:S(2)}) collective-permute-start(bf16[68,16,128]{2,1,0:T(8,128)(2,1)S(1)} %get-tuple-element.16.own), channel_id=1, source_target_pairs={{0,4},{4,0},{1,5},{5,1},{2,6},{6,2},{3,7},{7,3},{8,12},{12,8},{9,1... | collective-permute-start | bytes 835592 | tf_op jit(solution)/shard_map/ppermute | solution.py:231
  10.2 1.6 %collective-permute-start.3 = (bf16[34,16,128]{2,1,0:T(8,128)(2,1)S(1)}, bf16[34,16,128]{2,1,0:T(8,128)(2,1)S(1)}, u32[]{:S(2)}, u32[]{:S(2)}) collective-permute-start(bf16[34,16,128]{2,1,0:T(8,128)(2,1)S(1)} %get-tuple-element.19), channel_id=1, source_target_pairs={{0,1},{1,2},{2,3},{3,0},{4,5},{5,6},{6,7},{7,4},{8,9},{9,10},{10,1... | collective-permute-start | bytes 417800 | tf_op jit(solution)/shard_map/ppermute | solution.py:248
  11.7 2.2 %collective-permute-start.4 = (bf16[34,16,128]{2,1,0:T(8,128)(2,1)S(1)}, bf16[34,16,128]{2,1,0:T(8,128)(2,1)S(1)}, u32[]{:S(2)}, u32[]{:S(2)}) collective-permute-start(bf16[34,16,128]{2,1,0:T(8,128)(2,1)S(1)} %get-tuple-element.20), channel_id=1, source_target_pairs={{0,3},{1,0},{2,1},{3,2},{4,7},{5,4},{6,5},{7,6},{8,11},{9,8},{10,9... | collective-permute-start | bytes 417800 | tf_op jit(solution)/shard_map/ppermute | solution.py:249
  14.0 0.0 collective-permute-start.5
  14.0 4.7 %collective-permute-start.6 = (bf16[13,16,128]{2,1,0:T(8,128)(2,1)S(1)}, bf16[13,16,128]{2,1,0:T(8,128)(2,1)S(1)}, u32[]{:S(2)}, u32[]{:S(2)}) collective-permute-start(bf16[13,16,128]{2,1,0:T(8,128)(2,1)S(1)} %get-tuple-element.22), channel_id=1, source_target_pairs={{0,7},{1,4},{2,5},{3,6},{4,3},{5,0},{6,1},{7,2},{8,15},{9,12},{10,... | collective-permute-start | bytes 159752 | tf_op jit(solution)/shard_map/ppermute | solution.py:230
  18.7 0.0 collective-permute-done.2.across
  18.7 2.0 %modes.1 = (f32[4,128,16,128]{3,2,1,0:T(8,128)S(1)}, f32[4,64,128]{2,1,0:T(8,128)S(1)}) custom-call(bf16[68,16,128]{2,1,0:T(8,128)(2,1)S(1)} %get-tuple-element.16.own, bf16[68,16,128]{2,1,0:T(8,128)(2,1)S(1)} %collective-permute-done.2.across, bf16[256,256]{1,0:T(8,128)(2,1)S(1)} %sines.1.before.modes), custom_call_target="tpu_custom_call" | custom-call | bytes 6291456 | tf_op jit(solution)/shard_map/modes/pallas_call | solution.py:385
  20.7 0.4 %collective-permute-done.5.low = bf16[13,16,128]{2,1,0:T(8,128)(2,1)S(1)} collective-permute-done((bf16[13,16,128]{2,1,0:T(8,128)(2,1)S(1)}, bf16[13,16,128]{2,1,0:T(8,128)(2,1)S(1)}, u32[]{:S(2)}, u32[]{:S(2)}) %collective-permute-start.5) | collective-permute-done | bytes 53280 | tf_op jit(solution)/shard_map/ppermute | solution.py:229
  21.1 0.0 collective-permute-done.6.high
  21.1 0.0 collective-permute-done.3.below
  21.1 0.0 collective-permute-done.4.above
  21.1 6.2 %fields.1 = f32[8,8,2048]{2,1,0:T(8,128)} custom-call(f32[4,128,16,128]{3,2,1,0:T(8,128)S(1)} %get-tuple-element.17.beside, f32[4,64,128]{2,1,0:T(8,128)S(1)} %get-tuple-element.18.own_rows, bf16[34,16,128]{2,1,0:T(8,128)(2,1)S(1)} %collective-permute-done.3.below, bf16[34,16,128]{2,1,0:T(8,128)(2,1)S(1)} %collective-permute-done.4.above, ...), custom_call_target="tpu_custom_call" | custom-call | tf_op jit(solution)/shard_map/fields/pallas_call | solution.py:481
  (1 shorter events, 0.0 us)
Async XLA Ops:
  0.8 1.0 %copy-start = (bf16[8,8,2048]{2,1,0:T(8,128)(2,1)S(1)}, bf16[8,8,2048]{2,1,0:T(8,128)(2,1)}, u32[]{:S(2)}) copy-start(bf16[8,8,2048]{2,1,0:T(8,128)(2,1)} %orbitals.1) | copy-start | bytes 786436
  2.0 1.4 %collective-permute-start = (bf16[4,16,128]{2,1,0:T(8,128)(2,1)S(1)}, bf16[4,16,128]{2,1,0:T(8,128)(2,1)S(1)}, u32[]{:S(2)}, u32[]{:S(2)}) collective-permute-start(bf16[4,16,128]{2,1,0:T(8,128)(2,1)S(1)} %get-tuple-element.14.mine), channel_id=1, source_target_pairs={{0,8},{8,0},{16,24},{24,16},{1,9},{9,1},{17,25},{25,17},{2,10},{10... | collective-permute-start | bytes 49160 | tf_op jit(solution)/shard_map/ppermute | solution.py:154
  3.3 4.6 %collective-permute-start.1 = (bf16[4,16,128]{2,1,0:T(8,128)(2,1)S(1)}, bf16[4,16,128]{2,1,0:T(8,128)(2,1)S(1)}, u32[]{:S(2)}, u32[]{:S(2)}) collective-permute-start(bf16[4,16,128]{2,1,0:T(8,128)(2,1)S(1)} %nearer.1.after.mine), channel_id=1, source_target_pairs={{0,16},{8,24},{16,0},{24,8},{1,17},{9,25},{17,1},{25,9},{2,18},{10... | collective-permute-start | bytes 49160 | tf_op jit(solution)/shard_map/ppermute | solution.py:154
  8.0 10.7 %collective-permute-start.2 = (bf16[68,16,128]{2,1,0:T(8,128)(2,1)S(1)}, bf16[68,16,128]{2,1,0:T(8,128)(2,1)S(1)}, u32[]{:S(2)}, u32[]{:S(2)}) collective-permute-start(bf16[68,16,128]{2,1,0:T(8,128)(2,1)S(1)} %get-tuple-element.16.own), channel_id=1, source_target_pairs={{0,4},{4,0},{1,5},{5,1},{2,6},{6,2},{3,7},{7,3},{8,12},{12,8},{9,1... | collective-permute-start | bytes 835592 | tf_op jit(solution)/shard_map/ppermute | solution.py:231
  10.2 10.9 %collective-permute-start.3 = (bf16[34,16,128]{2,1,0:T(8,128)(2,1)S(1)}, bf16[34,16,128]{2,1,0:T(8,128)(2,1)S(1)}, u32[]{:S(2)}, u32[]{:S(2)}) collective-permute-start(bf16[34,16,128]{2,1,0:T(8,128)(2,1)S(1)} %get-tuple-element.19), channel_id=1, source_target_pairs={{0,1},{1,2},{2,3},{3,0},{4,5},{5,6},{6,7},{7,4},{8,9},{9,10},{10,1... | collective-permute-start | bytes 417800 | tf_op jit(solution)/shard_map/ppermute | solution.py:248
  11.7 9.3 %collective-permute-start.4 = (bf16[34,16,128]{2,1,0:T(8,128)(2,1)S(1)}, bf16[34,16,128]{2,1,0:T(8,128)(2,1)S(1)}, u32[]{:S(2)}, u32[]{:S(2)}) collective-permute-start(bf16[34,16,128]{2,1,0:T(8,128)(2,1)S(1)} %get-tuple-element.20), channel_id=1, source_target_pairs={{0,3},{1,0},{2,1},{3,2},{4,7},{5,4},{6,5},{7,6},{8,11},{9,8},{10,9... | collective-permute-start | bytes 417800 | tf_op jit(solution)/shard_map/ppermute | solution.py:249
  14.0 7.1 %collective-permute-start.5 = (bf16[13,16,128]{2,1,0:T(8,128)(2,1)S(1)}, bf16[13,16,128]{2,1,0:T(8,128)(2,1)S(1)}, u32[]{:S(2)}, u32[]{:S(2)}) collective-permute-start(bf16[13,16,128]{2,1,0:T(8,128)(2,1)S(1)} %get-tuple-element.21), channel_id=1, source_target_pairs={{0,5},{1,6},{2,7},{3,4},{4,1},{5,2},{6,3},{7,0},{8,13},{9,14},{10,... | collective-permute-start | bytes 159752 | tf_op jit(solution)/shard_map/ppermute | solution.py:229
  14.0 7.1 %collective-permute-start.6 = (bf16[13,16,128]{2,1,0:T(8,128)(2,1)S(1)}, bf16[13,16,128]{2,1,0:T(8,128)(2,1)S(1)}, u32[]{:S(2)}, u32[]{:S(2)}) collective-permute-start(bf16[13,16,128]{2,1,0:T(8,128)(2,1)S(1)} %get-tuple-element.22), channel_id=1, source_target_pairs={{0,7},{1,4},{2,5},{3,6},{4,3},{5,0},{6,1},{7,2},{8,15},{9,12},{10,... | collective-permute-start | bytes 159752 | tf_op jit(solution)/shard_map/ppermute | solution.py:230

commit v11 on v10

--- a/solution.py
+++ b/solution.py
@@ -370,14 +370,12 @@
     firsts = all_rows((own, across), rows)
     own_rows[...] = rows[:, : own_rows.shape[1], :]
 
-    def one_source(place, carry):
-        def put(start, end, value):
+    for place in range(hat.shape[0]):
+
+        def put(start, end, value, place=place):
             hat[place, start:end] = value
 
         densities((own, across), rows, firsts, place, parts, modes, put)
-        return carry
-
-    lax.fori_loop(0, hat.shape[0], one_source, 0)
 
 
 def modes_of(own, across, modes, count):
@@ -401,22 +399,19 @@
 
 
 def fields_kernel(beside, own_rows, below, above, low, high, modes, *refs):
-    out, rows, parts, back, hat, work_a, work_b, last, acc = refs
+    out, rows, parts, back, hat, work_a, work_b, last, acc, tails = refs
     count = beside.shape[0]
     pitch = ROWS + 1
-    tails = z_tails()
+    for step, tail in enumerate(z_tails()):
+        tails[step] = tail
     later = (below, above, low, high)
     firsts = all_rows(later, rows)
     offset = [0]
     for ref in later:
         offset.append(offset[-1] + spots_of(ref.shape[0]))
 
-    def one_density(place, carry):
-        def put(start, end, value):
-            hat[place, start:end] = value
-
-        densities(later, rows, firsts, place, parts, modes, put)
-        return carry
+    def put(start, end, value):
+        hat[start:end] = value
 
     def steps(place, half):
         part = pl.ds(half * SUB, SUB)
@@ -425,7 +420,7 @@
             which, at = place_of(x, y)
             if which < 2:
                 return beside[place, which * len(CORE) + at, part, :]
-            return hat[place, offset[which - 2] + at, part, :]
+            return hat[offset[which - 2] + at, part, :]
 
         for step in range(DEGREE):
             new = (work_a, work_b, work_a, None)[step]
@@ -450,7 +445,8 @@
                             last[CORE.index((x, y)), part, :] = value
                 here, pair_prev = ahead, pair
 
-    def one_source(place, carry):
+    for place in range(count):
+        densities(later, rows, firsts, place, parts, modes, put)
         for half in range(ROWS // SUB):
             steps(place, half)
         for at in range(len(CORE)):
@@ -459,12 +455,8 @@
         for at, (x, y) in enumerate(CORE):
             lanes = pl.ds((y - HALO) * pitch, ROWS)
             other = jnp.broadcast_to(own_rows[place, pl.ds(at, 1), :], (ROWS, LANES))
-            acc[x - HALO, lanes, :] = acc[x - HALO, lanes, :] + result[at] * other
-        return carry
-
-    lax.fori_loop(0, count, one_density, 0)
-    acc[...] = jnp.zeros(acc.shape, jnp.float32)
-    lax.fori_loop(0, count, one_source, 0)
+            value = result[at] * other
+            acc[x - HALO, lanes, :] = acc[x - HALO, lanes, :] + value if place else value
     for x in range(EDGE):
         for group in range(ROWS):
             tile = acc[x, pl.ds(group, EDGE, stride=pitch), :]
@@ -487,11 +479,12 @@
             pltpu.VMEM((count, rows, LANES), jnp.float32),
             pltpu.VMEM((cells, ROWS, 2 * LANES), jnp.bfloat16),
             pltpu.VMEM((len(CORE), ROWS, 2 * LANES), jnp.bfloat16),
-            pltpu.VMEM((count, cells, ROWS, LANES), jnp.float32),
+            pltpu.VMEM((cells, ROWS, LANES), jnp.float32),
             plane,
             plane,
             core,
             pltpu.VMEM((EDGE, EDGE * (ROWS + 1), LANES), jnp.float32),
+            pltpu.VMEM((DEGREE, SUB, LANES), jnp.float32),
         ],
         compiler_params=pltpu.CompilerParams(vmem_limit_bytes=24 * 2**20),
         name="fields",

time: 27.5 us -> 26.4 us (0.960)
  Pallas kernels: 8.85 us -> 7.11 us
  waiting for transfers between devices: 2.64 us -> 3.28 us
    pallas_call x1, Pallas kernels: 6.24 us -> 5.14 us  [fields(): pl.pallas_call(fields_kernel, out_shape=jax.ShapeDtypeStruct((EDGE, EDGE,...]
    ppermute x1, waiting for transfers between devices: 0.36 us -> 0.99 us  [exchange(): low = lax.ppermute(corner_low, both, diagonal(1, 1))]
    pallas_call x1, Pallas kernels: 1.99 us -> 1.36 us  [modes_of(): pl.pallas_call(modes_kernel, out_shape=[jax.ShapeDtypeStruct((count, cell...]
  transfers between devices with their start and end apart: 7 -> 7, of which waited for: 3 -> 3; matrix products, arithmetic and copies ran while one was open for 0% -> 0% of each run, Pallas kernels for 8% -> 6%
where the time goes in v11:
time: 26.4 us; the launch traced here: 26.2 us
  starting transfers between devices  14.1 us (53%)
  Pallas kernels  7.11 us (27%)
  waiting for transfers between devices  3.28 us (12%)
  local copies, waits for them, and re-layouts  1.03 us (4%)
  other arithmetic  0.7 us (3%)
    pallas_call x1, Pallas kernels, fields(): pl.pallas_call(fields_kernel, out_shape=jax.ShapeDtypeStruct((EDGE, EDGE,...  5.14 us
    ppermute x1, starting transfers between devices, exchange(): high = lax.ppermute(corner_high, both, diagonal(1, -1))  4.72 us
    ppermute x2, starting transfers between devices, gathered(): other = lax.ppermute(mine, 'orb', [(i, i ^ 1 << bit) for i in range(count)])  3.42 us
    ppermute x2, waiting for transfers between devices, gathered(): other = lax.ppermute(mine, 'orb', [(i, i ^ 1 << bit) for i in range(count)])  2.28 us
    ppermute x1, starting transfers between devices, exchange(): above = lax.ppermute(first, 'sy', ring('sy', -1))  2.25 us
    ppermute x1, starting transfers between devices, exchange(): across = lax.ppermute(block, 'sx', ring('sx', 1))  2.11 us
    ppermute x1, starting transfers between devices, exchange(): below = lax.ppermute(last, 'sy', ring('sy', 1))  1.58 us
    pallas_call x1, Pallas kernels, modes_of(): pl.pallas_call(modes_kernel, out_shape=[jax.ShapeDtypeStruct((count, cell...  1.36 us
  transfers between devices with their start and end apart: 7, of which 3 were waited for; matrix products, arithmetic and copies ran while one was open for 0% of the time, Pallas kernels for 6%

profile of v11, /device:TPU:0, one launch (start us, length us, event | category | flops | bytes accessed | tf_op | source)
XLA Modules:
  0.0 26.2 jit_solution(5220745595173595959)
XLA Ops:
  0.0 0.7 %pad_add_fusion = s32[2,2,2]{2,1,0:T(2,128)S(1)} fusion(s32[1,2,2]{2,1,0:T(2,128)} %bitcast.2, s32[1,2,2]{2,1,0:T(2,128)} %bitcast.3), kind=kLoop, calls=%fused_computation | loop fusion | flops 8 | bytes 64 | tf_op jit(solution)/shard_map/stack | solution.py:208
  0.7 0.1 broadcast_in_dim.3.entries
  0.8 0.0 copy-start
  0.8 1.0 %copy-done = bf16[8,8,2048]{2,1,0:T(8,128)(2,1)S(1)} copy-done((bf16[8,8,2048]{2,1,0:T(8,128)(2,1)S(1)}, bf16[8,8,2048]{2,1,0:T(8,128)(2,1)}, u32[]{:S(2)}) %copy-start) | copy-done | bytes 262168
  1.7 0.2 prepare.1
  2.0 0.5 %collective-permute-start = (bf16[4,16,128]{2,1,0:T(8,128)(2,1)S(1)}, bf16[4,16,128]{2,1,0:T(8,128)(2,1)S(1)}, u32[]{:S(2)}, u32[]{:S(2)}) collective-permute-start(bf16[4,16,128]{2,1,0:T(8,128)(2,1)S(1)} %get-tuple-element.14.mine), channel_id=1, source_target_pairs={{0,8},{8,0},{16,24},{24,16},{1,9},{9,1},{17,25},{25,17},{2,10},{10... | collective-permute-start | bytes 49160 | tf_op jit(solution)/shard_map/ppermute | solution.py:154
  2.5 0.8 %collective-permute-done.other = bf16[4,16,128]{2,1,0:T(8,128)(2,1)S(1)} collective-permute-done((bf16[4,16,128]{2,1,0:T(8,128)(2,1)S(1)}, bf16[4,16,128]{2,1,0:T(8,128)(2,1)S(1)}, u32[]{:S(2)}, u32[]{:S(2)}) %collective-permute-start) | collective-permute-done | bytes 16416 | tf_op jit(solution)/shard_map/ppermute | solution.py:154
  3.3 2.9 %collective-permute-start.1 = (bf16[4,16,128]{2,1,0:T(8,128)(2,1)S(1)}, bf16[4,16,128]{2,1,0:T(8,128)(2,1)S(1)}, u32[]{:S(2)}, u32[]{:S(2)}) collective-permute-start(bf16[4,16,128]{2,1,0:T(8,128)(2,1)S(1)} %nearer.1.after.mine), channel_id=1, source_target_pairs={{0,16},{8,24},{16,0},{24,8},{1,17},{9,25},{17,1},{25,9},{2,18},{10... | collective-permute-start | bytes 49160 | tf_op jit(solution)/shard_map/ppermute | solution.py:154
  6.2 0.3 %sines.1.before.modes = bf16[256,256]{1,0:T(8,128)(2,1)S(1)} custom-call(bf16[4,16,128]{2,1,0:T(8,128)(2,1)S(1)} %nearer.1.after.mine), custom_call_target="tpu_custom_call" | custom-call | bytes 2097152 | tf_op jit(solution)/shard_map/sines/pallas_call | solution.py:285
  6.5 1.4 %collective-permute-done.1.refs_0_ = bf16[4,16,128]{2,1,0:T(8,128)(2,1)S(1)} collective-permute-done((bf16[4,16,128]{2,1,0:T(8,128)(2,1)S(1)}, bf16[4,16,128]{2,1,0:T(8,128)(2,1)S(1)}, u32[]{:S(2)}, u32[]{:S(2)}) %collective-permute-start.1) | collective-permute-done | bytes 16416 | tf_op jit(solution)/shard_map/ppermute | solution.py:154
  8.0 0.1 messages.1
  8.0 2.1 %collective-permute-start.2 = (bf16[68,16,128]{2,1,0:T(8,128)(2,1)S(1)}, bf16[68,16,128]{2,1,0:T(8,128)(2,1)S(1)}, u32[]{:S(2)}, u32[]{:S(2)}) collective-permute-start(bf16[68,16,128]{2,1,0:T(8,128)(2,1)S(1)} %get-tuple-element.16.own), channel_id=1, source_target_pairs={{0,4},{4,0},{1,5},{5,1},{2,6},{6,2},{3,7},{7,3},{8,12},{12,8},{9,1... | collective-permute-start | bytes 835592 | tf_op jit(solution)/shard_map/ppermute | solution.py:231
  10.2 1.6 %collective-permute-start.3 = (bf16[34,16,128]{2,1,0:T(8,128)(2,1)S(1)}, bf16[34,16,128]{2,1,0:T(8,128)(2,1)S(1)}, u32[]{:S(2)}, u32[]{:S(2)}) collective-permute-start(bf16[34,16,128]{2,1,0:T(8,128)(2,1)S(1)} %get-tuple-element.19), channel_id=1, source_target_pairs={{0,1},{1,2},{2,3},{3,0},{4,5},{5,6},{6,7},{7,4},{8,9},{9,10},{10,1... | collective-permute-start | bytes 417800 | tf_op jit(solution)/shard_map/ppermute | solution.py:248
  11.7 2.2 %collective-permute-start.4 = (bf16[34,16,128]{2,1,0:T(8,128)(2,1)S(1)}, bf16[34,16,128]{2,1,0:T(8,128)(2,1)S(1)}, u32[]{:S(2)}, u32[]{:S(2)}) collective-permute-start(bf16[34,16,128]{2,1,0:T(8,128)(2,1)S(1)} %get-tuple-element.20), channel_id=1, source_target_pairs={{0,3},{1,0},{2,1},{3,2},{4,7},{5,4},{6,5},{7,6},{8,11},{9,8},{10,9... | collective-permute-start | bytes 417800 | tf_op jit(solution)/shard_map/ppermute | solution.py:249
  14.0 0.0 collective-permute-start.5
  14.0 4.7 %collective-permute-start.6 = (bf16[13,16,128]{2,1,0:T(8,128)(2,1)S(1)}, bf16[13,16,128]{2,1,0:T(8,128)(2,1)S(1)}, u32[]{:S(2)}, u32[]{:S(2)}) collective-permute-start(bf16[13,16,128]{2,1,0:T(8,128)(2,1)S(1)} %get-tuple-element.22), channel_id=1, source_target_pairs={{0,7},{1,4},{2,5},{3,6},{4,3},{5,0},{6,1},{7,2},{8,15},{9,12},{10,... | collective-permute-start | bytes 159752 | tf_op jit(solution)/shard_map/ppermute | solution.py:230
  18.7 0.0 collective-permute-done.2.across
  18.7 1.4 %modes.1 = (f32[4,128,16,128]{3,2,1,0:T(8,128)S(1)}, f32[4,64,128]{2,1,0:T(8,128)S(1)}) custom-call(bf16[68,16,128]{2,1,0:T(8,128)(2,1)S(1)} %get-tuple-element.16.own, bf16[68,16,128]{2,1,0:T(8,128)(2,1)S(1)} %collective-permute-done.2.across, bf16[256,256]{1,0:T(8,128)(2,1)S(1)} %sines.1.before.modes), custom_call_target="tpu_custom_call" | custom-call | bytes 6291456 | tf_op jit(solution)/shard_map/modes/pallas_call | solution.py:383
  20.1 1.0 %collective-permute-done.5.low = bf16[13,16,128]{2,1,0:T(8,128)(2,1)S(1)} collective-permute-done((bf16[13,16,128]{2,1,0:T(8,128)(2,1)S(1)}, bf16[13,16,128]{2,1,0:T(8,128)(2,1)S(1)}, u32[]{:S(2)}, u32[]{:S(2)}) %collective-permute-start.5) | collective-permute-done | bytes 53280 | tf_op jit(solution)/shard_map/ppermute | solution.py:229
  21.1 0.0 collective-permute-done.6.high
  21.1 0.0 collective-permute-done.3.below
  21.1 0.0 collective-permute-done.4.above
  21.1 5.1 %fields.1 = f32[8,8,2048]{2,1,0:T(8,128)} custom-call(f32[4,128,16,128]{3,2,1,0:T(8,128)S(1)} %get-tuple-element.17.beside, f32[4,64,128]{2,1,0:T(8,128)S(1)} %get-tuple-element.18.own_rows, bf16[34,16,128]{2,1,0:T(8,128)(2,1)S(1)} %collective-permute-done.3.below, bf16[34,16,128]{2,1,0:T(8,128)(2,1)S(1)} %collective-permute-done.4.above, ...), custom_call_target="tpu_custom_call" | custom-call | tf_op jit(solution)/shard_map/fields/pallas_call | solution.py:473
  (1 shorter events, 0.0 us)
Async XLA Ops:
  0.8 1.0 %copy-start = (bf16[8,8,2048]{2,1,0:T(8,128)(2,1)S(1)}, bf16[8,8,2048]{2,1,0:T(8,128)(2,1)}, u32[]{:S(2)}) copy-start(bf16[8,8,2048]{2,1,0:T(8,128)(2,1)} %orbitals.1) | copy-start | bytes 786436
  2.0 1.4 %collective-permute-start = (bf16[4,16,128]{2,1,0:T(8,128)(2,1)S(1)}, bf16[4,16,128]{2,1,0:T(8,128)(2,1)S(1)}, u32[]{:S(2)}, u32[]{:S(2)}) collective-permute-start(bf16[4,16,128]{2,1,0:T(8,128)(2,1)S(1)} %get-tuple-element.14.mine), channel_id=1, source_target_pairs={{0,8},{8,0},{16,24},{24,16},{1,9},{9,1},{17,25},{25,17},{2,10},{10... | collective-permute-start | bytes 49160 | tf_op jit(solution)/shard_map/ppermute | solution.py:154
  3.3 4.6 %collective-permute-start.1 = (bf16[4,16,128]{2,1,0:T(8,128)(2,1)S(1)}, bf16[4,16,128]{2,1,0:T(8,128)(2,1)S(1)}, u32[]{:S(2)}, u32[]{:S(2)}) collective-permute-start(bf16[4,16,128]{2,1,0:T(8,128)(2,1)S(1)} %nearer.1.after.mine), channel_id=1, source_target_pairs={{0,16},{8,24},{16,0},{24,8},{1,17},{9,25},{17,1},{25,9},{2,18},{10... | collective-permute-start | bytes 49160 | tf_op jit(solution)/shard_map/ppermute | solution.py:154
  8.0 10.7 %collective-permute-start.2 = (bf16[68,16,128]{2,1,0:T(8,128)(2,1)S(1)}, bf16[68,16,128]{2,1,0:T(8,128)(2,1)S(1)}, u32[]{:S(2)}, u32[]{:S(2)}) collective-permute-start(bf16[68,16,128]{2,1,0:T(8,128)(2,1)S(1)} %get-tuple-element.16.own), channel_id=1, source_target_pairs={{0,4},{4,0},{1,5},{5,1},{2,6},{6,2},{3,7},{7,3},{8,12},{12,8},{9,1... | collective-permute-start | bytes 835592 | tf_op jit(solution)/shard_map/ppermute | solution.py:231
  10.2 10.9 %collective-permute-start.3 = (bf16[34,16,128]{2,1,0:T(8,128)(2,1)S(1)}, bf16[34,16,128]{2,1,0:T(8,128)(2,1)S(1)}, u32[]{:S(2)}, u32[]{:S(2)}) collective-permute-start(bf16[34,16,128]{2,1,0:T(8,128)(2,1)S(1)} %get-tuple-element.19), channel_id=1, source_target_pairs={{0,1},{1,2},{2,3},{3,0},{4,5},{5,6},{6,7},{7,4},{8,9},{9,10},{10,1... | collective-permute-start | bytes 417800 | tf_op jit(solution)/shard_map/ppermute | solution.py:248
  11.7 9.3 %collective-permute-start.4 = (bf16[34,16,128]{2,1,0:T(8,128)(2,1)S(1)}, bf16[34,16,128]{2,1,0:T(8,128)(2,1)S(1)}, u32[]{:S(2)}, u32[]{:S(2)}) collective-permute-start(bf16[34,16,128]{2,1,0:T(8,128)(2,1)S(1)} %get-tuple-element.20), channel_id=1, source_target_pairs={{0,3},{1,0},{2,1},{3,2},{4,7},{5,4},{6,5},{7,6},{8,11},{9,8},{10,9... | collective-permute-start | bytes 417800 | tf_op jit(solution)/shard_map/ppermute | solution.py:249
  14.0 7.1 %collective-permute-start.5 = (bf16[13,16,128]{2,1,0:T(8,128)(2,1)S(1)}, bf16[13,16,128]{2,1,0:T(8,128)(2,1)S(1)}, u32[]{:S(2)}, u32[]{:S(2)}) collective-permute-start(bf16[13,16,128]{2,1,0:T(8,128)(2,1)S(1)} %get-tuple-element.21), channel_id=1, source_target_pairs={{0,5},{1,6},{2,7},{3,4},{4,1},{5,2},{6,3},{7,0},{8,13},{9,14},{10,... | collective-permute-start | bytes 159752 | tf_op jit(solution)/shard_map/ppermute | solution.py:229
  14.0 7.1 %collective-permute-start.6 = (bf16[13,16,128]{2,1,0:T(8,128)(2,1)S(1)}, bf16[13,16,128]{2,1,0:T(8,128)(2,1)S(1)}, u32[]{:S(2)}, u32[]{:S(2)}) collective-permute-start(bf16[13,16,128]{2,1,0:T(8,128)(2,1)S(1)} %get-tuple-element.22), channel_id=1, source_target_pairs={{0,7},{1,4},{2,5},{3,6},{4,3},{5,0},{6,1},{7,2},{8,15},{9,12},{10,... | collective-permute-start | bytes 159752 | tf_op jit(solution)/shard_map/ppermute | solution.py:230

commit v12 on v11

--- a/solution.py
+++ b/solution.py
@@ -366,31 +366,82 @@
     return firsts
 
 
-def modes_kernel(own, across, modes, hat, own_rows, rows, parts):
+def early(step):
+    cells = [
+        (x, y)
+        for x in range(1 + step, SIZE - 1 - step)
+        for y in range(HALO + 1 + step, HALO + EDGE - 1 - step)
+    ]
+    return {cell: at for at, cell in enumerate(cells)}
+
+
+EARLY = [early(step) for step in range(DEGREE - 1)]
+
+
+def one_step(targets, old, tail, density, put):
+    pairs = targets | {(x - 1, y - 1) for x, y in targets}
+    wanted = {(x + 1, y) for x, y in pairs} | {(x, y + 1) for x, y in pairs}
+    loaded, summed = {}, {}
+    rows = sorted({x for x, _ in pairs})
+    for x in rows:
+        for cell in sorted(cell for cell in wanted if cell[0] in (x, x + 1)):
+            if cell not in loaded:
+                loaded[cell] = old(*cell)
+        for y in range(SIZE):
+            if (x, y) in pairs:
+                summed[x, y] = loaded[x + 1, y] + loaded[x, y + 1]
+            if (x, y) in targets:
+                here = loaded.get((x, y)) if old is density else None
+                here = density(x, y) if here is None else here
+                put(x, y, summed[x, y] + summed[x - 1, y - 1] + tail[...] * here)
+
+
+def modes_kernel(own, across, modes, hat, own_rows, *refs):
+    stages, (rows, parts, tails) = refs[: DEGREE - 1], refs[DEGREE - 1 :]
+    for step, tail in enumerate(z_tails()):
+        tails[step] = tail
     firsts = all_rows((own, across), rows)
     own_rows[...] = rows[:, : own_rows.shape[1], :]
-
     for place in range(hat.shape[0]):
 
         def put(start, end, value, place=place):
             hat[place, start:end] = value
 
         densities((own, across), rows, firsts, place, parts, modes, put)
+        for half in range(ROWS // SUB):
+            part = pl.ds(half * SUB, SUB)
+
+            def start(x, y, place=place, part=part):
+                which, at = place_of(x, y)
+                return hat[place, which * len(CORE) + at, part, :]
+
+            old = start
+            for step, stage in enumerate(stages):
+
+                def load(x, y, place=place, part=part, stage=stage, step=step):
+                    return stage[place, EARLY[step][x, y], part, :]
+
+                def store(x, y, value, place=place, part=part, stage=stage, step=step):
+                    stage[place, EARLY[step][x, y], part, :] = value
+
+                one_step(set(EARLY[step]), old, tails.at[step], start, store)
+                old = load
 
 
 def modes_of(own, across, modes, count):
     cells = 2 * len(CORE)
+    lengths = [cells] + [len(stage) for stage in EARLY]
+    shapes = [(count, length, ROWS, LANES) for length in lengths]
+    shapes.insert(1, (count, len(CORE), LANES))
     return pl.pallas_call(
         modes_kernel,
-        out_shape=[
-            jax.ShapeDtypeStruct((count, cells, ROWS, LANES), jnp.float32),
-            jax.ShapeDtypeStruct((count, len(CORE), LANES), jnp.float32),
-        ],
+        out_shape=[jax.ShapeDtypeStruct(shape, jnp.float32) for shape in shapes],
         in_specs=[VMEM] * 3,
-        out_specs=[VMEM] * 2,
+        out_specs=[VMEM] * len(shapes),
         scratch_shapes=[
             pltpu.VMEM((count, cells, LANES), jnp.float32),
             pltpu.VMEM((cells, ROWS, 2 * LANES), jnp.bfloat16),
+            pltpu.VMEM((DEGREE, SUB, LANES), jnp.float32),
         ],
         compiler_params=pltpu.CompilerParams(vmem_limit_bytes=20 * 2**20),
         cost_estimate=pl.CostEstimate(flops=0, bytes_accessed=6 * 2**20, transcendentals=0),
@@ -398,8 +449,9 @@
     )(own, across, modes)
 
 
-def fields_kernel(beside, own_rows, below, above, low, high, modes, *refs):
-    out, rows, parts, back, hat, work_a, work_b, last, acc, tails = refs
+def fields_kernel(beside, own_rows, *refs):
+    stages, (below, above, low, high, modes, out) = refs[: DEGREE - 1], refs[DEGREE - 1 :][:6]
+    rows, parts, back, hat, work_a, work_b, last, acc, tails = refs[DEGREE + 5 :]
     count = beside.shape[0]
     pitch = ROWS + 1
     for step, tail in enumerate(z_tails()):
@@ -422,28 +474,25 @@
                 return beside[place, which * len(CORE) + at, part, :]
             return hat[offset[which - 2] + at, part, :]
 
+        old = start
         for step in range(DEGREE):
             new = (work_a, work_b, work_a, None)[step]
-            old = (None, work_a, work_b, work_a)[step]
-            targets, known = within(HALO - 1 - step), within(HALO - step)
-
-            def load(x):
-                return {y: start(x, y) if old is None else old[x, y] for y in known[x]}
-
-            here, pair_prev = load(step), {}
-            for x in range(step, SIZE - 1 - step):
-                ahead, pair = load(x + 1), {}
-                for y in range(SIZE - 1):
-                    if y in targets[x] or y + 1 in targets[x + 1]:
-                        pair[y] = ahead[y] + here[y + 1]
-                    if y in targets[x]:
-                        density = here[y] if old is None else start(x, y)
-                        value = pair[y] + pair_prev[y - 1] + tails[step] * density
-                        if new is not None:
-                            new[x, y] = value
-                        else:
-                            last[CORE.index((x, y)), part, :] = value
-                here, pair_prev = ahead, pair
+            ready = EARLY[step] if step < DEGREE - 1 else {}
+
+            def load(x, y, new=new, step=step, ready=ready):
+                if (x, y) in ready:
+                    return stages[step][place, ready[x, y], part, :]
+                return new[x, y]
+
+            def store(x, y, value, new=new):
+                if new is None:
+                    last[CORE.index((x, y)), part, :] = value
+                else:
+                    new[x, y] = value
+
+            cells = {(x, y) for x in range(SIZE) for y in within(HALO - 1 - step)[x]}
+            one_step(cells - set(ready), old, tails.at[step], start, store)
+            old = load
 
     for place in range(count):
         densities(later, rows, firsts, place, parts, modes, put)
@@ -465,7 +514,7 @@
 
 def fields(halo, modes, count):
     own, across, *later = halo
-    beside, own_rows = modes_of(own, across, modes, count)
+    beside, own_rows, *stages = modes_of(own, across, modes, count)
     plane = pltpu.VMEM((SIZE, SIZE, SUB, LANES), jnp.float32)
     core = pltpu.VMEM((len(CORE), ROWS, LANES), jnp.float32)
     cells = sum(spots_of(array.shape[0]) for array in later)
@@ -473,7 +522,7 @@
     return pl.pallas_call(
         fields_kernel,
         out_shape=jax.ShapeDtypeStruct((EDGE, EDGE, ROWS * LANES), jnp.float32),
-        in_specs=[VMEM] * 7,
+        in_specs=[VMEM] * (7 + len(stages)),
         out_specs=VMEM,
         scratch_shapes=[
             pltpu.VMEM((count, rows, LANES), jnp.float32),
@@ -488,7 +537,7 @@
         ],
         compiler_params=pltpu.CompilerParams(vmem_limit_bytes=24 * 2**20),
         name="fields",
-    )(beside, own_rows, *later, modes)
+    )(beside, own_rows, *stages, *later, modes)
 
 
 def body(orbitals, src_owner, src_slot):

time: 26.4 us -> 25.5 us (0.966)
  waiting for transfers between devices: 3.28 us -> 2.49 us
    pallas_call x1, Pallas kernels: 5.14 us -> 4.3 us  [fields(): pl.pallas_call(fields_kernel, out_shape=jax.ShapeDtypeStruct((EDGE, EDGE,...]
    ppermute x1, waiting for transfers between devices: 0.99 us -> 0.2 us  [exchange(): low = lax.ppermute(corner_low, both, diagonal(1, 1))]
    pallas_call x1, Pallas kernels: 1.36 us -> 2.15 us  [modes_of(): pl.pallas_call(modes_kernel, out_shape=[jax.ShapeDtypeStruct(shape, jnp.f...]
  transfers between devices with their start and end apart: 7 -> 7, of which waited for: 3 -> 3; matrix products, arithmetic and copies ran while one was open for 0% -> 0% of each run, Pallas kernels for 6% -> 10%
where the time goes in v12:
time: 25.5 us; the launch traced here: 25.4 us
  starting transfers between devices  14.1 us (55%)
  Pallas kernels  7.06 us (28%)
  waiting for transfers between devices  2.49 us (10%)
  local copies, waits for them, and re-layouts  1.03 us (4%)
  other arithmetic  0.7 us (3%)
    ppermute x1, starting transfers between devices, exchange(): high = lax.ppermute(corner_high, both, diagonal(1, -1))  4.72 us
    pallas_call x1, Pallas kernels, fields(): pl.pallas_call(fields_kernel, out_shape=jax.ShapeDtypeStruct((EDGE, EDGE,...  4.3 us
    ppermute x2, starting transfers between devices, gathered(): other = lax.ppermute(mine, 'orb', [(i, i ^ 1 << bit) for i in range(count)])  3.42 us
    ppermute x2, waiting for transfers between devices, gathered(): other = lax.ppermute(mine, 'orb', [(i, i ^ 1 << bit) for i in range(count)])  2.28 us
    ppermute x1, starting transfers between devices, exchange(): above = lax.ppermute(first, 'sy', ring('sy', -1))  2.25 us
    pallas_call x1, Pallas kernels, modes_of(): pl.pallas_call(modes_kernel, out_shape=[jax.ShapeDtypeStruct(shape, jnp.f...  2.15 us
    ppermute x1, starting transfers between devices, exchange(): across = lax.ppermute(block, 'sx', ring('sx', 1))  2.11 us
    ppermute x1, starting transfers between devices, exchange(): below = lax.ppermute(last, 'sy', ring('sy', 1))  1.58 us
  transfers between devices with their start and end apart: 7, of which 3 were waited for; matrix products, arithmetic and copies ran while one was open for 0% of the time, Pallas kernels for 10%

profile of v12, /device:TPU:0, one launch (start us, length us, event | category | flops | bytes accessed | tf_op | source)
XLA Modules:
  0.0 25.4 jit_solution(15232874941183110668)
XLA Ops:
  0.0 0.7 %pad_add_fusion = s32[2,2,2]{2,1,0:T(2,128)S(1)} fusion(s32[1,2,2]{2,1,0:T(2,128)} %bitcast.2, s32[1,2,2]{2,1,0:T(2,128)} %bitcast.3), kind=kLoop, calls=%fused_computation | loop fusion | flops 8 | bytes 64 | tf_op jit(solution)/shard_map/stack | solution.py:208
  0.7 0.1 broadcast_in_dim.3.entries
  0.8 0.0 copy-start
  0.8 1.0 %copy-done = bf16[8,8,2048]{2,1,0:T(8,128)(2,1)S(1)} copy-done((bf16[8,8,2048]{2,1,0:T(8,128)(2,1)S(1)}, bf16[8,8,2048]{2,1,0:T(8,128)(2,1)}, u32[]{:S(2)}) %copy-start) | copy-done | bytes 262168
  1.7 0.2 prepare.1
  2.0 0.5 %collective-permute-start = (bf16[4,16,128]{2,1,0:T(8,128)(2,1)S(1)}, bf16[4,16,128]{2,1,0:T(8,128)(2,1)S(1)}, u32[]{:S(2)}, u32[]{:S(2)}) collective-permute-start(bf16[4,16,128]{2,1,0:T(8,128)(2,1)S(1)} %get-tuple-element.17.mine), channel_id=1, source_target_pairs={{0,8},{8,0},{16,24},{24,16},{1,9},{9,1},{17,25},{25,17},{2,10},{10... | collective-permute-start | bytes 49160 | tf_op jit(solution)/shard_map/ppermute | solution.py:154
  2.5 0.8 %collective-permute-done.other = bf16[4,16,128]{2,1,0:T(8,128)(2,1)S(1)} collective-permute-done((bf16[4,16,128]{2,1,0:T(8,128)(2,1)S(1)}, bf16[4,16,128]{2,1,0:T(8,128)(2,1)S(1)}, u32[]{:S(2)}, u32[]{:S(2)}) %collective-permute-start) | collective-permute-done | bytes 16416 | tf_op jit(solution)/shard_map/ppermute | solution.py:154
  3.3 2.9 %collective-permute-start.1 = (bf16[4,16,128]{2,1,0:T(8,128)(2,1)S(1)}, bf16[4,16,128]{2,1,0:T(8,128)(2,1)S(1)}, u32[]{:S(2)}, u32[]{:S(2)}) collective-permute-start(bf16[4,16,128]{2,1,0:T(8,128)(2,1)S(1)} %nearer.1.after.mine), channel_id=1, source_target_pairs={{0,16},{8,24},{16,0},{24,8},{1,17},{9,25},{17,1},{25,9},{2,18},{10... | collective-permute-start | bytes 49160 | tf_op jit(solution)/shard_map/ppermute | solution.py:154
  6.2 0.3 %sines.1.before.modes.refs_7_ = bf16[256,256]{1,0:T(8,128)(2,1)S(1)} custom-call(bf16[4,16,128]{2,1,0:T(8,128)(2,1)S(1)} %nearer.1.after.mine), custom_call_target="tpu_custom_call" | custom-call | bytes 2097152 | tf_op jit(solution)/shard_map/sines/pallas_call | solution.py:285
  6.5 1.4 %collective-permute-done.1.refs_0_ = bf16[4,16,128]{2,1,0:T(8,128)(2,1)S(1)} collective-permute-done((bf16[4,16,128]{2,1,0:T(8,128)(2,1)S(1)}, bf16[4,16,128]{2,1,0:T(8,128)(2,1)S(1)}, u32[]{:S(2)}, u32[]{:S(2)}) %collective-permute-start.1) | collective-permute-done | bytes 16416 | tf_op jit(solution)/shard_map/ppermute | solution.py:154
  8.0 0.1 messages.1
  8.0 2.1 %collective-permute-start.2 = (bf16[68,16,128]{2,1,0:T(8,128)(2,1)S(1)}, bf16[68,16,128]{2,1,0:T(8,128)(2,1)S(1)}, u32[]{:S(2)}, u32[]{:S(2)}) collective-permute-start(bf16[68,16,128]{2,1,0:T(8,128)(2,1)S(1)} %get-tuple-element.19.own), channel_id=1, source_target_pairs={{0,4},{4,0},{1,5},{5,1},{2,6},{6,2},{3,7},{7,3},{8,12},{12,8},{9,1... | collective-permute-start | bytes 835592 | tf_op jit(solution)/shard_map/ppermute | solution.py:231
  10.2 1.6 %collective-permute-start.3 = (bf16[34,16,128]{2,1,0:T(8,128)(2,1)S(1)}, bf16[34,16,128]{2,1,0:T(8,128)(2,1)S(1)}, u32[]{:S(2)}, u32[]{:S(2)}) collective-permute-start(bf16[34,16,128]{2,1,0:T(8,128)(2,1)S(1)} %get-tuple-element.25), channel_id=1, source_target_pairs={{0,1},{1,2},{2,3},{3,0},{4,5},{5,6},{6,7},{7,4},{8,9},{9,10},{10,1... | collective-permute-start | bytes 417800 | tf_op jit(solution)/shard_map/ppermute | solution.py:248
  11.7 2.2 %collective-permute-start.4 = (bf16[34,16,128]{2,1,0:T(8,128)(2,1)S(1)}, bf16[34,16,128]{2,1,0:T(8,128)(2,1)S(1)}, u32[]{:S(2)}, u32[]{:S(2)}) collective-permute-start(bf16[34,16,128]{2,1,0:T(8,128)(2,1)S(1)} %get-tuple-element.26), channel_id=1, source_target_pairs={{0,3},{1,0},{2,1},{3,2},{4,7},{5,4},{6,5},{7,6},{8,11},{9,8},{10,9... | collective-permute-start | bytes 417800 | tf_op jit(solution)/shard_map/ppermute | solution.py:249
  14.0 0.0 collective-permute-start.5
  14.0 4.7 %collective-permute-start.6 = (bf16[13,16,128]{2,1,0:T(8,128)(2,1)S(1)}, bf16[13,16,128]{2,1,0:T(8,128)(2,1)S(1)}, u32[]{:S(2)}, u32[]{:S(2)}) collective-permute-start(bf16[13,16,128]{2,1,0:T(8,128)(2,1)S(1)} %get-tuple-element.28), channel_id=1, source_target_pairs={{0,7},{1,4},{2,5},{3,6},{4,3},{5,0},{6,1},{7,2},{8,15},{9,12},{10,... | collective-permute-start | bytes 159752 | tf_op jit(solution)/shard_map/ppermute | solution.py:230
  18.7 0.0 collective-permute-done.2.across
  18.7 2.1 %modes.1 = (f32[4,128,16,128]{3,2,1,0:T(8,128)S(1)}, f32[4,64,128]{2,1,0:T(8,128)S(1)}, f32[4,84,16,128]{3,2,1,0:T(8,128)S(1)}, f32[4,48,16,128]{3,2,1,0:T(8,128)S(1)}, f32[4,20,16,128]{3,2,1,0:T(8,128)S(1)}) custom-call(bf16[68,16,128]{2,1,0:T(8,128)(2,1)S(1)} %get-tuple-element.19.own, bf16[68,16,128]{2,1,0:T(8,128)(2,1)S(1)} %collective-permute-done.2.across, ...), custom_call_target="tpu_custom_call" | custom-call | bytes 6291456 | tf_op jit(solution)/shard_map/modes/pallas_call | solution.py:436
  20.9 0.2 collective-permute-done.5.refs_5_
  21.1 0.0 collective-permute-done.6.refs_6_
  21.1 0.0 collective-permute-done.3.refs_3_
  21.1 0.0 collective-permute-done.4.refs_4_
  21.1 4.3 %fields.1 = f32[8,8,2048]{2,1,0:T(8,128)} custom-call(f32[4,128,16,128]{3,2,1,0:T(8,128)S(1)} %get-tuple-element.20.beside, f32[4,64,128]{2,1,0:T(8,128)S(1)} %get-tuple-element.21.own_rows, f32[4,84,16,128]{3,2,1,0:T(8,128)S(1)} %get-tuple-element.22.refs_0_, f32[4,48,16,128]{3,2,1,0:T(8,128)S(1)} %get-tuple-element.23.refs_1_, ...), custom_call_target="tpu_custom_call" | custom-call | tf_op jit(solution)/shard_map/fields/pallas_call | solution.py:522
  (1 shorter events, 0.0 us)
Async XLA Ops:
  0.8 1.0 %copy-start = (bf16[8,8,2048]{2,1,0:T(8,128)(2,1)S(1)}, bf16[8,8,2048]{2,1,0:T(8,128)(2,1)}, u32[]{:S(2)}) copy-start(bf16[8,8,2048]{2,1,0:T(8,128)(2,1)} %orbitals.1) | copy-start | bytes 786436
  2.0 1.4 %collective-permute-start = (bf16[4,16,128]{2,1,0:T(8,128)(2,1)S(1)}, bf16[4,16,128]{2,1,0:T(8,128)(2,1)S(1)}, u32[]{:S(2)}, u32[]{:S(2)}) collective-permute-start(bf16[4,16,128]{2,1,0:T(8,128)(2,1)S(1)} %get-tuple-element.17.mine), channel_id=1, source_target_pairs={{0,8},{8,0},{16,24},{24,16},{1,9},{9,1},{17,25},{25,17},{2,10},{10... | collective-permute-start | bytes 49160 | tf_op jit(solution)/shard_map/ppermute | solution.py:154
  3.3 4.6 %collective-permute-start.1 = (bf16[4,16,128]{2,1,0:T(8,128)(2,1)S(1)}, bf16[4,16,128]{2,1,0:T(8,128)(2,1)S(1)}, u32[]{:S(2)}, u32[]{:S(2)}) collective-permute-start(bf16[4,16,128]{2,1,0:T(8,128)(2,1)S(1)} %nearer.1.after.mine), channel_id=1, source_target_pairs={{0,16},{8,24},{16,0},{24,8},{1,17},{9,25},{17,1},{25,9},{2,18},{10... | collective-permute-start | bytes 49160 | tf_op jit(solution)/shard_map/ppermute | solution.py:154
  8.0 10.7 %collective-permute-start.2 = (bf16[68,16,128]{2,1,0:T(8,128)(2,1)S(1)}, bf16[68,16,128]{2,1,0:T(8,128)(2,1)S(1)}, u32[]{:S(2)}, u32[]{:S(2)}) collective-permute-start(bf16[68,16,128]{2,1,0:T(8,128)(2,1)S(1)} %get-tuple-element.19.own), channel_id=1, source_target_pairs={{0,4},{4,0},{1,5},{5,1},{2,6},{6,2},{3,7},{7,3},{8,12},{12,8},{9,1... | collective-permute-start | bytes 835592 | tf_op jit(solution)/shard_map/ppermute | solution.py:231
  10.2 10.9 %collective-permute-start.3 = (bf16[34,16,128]{2,1,0:T(8,128)(2,1)S(1)}, bf16[34,16,128]{2,1,0:T(8,128)(2,1)S(1)}, u32[]{:S(2)}, u32[]{:S(2)}) collective-permute-start(bf16[34,16,128]{2,1,0:T(8,128)(2,1)S(1)} %get-tuple-element.25), channel_id=1, source_target_pairs={{0,1},{1,2},{2,3},{3,0},{4,5},{5,6},{6,7},{7,4},{8,9},{9,10},{10,1... | collective-permute-start | bytes 417800 | tf_op jit(solution)/shard_map/ppermute | solution.py:248
  11.7 9.3 %collective-permute-start.4 = (bf16[34,16,128]{2,1,0:T(8,128)(2,1)S(1)}, bf16[34,16,128]{2,1,0:T(8,128)(2,1)S(1)}, u32[]{:S(2)}, u32[]{:S(2)}) collective-permute-start(bf16[34,16,128]{2,1,0:T(8,128)(2,1)S(1)} %get-tuple-element.26), channel_id=1, source_target_pairs={{0,3},{1,0},{2,1},{3,2},{4,7},{5,4},{6,5},{7,6},{8,11},{9,8},{10,9... | collective-permute-start | bytes 417800 | tf_op jit(solution)/shard_map/ppermute | solution.py:249
  14.0 7.1 %collective-permute-start.5 = (bf16[13,16,128]{2,1,0:T(8,128)(2,1)S(1)}, bf16[13,16,128]{2,1,0:T(8,128)(2,1)S(1)}, u32[]{:S(2)}, u32[]{:S(2)}) collective-permute-start(bf16[13,16,128]{2,1,0:T(8,128)(2,1)S(1)} %get-tuple-element.27), channel_id=1, source_target_pairs={{0,5},{1,6},{2,7},{3,4},{4,1},{5,2},{6,3},{7,0},{8,13},{9,14},{10,... | collective-permute-start | bytes 159752 | tf_op jit(solution)/shard_map/ppermute | solution.py:229
  14.0 7.1 %collective-permute-start.6 = (bf16[13,16,128]{2,1,0:T(8,128)(2,1)S(1)}, bf16[13,16,128]{2,1,0:T(8,128)(2,1)S(1)}, u32[]{:S(2)}, u32[]{:S(2)}) collective-permute-start(bf16[13,16,128]{2,1,0:T(8,128)(2,1)S(1)} %get-tuple-element.28), channel_id=1, source_target_pairs={{0,7},{1,4},{2,5},{3,6},{4,3},{5,0},{6,1},{7,2},{8,15},{9,12},{10,... | collective-permute-start | bytes 159752 | tf_op jit(solution)/shard_map/ppermute | solution.py:230

commit v13 on v12

--- a/solution.py
+++ b/solution.py
@@ -343,7 +343,9 @@
     return (both[:, :LANES] + both[:, LANES:]).reshape(cells, ROWS, LANES)
 
 
-def densities(refs, rows, firsts, place, parts, modes, put):
+def densities(refs, rows, parts, modes, hat):
+    count = hat.shape[0]
+    firsts = all_rows(refs, rows)
     cells = [
         (ref, at, first + at)
         for ref, first in zip(refs, firsts)
@@ -354,9 +356,12 @@
         start, end = (len(cells) * at // pieces for at in (piece, piece + 1))
         for number in range(start, end):
             ref, at, row = cells[number]
-            other = jnp.broadcast_to(rows[place, pl.ds(row, 1), :], (ROWS, LANES))
-            keep(parts, number, ref[at].astype(jnp.float32) * other)
-        put(start, end, turned(parts, start, end, modes))
+            value = ref[at].astype(jnp.float32)
+            for place in range(count):
+                other = jnp.broadcast_to(rows[place, pl.ds(row, 1), :], (ROWS, LANES))
+                keep(parts.at[place], number, value * other)
+        for place in range(count):
+            hat[place, start:end] = turned(parts.at[place], start, end, modes)
 
 
 def all_rows(refs, rows):
@@ -400,14 +405,9 @@
     stages, (rows, parts, tails) = refs[: DEGREE - 1], refs[DEGREE - 1 :]
     for step, tail in enumerate(z_tails()):
         tails[step] = tail
-    firsts = all_rows((own, across), rows)
-    own_rows[...] = rows[:, : own_rows.shape[1], :]
+    densities((own, across), rows, parts, modes, hat)
+    own_rows[...] = rows[:, : own_rows.shape[1], :] * (-power_coeffs()[-1])
     for place in range(hat.shape[0]):
-
-        def put(start, end, value, place=place):
-            hat[place, start:end] = value
-
-        densities((own, across), rows, firsts, place, parts, modes, put)
         for half in range(ROWS // SUB):
             part = pl.ds(half * SUB, SUB)
 
@@ -440,7 +440,7 @@
         out_specs=[VMEM] * len(shapes),
         scratch_shapes=[
             pltpu.VMEM((count, cells, LANES), jnp.float32),
-            pltpu.VMEM((cells, ROWS, 2 * LANES), jnp.bfloat16),
+            pltpu.VMEM((count, cells, ROWS, 2 * LANES), jnp.bfloat16),
             pltpu.VMEM((DEGREE, SUB, LANES), jnp.float32),
         ],
         compiler_params=pltpu.CompilerParams(vmem_limit_bytes=20 * 2**20),
@@ -451,19 +451,16 @@
 
 def fields_kernel(beside, own_rows, *refs):
     stages, (below, above, low, high, modes, out) = refs[: DEGREE - 1], refs[DEGREE - 1 :][:6]
-    rows, parts, back, hat, work_a, work_b, last, acc, tails = refs[DEGREE + 5 :]
+    rows, parts, back, hat, work_a, work_b, last, acc, held, tails, sems = refs[DEGREE + 5 :]
     count = beside.shape[0]
     pitch = ROWS + 1
     for step, tail in enumerate(z_tails()):
         tails[step] = tail
     later = (below, above, low, high)
-    firsts = all_rows(later, rows)
     offset = [0]
     for ref in later:
         offset.append(offset[-1] + spots_of(ref.shape[0]))
-
-    def put(start, end, value):
-        hat[start:end] = value
+    densities(later, rows, parts, modes, hat)
 
     def steps(place, half):
         part = pl.ds(half * SUB, SUB)
@@ -472,7 +469,7 @@
             which, at = place_of(x, y)
             if which < 2:
                 return beside[place, which * len(CORE) + at, part, :]
-            return hat[offset[which - 2] + at, part, :]
+            return hat[place, offset[which - 2] + at, part, :]
 
         old = start
         for step in range(DEGREE):
@@ -486,7 +483,7 @@
 
             def store(x, y, value, new=new):
                 if new is None:
-                    last[CORE.index((x, y)), part, :] = value
+                    last[place, CORE.index((x, y)), part, :] = value
                 else:
                     new[x, y] = value
 
@@ -495,45 +492,59 @@
             old = load
 
     for place in range(count):
-        densities(later, rows, firsts, place, parts, modes, put)
         for half in range(ROWS // SUB):
             steps(place, half)
-        for at in range(len(CORE)):
-            keep(back, at, last[at])
-        result = turned(back, 0, len(CORE), modes)
-        for at, (x, y) in enumerate(CORE):
-            lanes = pl.ds((y - HALO) * pitch, ROWS)
-            other = jnp.broadcast_to(own_rows[place, pl.ds(at, 1), :], (ROWS, LANES))
-            value = result[at] * other
-            acc[x - HALO, lanes, :] = acc[x - HALO, lanes, :] + value if place else value
-    for x in range(EDGE):
-        for group in range(ROWS):
-            tile = acc[x, pl.ds(group, EDGE, stride=pitch), :]
-            out[x, :, pl.ds(group * LANES, LANES)] = tile * (-power_coeffs()[-1])
+    copies = []
+    for first in range(0, EDGE, 2):
+        spots = range(first * EDGE, (first + 2) * EDGE)
+        for place in range(count):
+            for at, spot in enumerate(spots):
+                keep(back, place * len(spots) + at, last[place, spot])
+        result = turned(back, 0, count * len(spots), modes)
+        for at, spot in enumerate(spots):
+            total = None
+            for place in range(count):
+                other = jnp.broadcast_to(own_rows[place, pl.ds(spot, 1), :], (ROWS, LANES))
+                value = result[place * len(spots) + at] * other
+                total = value if total is None else total + value
+            acc[spot // EDGE, pl.ds(spot % EDGE * pitch, ROWS), :] = total
+        for x in range(first, first + 2):
+            for group in range(ROWS):
+                tile = acc[x, pl.ds(group, EDGE, stride=pitch), :]
+                held[x, :, pl.ds(group * LANES, LANES)] = tile
+        rows_x = pl.ds(first, 2)
+        copies.append(
+            pltpu.make_async_copy(held.at[rows_x], out.at[rows_x], sems.at[first // 2])
+        )
+        copies[-1].start()
+    for copy in copies:
+        copy.wait()
 
 
 def fields(halo, modes, count):
     own, across, *later = halo
     beside, own_rows, *stages = modes_of(own, across, modes, count)
     plane = pltpu.VMEM((SIZE, SIZE, SUB, LANES), jnp.float32)
-    core = pltpu.VMEM((len(CORE), ROWS, LANES), jnp.float32)
     cells = sum(spots_of(array.shape[0]) for array in later)
     rows = ROWS * sum(array.shape[0] - spots_of(array.shape[0]) for array in later)
+    shape = (EDGE, EDGE, ROWS * LANES)
     return pl.pallas_call(
         fields_kernel,
-        out_shape=jax.ShapeDtypeStruct((EDGE, EDGE, ROWS * LANES), jnp.float32),
+        out_shape=jax.ShapeDtypeStruct(shape, jnp.float32),
         in_specs=[VMEM] * (7 + len(stages)),
-        out_specs=VMEM,
+        out_specs=pl.BlockSpec(memory_space=pl.ANY),
         scratch_shapes=[
             pltpu.VMEM((count, rows, LANES), jnp.float32),
-            pltpu.VMEM((cells, ROWS, 2 * LANES), jnp.bfloat16),
-            pltpu.VMEM((len(CORE), ROWS, 2 * LANES), jnp.bfloat16),
-            pltpu.VMEM((cells, ROWS, LANES), jnp.float32),
+            pltpu.VMEM((count, cells, ROWS, 2 * LANES), jnp.bfloat16),
+            pltpu.VMEM((count * 2 * EDGE, ROWS, 2 * LANES), jnp.bfloat16),
+            pltpu.VMEM((count, cells, ROWS, LANES), jnp.float32),
             plane,
             plane,
-            core,
+            pltpu.VMEM((count, len(CORE), ROWS, LANES), jnp.float32),
             pltpu.VMEM((EDGE, EDGE * (ROWS + 1), LANES), jnp.float32),
+            pltpu.VMEM(shape, jnp.float32),
             pltpu.VMEM((DEGREE, SUB, LANES), jnp.float32),
+            pltpu.SemaphoreType.DMA((EDGE // 2,)),
         ],
         compiler_params=pltpu.CompilerParams(vmem_limit_bytes=24 * 2**20),
         name="fields",

time: 25.5 us -> 25.3 us (level)
  no operation moved by 1% of the time
where the time goes in v13:
time: 25.3 us; the launch traced here: 25.1 us
  starting transfers between devices  14.1 us (56%)
  Pallas kernels  6.85 us (27%)
  waiting for transfers between devices  2.46 us (10%)
  local copies, waits for them, and re-layouts  1.03 us (4%)
  other arithmetic  0.7 us (3%)
    ppermute x1, starting transfers between devices, exchange(): high = lax.ppermute(corner_high, both, diagonal(1, -1))  4.72 us
    pallas_call x1, Pallas kernels, fields(): pl.pallas_call(fields_kernel, out_shape=jax.ShapeDtypeStruct(shape, jnp.f...  4.06 us
    ppermute x2, starting transfers between devices, gathered(): other = lax.ppermute(mine, 'orb', [(i, i ^ 1 << bit) for i in range(count)])  3.42 us
    ppermute x2, waiting for transfers between devices, gathered(): other = lax.ppermute(mine, 'orb', [(i, i ^ 1 << bit) for i in range(count)])  2.28 us
    ppermute x1, starting transfers between devices, exchange(): above = lax.ppermute(first, 'sy', ring('sy', -1))  2.25 us
    pallas_call x1, Pallas kernels, modes_of(): pl.pallas_call(modes_kernel, out_shape=[jax.ShapeDtypeStruct(shape, jnp.f...  2.18 us
    ppermute x1, starting transfers between devices, exchange(): across = lax.ppermute(block, 'sx', ring('sx', 1))  2.11 us
    ppermute x1, starting transfers between devices, exchange(): below = lax.ppermute(last, 'sy', ring('sy', 1))  1.58 us
  transfers between devices with their start and end apart: 7, of which 3 were waited for; matrix products, arithmetic and copies ran while one was open for 0% of the time, Pallas kernels for 10%

profile of v13, /device:TPU:0, one launch (start us, length us, event | category | flops | bytes accessed | tf_op | source)
XLA Modules:
  0.0 25.1 jit_solution(8972802117416557365)
XLA Ops:
  0.0 0.7 %pad_add_fusion = s32[2,2,2]{2,1,0:T(2,128)S(1)} fusion(s32[1,2,2]{2,1,0:T(2,128)} %bitcast.2, s32[1,2,2]{2,1,0:T(2,128)} %bitcast.3), kind=kLoop, calls=%fused_computation | loop fusion | flops 8 | bytes 64 | tf_op jit(solution)/shard_map/stack | solution.py:208
  0.7 0.1 broadcast_in_dim.3.entries
  0.8 0.0 copy-start
  0.8 1.0 %copy-done = bf16[8,8,2048]{2,1,0:T(8,128)(2,1)S(1)} copy-done((bf16[8,8,2048]{2,1,0:T(8,128)(2,1)S(1)}, bf16[8,8,2048]{2,1,0:T(8,128)(2,1)}, u32[]{:S(2)}) %copy-start) | copy-done | bytes 262168
  1.7 0.2 prepare.1
  2.0 0.5 %collective-permute-start = (bf16[4,16,128]{2,1,0:T(8,128)(2,1)S(1)}, bf16[4,16,128]{2,1,0:T(8,128)(2,1)S(1)}, u32[]{:S(2)}, u32[]{:S(2)}) collective-permute-start(bf16[4,16,128]{2,1,0:T(8,128)(2,1)S(1)} %get-tuple-element.17.mine), channel_id=1, source_target_pairs={{0,8},{8,0},{16,24},{24,16},{1,9},{9,1},{17,25},{25,17},{2,10},{10... | collective-permute-start | bytes 49160 | tf_op jit(solution)/shard_map/ppermute | solution.py:154
  2.5 0.8 %collective-permute-done.other = bf16[4,16,128]{2,1,0:T(8,128)(2,1)S(1)} collective-permute-done((bf16[4,16,128]{2,1,0:T(8,128)(2,1)S(1)}, bf16[4,16,128]{2,1,0:T(8,128)(2,1)S(1)}, u32[]{:S(2)}, u32[]{:S(2)}) %collective-permute-start) | collective-permute-done | bytes 16416 | tf_op jit(solution)/shard_map/ppermute | solution.py:154
  3.3 2.9 %collective-permute-start.1 = (bf16[4,16,128]{2,1,0:T(8,128)(2,1)S(1)}, bf16[4,16,128]{2,1,0:T(8,128)(2,1)S(1)}, u32[]{:S(2)}, u32[]{:S(2)}) collective-permute-start(bf16[4,16,128]{2,1,0:T(8,128)(2,1)S(1)} %nearer.1.after.mine), channel_id=1, source_target_pairs={{0,16},{8,24},{16,0},{24,8},{1,17},{9,25},{17,1},{25,9},{2,18},{10... | collective-permute-start | bytes 49160 | tf_op jit(solution)/shard_map/ppermute | solution.py:154
  6.2 0.3 %sines.1.before.modes.refs_7_ = bf16[256,256]{1,0:T(8,128)(2,1)S(1)} custom-call(bf16[4,16,128]{2,1,0:T(8,128)(2,1)S(1)} %nearer.1.after.mine), custom_call_target="tpu_custom_call" | custom-call | bytes 2097152 | tf_op jit(solution)/shard_map/sines/pallas_call | solution.py:285
  6.5 1.4 %collective-permute-done.1.refs_0_ = bf16[4,16,128]{2,1,0:T(8,128)(2,1)S(1)} collective-permute-done((bf16[4,16,128]{2,1,0:T(8,128)(2,1)S(1)}, bf16[4,16,128]{2,1,0:T(8,128)(2,1)S(1)}, u32[]{:S(2)}, u32[]{:S(2)}) %collective-permute-start.1) | collective-permute-done | bytes 16416 | tf_op jit(solution)/shard_map/ppermute | solution.py:154
  8.0 0.1 messages.1
  8.0 2.1 %collective-permute-start.2 = (bf16[68,16,128]{2,1,0:T(8,128)(2,1)S(1)}, bf16[68,16,128]{2,1,0:T(8,128)(2,1)S(1)}, u32[]{:S(2)}, u32[]{:S(2)}) collective-permute-start(bf16[68,16,128]{2,1,0:T(8,128)(2,1)S(1)} %get-tuple-element.19.own), channel_id=1, source_target_pairs={{0,4},{4,0},{1,5},{5,1},{2,6},{6,2},{3,7},{7,3},{8,12},{12,8},{9,1... | collective-permute-start | bytes 835592 | tf_op jit(solution)/shard_map/ppermute | solution.py:231
  10.2 1.6 %collective-permute-start.3 = (bf16[34,16,128]{2,1,0:T(8,128)(2,1)S(1)}, bf16[34,16,128]{2,1,0:T(8,128)(2,1)S(1)}, u32[]{:S(2)}, u32[]{:S(2)}) collective-permute-start(bf16[34,16,128]{2,1,0:T(8,128)(2,1)S(1)} %get-tuple-element.25), channel_id=1, source_target_pairs={{0,1},{1,2},{2,3},{3,0},{4,5},{5,6},{6,7},{7,4},{8,9},{9,10},{10,1... | collective-permute-start | bytes 417800 | tf_op jit(solution)/shard_map/ppermute | solution.py:248
  11.7 2.2 %collective-permute-start.4 = (bf16[34,16,128]{2,1,0:T(8,128)(2,1)S(1)}, bf16[34,16,128]{2,1,0:T(8,128)(2,1)S(1)}, u32[]{:S(2)}, u32[]{:S(2)}) collective-permute-start(bf16[34,16,128]{2,1,0:T(8,128)(2,1)S(1)} %get-tuple-element.26), channel_id=1, source_target_pairs={{0,3},{1,0},{2,1},{3,2},{4,7},{5,4},{6,5},{7,6},{8,11},{9,8},{10,9... | collective-permute-start | bytes 417800 | tf_op jit(solution)/shard_map/ppermute | solution.py:249
  14.0 0.0 collective-permute-start.5
  14.0 4.7 %collective-permute-start.6 = (bf16[13,16,128]{2,1,0:T(8,128)(2,1)S(1)}, bf16[13,16,128]{2,1,0:T(8,128)(2,1)S(1)}, u32[]{:S(2)}, u32[]{:S(2)}) collective-permute-start(bf16[13,16,128]{2,1,0:T(8,128)(2,1)S(1)} %get-tuple-element.28), channel_id=1, source_target_pairs={{0,7},{1,4},{2,5},{3,6},{4,3},{5,0},{6,1},{7,2},{8,15},{9,12},{10,... | collective-permute-start | bytes 159752 | tf_op jit(solution)/shard_map/ppermute | solution.py:230
  18.7 0.0 collective-permute-done.2.across
  18.7 2.2 %modes.1 = (f32[4,128,16,128]{3,2,1,0:T(8,128)S(1)}, f32[4,64,128]{2,1,0:T(8,128)S(1)}, f32[4,84,16,128]{3,2,1,0:T(8,128)S(1)}, f32[4,48,16,128]{3,2,1,0:T(8,128)S(1)}, f32[4,20,16,128]{3,2,1,0:T(8,128)S(1)}) custom-call(bf16[68,16,128]{2,1,0:T(8,128)(2,1)S(1)} %get-tuple-element.19.own, bf16[68,16,128]{2,1,0:T(8,128)(2,1)S(1)} %collective-permute-done.2.across, ...), custom_call_target="tpu_custom_call" | custom-call | bytes 6291456 | tf_op jit(solution)/shard_map/modes/pallas_call | solution.py:436
  20.9 0.2 collective-permute-done.5.refs_5_
  21.1 0.0 collective-permute-done.6.refs_6_
  21.1 0.0 collective-permute-done.3.refs_3_
  21.1 0.0 collective-permute-done.4.refs_4_
  21.1 4.1 %fields.1 = f32[8,8,2048]{2,1,0:T(8,128)} custom-call(f32[4,128,16,128]{3,2,1,0:T(8,128)S(1)} %get-tuple-element.20.beside, f32[4,64,128]{2,1,0:T(8,128)S(1)} %get-tuple-element.21.own_rows, f32[4,84,16,128]{3,2,1,0:T(8,128)S(1)} %get-tuple-element.22.refs_0_, f32[4,48,16,128]{3,2,1,0:T(8,128)S(1)} %get-tuple-element.23.refs_1_, ...), custom_call_target="tpu_custom_call" | custom-call | tf_op jit(solution)/shard_map/fields/pallas_call | solution.py:531
  (1 shorter events, 0.0 us)
Async XLA Ops:
  0.8 1.0 %copy-start = (bf16[8,8,2048]{2,1,0:T(8,128)(2,1)S(1)}, bf16[8,8,2048]{2,1,0:T(8,128)(2,1)}, u32[]{:S(2)}) copy-start(bf16[8,8,2048]{2,1,0:T(8,128)(2,1)} %orbitals.1) | copy-start | bytes 786436
  2.0 1.4 %collective-permute-start = (bf16[4,16,128]{2,1,0:T(8,128)(2,1)S(1)}, bf16[4,16,128]{2,1,0:T(8,128)(2,1)S(1)}, u32[]{:S(2)}, u32[]{:S(2)}) collective-permute-start(bf16[4,16,128]{2,1,0:T(8,128)(2,1)S(1)} %get-tuple-element.17.mine), channel_id=1, source_target_pairs={{0,8},{8,0},{16,24},{24,16},{1,9},{9,1},{17,25},{25,17},{2,10},{10... | collective-permute-start | bytes 49160 | tf_op jit(solution)/shard_map/ppermute | solution.py:154
  3.3 4.6 %collective-permute-start.1 = (bf16[4,16,128]{2,1,0:T(8,128)(2,1)S(1)}, bf16[4,16,128]{2,1,0:T(8,128)(2,1)S(1)}, u32[]{:S(2)}, u32[]{:S(2)}) collective-permute-start(bf16[4,16,128]{2,1,0:T(8,128)(2,1)S(1)} %nearer.1.after.mine), channel_id=1, source_target_pairs={{0,16},{8,24},{16,0},{24,8},{1,17},{9,25},{17,1},{25,9},{2,18},{10... | collective-permute-start | bytes 49160 | tf_op jit(solution)/shard_map/ppermute | solution.py:154
  8.0 10.7 %collective-permute-start.2 = (bf16[68,16,128]{2,1,0:T(8,128)(2,1)S(1)}, bf16[68,16,128]{2,1,0:T(8,128)(2,1)S(1)}, u32[]{:S(2)}, u32[]{:S(2)}) collective-permute-start(bf16[68,16,128]{2,1,0:T(8,128)(2,1)S(1)} %get-tuple-element.19.own), channel_id=1, source_target_pairs={{0,4},{4,0},{1,5},{5,1},{2,6},{6,2},{3,7},{7,3},{8,12},{12,8},{9,1... | collective-permute-start | bytes 835592 | tf_op jit(solution)/shard_map/ppermute | solution.py:231
  10.2 10.9 %collective-permute-start.3 = (bf16[34,16,128]{2,1,0:T(8,128)(2,1)S(1)}, bf16[34,16,128]{2,1,0:T(8,128)(2,1)S(1)}, u32[]{:S(2)}, u32[]{:S(2)}) collective-permute-start(bf16[34,16,128]{2,1,0:T(8,128)(2,1)S(1)} %get-tuple-element.25), channel_id=1, source_target_pairs={{0,1},{1,2},{2,3},{3,0},{4,5},{5,6},{6,7},{7,4},{8,9},{9,10},{10,1... | collective-permute-start | bytes 417800 | tf_op jit(solution)/shard_map/ppermute | solution.py:248
  11.7 9.3 %collective-permute-start.4 = (bf16[34,16,128]{2,1,0:T(8,128)(2,1)S(1)}, bf16[34,16,128]{2,1,0:T(8,128)(2,1)S(1)}, u32[]{:S(2)}, u32[]{:S(2)}) collective-permute-start(bf16[34,16,128]{2,1,0:T(8,128)(2,1)S(1)} %get-tuple-element.26), channel_id=1, source_target_pairs={{0,3},{1,0},{2,1},{3,2},{4,7},{5,4},{6,5},{7,6},{8,11},{9,8},{10,9... | collective-permute-start | bytes 417800 | tf_op jit(solution)/shard_map/ppermute | solution.py:249
  14.0 7.1 %collective-permute-start.5 = (bf16[13,16,128]{2,1,0:T(8,128)(2,1)S(1)}, bf16[13,16,128]{2,1,0:T(8,128)(2,1)S(1)}, u32[]{:S(2)}, u32[]{:S(2)}) collective-permute-start(bf16[13,16,128]{2,1,0:T(8,128)(2,1)S(1)} %get-tuple-element.27), channel_id=1, source_target_pairs={{0,5},{1,6},{2,7},{3,4},{4,1},{5,2},{6,3},{7,0},{8,13},{9,14},{10,... | collective-permute-start | bytes 159752 | tf_op jit(solution)/shard_map/ppermute | solution.py:229
  14.0 7.1 %collective-permute-start.6 = (bf16[13,16,128]{2,1,0:T(8,128)(2,1)S(1)}, bf16[13,16,128]{2,1,0:T(8,128)(2,1)S(1)}, u32[]{:S(2)}, u32[]{:S(2)}) collective-permute-start(bf16[13,16,128]{2,1,0:T(8,128)(2,1)S(1)} %get-tuple-element.28), channel_id=1, source_target_pairs={{0,7},{1,4},{2,5},{3,6},{4,3},{5,0},{6,1},{7,2},{8,15},{9,12},{10,... | collective-permute-start | bytes 159752 | tf_op jit(solution)/shard_map/ppermute | solution.py:230

commit v14 on v13

--- a/solution.py
+++ b/solution.py
@@ -123,51 +123,31 @@
     )(entries, orbitals)
 
 
-def chosen(entries, mine, others, bit):
-    owner, me = by_seat(entries[1]), lax.axis_index("orb")
+def partners():
     count = lax.axis_size("orb")
+    me = lax.axis_index("orb")
+    if count & (count - 1):
+        steps = range(1, count)
+        return [(ring("orb", step), lax.rem(me + count - step, count)) for step in steps]
+    steps = sorted(range(1, count), key=lambda step: step & -step, reverse=True)
+    return [([(i, i ^ step) for i in range(count)], me ^ step) for step in steps]
+
+
+def chosen(entries, mine, others):
+    owner = by_seat(entries[1])
+    holders = [holder for _, holder in partners()]
     picked = []
     for tile in range(mine.shape[0]):
         value = mine[tile].astype(jnp.float32)
-        for step, other in enumerate(others, 1):
-            if bit is None:
-                here = owner == lax.rem(me + count - step, count)
-            else:
-                here = (owner >> bit & 1) != (me >> bit & 1)
-            value = jnp.where(here, other[tile].astype(jnp.float32), value)
+        for holder, other in zip(holders, others):
+            value = jnp.where(owner == holder, other[tile].astype(jnp.float32), value)
         picked.append(value)
     return picked
 
 
-def nearer_kernel(bit, entries, mine, other, out):
-    for tile, value in enumerate(chosen(entries, mine, [other], bit)):
-        out[tile] = value.astype(jnp.bfloat16)
-
-
-def gathered(entries, mine):
-    count = lax.axis_size("orb")
-    if count & (count - 1):
-        others = [lax.ppermute(mine, "orb", ring("orb", step)) for step in range(1, count)]
-        return mine, others, None
-    bits = count.bit_length() - 1
-    for bit in range(bits):
-        other = lax.ppermute(mine, "orb", [(i, i ^ 1 << bit) for i in range(count)])
-        if bit == bits - 1:
-            return mine, [other], bit
-        mine = pl.pallas_call(
-            functools.partial(nearer_kernel, bit),
-            out_shape=jax.ShapeDtypeStruct(mine.shape, mine.dtype),
-            in_specs=[VMEM] * 3,
-            out_specs=VMEM,
-            compiler_params=SMALL,
-            name="nearer",
-        )(entries, mine, other)
-    return mine, [], None
-
-
-def messages_kernel(bit, before, entries, cells, mine, *refs):
+def messages_kernel(before, entries, cells, mine, *refs):
     others, (block, last, first, corner_low, corner_high) = refs[:-5], refs[-5:]
-    picked = chosen(entries, mine, others, bit)
+    picked = chosen(entries, mine, others)
 
     def pack(ref, spots):
         for at, (x, y) in enumerate(spots):
@@ -207,11 +187,11 @@
 def messages(orbitals, src_owner, src_slot):
     entries = spread_out(jnp.stack([src_slot, src_owner]))
     mine, cells = prepare(entries, orbitals)
-    mine, others, bit = gathered(entries, mine)
+    others = [lax.ppermute(mine, "orb", pairs) for pairs, _ in partners()]
     lengths = [EDGE * EDGE] + [EDGE * HALO] * 2 + [len(CORNER_LOW)] * 2
     modes = sines(mine)
     packed = pl.pallas_call(
-        functools.partial(messages_kernel, bit),
+        messages_kernel,
         out_shape=[
             jax.ShapeDtypeStruct((tiles(length), ROWS, LANES), jnp.bfloat16) for length in lengths
         ],

time: 25.3 us -> 25.5 us (level)
  waiting for transfers between devices: 2.46 us -> 3.48 us
  starting transfers between devices: 14.1 us -> 13.3 us
    ppermute x2 -> x3, waiting for transfers between devices: 2.28 us -> 3.42 us  [messages(): others = [lax.ppermute(mine, 'orb', pairs) for pairs, _ in partners()]]
    ppermute x1, starting transfers between devices: 2.11 us -> 1.58 us  [exchange(): across = lax.ppermute(block, 'sx', ring('sx', 1))]
    ppermute x2 -> x3, starting transfers between devices: 3.42 us -> 3.16 us  [messages(): others = [lax.ppermute(mine, 'orb', pairs) for pairs, _ in partners()]]
  transfers between devices with their start and end apart: 7 -> 8, of which waited for: 3 -> 4; matrix products, arithmetic and copies ran while one was open for 0% -> 0% of each run, Pallas kernels for 10% -> 10%
where the time goes in v14:
time: 25.5 us; the launch traced here: 25.4 us
  starting transfers between devices  13.3 us (52%)
  Pallas kernels  6.84 us (27%)
  waiting for transfers between devices  3.48 us (14%)
  local copies, waits for them, and re-layouts  1.03 us (4%)
  other arithmetic  0.7 us (3%)
    ppermute x1, starting transfers between devices, exchange(): high = lax.ppermute(corner_high, both, diagonal(1, -1))  4.72 us
    pallas_call x1, Pallas kernels, fields(): pl.pallas_call(fields_kernel, out_shape=jax.ShapeDtypeStruct(shape, jnp.f...  4.06 us
    ppermute x3, waiting for transfers between devices, messages(): others = [lax.ppermute(mine, 'orb', pairs) for pairs, _ in partners()]  3.42 us
    ppermute x3, starting transfers between devices, messages(): others = [lax.ppermute(mine, 'orb', pairs) for pairs, _ in partners()]  3.16 us
    ppermute x1, starting transfers between devices, exchange(): above = lax.ppermute(first, 'sy', ring('sy', -1))  2.25 us
    pallas_call x1, Pallas kernels, modes_of(): pl.pallas_call(modes_kernel, out_shape=[jax.ShapeDtypeStruct(shape, jnp.f...  2.18 us
    ppermute x1, starting transfers between devices, exchange(): across = lax.ppermute(block, 'sx', ring('sx', 1))  1.58 us
    ppermute x1, starting transfers between devices, exchange(): below = lax.ppermute(last, 'sy', ring('sy', 1))  1.58 us
  transfers between devices with their start and end apart: 8, of which 4 were waited for; matrix products, arithmetic and copies ran while one was open for 0% of the time, Pallas kernels for 10%

profile of v14, /device:TPU:0, one launch (start us, length us, event | category | flops | bytes accessed | tf_op | source)
XLA Modules:
  0.0 25.4 jit_solution(11911208072022960498)
XLA Ops:
  0.0 0.7 %pad_add_fusion = s32[2,2,2]{2,1,0:T(2,128)S(1)} fusion(s32[1,2,2]{2,1,0:T(2,128)} %bitcast.2, s32[1,2,2]{2,1,0:T(2,128)} %bitcast.3), kind=kLoop, calls=%fused_computation | loop fusion | flops 8 | bytes 64 | tf_op jit(solution)/shard_map/stack | solution.py:188
  0.7 0.1 broadcast_in_dim.3.entries
  0.8 0.0 copy-start
  0.8 1.0 %copy-done = bf16[8,8,2048]{2,1,0:T(8,128)(2,1)S(1)} copy-done((bf16[8,8,2048]{2,1,0:T(8,128)(2,1)S(1)}, bf16[8,8,2048]{2,1,0:T(8,128)(2,1)}, u32[]{:S(2)}) %copy-start) | copy-done | bytes 262168
  1.7 0.2 prepare.1
  2.0 2.4 %collective-permute-start.2 = (bf16[4,16,128]{2,1,0:T(8,128)(2,1)S(1)}, bf16[4,16,128]{2,1,0:T(8,128)(2,1)S(1)}, u32[]{:S(2)}, u32[]{:S(2)}) collective-permute-start(bf16[4,16,128]{2,1,0:T(8,128)(2,1)S(1)} %get-tuple-element.17.after.mine), channel_id=1, source_target_pairs={{0,24},{8,16},{16,8},{24,0},{1,25},{9,17},{17,9},{25,1},{2,26},{10... | collective-permute-start | bytes 49160 | tf_op jit(solution)/shard_map/ppermute | solution.py:190
  4.4 0.7 %collective-permute-start.1 = (bf16[4,16,128]{2,1,0:T(8,128)(2,1)S(1)}, bf16[4,16,128]{2,1,0:T(8,128)(2,1)S(1)}, u32[]{:S(2)}, u32[]{:S(2)}) collective-permute-start(bf16[4,16,128]{2,1,0:T(8,128)(2,1)S(1)} %get-tuple-element.17.after.mine), channel_id=1, source_target_pairs={{0,8},{8,0},{16,24},{24,16},{1,9},{9,1},{17,25},{25,17},{2,10},{10... | collective-permute-start | bytes 49160 | tf_op jit(solution)/shard_map/ppermute | solution.py:190
  5.1 0.0 collective-permute-start
  5.1 0.3 %sines.1.before.modes.refs_7_ = bf16[256,256]{1,0:T(8,128)(2,1)S(1)} custom-call(bf16[4,16,128]{2,1,0:T(8,128)(2,1)S(1)} %get-tuple-element.17.after.mine), custom_call_target="tpu_custom_call" | custom-call | bytes 2097152 | tf_op jit(solution)/shard_map/sines/pallas_call | solution.py:265
  5.4 0.4 %collective-permute-done.2.refs_2_ = bf16[4,16,128]{2,1,0:T(8,128)(2,1)S(1)} collective-permute-done((bf16[4,16,128]{2,1,0:T(8,128)(2,1)S(1)}, bf16[4,16,128]{2,1,0:T(8,128)(2,1)S(1)}, u32[]{:S(2)}, u32[]{:S(2)}) %collective-permute-start.2) | collective-permute-done | bytes 16416 | tf_op jit(solution)/shard_map/ppermute | solution.py:190
  5.9 0.1 collective-permute-done.1.refs_1_
  5.9 2.9 %collective-permute-done.refs_0_ = bf16[4,16,128]{2,1,0:T(8,128)(2,1)S(1)} collective-permute-done((bf16[4,16,128]{2,1,0:T(8,128)(2,1)S(1)}, bf16[4,16,128]{2,1,0:T(8,128)(2,1)S(1)}, u32[]{:S(2)}, u32[]{:S(2)}) %collective-permute-start) | collective-permute-done | bytes 16416 | tf_op jit(solution)/shard_map/ppermute | solution.py:190
  8.8 0.1 messages.1
  8.9 1.6 %collective-permute-start.3 = (bf16[68,16,128]{2,1,0:T(8,128)(2,1)S(1)}, bf16[68,16,128]{2,1,0:T(8,128)(2,1)S(1)}, u32[]{:S(2)}, u32[]{:S(2)}) collective-permute-start(bf16[68,16,128]{2,1,0:T(8,128)(2,1)S(1)} %get-tuple-element.19.own), channel_id=1, source_target_pairs={{0,4},{4,0},{1,5},{5,1},{2,6},{6,2},{3,7},{7,3},{8,12},{12,8},{9,1... | collective-permute-start | bytes 835592 | tf_op jit(solution)/shard_map/ppermute | solution.py:211
  10.5 1.6 %collective-permute-start.4 = (bf16[34,16,128]{2,1,0:T(8,128)(2,1)S(1)}, bf16[34,16,128]{2,1,0:T(8,128)(2,1)S(1)}, u32[]{:S(2)}, u32[]{:S(2)}) collective-permute-start(bf16[34,16,128]{2,1,0:T(8,128)(2,1)S(1)} %get-tuple-element.25), channel_id=1, source_target_pairs={{0,1},{1,2},{2,3},{3,0},{4,5},{5,6},{6,7},{7,4},{8,9},{9,10},{10,1... | collective-permute-start | bytes 417800 | tf_op jit(solution)/shard_map/ppermute | solution.py:228
  12.1 2.2 %collective-permute-start.5 = (bf16[34,16,128]{2,1,0:T(8,128)(2,1)S(1)}, bf16[34,16,128]{2,1,0:T(8,128)(2,1)S(1)}, u32[]{:S(2)}, u32[]{:S(2)}) collective-permute-start(bf16[34,16,128]{2,1,0:T(8,128)(2,1)S(1)} %get-tuple-element.26), channel_id=1, source_target_pairs={{0,3},{1,0},{2,1},{3,2},{4,7},{5,4},{6,5},{7,6},{8,11},{9,8},{10,9... | collective-permute-start | bytes 417800 | tf_op jit(solution)/shard_map/ppermute | solution.py:229
  14.3 0.0 collective-permute-start.6
  14.3 4.7 %collective-permute-start.7 = (bf16[13,16,128]{2,1,0:T(8,128)(2,1)S(1)}, bf16[13,16,128]{2,1,0:T(8,128)(2,1)S(1)}, u32[]{:S(2)}, u32[]{:S(2)}) collective-permute-start(bf16[13,16,128]{2,1,0:T(8,128)(2,1)S(1)} %get-tuple-element.28), channel_id=1, source_target_pairs={{0,7},{1,4},{2,5},{3,6},{4,3},{5,0},{6,1},{7,2},{8,15},{9,12},{10,... | collective-permute-start | bytes 159752 | tf_op jit(solution)/shard_map/ppermute | solution.py:210
  19.0 0.0 collective-permute-done.3.across
  19.1 2.2 %modes.1 = (f32[4,128,16,128]{3,2,1,0:T(8,128)S(1)}, f32[4,64,128]{2,1,0:T(8,128)S(1)}, f32[4,84,16,128]{3,2,1,0:T(8,128)S(1)}, f32[4,48,16,128]{3,2,1,0:T(8,128)S(1)}, f32[4,20,16,128]{3,2,1,0:T(8,128)S(1)}) custom-call(bf16[68,16,128]{2,1,0:T(8,128)(2,1)S(1)} %get-tuple-element.19.own, bf16[68,16,128]{2,1,0:T(8,128)(2,1)S(1)} %collective-permute-done.3.across, ...), custom_call_target="tpu_custom_call" | custom-call | bytes 6291456 | tf_op jit(solution)/shard_map/modes/pallas_call | solution.py:416
  21.2 0.1 collective-permute-done.6.refs_5_
  21.3 0.0 collective-permute-done.7.refs_6_
  21.3 0.0 collective-permute-done.4.refs_3_
  21.3 0.0 collective-permute-done.5.refs_4_
  21.3 4.1 %fields.1 = f32[8,8,2048]{2,1,0:T(8,128)} custom-call(f32[4,128,16,128]{3,2,1,0:T(8,128)S(1)} %get-tuple-element.20.beside, f32[4,64,128]{2,1,0:T(8,128)S(1)} %get-tuple-element.21.own_rows, f32[4,84,16,128]{3,2,1,0:T(8,128)S(1)} %get-tuple-element.22.refs_0_, f32[4,48,16,128]{3,2,1,0:T(8,128)S(1)} %get-tuple-element.23.refs_1_, ...), custom_call_target="tpu_custom_call" | custom-call | tf_op jit(solution)/shard_map/fields/pallas_call | solution.py:511
Async XLA Ops:
  0.8 1.0 %copy-start = (bf16[8,8,2048]{2,1,0:T(8,128)(2,1)S(1)}, bf16[8,8,2048]{2,1,0:T(8,128)(2,1)}, u32[]{:S(2)}) copy-start(bf16[8,8,2048]{2,1,0:T(8,128)(2,1)} %orbitals.1) | copy-start | bytes 786436
  2.0 3.9 %collective-permute-start.2 = (bf16[4,16,128]{2,1,0:T(8,128)(2,1)S(1)}, bf16[4,16,128]{2,1,0:T(8,128)(2,1)S(1)}, u32[]{:S(2)}, u32[]{:S(2)}) collective-permute-start(bf16[4,16,128]{2,1,0:T(8,128)(2,1)S(1)} %get-tuple-element.17.after.mine), channel_id=1, source_target_pairs={{0,24},{8,16},{16,8},{24,0},{1,25},{9,17},{17,9},{25,1},{2,26},{10... | collective-permute-start | bytes 49160 | tf_op jit(solution)/shard_map/ppermute | solution.py:190
  4.4 1.5 %collective-permute-start.1 = (bf16[4,16,128]{2,1,0:T(8,128)(2,1)S(1)}, bf16[4,16,128]{2,1,0:T(8,128)(2,1)S(1)}, u32[]{:S(2)}, u32[]{:S(2)}) collective-permute-start(bf16[4,16,128]{2,1,0:T(8,128)(2,1)S(1)} %get-tuple-element.17.after.mine), channel_id=1, source_target_pairs={{0,8},{8,0},{16,24},{24,16},{1,9},{9,1},{17,25},{25,17},{2,10},{10... | collective-permute-start | bytes 49160 | tf_op jit(solution)/shard_map/ppermute | solution.py:190
  5.1 3.7 %collective-permute-start = (bf16[4,16,128]{2,1,0:T(8,128)(2,1)S(1)}, bf16[4,16,128]{2,1,0:T(8,128)(2,1)S(1)}, u32[]{:S(2)}, u32[]{:S(2)}) collective-permute-start(bf16[4,16,128]{2,1,0:T(8,128)(2,1)S(1)} %get-tuple-element.17.after.mine), channel_id=1, source_target_pairs={{0,16},{8,24},{16,0},{24,8},{1,17},{9,25},{17,1},{25,9},{2,18},{10... | collective-permute-start | bytes 49160 | tf_op jit(solution)/shard_map/ppermute | solution.py:190
  8.9 10.1 %collective-permute-start.3 = (bf16[68,16,128]{2,1,0:T(8,128)(2,1)S(1)}, bf16[68,16,128]{2,1,0:T(8,128)(2,1)S(1)}, u32[]{:S(2)}, u32[]{:S(2)}) collective-permute-start(bf16[68,16,128]{2,1,0:T(8,128)(2,1)S(1)} %get-tuple-element.19.own), channel_id=1, source_target_pairs={{0,4},{4,0},{1,5},{5,1},{2,6},{6,2},{3,7},{7,3},{8,12},{12,8},{9,1... | collective-permute-start | bytes 835592 | tf_op jit(solution)/shard_map/ppermute | solution.py:211
  10.5 10.8 %collective-permute-start.4 = (bf16[34,16,128]{2,1,0:T(8,128)(2,1)S(1)}, bf16[34,16,128]{2,1,0:T(8,128)(2,1)S(1)}, u32[]{:S(2)}, u32[]{:S(2)}) collective-permute-start(bf16[34,16,128]{2,1,0:T(8,128)(2,1)S(1)} %get-tuple-element.25), channel_id=1, source_target_pairs={{0,1},{1,2},{2,3},{3,0},{4,5},{5,6},{6,7},{7,4},{8,9},{9,10},{10,1... | collective-permute-start | bytes 417800 | tf_op jit(solution)/shard_map/ppermute | solution.py:228
  12.1 9.2 %collective-permute-start.5 = (bf16[34,16,128]{2,1,0:T(8,128)(2,1)S(1)}, bf16[34,16,128]{2,1,0:T(8,128)(2,1)S(1)}, u32[]{:S(2)}, u32[]{:S(2)}) collective-permute-start(bf16[34,16,128]{2,1,0:T(8,128)(2,1)S(1)} %get-tuple-element.26), channel_id=1, source_target_pairs={{0,3},{1,0},{2,1},{3,2},{4,7},{5,4},{6,5},{7,6},{8,11},{9,8},{10,9... | collective-permute-start | bytes 417800 | tf_op jit(solution)/shard_map/ppermute | solution.py:229
  14.3 7.0 %collective-permute-start.6 = (bf16[13,16,128]{2,1,0:T(8,128)(2,1)S(1)}, bf16[13,16,128]{2,1,0:T(8,128)(2,1)S(1)}, u32[]{:S(2)}, u32[]{:S(2)}) collective-permute-start(bf16[13,16,128]{2,1,0:T(8,128)(2,1)S(1)} %get-tuple-element.27), channel_id=1, source_target_pairs={{0,5},{1,6},{2,7},{3,4},{4,1},{5,2},{6,3},{7,0},{8,13},{9,14},{10,... | collective-permute-start | bytes 159752 | tf_op jit(solution)/shard_map/ppermute | solution.py:209
  14.3 7.0 %collective-permute-start.7 = (bf16[13,16,128]{2,1,0:T(8,128)(2,1)S(1)}, bf16[13,16,128]{2,1,0:T(8,128)(2,1)S(1)}, u32[]{:S(2)}, u32[]{:S(2)}) collective-permute-start(bf16[13,16,128]{2,1,0:T(8,128)(2,1)S(1)} %get-tuple-element.28), channel_id=1, source_target_pairs={{0,7},{1,4},{2,5},{3,6},{4,3},{5,0},{6,1},{7,2},{8,15},{9,12},{10,... | collective-permute-start | bytes 159752 | tf_op jit(solution)/shard_map/ppermute | solution.py:210

commit v15 on v13

--- a/solution.py
+++ b/solution.py
@@ -209,7 +209,7 @@
     mine, cells = prepare(entries, orbitals)
     mine, others, bit = gathered(entries, mine)
     lengths = [EDGE * EDGE] + [EDGE * HALO] * 2 + [len(CORNER_LOW)] * 2
-    modes = sines(mine)
+    modes, tails = sines(mine)
     packed = pl.pallas_call(
         functools.partial(messages_kernel, bit),
         out_shape=[
@@ -220,7 +220,7 @@
         compiler_params=SMALL,
         name="messages",
     )(modes, entries, cells, mine, *others)
-    return packed, modes
+    return packed, modes, tails
 
 
 def exchange(block, last, first, corner_low, corner_high):
@@ -266,7 +266,7 @@
     return out_x + out_y
 
 
-def sines_kernel(after, out):
+def sines_kernel(after, out, tails):
     shape = (LANES, LANES)
     row, col = (lax.broadcasted_iota(jnp.int32, shape, axis) for axis in range(2))
     product = ((row % NZ + 1) * (col % NZ + 1)).astype(jnp.float32)
@@ -279,14 +279,19 @@
     for first in (0, LANES):
         out[pl.ds(first, LANES), pl.ds(0, LANES)] = high
         out[pl.ds(first, LANES), pl.ds(LANES, LANES)] = low
+    for step, tail in enumerate(z_tails()):
+        tails[step] = tail
 
 
 def sines(after):
     return pl.pallas_call(
         sines_kernel,
-        out_shape=jax.ShapeDtypeStruct((2 * LANES, 2 * LANES), jnp.bfloat16),
+        out_shape=[
+            jax.ShapeDtypeStruct((2 * LANES, 2 * LANES), jnp.bfloat16),
+            jax.ShapeDtypeStruct((DEGREE, SUB, LANES), jnp.float32),
+        ],
         in_specs=[pl.BlockSpec(memory_space=pl.ANY)],
-        out_specs=VMEM,
+        out_specs=[VMEM] * 2,
         compiler_params=SMALL,
         cost_estimate=pl.CostEstimate(flops=0, bytes_accessed=2 * 2**20, transcendentals=0),
         name="sines",
@@ -316,17 +321,19 @@
 CORE = [(x, y) for x in range(HALO, HALO + EDGE) for y in range(HALO, HALO + EDGE)]
 
 
-def source_rows(ref, out, first):
-    shape = (LANES, LANES)
-    lane = lax.broadcasted_iota(jnp.int32, shape, 1) % NZ
+def all_rows(refs, rows):
+    count = rows.shape[0]
+    shape = (LANES, count * LANES)
+    lane = lax.broadcasted_iota(jnp.int32, shape, 1)
     line = lax.broadcasted_iota(jnp.int32, shape, 0)
-    packed = ref[spots_of(ref.shape[0]) :].reshape(-1, LANES)
-    for place in range(out.shape[0]):
-        repeat = (line == lane + place * NZ).astype(jnp.bfloat16)
-        out[place, pl.ds(first, packed.shape[0]), :] = jnp.dot(
-            packed, repeat, preferred_element_type=jnp.float32
-        )
-    return first + packed.shape[0]
+    repeat = (line == lane // LANES * NZ + lane % NZ).astype(jnp.bfloat16)
+    packed = [ref[spots_of(ref.shape[0]) :].reshape(-1, LANES) for ref in refs]
+    firsts = [sum(part.shape[0] for part in packed[:at]) for at in range(len(packed))]
+    packed = jnp.concatenate(packed, axis=0)
+    spread = jnp.dot(packed, repeat, preferred_element_type=jnp.float32)
+    for place in range(count):
+        rows[place, : packed.shape[0], :] = spread[:, place * LANES : (place + 1) * LANES]
+    return firsts
 
 
 def keep(parts, at, value):
@@ -364,13 +371,6 @@
             hat[place, start:end] = turned(parts.at[place], start, end, modes)
 
 
-def all_rows(refs, rows):
-    firsts = [0]
-    for ref in refs:
-        firsts.append(source_rows(ref, rows, firsts[-1]))
-    return firsts
-
-
 def early(step):
     cells = [
         (x, y)
@@ -401,10 +401,8 @@
                 put(x, y, summed[x, y] + summed[x - 1, y - 1] + tail[...] * here)
 
 
-def modes_kernel(own, across, modes, hat, own_rows, *refs):
-    stages, (rows, parts, tails) = refs[: DEGREE - 1], refs[DEGREE - 1 :]
-    for step, tail in enumerate(z_tails()):
-        tails[step] = tail
+def modes_kernel(own, across, modes, tails, hat, own_rows, *refs):
+    stages, (rows, parts) = refs[: DEGREE - 1], refs[DEGREE - 1 :]
     densities((own, across), rows, parts, modes, hat)
     own_rows[...] = rows[:, : own_rows.shape[1], :] * (-power_coeffs()[-1])
     for place in range(hat.shape[0]):
@@ -428,7 +426,7 @@
                 old = load
 
 
-def modes_of(own, across, modes, count):
+def modes_of(own, across, modes, tails, count):
     cells = 2 * len(CORE)
     lengths = [cells] + [len(stage) for stage in EARLY]
     shapes = [(count, length, ROWS, LANES) for length in lengths]
@@ -436,26 +434,26 @@
     return pl.pallas_call(
         modes_kernel,
         out_shape=[jax.ShapeDtypeStruct(shape, jnp.float32) for shape in shapes],
-        in_specs=[VMEM] * 3,
+        in_specs=[VMEM] * 4,
         out_specs=[VMEM] * len(shapes),
         scratch_shapes=[
             pltpu.VMEM((count, cells, LANES), jnp.float32),
             pltpu.VMEM((count, cells, ROWS, 2 * LANES), jnp.bfloat16),
-            pltpu.VMEM((DEGREE, SUB, LANES), jnp.float32),
         ],
         compiler_params=pltpu.CompilerParams(vmem_limit_bytes=20 * 2**20),
         cost_estimate=pl.CostEstimate(flops=0, bytes_accessed=6 * 2**20, transcendentals=0),
         name="modes",
-    )(own, across, modes)
+    )(own, across, modes, tails)
 
 
 def fields_kernel(beside, own_rows, *refs):
-    stages, (below, above, low, high, modes, out) = refs[: DEGREE - 1], refs[DEGREE - 1 :][:6]
-    rows, parts, back, hat, work_a, work_b, last, acc, held, tails, sems = refs[DEGREE + 5 :]
+    stages, (below, above, low, high, modes, tails, out) = (
+        refs[: DEGREE - 1],
+        refs[DEGREE - 1 :][:7],
+    )
+    rows, parts, back, hat, work_a, work_b, last, acc, held, sems = refs[DEGREE + 6 :]
     count = beside.shape[0]
     pitch = ROWS + 1
-    for step, tail in enumerate(z_tails()):
-        tails[step] = tail
     later = (below, above, low, high)
     offset = [0]
     for ref in later:
@@ -521,9 +519,9 @@
         copy.wait()
 
 
-def fields(halo, modes, count):
+def fields(halo, modes, tails, count):
     own, across, *later = halo
-    beside, own_rows, *stages = modes_of(own, across, modes, count)
+    beside, own_rows, *stages = modes_of(own, across, modes, tails, count)
     plane = pltpu.VMEM((SIZE, SIZE, SUB, LANES), jnp.float32)
     cells = sum(spots_of(array.shape[0]) for array in later)
     rows = ROWS * sum(array.shape[0] - spots_of(array.shape[0]) for array in later)
@@ -531,7 +529,7 @@
     return pl.pallas_call(
         fields_kernel,
         out_shape=jax.ShapeDtypeStruct(shape, jnp.float32),
-        in_specs=[VMEM] * (7 + len(stages)),
+        in_specs=[VMEM] * (8 + len(stages)),
         out_specs=pl.BlockSpec(memory_space=pl.ANY),
         scratch_shapes=[
             pltpu.VMEM((count, rows, LANES), jnp.float32),
@@ -543,17 +541,16 @@
             pltpu.VMEM((count, len(CORE), ROWS, LANES), jnp.float32),
             pltpu.VMEM((EDGE, EDGE * (ROWS + 1), LANES), jnp.float32),
             pltpu.VMEM(shape, jnp.float32),
-            pltpu.VMEM((DEGREE, SUB, LANES), jnp.float32),
             pltpu.SemaphoreType.DMA((EDGE // 2,)),
         ],
         compiler_params=pltpu.CompilerParams(vmem_limit_bytes=24 * 2**20),
         name="fields",
-    )(beside, own_rows, *stages, *later, modes)
+    )(beside, own_rows, *stages, *later, modes, tails)
 
 
 def body(orbitals, src_owner, src_slot):
-    packed, modes = messages(orbitals, src_owner, src_slot)
-    return fields((packed[0], *exchange(*packed)), modes, src_slot.size)
+    packed, modes, tails = messages(orbitals, src_owner, src_slot)
+    return fields((packed[0], *exchange(*packed)), modes, tails, src_slot.size)
 
 
 def solution(mesh):

time: 25.3 us -> 25.2 us (level)
  no operation moved by 1% of the time
where the time goes in v15:
time: 25.2 us; the launch traced here: 25.1 us
  starting transfers between devices  14.1 us (56%)
  Pallas kernels  6.84 us (27%)
  waiting for transfers between devices  2.4 us (10%)
  local copies, waits for them, and re-layouts  1.03 us (4%)
  other arithmetic  0.7 us (3%)
    ppermute x1, starting transfers between devices, exchange(): high = lax.ppermute(corner_high, both, diagonal(1, -1))  4.72 us
    pallas_call x1, Pallas kernels, fields(): pl.pallas_call(fields_kernel, out_shape=jax.ShapeDtypeStruct(shape, jnp.f...  3.99 us
    ppermute x2, starting transfers between devices, gathered(): other = lax.ppermute(mine, 'orb', [(i, i ^ 1 << bit) for i in range(count)])  3.42 us
    ppermute x2, waiting for transfers between devices, gathered(): other = lax.ppermute(mine, 'orb', [(i, i ^ 1 << bit) for i in range(count)])  2.26 us
    ppermute x1, starting transfers between devices, exchange(): above = lax.ppermute(first, 'sy', ring('sy', -1))  2.25 us
    pallas_call x1, Pallas kernels, modes_of(): pl.pallas_call(modes_kernel, out_shape=[jax.ShapeDtypeStruct(shape, jnp.f...  2.21 us
    ppermute x1, starting transfers between devices, exchange(): across = lax.ppermute(block, 'sx', ring('sx', 1))  2.11 us
    ppermute x1, starting transfers between devices, exchange(): below = lax.ppermute(last, 'sy', ring('sy', 1))  1.58 us
  transfers between devices with their start and end apart: 7, of which 3 were waited for; matrix products, arithmetic and copies ran while one was open for 0% of the time, Pallas kernels for 10%

profile of v15, /device:TPU:0, one launch (start us, length us, event | category | flops | bytes accessed | tf_op | source)
XLA Modules:
  0.0 25.1 jit_solution(1914541961749843792)
XLA Ops:
  0.0 0.7 %pad_add_fusion = s32[2,2,2]{2,1,0:T(2,128)S(1)} fusion(s32[1,2,2]{2,1,0:T(2,128)} %bitcast.2, s32[1,2,2]{2,1,0:T(2,128)} %bitcast.3), kind=kLoop, calls=%fused_computation | loop fusion | flops 8 | bytes 64 | tf_op jit(solution)/shard_map/stack | solution.py:208
  0.7 0.1 broadcast_in_dim.3.entries
  0.8 0.0 copy-start
  0.8 1.0 %copy-done = bf16[8,8,2048]{2,1,0:T(8,128)(2,1)S(1)} copy-done((bf16[8,8,2048]{2,1,0:T(8,128)(2,1)S(1)}, bf16[8,8,2048]{2,1,0:T(8,128)(2,1)}, u32[]{:S(2)}) %copy-start) | copy-done | bytes 262168
  1.7 0.2 prepare.1
  2.0 0.5 %collective-permute-start = (bf16[4,16,128]{2,1,0:T(8,128)(2,1)S(1)}, bf16[4,16,128]{2,1,0:T(8,128)(2,1)S(1)}, u32[]{:S(2)}, u32[]{:S(2)}) collective-permute-start(bf16[4,16,128]{2,1,0:T(8,128)(2,1)S(1)} %get-tuple-element.19.mine), channel_id=1, source_target_pairs={{0,8},{8,0},{16,24},{24,16},{1,9},{9,1},{17,25},{25,17},{2,10},{10... | collective-permute-start | bytes 49160 | tf_op jit(solution)/shard_map/ppermute | solution.py:154
  2.5 0.8 %collective-permute-done.other = bf16[4,16,128]{2,1,0:T(8,128)(2,1)S(1)} collective-permute-done((bf16[4,16,128]{2,1,0:T(8,128)(2,1)S(1)}, bf16[4,16,128]{2,1,0:T(8,128)(2,1)S(1)}, u32[]{:S(2)}, u32[]{:S(2)}) %collective-permute-start) | collective-permute-done | bytes 16416 | tf_op jit(solution)/shard_map/ppermute | solution.py:154
  3.3 2.9 %collective-permute-start.1 = (bf16[4,16,128]{2,1,0:T(8,128)(2,1)S(1)}, bf16[4,16,128]{2,1,0:T(8,128)(2,1)S(1)}, u32[]{:S(2)}, u32[]{:S(2)}) collective-permute-start(bf16[4,16,128]{2,1,0:T(8,128)(2,1)S(1)} %nearer.1.after.mine), channel_id=1, source_target_pairs={{0,16},{8,24},{16,0},{24,8},{1,17},{9,25},{17,1},{25,9},{2,18},{10... | collective-permute-start | bytes 49160 | tf_op jit(solution)/shard_map/ppermute | solution.py:154
  6.2 0.3 %sines.1 = (bf16[256,256]{1,0:T(8,128)(2,1)S(1)}, f32[4,8,128]{2,1,0:T(8,128)S(1)}) custom-call(bf16[4,16,128]{2,1,0:T(8,128)(2,1)S(1)} %nearer.1.after.mine), custom_call_target="tpu_custom_call" | custom-call | bytes 2097152 | tf_op jit(solution)/shard_map/sines/pallas_call | solution.py:287
  6.5 1.4 %collective-permute-done.1.refs_0_ = bf16[4,16,128]{2,1,0:T(8,128)(2,1)S(1)} collective-permute-done((bf16[4,16,128]{2,1,0:T(8,128)(2,1)S(1)}, bf16[4,16,128]{2,1,0:T(8,128)(2,1)S(1)}, u32[]{:S(2)}, u32[]{:S(2)}) %collective-permute-start.1) | collective-permute-done | bytes 16416 | tf_op jit(solution)/shard_map/ppermute | solution.py:154
  8.0 0.1 messages.1
  8.0 2.1 %collective-permute-start.2 = (bf16[68,16,128]{2,1,0:T(8,128)(2,1)S(1)}, bf16[68,16,128]{2,1,0:T(8,128)(2,1)S(1)}, u32[]{:S(2)}, u32[]{:S(2)}) collective-permute-start(bf16[68,16,128]{2,1,0:T(8,128)(2,1)S(1)} %get-tuple-element.22.own), channel_id=1, source_target_pairs={{0,4},{4,0},{1,5},{5,1},{2,6},{6,2},{3,7},{7,3},{8,12},{12,8},{9,1... | collective-permute-start | bytes 835592 | tf_op jit(solution)/shard_map/ppermute | solution.py:231
  10.2 1.6 %collective-permute-start.3 = (bf16[34,16,128]{2,1,0:T(8,128)(2,1)S(1)}, bf16[34,16,128]{2,1,0:T(8,128)(2,1)S(1)}, u32[]{:S(2)}, u32[]{:S(2)}) collective-permute-start(bf16[34,16,128]{2,1,0:T(8,128)(2,1)S(1)} %get-tuple-element.29), channel_id=1, source_target_pairs={{0,1},{1,2},{2,3},{3,0},{4,5},{5,6},{6,7},{7,4},{8,9},{9,10},{10,1... | collective-permute-start | bytes 417800 | tf_op jit(solution)/shard_map/ppermute | solution.py:248
  11.7 2.2 %collective-permute-start.4 = (bf16[34,16,128]{2,1,0:T(8,128)(2,1)S(1)}, bf16[34,16,128]{2,1,0:T(8,128)(2,1)S(1)}, u32[]{:S(2)}, u32[]{:S(2)}) collective-permute-start(bf16[34,16,128]{2,1,0:T(8,128)(2,1)S(1)} %get-tuple-element.30), channel_id=1, source_target_pairs={{0,3},{1,0},{2,1},{3,2},{4,7},{5,4},{6,5},{7,6},{8,11},{9,8},{10,9... | collective-permute-start | bytes 417800 | tf_op jit(solution)/shard_map/ppermute | solution.py:249
  14.0 0.0 collective-permute-start.5
  14.0 4.7 %collective-permute-start.6 = (bf16[13,16,128]{2,1,0:T(8,128)(2,1)S(1)}, bf16[13,16,128]{2,1,0:T(8,128)(2,1)S(1)}, u32[]{:S(2)}, u32[]{:S(2)}) collective-permute-start(bf16[13,16,128]{2,1,0:T(8,128)(2,1)S(1)} %get-tuple-element.32), channel_id=1, source_target_pairs={{0,7},{1,4},{2,5},{3,6},{4,3},{5,0},{6,1},{7,2},{8,15},{9,12},{10,... | collective-permute-start | bytes 159752 | tf_op jit(solution)/shard_map/ppermute | solution.py:230
  18.7 0.0 collective-permute-done.2.across
  18.7 2.2 %modes.1 = (f32[4,128,16,128]{3,2,1,0:T(8,128)S(1)}, f32[4,64,128]{2,1,0:T(8,128)S(1)}, f32[4,84,16,128]{3,2,1,0:T(8,128)S(1)}, f32[4,48,16,128]{3,2,1,0:T(8,128)S(1)}, f32[4,20,16,128]{3,2,1,0:T(8,128)S(1)}) custom-call(bf16[68,16,128]{2,1,0:T(8,128)(2,1)S(1)} %get-tuple-element.22.own, bf16[68,16,128]{2,1,0:T(8,128)(2,1)S(1)} %collective-permute-done.2.across, ...), custom_call_target="tpu_custom_call" | custom-call | bytes 6291456 | tf_op jit(solution)/shard_map/modes/pallas_call | solution.py:434
  20.9 0.1 collective-permute-done.5.refs_5_
  21.1 0.0 collective-permute-done.6.refs_6_
  21.1 0.0 collective-permute-done.3.refs_3_
  21.1 0.0 collective-permute-done.4.refs_4_
  21.1 4.0 %fields.1 = f32[8,8,2048]{2,1,0:T(8,128)} custom-call(f32[4,128,16,128]{3,2,1,0:T(8,128)S(1)} %get-tuple-element.24.beside, f32[4,64,128]{2,1,0:T(8,128)S(1)} %get-tuple-element.25.own_rows, f32[4,84,16,128]{3,2,1,0:T(8,128)S(1)} %get-tuple-element.26.refs_0_, f32[4,48,16,128]{3,2,1,0:T(8,128)S(1)} %get-tuple-element.27.refs_1_, ...), custom_call_target="tpu_custom_call" | custom-call | tf_op jit(solution)/shard_map/fields/pallas_call | solution.py:529
  (1 shorter events, 0.0 us)
Async XLA Ops:
  0.8 1.0 %copy-start = (bf16[8,8,2048]{2,1,0:T(8,128)(2,1)S(1)}, bf16[8,8,2048]{2,1,0:T(8,128)(2,1)}, u32[]{:S(2)}) copy-start(bf16[8,8,2048]{2,1,0:T(8,128)(2,1)} %orbitals.1) | copy-start | bytes 786436
  2.0 1.4 %collective-permute-start = (bf16[4,16,128]{2,1,0:T(8,128)(2,1)S(1)}, bf16[4,16,128]{2,1,0:T(8,128)(2,1)S(1)}, u32[]{:S(2)}, u32[]{:S(2)}) collective-permute-start(bf16[4,16,128]{2,1,0:T(8,128)(2,1)S(1)} %get-tuple-element.19.mine), channel_id=1, source_target_pairs={{0,8},{8,0},{16,24},{24,16},{1,9},{9,1},{17,25},{25,17},{2,10},{10... | collective-permute-start | bytes 49160 | tf_op jit(solution)/shard_map/ppermute | solution.py:154
  3.3 4.6 %collective-permute-start.1 = (bf16[4,16,128]{2,1,0:T(8,128)(2,1)S(1)}, bf16[4,16,128]{2,1,0:T(8,128)(2,1)S(1)}, u32[]{:S(2)}, u32[]{:S(2)}) collective-permute-start(bf16[4,16,128]{2,1,0:T(8,128)(2,1)S(1)} %nearer.1.after.mine), channel_id=1, source_target_pairs={{0,16},{8,24},{16,0},{24,8},{1,17},{9,25},{17,1},{25,9},{2,18},{10... | collective-permute-start | bytes 49160 | tf_op jit(solution)/shard_map/ppermute | solution.py:154
  8.0 10.7 %collective-permute-start.2 = (bf16[68,16,128]{2,1,0:T(8,128)(2,1)S(1)}, bf16[68,16,128]{2,1,0:T(8,128)(2,1)S(1)}, u32[]{:S(2)}, u32[]{:S(2)}) collective-permute-start(bf16[68,16,128]{2,1,0:T(8,128)(2,1)S(1)} %get-tuple-element.22.own), channel_id=1, source_target_pairs={{0,4},{4,0},{1,5},{5,1},{2,6},{6,2},{3,7},{7,3},{8,12},{12,8},{9,1... | collective-permute-start | bytes 835592 | tf_op jit(solution)/shard_map/ppermute | solution.py:231
  10.2 10.9 %collective-permute-start.3 = (bf16[34,16,128]{2,1,0:T(8,128)(2,1)S(1)}, bf16[34,16,128]{2,1,0:T(8,128)(2,1)S(1)}, u32[]{:S(2)}, u32[]{:S(2)}) collective-permute-start(bf16[34,16,128]{2,1,0:T(8,128)(2,1)S(1)} %get-tuple-element.29), channel_id=1, source_target_pairs={{0,1},{1,2},{2,3},{3,0},{4,5},{5,6},{6,7},{7,4},{8,9},{9,10},{10,1... | collective-permute-start | bytes 417800 | tf_op jit(solution)/shard_map/ppermute | solution.py:248
  11.7 9.3 %collective-permute-start.4 = (bf16[34,16,128]{2,1,0:T(8,128)(2,1)S(1)}, bf16[34,16,128]{2,1,0:T(8,128)(2,1)S(1)}, u32[]{:S(2)}, u32[]{:S(2)}) collective-permute-start(bf16[34,16,128]{2,1,0:T(8,128)(2,1)S(1)} %get-tuple-element.30), channel_id=1, source_target_pairs={{0,3},{1,0},{2,1},{3,2},{4,7},{5,4},{6,5},{7,6},{8,11},{9,8},{10,9... | collective-permute-start | bytes 417800 | tf_op jit(solution)/shard_map/ppermute | solution.py:249
  14.0 7.1 %collective-permute-start.5 = (bf16[13,16,128]{2,1,0:T(8,128)(2,1)S(1)}, bf16[13,16,128]{2,1,0:T(8,128)(2,1)S(1)}, u32[]{:S(2)}, u32[]{:S(2)}) collective-permute-start(bf16[13,16,128]{2,1,0:T(8,128)(2,1)S(1)} %get-tuple-element.31), channel_id=1, source_target_pairs={{0,5},{1,6},{2,7},{3,4},{4,1},{5,2},{6,3},{7,0},{8,13},{9,14},{10,... | collective-permute-start | bytes 159752 | tf_op jit(solution)/shard_map/ppermute | solution.py:229
  14.0 7.1 %collective-permute-start.6 = (bf16[13,16,128]{2,1,0:T(8,128)(2,1)S(1)}, bf16[13,16,128]{2,1,0:T(8,128)(2,1)S(1)}, u32[]{:S(2)}, u32[]{:S(2)}) collective-permute-start(bf16[13,16,128]{2,1,0:T(8,128)(2,1)S(1)} %get-tuple-element.32), channel_id=1, source_target_pairs={{0,7},{1,4},{2,5},{3,6},{4,3},{5,0},{6,1},{7,2},{8,15},{9,12},{10,... | collective-permute-start | bytes 159752 | tf_op jit(solution)/shard_map/ppermute | solution.py:230

commit v16 on v15

--- a/solution.py
+++ b/solution.py
@@ -189,7 +189,9 @@
         for tile in range(rows.shape[0] // ROWS):
             ref[used + tile] = rows[tile * ROWS : (tile + 1) * ROWS]
 
-    pack(block, [(x, y) for x in range(EDGE) for y in range(EDGE)])
+    for tile in range(block.shape[0]):
+        rows = picked[tile] if tile < len(picked) else jnp.zeros((ROWS, LANES), jnp.float32)
+        block[tile] = rows.astype(jnp.bfloat16)
     pack(last, [(x, y) for x in range(EDGE) for y in range(EDGE - HALO, EDGE)])
     pack(first, [(x, y) for x in range(EDGE) for y in range(HALO)])
     pack(corner_low, CORNER_LOW)
@@ -208,46 +210,50 @@
     entries = spread_out(jnp.stack([src_slot, src_owner]))
     mine, cells = prepare(entries, orbitals)
     mine, others, bit = gathered(entries, mine)
-    lengths = [EDGE * EDGE] + [EDGE * HALO] * 2 + [len(CORNER_LOW)] * 2
+    lengths = [EDGE * HALO] * 2 + [len(CORNER_LOW)] * 2
     modes, tails = sines(mine)
     packed = pl.pallas_call(
         functools.partial(messages_kernel, bit),
         out_shape=[
-            jax.ShapeDtypeStruct((tiles(length), ROWS, LANES), jnp.bfloat16) for length in lengths
+            jax.ShapeDtypeStruct((length, ROWS, LANES), jnp.bfloat16)
+            for length in [tiles(len(CORNER_LOW)) + 1] + [tiles(length) for length in lengths]
         ],
         in_specs=[pl.BlockSpec(memory_space=pl.ANY)] + [VMEM] * (3 + len(others)),
         out_specs=[VMEM] * 5,
         compiler_params=SMALL,
         name="messages",
     )(modes, entries, cells, mine, *others)
-    return packed, modes, tails
-
-
-def exchange(block, last, first, corner_low, corner_high):
+    return cells, packed, modes, tails
+
+
+def across_x(tiles, used):
+    if lax.axis_size("sx") == 2:
+        return lax.ppermute(tiles, "sx", ring("sx", 1))
+    half = used // 2
+    low = lax.ppermute(tiles[:half], "sx", ring("sx", -1))
+    return jnp.concatenate([low, lax.ppermute(tiles[half:used], "sx", ring("sx", 1))], axis=0)
+
+
+def across_corner(cells, step_y):
     both = ("sx", "sy")
     if lax.axis_size("sx") == 2:
-        low = lax.ppermute(corner_low, both, diagonal(1, 1))
-        high = lax.ppermute(corner_high, both, diagonal(1, -1))
-        across = lax.ppermute(block, "sx", ring("sx", 1))
-    else:
-        def two_ways(cells, half, axes, down, up, merge):
-            end = 2 * half
-            back = lax.ppermute(jnp.concatenate([cells[:half], cells[end:]]), axes, down)
-            ahead = lax.ppermute(jnp.concatenate([cells[half:end], cells[end:]]), axes, up)
-            return jnp.concatenate([back[:half], ahead[:half], merge(back[half:], ahead[half:])])
-
-        def halves(back, ahead):
-            return jnp.concatenate([back[: back.shape[0] // 2], ahead[ahead.shape[0] // 2 :]])
-
-        def rows(back, ahead):
-            return jnp.concatenate([back[:, :SPLIT], ahead[:, SPLIT:]], axis=1)
-
-        low = two_ways(corner_low, SPLIT, both, diagonal(-1, 1), diagonal(1, 1), rows)
-        high = two_ways(corner_high, SPLIT, both, diagonal(-1, -1), diagonal(1, -1), rows)
-        across = two_ways(block, EDGE * HALO, "sx", ring("sx", -1), ring("sx", 1), halves)
+        return lax.ppermute(cells, both, diagonal(1, step_y))
+    end = 2 * SPLIT
+    back, ahead = (
+        lax.ppermute(jnp.concatenate([part, cells[end:]]), both, diagonal(step_x, step_y))
+        for part, step_x in ((cells[:SPLIT], -1), (cells[SPLIT:end], 1))
+    )
+    rows = jnp.concatenate([back[SPLIT:, :SPLIT], ahead[SPLIT:, SPLIT:]], axis=1)
+    return jnp.concatenate([back[:SPLIT], ahead[:SPLIT], rows], axis=0)
+
+
+def exchange(cells, sources, last, first, corner_low, corner_high):
+    beside = (cells, across_x(cells, cells.shape[0]))
+    rows = (sources, across_x(sources, EDGE * EDGE // ROWS))
     below = lax.ppermute(last, "sy", ring("sy", 1))
     above = lax.ppermute(first, "sy", ring("sy", -1))
-    return across, below, above, low, high
+    low, high = across_corner(corner_low, 1), across_corner(corner_high, -1)
+    return beside, rows, (below, above, low, high)
 
 
 def place_of(x, y):
@@ -327,7 +333,7 @@
     lane = lax.broadcasted_iota(jnp.int32, shape, 1)
     line = lax.broadcasted_iota(jnp.int32, shape, 0)
     repeat = (line == lane // LANES * NZ + lane % NZ).astype(jnp.bfloat16)
-    packed = [ref[spots_of(ref.shape[0]) :].reshape(-1, LANES) for ref in refs]
+    packed = [ref[...].reshape(-1, LANES) for ref in refs]
     firsts = [sum(part.shape[0] for part in packed[:at]) for at in range(len(packed))]
     packed = jnp.concatenate(packed, axis=0)
     spread = jnp.dot(packed, repeat, preferred_element_type=jnp.float32)
@@ -350,13 +356,13 @@
     return (both[:, :LANES] + both[:, LANES:]).reshape(cells, ROWS, LANES)
 
 
-def densities(refs, rows, parts, modes, hat):
+def densities(refs, sources, rows, parts, modes, hat):
     count = hat.shape[0]
-    firsts = all_rows(refs, rows)
+    firsts = all_rows(sources, rows)
     cells = [
         (ref, at, first + at)
         for ref, first in zip(refs, firsts)
-        for at in range(spots_of(ref.shape[0]))
+        for at in range(ref.shape[0])
     ]
     pieces = -(-len(cells) // 48)
     for piece in range(pieces):
@@ -401,9 +407,11 @@
                 put(x, y, summed[x, y] + summed[x - 1, y - 1] + tail[...] * here)
 
 
-def modes_kernel(own, across, modes, tails, hat, own_rows, *refs):
+def modes_kernel(own, across, own_sources, sources, modes, tails, hat, own_rows, *refs):
     stages, (rows, parts) = refs[: DEGREE - 1], refs[DEGREE - 1 :]
-    densities((own, across), rows, parts, modes, hat)
+    used = pl.ds(0, EDGE * EDGE // ROWS)
+    sources = (own_sources.at[used], sources.at[used])
+    densities((own, across), sources, rows, parts, modes, hat)
     own_rows[...] = rows[:, : own_rows.shape[1], :] * (-power_coeffs()[-1])
     for place in range(hat.shape[0]):
         for half in range(ROWS // SUB):
@@ -426,7 +434,7 @@
                 old = load
 
 
-def modes_of(own, across, modes, tails, count):
+def modes_of(beside, sources, modes, tails, count):
     cells = 2 * len(CORE)
     lengths = [cells] + [len(stage) for stage in EARLY]
     shapes = [(count, length, ROWS, LANES) for length in lengths]
@@ -434,7 +442,7 @@
     return pl.pallas_call(
         modes_kernel,
         out_shape=[jax.ShapeDtypeStruct(shape, jnp.float32) for shape in shapes],
-        in_specs=[VMEM] * 4,
+        in_specs=[VMEM] * 6,
         out_specs=[VMEM] * len(shapes),
         scratch_shapes=[
             pltpu.VMEM((count, cells, LANES), jnp.float32),
@@ -443,7 +451,7 @@
         compiler_params=pltpu.CompilerParams(vmem_limit_bytes=20 * 2**20),
         cost_estimate=pl.CostEstimate(flops=0, bytes_accessed=6 * 2**20, transcendentals=0),
         name="modes",
-    )(own, across, modes, tails)
+    )(*beside, *sources, modes, tails)
 
 
 def fields_kernel(beside, own_rows, *refs):
@@ -458,7 +466,11 @@
     offset = [0]
     for ref in later:
         offset.append(offset[-1] + spots_of(ref.shape[0]))
-    densities(later, rows, parts, modes, hat)
+    cells = [ref.at[pl.ds(0, spots_of(ref.shape[0]))] for ref in later]
+    sources = [
+        ref.at[pl.ds(spots_of(ref.shape[0]), ref.shape[0] - spots_of(ref.shape[0]))] for ref in later
+    ]
+    densities(cells, sources, rows, parts, modes, hat)
 
     def steps(place, half):
         part = pl.ds(half * SUB, SUB)
@@ -519,9 +531,8 @@
         copy.wait()
 
 
-def fields(halo, modes, tails, count):
-    own, across, *later = halo
-    beside, own_rows, *stages = modes_of(own, across, modes, tails, count)
+def fields(beside, sources, later, modes, tails, count):
+    beside, own_rows, *stages = modes_of(beside, sources, modes, tails, count)
     plane = pltpu.VMEM((SIZE, SIZE, SUB, LANES), jnp.float32)
     cells = sum(spots_of(array.shape[0]) for array in later)
     rows = ROWS * sum(array.shape[0] - spots_of(array.shape[0]) for array in later)
@@ -549,8 +560,8 @@
 
 
 def body(orbitals, src_owner, src_slot):
-    packed, modes, tails = messages(orbitals, src_owner, src_slot)
-    return fields((packed[0], *exchange(*packed)), modes, tails, src_slot.size)
+    cells, packed, modes, tails = messages(orbitals, src_owner, src_slot)
+    return fields(*exchange(cells, *packed), modes, tails, src_slot.size)
 
 
 def solution(mesh):

time: 25.2 us -> 27.3 us (1.083)
  waiting for transfers between devices: 2.4 us -> 6.93 us
  starting transfers between devices: 14.1 us -> 11.7 us
    ppermute x3 -> x4, waiting for transfers between devices: 0.14 us -> 3.8 us  [the longest x2 2.94 us: across_x(): return lax.ppermute(tiles, 'sx', ring('sx', 1))]
    ppermute x2, starting transfers between devices: 3.42 us -> 1.56 us  [gathered(): other = lax.ppermute(mine, 'orb', [(i, i ^ 1 << bit) for i in range(count)])]
    ppermute x2, waiting for transfers between devices: 2.26 us -> 3.13 us  [gathered(): other = lax.ppermute(mine, 'orb', [(i, i ^ 1 << bit) for i in range(count)])]
    ppermute x3 -> x4, starting transfers between devices: 6.84 us -> 6.23 us  [the longest x2 3.38 us: across_x(): return lax.ppermute(tiles, 'sx', ring('sx', 1))]
  transfers between devices with their start and end apart: 7 -> 8, of which waited for: 3 -> 4; matrix products, arithmetic and copies ran while one was open for 0% -> 0% of each run, Pallas kernels for 10% -> 9%
where the time goes in v16:
time: 27.3 us; the launch traced here: 27.1 us
  starting transfers between devices  11.7 us (43%)
  waiting for transfers between devices  6.93 us (25%)
  Pallas kernels  6.77 us (25%)
  local copies, waits for them, and re-layouts  1.03 us (4%)
  other arithmetic  0.7 us (3%)
    pallas_call x1, Pallas kernels, fields(): pl.pallas_call(fields_kernel, out_shape=jax.ShapeDtypeStruct(shape, jnp.f...  3.98 us
    ppermute x2, starting transfers between devices, across_x(): return lax.ppermute(tiles, 'sx', ring('sx', 1))  3.38 us
    ppermute x2, waiting for transfers between devices, gathered(): other = lax.ppermute(mine, 'orb', [(i, i ^ 1 << bit) for i in range(count)])  3.13 us
    ppermute x2, waiting for transfers between devices, across_x(): return lax.ppermute(tiles, 'sx', ring('sx', 1))  2.94 us
    ppermute x2, starting transfers between devices, across_corner(): return lax.ppermute(cells, both, diagonal(1, step_y))  2.84 us
    ppermute x1, starting transfers between devices, exchange(): above = lax.ppermute(first, 'sy', ring('sy', -1))  2.25 us
    pallas_call x1, Pallas kernels, modes_of(): pl.pallas_call(modes_kernel, out_shape=[jax.ShapeDtypeStruct(shape, jnp.f...  2.2 us
    ppermute x1, starting transfers between devices, exchange(): below = lax.ppermute(last, 'sy', ring('sy', 1))  1.63 us
  transfers between devices with their start and end apart: 8, of which 4 were waited for; matrix products, arithmetic and copies ran while one was open for 0% of the time, Pallas kernels for 9%

profile of v16, /device:TPU:0, one launch (start us, length us, event | category | flops | bytes accessed | tf_op | source)
XLA Modules:
  0.0 27.1 jit_solution(16567849878617289782)
XLA Ops:
  0.0 0.7 %pad_add_fusion = s32[2,2,2]{2,1,0:T(2,128)S(1)} fusion(s32[1,2,2]{2,1,0:T(2,128)} %bitcast.2, s32[1,2,2]{2,1,0:T(2,128)} %bitcast.3), kind=kLoop, calls=%fused_computation | loop fusion | flops 8 | bytes 64 | tf_op jit(solution)/shard_map/stack | solution.py:210
  0.7 0.1 broadcast_in_dim.3.entries
  0.8 0.0 copy-start
  0.8 1.0 %copy-done = bf16[8,8,2048]{2,1,0:T(8,128)(2,1)S(1)} copy-done((bf16[8,8,2048]{2,1,0:T(8,128)(2,1)S(1)}, bf16[8,8,2048]{2,1,0:T(8,128)(2,1)}, u32[]{:S(2)}) %copy-start) | copy-done | bytes 262168
  1.7 0.2 prepare.1
  2.0 3.0 %collective-permute-start = (bf16[64,16,128]{2,1,0:T(8,128)(2,1)S(1)}, bf16[64,16,128]{2,1,0:T(8,128)(2,1)S(1)}, u32[]{:S(2)}, u32[]{:S(2)}) collective-permute-start(bf16[64,16,128]{2,1,0:T(8,128)(2,1)S(1)} %get-tuple-element.19.cells.own), channel_id=1, source_target_pairs={{0,4},{4,0},{1,5},{5,1},{2,6},{6,2},{3,7},{7,3},{8,12},{12,8},{9,1... | collective-permute-start | bytes 786440 | tf_op jit(solution)/shard_map/ppermute | solution.py:231
  5.0 0.0 collective-permute-start.1
  5.0 1.2 %collective-permute-done.1.other = bf16[4,16,128]{2,1,0:T(8,128)(2,1)S(1)} collective-permute-done((bf16[4,16,128]{2,1,0:T(8,128)(2,1)S(1)}, bf16[4,16,128]{2,1,0:T(8,128)(2,1)S(1)}, u32[]{:S(2)}, u32[]{:S(2)}) %collective-permute-start.1) | collective-permute-done | bytes 16416 | tf_op jit(solution)/shard_map/ppermute | solution.py:154
  6.2 1.6 %collective-permute-start.2 = (bf16[4,16,128]{2,1,0:T(8,128)(2,1)S(1)}, bf16[4,16,128]{2,1,0:T(8,128)(2,1)S(1)}, u32[]{:S(2)}, u32[]{:S(2)}) collective-permute-start(bf16[4,16,128]{2,1,0:T(8,128)(2,1)S(1)} %nearer.1.after.mine), channel_id=1, source_target_pairs={{0,16},{8,24},{16,0},{24,8},{1,17},{9,25},{17,1},{25,9},{2,18},{10... | collective-permute-start | bytes 49160 | tf_op jit(solution)/shard_map/ppermute | solution.py:154
  7.8 0.3 %sines.1 = (bf16[256,256]{1,0:T(8,128)(2,1)S(1)}, f32[4,8,128]{2,1,0:T(8,128)S(1)}) custom-call(bf16[4,16,128]{2,1,0:T(8,128)(2,1)S(1)} %nearer.1.after.mine), custom_call_target="tpu_custom_call" | custom-call | bytes 2097152 | tf_op jit(solution)/shard_map/sines/pallas_call | solution.py:293
  8.1 1.9 %collective-permute-done.2.refs_0_ = bf16[4,16,128]{2,1,0:T(8,128)(2,1)S(1)} collective-permute-done((bf16[4,16,128]{2,1,0:T(8,128)(2,1)S(1)}, bf16[4,16,128]{2,1,0:T(8,128)(2,1)S(1)}, u32[]{:S(2)}, u32[]{:S(2)}) %collective-permute-start.2) | collective-permute-done | bytes 16416 | tf_op jit(solution)/shard_map/ppermute | solution.py:154
  10.1 1.6 %collective-permute-start.4 = (bf16[34,16,128]{2,1,0:T(8,128)(2,1)S(1)}, bf16[34,16,128]{2,1,0:T(8,128)(2,1)S(1)}, u32[]{:S(2)}, u32[]{:S(2)}) collective-permute-start(bf16[34,16,128]{2,1,0:T(8,128)(2,1)S(1)} %get-tuple-element.29), channel_id=1, source_target_pairs={{0,1},{1,2},{2,3},{3,0},{4,5},{5,6},{6,7},{7,4},{8,9},{9,10},{10,1... | collective-permute-start | bytes 417800 | tf_op jit(solution)/shard_map/ppermute | solution.py:253
  11.7 2.2 %collective-permute-start.5 = (bf16[34,16,128]{2,1,0:T(8,128)(2,1)S(1)}, bf16[34,16,128]{2,1,0:T(8,128)(2,1)S(1)}, u32[]{:S(2)}, u32[]{:S(2)}) collective-permute-start(bf16[34,16,128]{2,1,0:T(8,128)(2,1)S(1)} %get-tuple-element.30), channel_id=1, source_target_pairs={{0,3},{1,0},{2,1},{3,2},{4,7},{5,4},{6,5},{7,6},{8,11},{9,8},{10,9... | collective-permute-start | bytes 417800 | tf_op jit(solution)/shard_map/ppermute | solution.py:254
  13.9 0.3 %collective-permute-start.3 = (bf16[14,16,128]{2,1,0:T(8,128)(2,1)S(1)}, bf16[14,16,128]{2,1,0:T(8,128)(2,1)S(1)}, u32[]{:S(2)}, u32[]{:S(2)}) collective-permute-start(bf16[14,16,128]{2,1,0:T(8,128)(2,1)S(1)} %get-tuple-element.22.own_sources), channel_id=1, source_target_pairs={{0,4},{4,0},{1,5},{5,1},{2,6},{6,2},{3,7},{7,3},{8,12},{12,8},{9,1... | collective-permute-start | bytes 172040 | tf_op jit(solution)/shard_map/ppermute | solution.py:231
  14.3 0.9 %collective-permute-start.6 = (bf16[13,16,128]{2,1,0:T(8,128)(2,1)S(1)}, bf16[13,16,128]{2,1,0:T(8,128)(2,1)S(1)}, u32[]{:S(2)}, u32[]{:S(2)}) collective-permute-start(bf16[13,16,128]{2,1,0:T(8,128)(2,1)S(1)} %get-tuple-element.31), channel_id=1, source_target_pairs={{0,5},{1,6},{2,7},{3,4},{4,1},{5,2},{6,3},{7,0},{8,13},{9,14},{10,... | collective-permute-start | bytes 159752 | tf_op jit(solution)/shard_map/ppermute | solution.py:240
  15.2 2.9 %collective-permute-done.3.sources = bf16[14,16,128]{2,1,0:T(8,128)(2,1)S(1)} collective-permute-done((bf16[14,16,128]{2,1,0:T(8,128)(2,1)S(1)}, bf16[14,16,128]{2,1,0:T(8,128)(2,1)S(1)}, u32[]{:S(2)}, u32[]{:S(2)}) %collective-permute-start.3) | collective-permute-done | bytes 57376 | tf_op jit(solution)/shard_map/ppermute | solution.py:231
  18.1 2.0 %collective-permute-start.7 = (bf16[13,16,128]{2,1,0:T(8,128)(2,1)S(1)}, bf16[13,16,128]{2,1,0:T(8,128)(2,1)S(1)}, u32[]{:S(2)}, u32[]{:S(2)}) collective-permute-start(bf16[13,16,128]{2,1,0:T(8,128)(2,1)S(1)} %get-tuple-element.32), channel_id=1, source_target_pairs={{0,7},{1,4},{2,5},{3,6},{4,3},{5,0},{6,1},{7,2},{8,15},{9,12},{10,... | collective-permute-start | bytes 159752 | tf_op jit(solution)/shard_map/ppermute | solution.py:240
  20.1 0.0 collective-permute-done.across
  20.1 2.2 %modes.1 = (f32[4,128,16,128]{3,2,1,0:T(8,128)S(1)}, f32[4,64,128]{2,1,0:T(8,128)S(1)}, f32[4,84,16,128]{3,2,1,0:T(8,128)S(1)}, f32[4,48,16,128]{3,2,1,0:T(8,128)S(1)}, f32[4,20,16,128]{3,2,1,0:T(8,128)S(1)}) custom-call(bf16[64,16,128]{2,1,0:T(8,128)(2,1)S(1)} %get-tuple-element.19.cells.own, bf16[64,16,128]{2,1,0:T(8,128)(2,1)S(1)} %collective-permute-done.across, ...), custom_call_target="tpu_custom_call" | custom-call | bytes 6291456 | tf_op jit(solution)/shard_map/modes/pallas_call | solution.py:442
  22.3 0.0 collective-permute-done.6.refs_5_
  22.3 0.9 %collective-permute-done.7.refs_6_ = bf16[13,16,128]{2,1,0:T(8,128)(2,1)S(1)} collective-permute-done((bf16[13,16,128]{2,1,0:T(8,128)(2,1)S(1)}, bf16[13,16,128]{2,1,0:T(8,128)(2,1)S(1)}, u32[]{:S(2)}, u32[]{:S(2)}) %collective-permute-start.7) | collective-permute-done | bytes 53280 | tf_op jit(solution)/shard_map/ppermute | solution.py:240
  23.1 0.0 collective-permute-done.4.refs_3_
  23.1 0.0 collective-permute-done.5.refs_4_
  23.2 4.0 %fields.1 = f32[8,8,2048]{2,1,0:T(8,128)} custom-call(f32[4,128,16,128]{3,2,1,0:T(8,128)S(1)} %get-tuple-element.24.beside, f32[4,64,128]{2,1,0:T(8,128)S(1)} %get-tuple-element.25.own_rows, f32[4,84,16,128]{3,2,1,0:T(8,128)S(1)} %get-tuple-element.26.refs_0_, f32[4,48,16,128]{3,2,1,0:T(8,128)S(1)} %get-tuple-element.27.refs_1_, ...), custom_call_target="tpu_custom_call" | custom-call | tf_op jit(solution)/shard_map/fields/pallas_call | solution.py:540
  (2 shorter events, 0.1 us)
Async XLA Ops:
  0.8 1.0 %copy-start = (bf16[8,8,2048]{2,1,0:T(8,128)(2,1)S(1)}, bf16[8,8,2048]{2,1,0:T(8,128)(2,1)}, u32[]{:S(2)}) copy-start(bf16[8,8,2048]{2,1,0:T(8,128)(2,1)} %orbitals.1) | copy-start | bytes 786436
  2.0 18.1 %collective-permute-start = (bf16[64,16,128]{2,1,0:T(8,128)(2,1)S(1)}, bf16[64,16,128]{2,1,0:T(8,128)(2,1)S(1)}, u32[]{:S(2)}, u32[]{:S(2)}) collective-permute-start(bf16[64,16,128]{2,1,0:T(8,128)(2,1)S(1)} %get-tuple-element.19.cells.own), channel_id=1, source_target_pairs={{0,4},{4,0},{1,5},{5,1},{2,6},{6,2},{3,7},{7,3},{8,12},{12,8},{9,1... | collective-permute-start | bytes 786440 | tf_op jit(solution)/shard_map/ppermute | solution.py:231
  5.0 1.2 %collective-permute-start.1 = (bf16[4,16,128]{2,1,0:T(8,128)(2,1)S(1)}, bf16[4,16,128]{2,1,0:T(8,128)(2,1)S(1)}, u32[]{:S(2)}, u32[]{:S(2)}) collective-permute-start(bf16[4,16,128]{2,1,0:T(8,128)(2,1)S(1)} %get-tuple-element.20.mine), channel_id=1, source_target_pairs={{0,8},{8,0},{16,24},{24,16},{1,9},{9,1},{17,25},{25,17},{2,10},{10... | collective-permute-start | bytes 49160 | tf_op jit(solution)/shard_map/ppermute | solution.py:154
  6.2 3.8 %collective-permute-start.2 = (bf16[4,16,128]{2,1,0:T(8,128)(2,1)S(1)}, bf16[4,16,128]{2,1,0:T(8,128)(2,1)S(1)}, u32[]{:S(2)}, u32[]{:S(2)}) collective-permute-start(bf16[4,16,128]{2,1,0:T(8,128)(2,1)S(1)} %nearer.1.after.mine), channel_id=1, source_target_pairs={{0,16},{8,24},{16,0},{24,8},{1,17},{9,25},{17,1},{25,9},{2,18},{10... | collective-permute-start | bytes 49160 | tf_op jit(solution)/shard_map/ppermute | solution.py:154
  10.1 13.1 %collective-permute-start.4 = (bf16[34,16,128]{2,1,0:T(8,128)(2,1)S(1)}, bf16[34,16,128]{2,1,0:T(8,128)(2,1)S(1)}, u32[]{:S(2)}, u32[]{:S(2)}) collective-permute-start(bf16[34,16,128]{2,1,0:T(8,128)(2,1)S(1)} %get-tuple-element.29), channel_id=1, source_target_pairs={{0,1},{1,2},{2,3},{3,0},{4,5},{5,6},{6,7},{7,4},{8,9},{9,10},{10,1... | collective-permute-start | bytes 417800 | tf_op jit(solution)/shard_map/ppermute | solution.py:253
  11.7 11.5 %collective-permute-start.5 = (bf16[34,16,128]{2,1,0:T(8,128)(2,1)S(1)}, bf16[34,16,128]{2,1,0:T(8,128)(2,1)S(1)}, u32[]{:S(2)}, u32[]{:S(2)}) collective-permute-start(bf16[34,16,128]{2,1,0:T(8,128)(2,1)S(1)} %get-tuple-element.30), channel_id=1, source_target_pairs={{0,3},{1,0},{2,1},{3,2},{4,7},{5,4},{6,5},{7,6},{8,11},{9,8},{10,9... | collective-permute-start | bytes 417800 | tf_op jit(solution)/shard_map/ppermute | solution.py:254
  13.9 4.2 %collective-permute-start.3 = (bf16[14,16,128]{2,1,0:T(8,128)(2,1)S(1)}, bf16[14,16,128]{2,1,0:T(8,128)(2,1)S(1)}, u32[]{:S(2)}, u32[]{:S(2)}) collective-permute-start(bf16[14,16,128]{2,1,0:T(8,128)(2,1)S(1)} %get-tuple-element.22.own_sources), channel_id=1, source_target_pairs={{0,4},{4,0},{1,5},{5,1},{2,6},{6,2},{3,7},{7,3},{8,12},{12,8},{9,1... | collective-permute-start | bytes 172040 | tf_op jit(solution)/shard_map/ppermute | solution.py:231
  14.3 8.0 %collective-permute-start.6 = (bf16[13,16,128]{2,1,0:T(8,128)(2,1)S(1)}, bf16[13,16,128]{2,1,0:T(8,128)(2,1)S(1)}, u32[]{:S(2)}, u32[]{:S(2)}) collective-permute-start(bf16[13,16,128]{2,1,0:T(8,128)(2,1)S(1)} %get-tuple-element.31), channel_id=1, source_target_pairs={{0,5},{1,6},{2,7},{3,4},{4,1},{5,2},{6,3},{7,0},{8,13},{9,14},{10,... | collective-permute-start | bytes 159752 | tf_op jit(solution)/shard_map/ppermute | solution.py:240
  18.1 5.0 %collective-permute-start.7 = (bf16[13,16,128]{2,1,0:T(8,128)(2,1)S(1)}, bf16[13,16,128]{2,1,0:T(8,128)(2,1)S(1)}, u32[]{:S(2)}, u32[]{:S(2)}) collective-permute-start(bf16[13,16,128]{2,1,0:T(8,128)(2,1)S(1)} %get-tuple-element.32), channel_id=1, source_target_pairs={{0,7},{1,4},{2,5},{3,6},{4,3},{5,0},{6,1},{7,2},{8,15},{9,12},{10,... | collective-permute-start | bytes 159752 | tf_op jit(solution)/shard_map/ppermute | solution.py:240

commit v17 on v16

--- a/solution.py
+++ b/solution.py
@@ -165,37 +165,40 @@
     return mine, [], None
 
 
+def pack(ref, spots, cells, picked):
+    runs = []
+    for at, (x, y) in enumerate(spots):
+        ref[at] = cells[x * EDGE + y]
+        if runs and runs[-1][0] == x and runs[-1][2] == y:
+            runs[-1][2] = y + 1
+        else:
+            runs.append([x, y, y + 1])
+    parts = [
+        picked[x * EDGE // ROWS][x * EDGE % ROWS + low : x * EDGE % ROWS + high]
+        for x, low, high in runs
+    ]
+    used = len(spots)
+    if used % ROWS:
+        parts.append(jnp.zeros((ROWS - used % ROWS, LANES), jnp.float32))
+    rows = jnp.concatenate(parts, axis=0).astype(jnp.bfloat16)
+    for tile in range(rows.shape[0] // ROWS):
+        ref[used + tile] = rows[tile * ROWS : (tile + 1) * ROWS]
+
+
 def messages_kernel(bit, before, entries, cells, mine, *refs):
-    others, (block, last, first, corner_low, corner_high) = refs[:-5], refs[-5:]
+    others, (sources, last, first, corner) = refs[:-4], refs[-4:]
     picked = chosen(entries, mine, others, bit)
-
-    def pack(ref, spots):
-        for at, (x, y) in enumerate(spots):
-            ref[at] = cells[x * EDGE + y]
-        used = len(spots)
-        runs = []
-        for x, y in spots:
-            if runs and runs[-1][0] == x and runs[-1][2] == y:
-                runs[-1][2] = y + 1
-            else:
-                runs.append([x, y, y + 1])
-        parts = [
-            picked[x * EDGE // ROWS][x * EDGE % ROWS + low : x * EDGE % ROWS + high]
-            for x, low, high in runs
-        ]
-        if used % ROWS:
-            parts.append(jnp.zeros((ROWS - used % ROWS, LANES), jnp.float32))
-        rows = jnp.concatenate(parts, axis=0).astype(jnp.bfloat16)
-        for tile in range(rows.shape[0] // ROWS):
-            ref[used + tile] = rows[tile * ROWS : (tile + 1) * ROWS]
-
-    for tile in range(block.shape[0]):
+    for tile in range(sources.shape[0]):
         rows = picked[tile] if tile < len(picked) else jnp.zeros((ROWS, LANES), jnp.float32)
-        block[tile] = rows.astype(jnp.bfloat16)
-    pack(last, [(x, y) for x in range(EDGE) for y in range(EDGE - HALO, EDGE)])
-    pack(first, [(x, y) for x in range(EDGE) for y in range(HALO)])
-    pack(corner_low, CORNER_LOW)
-    pack(corner_high, CORNER_HIGH)
+        sources[tile] = rows.astype(jnp.bfloat16)
+    pack(last, [(x, y) for x in range(EDGE) for y in range(EDGE - HALO, EDGE)], cells, picked)
+    pack(first, [(x, y) for x in range(EDGE) for y in range(HALO)], cells, picked)
+    pack(corner, CORNER_LOW, cells, picked)
+
+
+def corner_kernel(before, cells, sources, corner):
+    picked = [sources[tile].astype(jnp.float32) for tile in range(EDGE * EDGE // ROWS)]
+    pack(corner, CORNER_HIGH, cells, picked)
 
 
 def tiles(spots):
@@ -210,20 +213,27 @@
     entries = spread_out(jnp.stack([src_slot, src_owner]))
     mine, cells = prepare(entries, orbitals)
     mine, others, bit = gathered(entries, mine)
-    lengths = [EDGE * HALO] * 2 + [len(CORNER_LOW)] * 2
     modes, tails = sines(mine)
-    packed = pl.pallas_call(
+    lengths = [tiles(len(CORNER_LOW)) + 1] + [tiles(EDGE * HALO)] * 2 + [tiles(len(CORNER_LOW))]
+    any_space = pl.BlockSpec(memory_space=pl.ANY)
+    sources, last, first, low = pl.pallas_call(
         functools.partial(messages_kernel, bit),
-        out_shape=[
-            jax.ShapeDtypeStruct((length, ROWS, LANES), jnp.bfloat16)
-            for length in [tiles(len(CORNER_LOW)) + 1] + [tiles(length) for length in lengths]
-        ],
-        in_specs=[pl.BlockSpec(memory_space=pl.ANY)] + [VMEM] * (3 + len(others)),
-        out_specs=[VMEM] * 5,
+        out_shape=[jax.ShapeDtypeStruct((length, ROWS, LANES), jnp.bfloat16) for length in lengths],
+        in_specs=[any_space] + [VMEM] * (3 + len(others)),
+        out_specs=[VMEM] * 4,
         compiler_params=SMALL,
         name="messages",
     )(modes, entries, cells, mine, *others)
-    return cells, packed, modes, tails
+    beside = (cells, across_x(cells, cells.shape[0]))
+    high = pl.pallas_call(
+        corner_kernel,
+        out_shape=jax.ShapeDtypeStruct((tiles(len(CORNER_HIGH)), ROWS, LANES), jnp.bfloat16),
+        in_specs=[any_space] + [VMEM] * 2,
+        out_specs=VMEM,
+        compiler_params=SMALL,
+        name="corner",
+    )(beside[1], cells, sources)
+    return beside, (sources, last, first, low, high), modes, tails
 
 
 def across_x(tiles, used):
@@ -247,13 +257,12 @@
     return jnp.concatenate([back[:SPLIT], ahead[:SPLIT], rows], axis=0)
 
 
-def exchange(cells, sources, last, first, corner_low, corner_high):
-    beside = (cells, across_x(cells, cells.shape[0]))
+def exchange(sources, last, first, corner_low, corner_high):
     rows = (sources, across_x(sources, EDGE * EDGE // ROWS))
     below = lax.ppermute(last, "sy", ring("sy", 1))
     above = lax.ppermute(first, "sy", ring("sy", -1))
     low, high = across_corner(corner_low, 1), across_corner(corner_high, -1)
-    return beside, rows, (below, above, low, high)
+    return rows, (below, above, low, high)
 
 
 def place_of(x, y):
@@ -560,8 +569,8 @@
 
 
 def body(orbitals, src_owner, src_slot):
-    cells, packed, modes, tails = messages(orbitals, src_owner, src_slot)
-    return fields(*exchange(cells, *packed), modes, tails, src_slot.size)
+    beside, packed, modes, tails = messages(orbitals, src_owner, src_slot)
+    return fields(beside, *exchange(*packed), modes, tails, src_slot.size)
 
 
 def solution(mesh):

time: 27.3 us -> 25.7 us (0.941)
  waiting for transfers between devices: 6.93 us -> 3.45 us
  starting transfers between devices: 11.7 us -> 13.6 us
    ppermute x2, waiting for transfers between devices: 2.94 us -> 0.01 us  [across_x(): return lax.ppermute(tiles, 'sx', ring('sx', 1))]
    ppermute x2, starting transfers between devices: 2.84 us -> 4.78 us  [across_corner(): return lax.ppermute(cells, both, diagonal(1, step_y))]
    ppermute x2, waiting for transfers between devices: 0.86 us -> 0.31 us  [across_corner(): return lax.ppermute(cells, both, diagonal(1, step_y))]
  transfers between devices with their start and end apart: 8 -> 8, of which waited for: 4 -> 3; matrix products, arithmetic and copies ran while one was open for 0% -> 0% of each run, Pallas kernels for 9% -> 10%
where the time goes in v17:
time: 25.7 us; the launch traced here: 25.6 us
  starting transfers between devices  13.6 us (53%)
  Pallas kernels  6.77 us (26%)
  waiting for transfers between devices  3.45 us (13%)
  local copies, waits for them, and re-layouts  1.03 us (4%)
  other arithmetic  0.7 us (3%)
    ppermute x2, starting transfers between devices, across_corner(): return lax.ppermute(cells, both, diagonal(1, step_y))  4.78 us
    pallas_call x1, Pallas kernels, fields(): pl.pallas_call(fields_kernel, out_shape=jax.ShapeDtypeStruct(shape, jnp.f...  3.98 us
    ppermute x2, starting transfers between devices, across_x(): return lax.ppermute(tiles, 'sx', ring('sx', 1))  3.38 us
    ppermute x2, waiting for transfers between devices, gathered(): other = lax.ppermute(mine, 'orb', [(i, i ^ 1 << bit) for i in range(count)])  3.13 us
    ppermute x1, starting transfers between devices, exchange(): above = lax.ppermute(first, 'sy', ring('sy', -1))  2.25 us
    pallas_call x1, Pallas kernels, modes_of(): pl.pallas_call(modes_kernel, out_shape=[jax.ShapeDtypeStruct(shape, jnp.f...  2.2 us
    ppermute x1, starting transfers between devices, exchange(): below = lax.ppermute(last, 'sy', ring('sy', 1))  1.63 us
    ppermute x2, starting transfers between devices, gathered(): other = lax.ppermute(mine, 'orb', [(i, i ^ 1 << bit) for i in range(count)])  1.56 us
  transfers between devices with their start and end apart: 8, of which 3 were waited for; matrix products, arithmetic and copies ran while one was open for 0% of the time, Pallas kernels for 10%

profile of v17, /device:TPU:0, one launch (start us, length us, event | category | flops | bytes accessed | tf_op | source)
XLA Modules:
  0.0 25.6 jit_solution(7687157385394222999)
XLA Ops:
  0.0 0.7 %pad_add_fusion = s32[2,2,2]{2,1,0:T(2,128)S(1)} fusion(s32[1,2,2]{2,1,0:T(2,128)} %bitcast.2, s32[1,2,2]{2,1,0:T(2,128)} %bitcast.3), kind=kLoop, calls=%fused_computation | loop fusion | flops 8 | bytes 64 | tf_op jit(solution)/shard_map/stack | solution.py:213
  0.7 0.1 broadcast_in_dim.3.entries
  0.8 0.0 copy-start
  0.8 1.0 %copy-done = bf16[8,8,2048]{2,1,0:T(8,128)(2,1)S(1)} copy-done((bf16[8,8,2048]{2,1,0:T(8,128)(2,1)S(1)}, bf16[8,8,2048]{2,1,0:T(8,128)(2,1)}, u32[]{:S(2)}) %copy-start) | copy-done | bytes 262168
  1.7 0.2 prepare.1
  2.0 3.0 %collective-permute-start = (bf16[64,16,128]{2,1,0:T(8,128)(2,1)S(1)}, bf16[64,16,128]{2,1,0:T(8,128)(2,1)S(1)}, u32[]{:S(2)}, u32[]{:S(2)}) collective-permute-start(bf16[64,16,128]{2,1,0:T(8,128)(2,1)S(1)} %get-tuple-element.18.cells.own), channel_id=1, source_target_pairs={{0,4},{4,0},{1,5},{5,1},{2,6},{6,2},{3,7},{7,3},{8,12},{12,8},{9,1... | collective-permute-start | bytes 786440 | tf_op jit(solution)/shard_map/ppermute | solution.py:241
  5.0 0.0 collective-permute-start.1
  5.0 1.2 %collective-permute-done.1.other = bf16[4,16,128]{2,1,0:T(8,128)(2,1)S(1)} collective-permute-done((bf16[4,16,128]{2,1,0:T(8,128)(2,1)S(1)}, bf16[4,16,128]{2,1,0:T(8,128)(2,1)S(1)}, u32[]{:S(2)}, u32[]{:S(2)}) %collective-permute-start.1) | collective-permute-done | bytes 16416 | tf_op jit(solution)/shard_map/ppermute | solution.py:154
  6.2 1.6 %collective-permute-start.2 = (bf16[4,16,128]{2,1,0:T(8,128)(2,1)S(1)}, bf16[4,16,128]{2,1,0:T(8,128)(2,1)S(1)}, u32[]{:S(2)}, u32[]{:S(2)}) collective-permute-start(bf16[4,16,128]{2,1,0:T(8,128)(2,1)S(1)} %nearer.1.after.mine), channel_id=1, source_target_pairs={{0,16},{8,24},{16,0},{24,8},{1,17},{9,25},{17,1},{25,9},{2,18},{10... | collective-permute-start | bytes 49160 | tf_op jit(solution)/shard_map/ppermute | solution.py:154
  7.8 0.3 %sines.1 = (bf16[256,256]{1,0:T(8,128)(2,1)S(1)}, f32[4,8,128]{2,1,0:T(8,128)S(1)}) custom-call(bf16[4,16,128]{2,1,0:T(8,128)(2,1)S(1)} %nearer.1.after.mine), custom_call_target="tpu_custom_call" | custom-call | bytes 2097152 | tf_op jit(solution)/shard_map/sines/pallas_call | solution.py:302
  8.1 1.9 %collective-permute-done.2.refs_0_ = bf16[4,16,128]{2,1,0:T(8,128)(2,1)S(1)} collective-permute-done((bf16[4,16,128]{2,1,0:T(8,128)(2,1)S(1)}, bf16[4,16,128]{2,1,0:T(8,128)(2,1)S(1)}, u32[]{:S(2)}, u32[]{:S(2)}) %collective-permute-start.2) | collective-permute-done | bytes 16416 | tf_op jit(solution)/shard_map/ppermute | solution.py:154
  10.0 1.6 %collective-permute-start.4 = (bf16[34,16,128]{2,1,0:T(8,128)(2,1)S(1)}, bf16[34,16,128]{2,1,0:T(8,128)(2,1)S(1)}, u32[]{:S(2)}, u32[]{:S(2)}) collective-permute-start(bf16[34,16,128]{2,1,0:T(8,128)(2,1)S(1)} %get-tuple-element.28), channel_id=1, source_target_pairs={{0,1},{1,2},{2,3},{3,0},{4,5},{5,6},{6,7},{7,4},{8,9},{9,10},{10,1... | collective-permute-start | bytes 417800 | tf_op jit(solution)/shard_map/ppermute | solution.py:262
  11.7 2.2 %collective-permute-start.5 = (bf16[34,16,128]{2,1,0:T(8,128)(2,1)S(1)}, bf16[34,16,128]{2,1,0:T(8,128)(2,1)S(1)}, u32[]{:S(2)}, u32[]{:S(2)}) collective-permute-start(bf16[34,16,128]{2,1,0:T(8,128)(2,1)S(1)} %get-tuple-element.29), channel_id=1, source_target_pairs={{0,3},{1,0},{2,1},{3,2},{4,7},{5,4},{6,5},{7,6},{8,11},{9,8},{10,9... | collective-permute-start | bytes 417800 | tf_op jit(solution)/shard_map/ppermute | solution.py:263
  13.9 0.3 %collective-permute-start.3 = (bf16[14,16,128]{2,1,0:T(8,128)(2,1)S(1)}, bf16[14,16,128]{2,1,0:T(8,128)(2,1)S(1)}, u32[]{:S(2)}, u32[]{:S(2)}) collective-permute-start(bf16[14,16,128]{2,1,0:T(8,128)(2,1)S(1)} %get-tuple-element.21.own_sources.sources), channel_id=1, source_target_pairs={{0,4},{4,0},{1,5},{5,1},{2,6},{6,2},{3,7},{7,3},{8,12},{12,8},{9,1... | collective-permute-start | bytes 172040 | tf_op jit(solution)/shard_map/ppermute | solution.py:241
  14.3 0.9 %collective-permute-start.6 = (bf16[13,16,128]{2,1,0:T(8,128)(2,1)S(1)}, bf16[13,16,128]{2,1,0:T(8,128)(2,1)S(1)}, u32[]{:S(2)}, u32[]{:S(2)}) collective-permute-start(bf16[13,16,128]{2,1,0:T(8,128)(2,1)S(1)} %get-tuple-element.30), channel_id=1, source_target_pairs={{0,5},{1,6},{2,7},{3,4},{4,1},{5,2},{6,3},{7,0},{8,13},{9,14},{10,... | collective-permute-start | bytes 159752 | tf_op jit(solution)/shard_map/ppermute | solution.py:250
  15.2 0.0 collective-permute-done.across.before
  15.2 3.9 %collective-permute-start.7 = (bf16[13,16,128]{2,1,0:T(8,128)(2,1)S(1)}, bf16[13,16,128]{2,1,0:T(8,128)(2,1)S(1)}, u32[]{:S(2)}, u32[]{:S(2)}) collective-permute-start(bf16[13,16,128]{2,1,0:T(8,128)(2,1)S(1)} %corner.1), channel_id=1, source_target_pairs={{0,7},{1,4},{2,5},{3,6},{4,3},{5,0},{6,1},{7,2},{8,15},{9,12},{10,... | collective-permute-start | bytes 159752 | tf_op jit(solution)/shard_map/ppermute | solution.py:250
  19.1 0.0 collective-permute-done.3.sources
  19.1 2.2 %modes.1 = (f32[4,128,16,128]{3,2,1,0:T(8,128)S(1)}, f32[4,64,128]{2,1,0:T(8,128)S(1)}, f32[4,84,16,128]{3,2,1,0:T(8,128)S(1)}, f32[4,48,16,128]{3,2,1,0:T(8,128)S(1)}, f32[4,20,16,128]{3,2,1,0:T(8,128)S(1)}) custom-call(bf16[64,16,128]{2,1,0:T(8,128)(2,1)S(1)} %get-tuple-element.18.cells.own, bf16[64,16,128]{2,1,0:T(8,128)(2,1)S(1)} %collective-permute-done.across.before, ...), custom_call_target="tpu_custom_call" | custom-call | bytes 6291456 | tf_op jit(solution)/shard_map/modes/pallas_call | solution.py:451
  21.3 0.3 %collective-permute-done.6.refs_5_ = bf16[13,16,128]{2,1,0:T(8,128)(2,1)S(1)} collective-permute-done((bf16[13,16,128]{2,1,0:T(8,128)(2,1)S(1)}, bf16[13,16,128]{2,1,0:T(8,128)(2,1)S(1)}, u32[]{:S(2)}, u32[]{:S(2)}) %collective-permute-start.6) | collective-permute-done | bytes 53280 | tf_op jit(solution)/shard_map/ppermute | solution.py:250
  21.6 0.0 collective-permute-done.4.refs_3_
  21.6 0.0 collective-permute-done.5.refs_4_
  21.6 0.0 collective-permute-done.7.refs_6_
  21.6 4.0 %fields.1 = f32[8,8,2048]{2,1,0:T(8,128)} custom-call(f32[4,128,16,128]{3,2,1,0:T(8,128)S(1)} %get-tuple-element.23.beside, f32[4,64,128]{2,1,0:T(8,128)S(1)} %get-tuple-element.24.own_rows, f32[4,84,16,128]{3,2,1,0:T(8,128)S(1)} %get-tuple-element.25.refs_0_, f32[4,48,16,128]{3,2,1,0:T(8,128)S(1)} %get-tuple-element.26.refs_1_, ...), custom_call_target="tpu_custom_call" | custom-call | tf_op jit(solution)/shard_map/fields/pallas_call | solution.py:549
  (3 shorter events, 0.1 us)
Async XLA Ops:
  0.8 1.0 %copy-start = (bf16[8,8,2048]{2,1,0:T(8,128)(2,1)S(1)}, bf16[8,8,2048]{2,1,0:T(8,128)(2,1)}, u32[]{:S(2)}) copy-start(bf16[8,8,2048]{2,1,0:T(8,128)(2,1)} %orbitals.1) | copy-start | bytes 786436
  2.0 13.2 %collective-permute-start = (bf16[64,16,128]{2,1,0:T(8,128)(2,1)S(1)}, bf16[64,16,128]{2,1,0:T(8,128)(2,1)S(1)}, u32[]{:S(2)}, u32[]{:S(2)}) collective-permute-start(bf16[64,16,128]{2,1,0:T(8,128)(2,1)S(1)} %get-tuple-element.18.cells.own), channel_id=1, source_target_pairs={{0,4},{4,0},{1,5},{5,1},{2,6},{6,2},{3,7},{7,3},{8,12},{12,8},{9,1... | collective-permute-start | bytes 786440 | tf_op jit(solution)/shard_map/ppermute | solution.py:241
  5.0 1.2 %collective-permute-start.1 = (bf16[4,16,128]{2,1,0:T(8,128)(2,1)S(1)}, bf16[4,16,128]{2,1,0:T(8,128)(2,1)S(1)}, u32[]{:S(2)}, u32[]{:S(2)}) collective-permute-start(bf16[4,16,128]{2,1,0:T(8,128)(2,1)S(1)} %get-tuple-element.19.mine), channel_id=1, source_target_pairs={{0,8},{8,0},{16,24},{24,16},{1,9},{9,1},{17,25},{25,17},{2,10},{10... | collective-permute-start | bytes 49160 | tf_op jit(solution)/shard_map/ppermute | solution.py:154
  6.2 3.8 %collective-permute-start.2 = (bf16[4,16,128]{2,1,0:T(8,128)(2,1)S(1)}, bf16[4,16,128]{2,1,0:T(8,128)(2,1)S(1)}, u32[]{:S(2)}, u32[]{:S(2)}) collective-permute-start(bf16[4,16,128]{2,1,0:T(8,128)(2,1)S(1)} %nearer.1.after.mine), channel_id=1, source_target_pairs={{0,16},{8,24},{16,0},{24,8},{1,17},{9,25},{17,1},{25,9},{2,18},{10... | collective-permute-start | bytes 49160 | tf_op jit(solution)/shard_map/ppermute | solution.py:154
  10.0 11.5 %collective-permute-start.4 = (bf16[34,16,128]{2,1,0:T(8,128)(2,1)S(1)}, bf16[34,16,128]{2,1,0:T(8,128)(2,1)S(1)}, u32[]{:S(2)}, u32[]{:S(2)}) collective-permute-start(bf16[34,16,128]{2,1,0:T(8,128)(2,1)S(1)} %get-tuple-element.28), channel_id=1, source_target_pairs={{0,1},{1,2},{2,3},{3,0},{4,5},{5,6},{6,7},{7,4},{8,9},{9,10},{10,1... | collective-permute-start | bytes 417800 | tf_op jit(solution)/shard_map/ppermute | solution.py:262
  11.7 9.9 %collective-permute-start.5 = (bf16[34,16,128]{2,1,0:T(8,128)(2,1)S(1)}, bf16[34,16,128]{2,1,0:T(8,128)(2,1)S(1)}, u32[]{:S(2)}, u32[]{:S(2)}) collective-permute-start(bf16[34,16,128]{2,1,0:T(8,128)(2,1)S(1)} %get-tuple-element.29), channel_id=1, source_target_pairs={{0,3},{1,0},{2,1},{3,2},{4,7},{5,4},{6,5},{7,6},{8,11},{9,8},{10,9... | collective-permute-start | bytes 417800 | tf_op jit(solution)/shard_map/ppermute | solution.py:263
  13.9 5.1 %collective-permute-start.3 = (bf16[14,16,128]{2,1,0:T(8,128)(2,1)S(1)}, bf16[14,16,128]{2,1,0:T(8,128)(2,1)S(1)}, u32[]{:S(2)}, u32[]{:S(2)}) collective-permute-start(bf16[14,16,128]{2,1,0:T(8,128)(2,1)S(1)} %get-tuple-element.21.own_sources.sources), channel_id=1, source_target_pairs={{0,4},{4,0},{1,5},{5,1},{2,6},{6,2},{3,7},{7,3},{8,12},{12,8},{9,1... | collective-permute-start | bytes 172040 | tf_op jit(solution)/shard_map/ppermute | solution.py:241
  14.3 7.3 %collective-permute-start.6 = (bf16[13,16,128]{2,1,0:T(8,128)(2,1)S(1)}, bf16[13,16,128]{2,1,0:T(8,128)(2,1)S(1)}, u32[]{:S(2)}, u32[]{:S(2)}) collective-permute-start(bf16[13,16,128]{2,1,0:T(8,128)(2,1)S(1)} %get-tuple-element.30), channel_id=1, source_target_pairs={{0,5},{1,6},{2,7},{3,4},{4,1},{5,2},{6,3},{7,0},{8,13},{9,14},{10,... | collective-permute-start | bytes 159752 | tf_op jit(solution)/shard_map/ppermute | solution.py:250
  15.2 6.4 %collective-permute-start.7 = (bf16[13,16,128]{2,1,0:T(8,128)(2,1)S(1)}, bf16[13,16,128]{2,1,0:T(8,128)(2,1)S(1)}, u32[]{:S(2)}, u32[]{:S(2)}) collective-permute-start(bf16[13,16,128]{2,1,0:T(8,128)(2,1)S(1)} %corner.1), channel_id=1, source_target_pairs={{0,7},{1,4},{2,5},{3,6},{4,3},{5,0},{6,1},{7,2},{8,15},{9,12},{10,... | collective-permute-start | bytes 159752 | tf_op jit(solution)/shard_map/ppermute | solution.py:250
